TPU v7x, 256 devices: a whole 4x4x8 slice. The times are simulated.
256 devices in a mesh: dp: 32 (over x, z), cent: 8 (over y, core).
Axes of the slice: x: 4, y: 4, z: 8, core: 2. Of those that a mesh axis runs over, the one named last changes fastest.
Arguments:
- embeddings: bfloat16 [16384, 1024], P('dp'), may hold values from -20 to 20
- centroids: bfloat16 [32768, 1024], P(('cent', 'dp')), may hold values from -0.5 to 0.5
- masses: float32 [32768], P(('cent', 'dp')), may hold values from 0.05 to 2
Outputs:
- new_centroids: float32 [32768, 1024], P(('cent', 'dp'))
- new_masses: float32 [32768], P(('cent', 'dp'))
- row_energy: float32 [16384], P('dp')
All inputs are finite; a program needn't handle non-finite values.
Results may differ from a plain program's by a relative error of at most 0.0023.
Values may be sent and summed in bfloat16 or wider, within the bound.
No kernel may reach another device: no remote copies, remote signals or barrier semaphores. Data moves between devices by JAX's collectives and lax.ppermute only.
A program may use at most 128 MiB of HBM per device.

v0:
```python
import jax
import jax.numpy as jnp
from jax import lax
from jax.sharding import PartitionSpec as P


def local_pair(logits):
    local_high = jnp.max(logits, axis=1)
    local_total = jnp.sum(jnp.exp(logits - local_high[:, None]), axis=1)
    return (local_high, local_total)


def energy_cent(local_high, local_total):
    highest = lax.pmax(local_high, "cent")
    total = lax.psum(local_total * jnp.exp(local_high - highest), "cent")
    return highest + jnp.log(total)


def score_rows(rows, table):
    squares = jnp.sum(jnp.square(table.astype(jnp.float32)), axis=1)
    product = lax.dot_general(
        rows, table, (((1,), (1,)), ((), ())), preferred_element_type=jnp.float32
    )
    return 2.0 * product - squares[None, :]


def weighted(weights, rows):
    return lax.dot_general(
        weights.astype(jnp.bfloat16),
        rows,
        (((0,), (0,)), ((), ())),
        preferred_element_type=jnp.float32,
    )


def shards(embeddings, centroids, masses):
    logits = score_rows(embeddings, lax.all_gather(centroids, "dp", axis=0, tiled=True))
    local_high, local_total = local_pair(logits)
    row_energy = energy_cent(local_high, local_total)
    weights = jnp.exp(logits - row_energy[:, None])
    partial_counts = jnp.sum(weights, axis=0)
    partial_sums = weighted(weights, embeddings)
    sums, counts = (
        lax.psum_scatter(partial_sums, "dp", scatter_dimension=0, tiled=True),
        lax.psum_scatter(partial_counts, "dp", scatter_dimension=0, tiled=True),
    )
    new_masses = masses + counts
    new_centroids = (masses[:, None] * centroids.astype(jnp.float32) + sums) / new_masses[:, None]
    return (new_centroids, new_masses, row_energy)


def solution(mesh):
    in_specs = (P("dp", None), P(("cent", "dp"), None), P(("cent", "dp")))
    out_specs = (P(("cent", "dp"), None), P(("cent", "dp")), P("dp"))
    return jax.shard_map(shards, mesh=mesh, in_specs=in_specs, out_specs=out_specs, check_vma=False)
```

profile of v0, /device:TPU:1, one launch (start us, length us, event | category | flops | bytes accessed | tf_op | source)
XLA Modules:
  0.0 413.5 jit_solution(2382867540721738784)
XLA Ops:
  7.2 0.0 copy-start
  7.2 0.0 all-gather.2.cloned.1.call-start
  7.2 0.7 all-gather.2.cloned.1.call-update
  7.9 0.0 reduce-scatter.2.cloned.1.call-start
  8.0 104.4 %all-gather.2.cloned.1.call-done = bf16[4096,1024]{1,0:T(8,128)(2,1)} async-done(((bf16[128,1024]{1,0:T(8,128)(2,1)}), bf16[4096,1024]{1,0:T(8,128)(2,1)}) %all-gather.2.cloned.1.call-update) | async-done | bytes 8388624 | tf_op jit(solution)/shard_map/all_gather | solution.py:37
  112.3 0.0 copy-start.1
  112.3 5.2 %multiply_reduce_fusion = f32[4096]{0:T(1024)S(1)} fusion(bf16[4096,1024]{1,0:T(8,128)(2,1)} %all-gather.2.cloned.1.call-done), kind=kLoop, calls=%fused_computation | loop fusion | flops 12578816 | bytes 8404992 | tf_op jit(solution)/shard_map/reduce_sum | solution.py:20
  117.6 0.0 copy-done
  117.6 0.5 copy-done.1
  118.1 6.9 %fusion.5 = (f32[512]{0:T(512)S(1)}, f32[512,4096]{1,0:T(8,128)}) fusion(f32[4096]{0:T(1024)S(1)} %multiply_reduce_fusion, bf16[512,1024]{1,0:T(8,128)(2,1)S(1)} %copy-done, bf16[4096,1024]{1,0:T(8,128)(2,1)S(1)} %copy-done.1), kind=kOutput, calls=%fused_computation.12 | convolution fusion | flops 4301258240 | bytes 17844224 | tf_op jit(solution)/shard_map/dot_general | solution.py:21
  125.0 12.8 %pmax.7 = f32[512]{0:T(512)S(1)} all-reduce(f32[512]{0:T(512)S(1)} %get-tuple-element.3), channel_id=1, replica_groups=mesh['dp'=32,'cent'=8] {'cent'}, use_global_device_ids=true, to_apply=%region_2.0 | all-reduce | flops 512 | bytes 4096 | tf_op jit(solution)/shard_map/pmax | solution.py:14
  137.9 4.6 %exponential_reduce_fusion = f32[512]{0:T(512)S(1)} fusion(f32[512,4096]{1,0:T(8,128)} %get-tuple-element.4, f32[512]{0:T(512)S(1)} %get-tuple-element.3), kind=kLoop, calls=%fused_computation.2 | loop fusion | flops 4193792 | bytes 8392704 | tf_op jit(solution)/shard_map/reduce_sum | solution.py:9
  142.5 14.2 %psum.7 = f32[512]{0:T(512)S(1)} all-reduce(f32[512]{0:T(512)S(1)} %exponential_multiply_fusion), channel_id=1, replica_groups=mesh['dp'=32,'cent'=8] {'cent'}, use_global_device_ids=true, to_apply=%region_4.0 | all-reduce | flops 512 | bytes 4096 | tf_op jit(solution)/shard_map/psum | solution.py:15
  156.7 0.0 copy-start.3
  156.7 11.9 %fusion.2 = f32[4096,1024]{1,0:T(8,128)} fusion(bf16[512,1024]{1,0:T(8,128)(2,1)S(1)} %copy-done, f32[512,4096]{1,0:T(8,128)} %get-tuple-element.4, f32[512]{0:T(512)S(1)} %log_add_fusion), kind=kOutput, calls=%fused_computation.6 | convolution fusion | flops 4299161600 | bytes 26216448 | tf_op jit(solution)/shard_map/dot_general | solution.py:28
  168.6 0.0 copy-start.6
  168.7 0.0 reduce-scatter.2.cloned.1.call-update
  168.7 0.0 copy-start.4
  168.7 0.0 copy-start.2
  168.7 0.6 copy-done.6
  169.3 0.6 dynamic-slice
  170.6 0.0 copy-done.3
  170.6 4.7 %fusion = f32[4096]{0:T(1024)S(1)} fusion(f32[512,4096]{1,0:T(8,128)} %get-tuple-element.4, f32[512]{0:T(512)S(1)} %log_add_fusion), kind=kLoop, calls=%fused_computation.4 | loop fusion | flops 4190208 | bytes 8407040 | tf_op jit(solution)/shard_map/reduce_sum | solution.py:41
  175.3 112.5 %all-reduce = f32[4096]{0:T(1024)S(1)} all-reduce(f32[4096]{0:T(1024)S(1)} %fusion), channel_id=3, replica_groups=mesh['dp'=32,'cent'=8] {'dp'}, use_global_device_ids=true, to_apply=%region_7.0.clone | all-reduce | flops 4096 | bytes 32768
  287.9 0.0 copy-done.4
  287.9 0.1 dynamic-slice_add_fusion
  288.0 0.0 copy-start.5
  288.0 116.7 %reduce-scatter.2.cloned.1.call-done = f32[128,1024]{1,0:T(8,128)} async-done(((f32[4096,1024]{1,0:T(8,128)}), f32[128,1024]{1,0:T(8,128)}) %reduce-scatter.2.cloned.1.call-update) | async-done | bytes 524304 | tf_op jit(solution)/shard_map/reduce_scatter | solution.py:44
  404.7 0.0 copy-done.2
  404.7 2.0 add_divide_fusion
  406.7 0.0 copy-done.5
  (2 shorter events, 0.0 us)
Async XLA Ops:
  7.2 110.4 %copy-start = (bf16[512,1024]{1,0:T(8,128)(2,1)S(1)}, bf16[512,1024]{1,0:T(8,128)(2,1)}, u32[]{:S(2)}) copy-start(bf16[512,1024]{1,0:T(8,128)(2,1)} %param.3) | copy-start | bytes 3145732
  7.2 105.1 %all-gather.2.cloned.1.call-start = ((), (), s32[]{:S(2)}) async-start(), calls=%async_computation.1 | async-start | bytes 8650752 | tf_op jit(solution)/shard_map/all_gather | solution.py:37
  7.9 396.8 %reduce-scatter.2.cloned.1.call-start = ((), (), s32[]{:S(2)}) async-start(), calls=%async_computation.2 | async-start | bytes 17301504 | tf_op jit(solution)/shard_map/reduce_scatter | solution.py:44
  112.3 5.8 %copy-start.1 = (bf16[4096,1024]{1,0:T(8,128)(2,1)S(1)}, bf16[4096,1024]{1,0:T(8,128)(2,1)}, u32[]{:S(2)}) copy-start(bf16[4096,1024]{1,0:T(8,128)(2,1)} %all-gather.2.cloned.1.call-done) | copy-start | bytes 25165828
  156.7 13.9 %copy-start.3 = (f32[512]{0:T(512)}, f32[512]{0:T(512)S(1)}, u32[]{:S(2)}) copy-start(f32[512]{0:T(512)S(1)} %log_add_fusion) | copy-start | bytes 6148
  168.6 0.7 copy-start.6
  168.7 119.2 %copy-start.4 = (f32[128]{0:T(128)S(1)}, f32[128]{0:T(128)}, u32[]{:S(2)}) copy-start(f32[128]{0:T(128)} %param.5) | copy-start | bytes 1540
  168.7 236.0 %copy-start.2 = (bf16[128,1024]{1,0:T(8,128)(2,1)S(1)}, bf16[128,1024]{1,0:T(8,128)(2,1)}, u32[]{:S(2)}) copy-start(bf16[128,1024]{1,0:T(8,128)(2,1)} %param.4) | copy-start | bytes 786436
  288.0 118.7 %copy-start.5 = (f32[128]{0:T(128)}, f32[128]{0:T(128)S(1)}, u32[]{:S(2)}) copy-start(f32[128]{0:T(128)S(1)} %dynamic-slice_add_fusion) | copy-start | bytes 1540
Sparse Core Ops, SparseCore 0:
  10.6 101.6 all-gather.1
  168.8 235.8 reduce-scatter.1
where the time goes:
time: 417 us; the launch traced here: 414 us
  waiting for transfers between devices  222 us (53%)
  blocking collectives  140 us (34%)
  matrix products  18.9 us (5%)
  other arithmetic  16.7 us (4%)
  between operations  14.7 us (4%)
    reduce_scatter x1, waiting for transfers between devices, shards(): lax.psum_scatter(partial_sums, 'dp', scatter_dimension=0, tiled=True)  117 us
    unnamed x1, blocking collectives  113 us
    all_gather x1, waiting for transfers between devices, shards(): lax.all_gather(centroids, 'dp', axis=0, tiled=True)  104 us
    psum x1, blocking collectives, energy_cent(): total = lax.psum(local_total * jnp.exp(local_high - highest), 'cent')  14.2 us
    pmax x1, blocking collectives, energy_cent(): highest = lax.pmax(local_high, 'cent')  12.8 us
    dot_general x1, matrix products, weighted(): lax.dot_general(weights.astype(jnp.bfloat16), rows, (((0,), (0,)), ((), (...  11.9 us
  transfers between devices with their start and end apart: 2, of which 2 were waited for; matrix products, arithmetic and copies ran while one was open for 1% of the time, Pallas kernels for 0%

commit v1 on v0

v1 whole, which is shorter than its diff:
```python
import functools

import jax
import jax.numpy as jnp
from jax import lax
from jax.experimental import pallas as pl
from jax.experimental.pallas import tpu as pltpu
from jax.sharding import Mesh, PartitionSpec as P

NX, NZ, NY, NC = 4, 8, 4, 2
BF16, F32 = jnp.bfloat16, jnp.float32
TAIL = 16
ORDER = (2, 1, 3, 0)
VMEM_LIMIT = 30 * 1024 * 1024


def shift_x(value, by):
    return lax.ppermute(value, "x", [(i, (i + by) % NX) for i in range(NX)])


def swap_cores(value):
    return lax.ppermute(value, "c", [(0, 1), (1, 0)])


def along_z(value, by):
    pairs = []
    for z in range(NZ):
        pairs.append((z * NC, (z + by) % NZ * NC))
        pairs.append((z * NC + 1, (z - by) % NZ * NC + 1))
    return lax.ppermute(value, ("z", "c"), pairs)


def along_y(value, by):
    pairs = []
    for y in range(NY):
        pairs.append((y * NC, (y + by) % NY * NC))
        pairs.append((y * NC + 1, (y - by) % NY * NC + 1))
    return lax.ppermute(value, ("y", "c"), pairs)


def swap_halves(value):
    pairs = []
    for y in range(NY):
        pairs.append((y * NC, (y ^ 1) * NC))
        pairs.append((y * NC + 1, (y + 1 if y % 2 else y - 1) % NY * NC + 1))
    return lax.ppermute(value, ("y", "c"), pairs)


def pick(place, first, second):
    return jnp.where(place == 0, first, second)


def combine(parts):
    high = functools.reduce(jnp.maximum, parts)
    return high + jnp.log(sum(jnp.exp(p - high) for p in parts))


def energies(local, h, y, z, c):
    steps = [local[0]] + [pick(h, v, v[::-1]) for v in local[1:]]
    mine = jnp.concatenate([v.reshape(-1, v.shape[-1]) for v in steps])
    other = swap_cores(mine)

    def split(flat):
        out, at = [], 0
        for v in steps:
            n = v.shape[0] * v.shape[1]
            out.append(flat[at : at + n].reshape(v.shape))
            at += n
        return out

    back, ahead = split(pick(c, mine, other)), split(pick(c, other, mine))
    both = lambda k: jnp.concatenate([back[k], ahead[k]], axis=1)
    block = jnp.stack([both(0), ahead[1], ahead[2], ahead[3], both(4), back[3], back[2], back[1]])

    none = jnp.full_like(block, -1e30)
    parts = [pick(c, block, none)]
    for d in range(1, 4):
        got = along_z(block, d)
        parts.append(pick(c, jnp.roll(got, -d, axis=0), jnp.roll(got, d, axis=0)))
    parts.append(pick(c, jnp.roll(along_z(block, 4), 4, axis=0), none))
    part = combine(parts)
    block = combine([part, swap_cores(part)])

    parts = [pick(c, block, none), along_y(block, 1), pick(c, along_y(block, 2), none)]
    part = combine(parts)
    block = combine([part, swap_cores(part)])

    own = lambda v: pick(c, v[:, :1], v[:, 1:])
    out = [own(block[0])]
    for k in range(1, 4):
        v = pick(c, block[NZ - k], block[k])
        out.append(pick(h, v, v[::-1]))
    v = own(block[4])
    out.append(pick(h, v, v[::-1]))
    return jnp.concatenate([v.reshape(1, -1) for v in out], axis=1), block[0].reshape(-1)


def turned(column):
    n = column.shape[0]
    return jnp.transpose(jnp.broadcast_to(column, (n, n)))


def write_message(message, at, total, row):
    n, width = total.shape
    message[at : at + n, :] = total.astype(BF16)
    high = row.astype(BF16)
    tail = [high, (row - high.astype(F32)).astype(BF16)]
    if width > 2 * n:
        tail.append(jnp.zeros((TAIL, width - 2 * n), BF16))
    message[at + n : at + n + TAIL, :] = jnp.concatenate(tail, axis=1)


def read_message(message, at, n):
    total = message[at : at + n, :].astype(F32)
    tail = message[at + n : at + n + TAIL, :].astype(F32)
    return total, tail[:, :n] + tail[:, n : 2 * n]


def weigh_kernel(sizes, energy, *refs):
    pieces = len(sizes)
    logits, slab = refs[:pieces], refs[pieces : 2 * pieces]
    message, keep, keep_count = refs[2 * pieces :]
    n, width = keep.shape
    counts, sets, at = None, [], 0
    for p, size in enumerate(sizes):
        w = jnp.exp(logits[p][...] - energy[:, at : at + size])
        at += size
        for cut in range(0, size, sizes[-1]):
            part = w[:, cut : cut + sizes[-1]]
            counts = part if counts is None else counts + part
        sets.append(w.astype(BF16))
    column = jnp.sum(counts, axis=1, keepdims=True)
    tile = min(256, width)
    totals = []
    for at in range(0, width, tile):
        acc = None
        for p in range(pieces):
            if sizes[p] < sizes[1] and p == pieces - 1:
                continue
            w, rows = sets[p], slab[p][:, at : at + tile]
            if sizes[p] < sizes[1]:
                w = jnp.concatenate([w, sets[p + 1]], axis=1)
                rows = jnp.concatenate([rows, slab[p + 1][:, at : at + tile]])
            term = jnp.dot(w, rows, preferred_element_type=F32)
            acc = term if acc is None else acc + term
        keep[:, at : at + tile] = acc[:n]
        totals.append(acc[n:])
    keep_count[...] = turned(column[:n])[:TAIL]
    write_message(message, 0, jnp.concatenate(totals, axis=1), turned(column[n:])[:TAIL])


def weigh(first, count, logits, energy, slab):
    span, width = logits[0].shape[0] // NX, slab[0].shape[1]
    n = span // NC
    sizes = tuple(p.shape[0] for p in slab)
    block = lambda rows, cols: pl.BlockSpec((rows, cols), lambda i: (i, 0))
    whole = lambda v: pl.BlockSpec(v.shape, lambda i: (0, 0))
    return pl.pallas_call(
        functools.partial(weigh_kernel, sizes),
        grid=(count,),
        in_specs=[whole(energy)]
        + [pl.BlockSpec((span, p.shape[1]), lambda i: (i + first, 0)) for p in logits]
        + [whole(p) for p in slab],
        out_specs=(block(n + TAIL, width), block(n, width), block(TAIL, n)),
        out_shape=(
            jax.ShapeDtypeStruct((count * (n + TAIL), width), BF16),
            jax.ShapeDtypeStruct((count * n, width), F32),
            jax.ShapeDtypeStruct((count * TAIL, n), F32),
        ),
        compiler_params=pltpu.CompilerParams(vmem_limit_bytes=VMEM_LIMIT),
        cost_estimate=pl.CostEstimate(
            flops=2 * count * span * sum(sizes) * width,
            bytes_accessed=4 * count * span * sum(sizes) + 2 * sum(sizes) * width,
            transcendentals=count * span * sum(sizes),
        ),
    )(energy, *logits, *slab)


def call(kernel, out_shape, *args):
    return pl.pallas_call(
        kernel,
        out_shape=out_shape,
        compiler_params=pltpu.CompilerParams(vmem_limit_bytes=VMEM_LIMIT),
    )(*args)


def add_kernel(n, got, keep, keep_count, *messages):
    for i, message in enumerate(messages):
        total, row = read_message(got, i * (n + TAIL), n)
        total = total + keep[i * n : (i + 1) * n, :]
        write_message(message, 0, total, row + keep_count[i * TAIL : (i + 1) * TAIL, :])


def add(got, keep, keep_count):
    n = keep_count.shape[1]
    shape = jax.ShapeDtypeStruct((n + TAIL, got.shape[1]), BF16)
    return call(functools.partial(add_kernel, n), (shape,) * (NX - 1), got, keep, keep_count)


def update_kernel(n, keep, keep_count, got, one, two, three, masses, centroids, new_centroids, new_masses):
    total, row = keep[...], keep_count[...]
    for message in (got, one, two, three):
        t, r = read_message(message, 0, n)
        total, row = total + t, row + r
    mass = masses[...]
    new = mass + row[:1]
    new_masses[...] = new
    column = lambda v: jnp.transpose(jnp.broadcast_to(v, (n, n)))[:, :1]
    new_centroids[...] = (column(mass) * centroids[...].astype(F32) + total) / column(new)


def update(keep, keep_count, got, others, masses, centroids):
    n, width = centroids.shape
    out = (jax.ShapeDtypeStruct((n, width), F32), jax.ShapeDtypeStruct((1, n), F32))
    return call(
        functools.partial(update_kernel, n), out, keep, keep_count, got, *others, masses.reshape(1, n), centroids
    )


def shards(embeddings, centroids, masses):
    z, y, c = (lax.axis_index(a) for a in ("z", "y", "c"))
    rows, width = embeddings.shape
    half, sub = rows // 2, rows // 4
    h = lax.rem(y, 2)

    mine = lax.dynamic_slice_in_dim(embeddings, h * half, half, 0)
    stream = along_z(mine, 1)
    last = along_z(lax.dynamic_slice_in_dim(mine, c * sub, sub, 0), NZ // 2)
    own = lax.dynamic_slice_in_dim(embeddings.reshape(2, 2, sub, width), c, 1, 1).reshape(half, width)
    near = {d: shift_x(centroids, -d) for d in (1, 2, 3)}
    pieces = [own, stream, swap_halves(stream)]
    for step in range(2, NZ // 2):
        stream = along_z(stream, 1)
        pieces += [stream, swap_halves(stream)]
    pieces += [last, swap_halves(last)]

    near[0] = centroids
    mine = jnp.concatenate([near[d] for d in ORDER])
    other = swap_cores(mine)
    table = jnp.stack([mine.reshape(NX, -1, width), other.reshape(NX, -1, width)], axis=1).reshape(-1, width)
    squares = jnp.sum(jnp.square(table.astype(F32)), axis=1)[:, None]

    logits, local = [], []
    for piece in pieces:
        scores = 2.0 * lax.dot_general(table, piece, (((1,), (1,)), ((), ())), preferred_element_type=F32) - squares
        high = jnp.max(scores, axis=0)
        local.append(high + jnp.log(jnp.sum(jnp.exp(scores - high[None, :]), axis=0)))
        logits.append(scores)
    steps = [local[0].reshape(2, 1, sub)]
    steps += [jnp.stack(local[k : k + 2]).reshape(2, 2, sub) for k in (1, 3, 5)]
    steps += [jnp.stack(local[7:]).reshape(2, 1, sub)]
    energy, row_energy = energies(steps, h, y, z, c)

    message, keep, keep_count = weigh(0, NX - 1, logits, energy, pieces)
    sent = add(swap_cores(message), keep, keep_count)
    message, keep, keep_count = weigh(NX - 1, 1, logits, energy, pieces)
    others = [shift_x(m, d) for m, d in zip(sent, ORDER)]
    new_centroids, new_masses = update(keep, keep_count, swap_cores(message), others, masses, centroids)
    return new_centroids, new_masses.reshape(-1), row_energy


def solution(mesh):
    grid = Mesh(mesh.devices.reshape(NX, NZ, NY, NC), ("x", "z", "y", "c"))
    rows, cents = ("x", "z"), ("y", "c", "x", "z")
    return jax.shard_map(
        shards,
        mesh=grid,
        in_specs=(P(rows, None), P(cents, None), P(cents)),
        out_specs=(P(cents, None), P(cents), P(rows)),
        check_vma=False,
    )
```

time: 417 us -> 143 us (0.34)
  waiting for transfers between devices: 222 us -> 44.7 us
  blocking collectives: 140 us -> 0 us
  starting transfers between devices: 0.08 us -> 53.1 us
  local copies, waits for them, and re-layouts: 1.75 us -> 18.2 us
  between operations: 14.7 us -> 1.18 us
  other arithmetic: 16.7 us -> 5.33 us
  Pallas kernels: 0 us -> 9.28 us
  matrix products: 18.9 us -> 10.9 us
    reduce_scatter x1 -> x0, waiting for transfers between devices: 117 us -> none  [shards(): lax.psum_scatter(partial_sums, 'dp', scatter_dimension=0, tiled=True)]
    unnamed x1 -> x0, blocking collectives: 113 us -> none
    all_gather x1 -> x0, waiting for transfers between devices: 104 us -> none  [shards(): lax.all_gather(centroids, 'dp', axis=0, tiled=True)]
    ppermute x0 -> x26, starting transfers between devices: none -> 53.1 us  [the longest x8 24.4 us: along_z(): return lax.ppermute(value, ('z', 'c'), pairs)]
    ppermute x0 -> x26, waiting for transfers between devices: none -> 44.7 us  [the longest x6 15.7 us: shift_x(): return lax.ppermute(value, 'x', [(i, (i + by) % NX) for i in range(NX)])]
    unnamed x15 -> x70, local copies, waits for them, and re-layouts: 1.75 us -> 17.1 us
    psum x1 -> x0, blocking collectives: 14.2 us -> none  [energy_cent(): total = lax.psum(local_total * jnp.exp(local_high - highest), 'cent')]
    pmax x1 -> x0, blocking collectives: 12.8 us -> none  [energy_cent(): highest = lax.pmax(local_high, 'cent')]
  transfers between devices with their start and end apart: 2 -> 26, of which waited for: 2 -> 13; matrix products, arithmetic and copies ran while one was open for 1% -> 10% of each run, Pallas kernels for 0% -> 2%
where the time goes in v1:
time: 143 us
  starting transfers between devices  53.1 us (37%)
  waiting for transfers between devices  44.7 us (31%)
  local copies, waits for them, and re-layouts  18.2 us (13%)
  matrix products  10.9 us (8%)
  Pallas kernels  9.28 us (6%)
  other arithmetic  5.33 us (4%)
    ppermute x8, starting transfers between devices, along_z(): return lax.ppermute(value, ('z', 'c'), pairs)  24.4 us
    unnamed x70, local copies, waits for them, and re-layouts  17.1 us
    ppermute x6, waiting for transfers between devices, shift_x(): return lax.ppermute(value, 'x', [(i, (i + by) % NX) for i in range(NX)])  15.7 us
    ppermute x8, waiting for transfers between devices, along_z(): return lax.ppermute(value, ('z', 'c'), pairs)  15 us
    dot_general x9, matrix products, shards(): lax.dot_general(table, piece, (((1,), (1,)), ((), ())), preferred_element...  10.9 us
    ppermute x6, starting transfers between devices, shift_x(): return lax.ppermute(value, 'x', [(i, (i + by) % NX) for i in range(NX)])  10.5 us
    ppermute x4, starting transfers between devices, swap_halves(): return lax.ppermute(value, ('y', 'c'), pairs)  8.16 us
    pallas_call x2, Pallas kernels, weigh(): pl.pallas_call(functools.partial(weigh_kernel, sizes), grid=(count,), in_...  7.98 us
  transfers between devices with their start and end apart: 26, of which 13 were waited for; matrix products, arithmetic and copies ran while one was open for 10% of the time, Pallas kernels for 2%

profile of v1, /device:TPU:1, one launch (start us, length us, event | category | flops | bytes accessed | tf_op | source)
XLA Modules:
  0.0 142.7 jit_solution(17259165755571601833)
XLA Ops:
  0.7 3.7 %collective-permute-start = (bf16[128,1024]{1,0:T(8,128)(2,1)}, bf16[128,1024]{1,0:T(8,128)(2,1)}, u32[]{:S(2)}, u32[]{:S(2)}) collective-permute-start(bf16[128,1024]{1,0:T(8,128)(2,1)} %centroids.1), channel_id=1, source_target_pairs={{0,128},{64,192},{128,0},{192,64},{1,129},{65,193},{129,1},{193,65... | collective-permute-start | bytes 786440 | tf_op jit(solution)/shard_map/ppermute | solution.py:18
  5.8 5.7 %collective-permute-start.4 = (bf16[256,1024]{1,0:T(8,128)(2,1)S(1)}, bf16[256,1024]{1,0:T(8,128)(2,1)S(1)}, u32[]{:S(2)}, u32[]{:S(2)}) collective-permute-start(bf16[256,1024]{1,0:T(8,128)(2,1)S(1)} %constant_dynamic-slice_fusion.1), channel_id=1, source_target_pairs={{0,8},{1,57},{8,16},{9,1},{16,24},{17,9},{24,32},{25,17},{32,40},{... | collective-permute-start | bytes 1572872 | tf_op jit(solution)/shard_map/ppermute | solution.py:30
  12.5 3.9 %collective-permute-done.1 = bf16[128,1024]{1,0:T(8,128)(2,1)S(1)} collective-permute-done((bf16[128,1024]{1,0:T(8,128)(2,1)}, bf16[128,1024]{1,0:T(8,128)(2,1)S(1)}, u32[]{:S(2)}, u32[]{:S(2)}) %collective-permute-start.1) | collective-permute-done | bytes 262176 | tf_op jit(solution)/shard_map/ppermute | solution.py:18
  16.7 1.4 collective-permute-start.3
  18.1 5.4 %collective-permute-start.6 = (bf16[256,1024]{1,0:T(8,128)(2,1)S(1)}, bf16[256,1024]{1,0:T(8,128)(2,1)}, u32[]{:S(2)}, u32[]{:S(2)}) collective-permute-start(bf16[256,1024]{1,0:T(8,128)(2,1)S(1)} %collective-permute-done.4.refs_10_), channel_id=1, source_target_pairs={{0,8},{1,57},{8,16},{9,1},{16,24},{17,9},{24,32},{25,17},{32,40},{... | collective-permute-start | bytes 1572872 | tf_op jit(solution)/shard_map/ppermute | solution.py:30
  24.3 1.4 %collective-permute-start.10 = (bf16[128,1024]{1,0:T(8,128)(2,1)}, bf16[128,1024]{1,0:T(8,128)(2,1)S(1)}, u32[]{:S(2)}, u32[]{:S(2)}) collective-permute-start(bf16[128,1024]{1,0:T(8,128)(2,1)} %constant_dynamic-slice_fusion), channel_id=1, source_target_pairs={{0,32},{1,33},{8,40},{9,41},{16,48},{17,49},{24,56},{25,57},{32,0}... | collective-permute-start | bytes 786440 | tf_op jit(solution)/shard_map/ppermute | solution.py:30
  25.8 13.4 %collective-permute-done.10.refs_16_ = bf16[128,1024]{1,0:T(8,128)(2,1)S(1)} collective-permute-done((bf16[128,1024]{1,0:T(8,128)(2,1)}, bf16[128,1024]{1,0:T(8,128)(2,1)S(1)}, u32[]{:S(2)}, u32[]{:S(2)}) %collective-permute-start.10) | collective-permute-done | bytes 262176 | tf_op jit(solution)/shard_map/ppermute | solution.py:30
  39.2 2.7 %collective-permute-start.11 = (bf16[128,1024]{1,0:T(8,128)(2,1)S(1)}, bf16[128,1024]{1,0:T(8,128)(2,1)S(1)}, u32[]{:S(2)}, u32[]{:S(2)}) collective-permute-start(bf16[128,1024]{1,0:T(8,128)(2,1)S(1)} %collective-permute-done.10.refs_16_), channel_id=1, source_target_pairs={{0,2},{1,7},{2,0},{3,5},{4,6},{5,3},{6,4},{7,1},{8,10},{9,15},{10,... | collective-permute-start | bytes 786440 | tf_op jit(solution)/shard_map/ppermute | solution.py:46
  41.9 2.6 %collective-permute-start.7 = (bf16[256,1024]{1,0:T(8,128)(2,1)}, bf16[256,1024]{1,0:T(8,128)(2,1)}, u32[]{:S(2)}, u32[]{:S(2)}) collective-permute-start(bf16[256,1024]{1,0:T(8,128)(2,1)} %collective-permute-done.6.refs_12_), channel_id=1, source_target_pairs={{0,2},{1,7},{2,0},{3,5},{4,6},{5,3},{6,4},{7,1},{8,10},{9,15},{10,... | collective-permute-start | bytes 1572872 | tf_op jit(solution)/shard_map/ppermute | solution.py:46
  44.6 2.6 %collective-permute-start.8 = (bf16[256,1024]{1,0:T(8,128)(2,1)}, bf16[256,1024]{1,0:T(8,128)(2,1)}, u32[]{:S(2)}, u32[]{:S(2)}) collective-permute-start(bf16[256,1024]{1,0:T(8,128)(2,1)} %collective-permute-done.6.refs_12_), channel_id=1, source_target_pairs={{0,8},{1,57},{8,16},{9,1},{16,24},{17,9},{24,32},{25,17},{32,40},{... | collective-permute-start | bytes 1572872 | tf_op jit(solution)/shard_map/ppermute | solution.py:30
  47.2 1.7 %multiply_reduce_fusion = f32[4,2,128]{2,1,0:T(2,128)S(1)} fusion(bf16[4,1,128,1024]{3,2,1,0:T(8,128)(2,1)} %bitcast.1, bf16[4,1,128,1024]{3,2,1,0:T(8,128)(2,1)S(1)} %bitcast.118), kind=kLoop, calls=%fused_computation | loop fusion | flops 4193280 | bytes 2101248 | tf_op jit(solution)/shard_map/reduce_sum | solution.py:241
  48.9 1.4 pad_maximum_fusion
  57.2 2.6 %fusion.29 = (f32[256]{0:T(256)S(1)}, f32[1024,256]{1,0:T(8,128)S(1)}) fusion(f32[1024]{0:T(1024)S(1)} %bitcast.125, bf16[1024,1024]{1,0:T(8,128)(2,1)} %bitcast.114, bf16[256,1024]{1,0:T(8,128)(2,1)} %collective-permute-done.6.refs_12_), kind=kOutput, calls=%fused_computation.103 | convolution fusion | flops 537657088 | bytes 3675136 | tf_op jit(solution)/shard_map/dot_general | solution.py:245
  60.0 1.9 %fusion.28 = (f32[256]{0:T(256)S(1)}, f32[1024,256]{1,0:T(8,128)S(1)}) fusion(f32[1024]{0:T(1024)S(1)} %bitcast.126, bf16[1024,1024]{1,0:T(8,128)(2,1)S(1)} %bitcast.115, bf16[256,1024]{1,0:T(8,128)(2,1)} %collective-permute-done.7.refs_13_), kind=kOutput, calls=%fused_computation.102 | convolution fusion | flops 537657088 | bytes 3675136 | tf_op jit(solution)/shard_map/dot_general | solution.py:245
  62.2 1.9 %fusion.31 = (f32[256]{0:T(256)S(1)}, f32[1024,256]{1,0:T(8,128)S(1)}) fusion(f32[1024]{0:T(1024)S(1)} %bitcast.127, bf16[1024,1024]{1,0:T(8,128)(2,1)S(1)} %bitcast.116, bf16[256,1024]{1,0:T(8,128)(2,1)} %collective-permute-done.8.refs_14_), kind=kOutput, calls=%fused_computation.105 | convolution fusion | flops 537657088 | bytes 3675136 | tf_op jit(solution)/shard_map/dot_general | solution.py:245
  64.4 2.7 %collective-permute-start.9 = (bf16[256,1024]{1,0:T(8,128)(2,1)}, bf16[256,1024]{1,0:T(8,128)(2,1)S(1)}, u32[]{:S(2)}, u32[]{:S(2)}) collective-permute-start(bf16[256,1024]{1,0:T(8,128)(2,1)} %collective-permute-done.8.refs_14_), channel_id=1, source_target_pairs={{0,2},{1,7},{2,0},{3,5},{4,6},{5,3},{6,4},{7,1},{8,10},{9,15},{10,... | collective-permute-start | bytes 1572872 | tf_op jit(solution)/shard_map/ppermute | solution.py:46
  67.1 6.8 %collective-permute-done.9.refs_15_ = bf16[256,1024]{1,0:T(8,128)(2,1)S(1)} collective-permute-done((bf16[256,1024]{1,0:T(8,128)(2,1)}, bf16[256,1024]{1,0:T(8,128)(2,1)S(1)}, u32[]{:S(2)}, u32[]{:S(2)}) %collective-permute-start.9) | collective-permute-done | bytes 524320 | tf_op jit(solution)/shard_map/ppermute | solution.py:46
  76.1 1.7 %collective-permute-start.12 = (f32[16,128]{1,0:T(8,128)S(1)}, f32[16,128]{1,0:T(8,128)S(1)}, u32[]{:S(2)}, u32[]{:S(2)}) collective-permute-start(f32[16,128]{1,0:T(8,128)S(1)} %concatenate.47), channel_id=1, source_target_pairs={{0,1},{1,0},{2,3},{3,2},{4,5},{5,4},{6,7},{7,6},{8,9},{9,8},{10,11... | collective-permute-start | bytes 24584 | tf_op jit(solution)/shard_map/ppermute | solution.py:22
  78.8 3.1 %collective-permute-start.15 = (f32[8,2,2,128]{3,0,2,1:T(8,128)S(1)}, f32[8,2,2,128]{3,0,2,1:T(8,128)S(1)}, u32[]{:S(2)}, u32[]{:S(2)}) collective-permute-start(f32[8,2,2,128]{3,0,2,1:T(8,128)S(1)} %stack.39), channel_id=1, source_target_pairs={{0,24},{1,41},{8,32},{9,49},{16,40},{17,57},{24,48},{25,1},{32,56}... | collective-permute-start | bytes 49160 | tf_op jit(solution)/shard_map/ppermute | solution.py:30
  81.9 4.0 %collective-permute-start.16 = (f32[8,2,2,128]{3,0,2,1:T(8,128)S(1)}, f32[8,2,2,128]{3,0,2,1:T(8,128)S(1)}, u32[]{:S(2)}, u32[]{:S(2)}) collective-permute-start(f32[8,2,2,128]{3,0,2,1:T(8,128)S(1)} %stack.39), channel_id=1, source_target_pairs={{0,32},{1,33},{8,40},{9,41},{16,48},{17,49},{24,56},{25,57},{32,0}... | collective-permute-start | bytes 49160 | tf_op jit(solution)/shard_map/ppermute | solution.py:30
  86.7 1.4 collective-permute-start.13
  88.1 1.6 %collective-permute-done.14 = f32[8,2,2,128]{3,0,2,1:T(8,128)S(1)} collective-permute-done((f32[8,2,2,128]{3,0,2,1:T(8,128)S(1)}, f32[8,2,2,128]{3,0,2,1:T(8,128)S(1)}, u32[]{:S(2)}, u32[]{:S(2)}) %collective-permute-start.14) | collective-permute-done | bytes 16416 | tf_op jit(solution)/shard_map/ppermute | solution.py:30
  89.8 3.4 %collective-permute-start.17 = (f32[8,2,2,128]{3,0,2,1:T(8,128)S(1)}, f32[8,2,2,128]{3,0,2,1:T(8,128)S(1)}, u32[]{:S(2)}, u32[]{:S(2)}) collective-permute-start(f32[8,2,2,128]{3,0,2,1:T(8,128)S(1)} %log_add_fusion.3), channel_id=1, source_target_pairs={{0,1},{1,0},{2,3},{3,2},{4,5},{5,4},{6,7},{7,6},{8,9},{9,8},{10,11... | collective-permute-start | bytes 49160 | tf_op jit(solution)/shard_map/ppermute | solution.py:22
  94.1 2.7 %collective-permute-start.18 = (f32[8,2,2,128]{3,0,2,1:T(8,128)S(1)}, f32[8,2,2,128]{3,0,2,1:T(8,128)S(1)}, u32[]{:S(2)}, u32[]{:S(2)}) collective-permute-start(f32[8,2,2,128]{3,0,2,1:T(8,128)S(1)} %log_add_fusion.2), channel_id=1, source_target_pairs={{0,2},{1,7},{2,4},{3,1},{4,6},{5,3},{6,0},{7,5},{8,10},{9,15},{10,... | collective-permute-start | bytes 49160 | tf_op jit(solution)/shard_map/ppermute | solution.py:38
  97.7 3.2 %collective-permute-done.19 = f32[8,2,2,128]{3,0,2,1:T(8,128)S(1)} collective-permute-done((f32[8,2,2,128]{3,0,2,1:T(8,128)S(1)}, f32[8,2,2,128]{3,0,2,1:T(8,128)S(1)}, u32[]{:S(2)}, u32[]{:S(2)}) %collective-permute-start.19) | collective-permute-done | bytes 16416 | tf_op jit(solution)/shard_map/ppermute | solution.py:38
  106.1 1.2 copy-done.8
  115.8 5.3 %shard_map.59 = (bf16[432,1024]{1,0:T(8,128)(2,1)S(1)}, f32[384,1024]{1,0:T(8,128)S(1)}, f32[48,128]{1,0:T(8,128)S(1)}) custom-call(f32[1,2048]{1,0:T(1,128)S(1)} %constant_dynamic-update-slice_fusion.4.energy, f32[1024,256]{1,0:T(8,128)S(1)} %get-tuple-element.59.refs_0_, f32[1024,256]{1,0:T(8,128)S(1)} %copy-done.2, ...), custom_call_target="tpu_custom_call" | custom-call | flops 3221225472 | bytes 10485760 | tf_op jit(solution)/shard_map/pallas_call | solution.py:158
  121.4 2.7 %shard_map.58 = (bf16[144,1024]{1,0:T(8,128)(2,1)S(1)}, f32[128,1024]{1,0:T(8,128)S(1)}, f32[16,128]{1,0:T(8,128)S(1)}) custom-call(f32[1,2048]{1,0:T(1,128)S(1)} %constant_dynamic-update-slice_fusion.4.energy, f32[1024,256]{1,0:T(8,128)S(1)} %get-tuple-element.59.refs_0_, f32[1024,256]{1,0:T(8,128)S(1)} %copy-done.2, ...), custom_call_target="tpu_custom_call" | custom-call | flops 1073741824 | bytes 6291456 | tf_op jit(solution)/shard_map/pallas_call | solution.py:158
  124.7 2.7 %collective-permute-start.23 = (bf16[144,1024]{1,0:T(8,128)(2,1)S(1)}, bf16[144,1024]{1,0:T(8,128)(2,1)S(1)}, u32[]{:S(2)}, u32[]{:S(2)}) collective-permute-start(bf16[144,1024]{1,0:T(8,128)(2,1)S(1)} %get-tuple-element.20), channel_id=1, source_target_pairs={{0,128},{64,192},{128,0},{192,64},{1,129},{65,193},{129,1},{193,65... | collective-permute-start | bytes 884744 | tf_op jit(solution)/shard_map/ppermute | solution.py:18
  127.7 2.3 %collective-permute-start.25 = (bf16[144,1024]{1,0:T(8,128)(2,1)S(1)}, bf16[144,1024]{1,0:T(8,128)(2,1)S(1)}, u32[]{:S(2)}, u32[]{:S(2)}) collective-permute-start(bf16[144,1024]{1,0:T(8,128)(2,1)S(1)} %get-tuple-element.22), channel_id=1, source_target_pairs={{0,192},{64,0},{128,64},{192,128},{1,193},{65,1},{129,65},{193,129... | collective-permute-start | bytes 884744 | tf_op jit(solution)/shard_map/ppermute | solution.py:18
  130.0 4.8 %collective-permute-done.23.one = bf16[144,1024]{1,0:T(8,128)(2,1)S(1)} collective-permute-done((bf16[144,1024]{1,0:T(8,128)(2,1)S(1)}, bf16[144,1024]{1,0:T(8,128)(2,1)S(1)}, u32[]{:S(2)}, u32[]{:S(2)}) %collective-permute-start.23) | collective-permute-done | bytes 294944 | tf_op jit(solution)/shard_map/ppermute | solution.py:18
  134.8 6.8 %collective-permute-done.24.two = bf16[144,1024]{1,0:T(8,128)(2,1)S(1)} collective-permute-done((bf16[144,1024]{1,0:T(8,128)(2,1)S(1)}, bf16[144,1024]{1,0:T(8,128)(2,1)S(1)}, u32[]{:S(2)}, u32[]{:S(2)}) %collective-permute-start.24) | collective-permute-done | bytes 294944 | tf_op jit(solution)/shard_map/ppermute | solution.py:18
  (165 shorter events, 32.7 us)
Async XLA Ops:
  0.6 16.0 %copy-start.26 = (bf16[128,1024]{1,0:T(8,128)(2,1)S(1)}, bf16[128,1024]{1,0:T(8,128)(2,1)}, u32[]{:S(2)}) copy-start(bf16[128,1024]{1,0:T(8,128)(2,1)} %centroids.1) | copy-start | bytes 786436
  0.7 10.8 %collective-permute-start = (bf16[128,1024]{1,0:T(8,128)(2,1)}, bf16[128,1024]{1,0:T(8,128)(2,1)}, u32[]{:S(2)}, u32[]{:S(2)}) collective-permute-start(bf16[128,1024]{1,0:T(8,128)(2,1)} %centroids.1), channel_id=1, source_target_pairs={{0,128},{64,192},{128,0},{192,64},{1,129},{65,193},{129,1},{193,65... | collective-permute-start | bytes 786440 | tf_op jit(solution)/shard_map/ppermute | solution.py:18
  4.3 12.0 %collective-permute-start.1 = (bf16[128,1024]{1,0:T(8,128)(2,1)}, bf16[128,1024]{1,0:T(8,128)(2,1)S(1)}, u32[]{:S(2)}, u32[]{:S(2)}) collective-permute-start(bf16[128,1024]{1,0:T(8,128)(2,1)} %centroids.1), channel_id=1, source_target_pairs={{0,192},{64,0},{128,64},{192,128},{1,193},{65,1},{129,65},{193,129... | collective-permute-start | bytes 786440 | tf_op jit(solution)/shard_map/ppermute | solution.py:18
  5.2 11.5 %collective-permute-start.2 = (bf16[128,1024]{1,0:T(8,128)(2,1)}, bf16[128,1024]{1,0:T(8,128)(2,1)S(1)}, u32[]{:S(2)}, u32[]{:S(2)}) collective-permute-start(bf16[128,1024]{1,0:T(8,128)(2,1)} %centroids.1), channel_id=1, source_target_pairs={{0,64},{64,128},{128,192},{192,0},{1,65},{65,129},{129,193},{193,1... | collective-permute-start | bytes 786440 | tf_op jit(solution)/shard_map/ppermute | solution.py:18
  5.8 12.3 %collective-permute-start.4 = (bf16[256,1024]{1,0:T(8,128)(2,1)S(1)}, bf16[256,1024]{1,0:T(8,128)(2,1)S(1)}, u32[]{:S(2)}, u32[]{:S(2)}) collective-permute-start(bf16[256,1024]{1,0:T(8,128)(2,1)S(1)} %constant_dynamic-slice_fusion.1), channel_id=1, source_target_pairs={{0,8},{1,57},{8,16},{9,1},{16,24},{17,9},{24,32},{25,17},{32,40},{... | collective-permute-start | bytes 1572872 | tf_op jit(solution)/shard_map/ppermute | solution.py:30
  16.7 30.5 %collective-permute-start.3 = (bf16[512,1024]{1,0:T(8,128)(2,1)S(1)}, bf16[512,1024]{1,0:T(8,128)(2,1)}, u32[]{:S(2)}, u32[]{:S(2)}) collective-permute-start(bf16[512,1024]{1,0:T(8,128)(2,1)S(1)} %constant_dynamic-update-slice_fusion), channel_id=1, source_target_pairs={{0,1},{1,0},{2,3},{3,2},{4,5},{5,4},{6,7},{7,6},{8,9},{9,8},{10,11... | collective-permute-start | bytes 3145736 | tf_op jit(solution)/shard_map/ppermute | solution.py:22
  18.1 32.2 %copy-start.19 = (bf16[256,1024]{1,0:T(8,128)(2,1)}, bf16[256,1024]{1,0:T(8,128)(2,1)S(1)}, u32[]{:S(2)}) copy-start(bf16[256,1024]{1,0:T(8,128)(2,1)S(1)} %collective-permute-done.4.refs_10_) | copy-start | bytes 1572868
  18.1 23.8 %collective-permute-start.6 = (bf16[256,1024]{1,0:T(8,128)(2,1)S(1)}, bf16[256,1024]{1,0:T(8,128)(2,1)}, u32[]{:S(2)}, u32[]{:S(2)}) collective-permute-start(bf16[256,1024]{1,0:T(8,128)(2,1)S(1)} %collective-permute-done.4.refs_10_), channel_id=1, source_target_pairs={{0,8},{1,57},{8,16},{9,1},{16,24},{17,9},{24,32},{25,17},{32,40},{... | collective-permute-start | bytes 1572872 | tf_op jit(solution)/shard_map/ppermute | solution.py:30
  24.3 14.9 %collective-permute-start.10 = (bf16[128,1024]{1,0:T(8,128)(2,1)}, bf16[128,1024]{1,0:T(8,128)(2,1)S(1)}, u32[]{:S(2)}, u32[]{:S(2)}) collective-permute-start(bf16[128,1024]{1,0:T(8,128)(2,1)} %constant_dynamic-slice_fusion), channel_id=1, source_target_pairs={{0,32},{1,33},{8,40},{9,41},{16,48},{17,49},{24,56},{25,57},{32,0}... | collective-permute-start | bytes 786440 | tf_op jit(solution)/shard_map/ppermute | solution.py:30
  25.8 24.6 %copy-start.15 = (bf16[2,1,128,1024]{3,2,1,0:T(8,128)(2,1)}, bf16[2,1,128,1024]{3,2,1,0:T(8,128)(2,1)S(1)}, u32[]{:S(2)}) copy-start(bf16[2,1,128,1024]{3,2,1,0:T(8,128)(2,1)S(1)} %constant_dynamic-slice_fusion.2) | copy-start | bytes 1572868
  39.2 14.6 %collective-permute-start.11 = (bf16[128,1024]{1,0:T(8,128)(2,1)S(1)}, bf16[128,1024]{1,0:T(8,128)(2,1)S(1)}, u32[]{:S(2)}, u32[]{:S(2)}) collective-permute-start(bf16[128,1024]{1,0:T(8,128)(2,1)S(1)} %collective-permute-done.10.refs_16_), channel_id=1, source_target_pairs={{0,2},{1,7},{2,0},{3,5},{4,6},{5,3},{6,4},{7,1},{8,10},{9,15},{10,... | collective-permute-start | bytes 786440 | tf_op jit(solution)/shard_map/ppermute | solution.py:46
  41.9 9.8 %collective-permute-start.5 = (bf16[256,1024]{1,0:T(8,128)(2,1)S(1)}, bf16[256,1024]{1,0:T(8,128)(2,1)S(1)}, u32[]{:S(2)}, u32[]{:S(2)}) collective-permute-start(bf16[256,1024]{1,0:T(8,128)(2,1)S(1)} %collective-permute-done.4.refs_10_), channel_id=1, source_target_pairs={{0,2},{1,7},{2,0},{3,5},{4,6},{5,3},{6,4},{7,1},{8,10},{9,15},{10,... | collective-permute-start | bytes 1572872 | tf_op jit(solution)/shard_map/ppermute | solution.py:46
  41.9 18.1 %collective-permute-start.7 = (bf16[256,1024]{1,0:T(8,128)(2,1)}, bf16[256,1024]{1,0:T(8,128)(2,1)}, u32[]{:S(2)}, u32[]{:S(2)}) collective-permute-start(bf16[256,1024]{1,0:T(8,128)(2,1)} %collective-permute-done.6.refs_12_), channel_id=1, source_target_pairs={{0,2},{1,7},{2,0},{3,5},{4,6},{5,3},{6,4},{7,1},{8,10},{9,15},{10,... | collective-permute-start | bytes 1572872 | tf_op jit(solution)/shard_map/ppermute | solution.py:46
  44.6 17.6 %collective-permute-start.8 = (bf16[256,1024]{1,0:T(8,128)(2,1)}, bf16[256,1024]{1,0:T(8,128)(2,1)}, u32[]{:S(2)}, u32[]{:S(2)}) collective-permute-start(bf16[256,1024]{1,0:T(8,128)(2,1)} %collective-permute-done.6.refs_12_), channel_id=1, source_target_pairs={{0,8},{1,57},{8,16},{9,1},{16,24},{17,9},{24,32},{25,17},{32,40},{... | collective-permute-start | bytes 1572872 | tf_op jit(solution)/shard_map/ppermute | solution.py:30
  64.4 9.5 %collective-permute-start.9 = (bf16[256,1024]{1,0:T(8,128)(2,1)}, bf16[256,1024]{1,0:T(8,128)(2,1)S(1)}, u32[]{:S(2)}, u32[]{:S(2)}) collective-permute-start(bf16[256,1024]{1,0:T(8,128)(2,1)} %collective-permute-done.8.refs_14_), channel_id=1, source_target_pairs={{0,2},{1,7},{2,0},{3,5},{4,6},{5,3},{6,4},{7,1},{8,10},{9,15},{10,... | collective-permute-start | bytes 1572872 | tf_op jit(solution)/shard_map/ppermute | solution.py:46
  76.1 2.6 %collective-permute-start.12 = (f32[16,128]{1,0:T(8,128)S(1)}, f32[16,128]{1,0:T(8,128)S(1)}, u32[]{:S(2)}, u32[]{:S(2)}) collective-permute-start(f32[16,128]{1,0:T(8,128)S(1)} %concatenate.47), channel_id=1, source_target_pairs={{0,1},{1,0},{2,3},{3,2},{4,5},{5,4},{6,7},{7,6},{8,9},{9,8},{10,11... | collective-permute-start | bytes 24584 | tf_op jit(solution)/shard_map/ppermute | solution.py:22
  78.8 9.3 %collective-permute-start.15 = (f32[8,2,2,128]{3,0,2,1:T(8,128)S(1)}, f32[8,2,2,128]{3,0,2,1:T(8,128)S(1)}, u32[]{:S(2)}, u32[]{:S(2)}) collective-permute-start(f32[8,2,2,128]{3,0,2,1:T(8,128)S(1)} %stack.39), channel_id=1, source_target_pairs={{0,24},{1,41},{8,32},{9,49},{16,40},{17,57},{24,48},{25,1},{32,56}... | collective-permute-start | bytes 49160 | tf_op jit(solution)/shard_map/ppermute | solution.py:30
  81.9 7.9 %collective-permute-start.16 = (f32[8,2,2,128]{3,0,2,1:T(8,128)S(1)}, f32[8,2,2,128]{3,0,2,1:T(8,128)S(1)}, u32[]{:S(2)}, u32[]{:S(2)}) collective-permute-start(f32[8,2,2,128]{3,0,2,1:T(8,128)S(1)} %stack.39), channel_id=1, source_target_pairs={{0,32},{1,33},{8,40},{9,41},{16,48},{17,49},{24,56},{25,57},{32,0}... | collective-permute-start | bytes 49160 | tf_op jit(solution)/shard_map/ppermute | solution.py:30
  85.9 3.8 %collective-permute-start.14 = (f32[8,2,2,128]{3,0,2,1:T(8,128)S(1)}, f32[8,2,2,128]{3,0,2,1:T(8,128)S(1)}, u32[]{:S(2)}, u32[]{:S(2)}) collective-permute-start(f32[8,2,2,128]{3,0,2,1:T(8,128)S(1)} %stack.39), channel_id=1, source_target_pairs={{0,16},{1,49},{8,24},{9,57},{16,32},{17,1},{24,40},{25,9},{32,48},... | collective-permute-start | bytes 49160 | tf_op jit(solution)/shard_map/ppermute | solution.py:30
  86.7 3.1 %collective-permute-start.13 = (f32[8,2,2,128]{3,0,2,1:T(8,128)S(1)}, f32[8,2,2,128]{3,0,2,1:T(8,128)S(1)}, u32[]{:S(2)}, u32[]{:S(2)}) collective-permute-start(f32[8,2,2,128]{3,0,2,1:T(8,128)S(1)} %stack.39), channel_id=1, source_target_pairs={{0,8},{1,57},{8,16},{9,1},{16,24},{17,9},{24,32},{25,17},{32,40},{... | collective-permute-start | bytes 49160 | tf_op jit(solution)/shard_map/ppermute | solution.py:30
  89.8 4.2 %collective-permute-start.17 = (f32[8,2,2,128]{3,0,2,1:T(8,128)S(1)}, f32[8,2,2,128]{3,0,2,1:T(8,128)S(1)}, u32[]{:S(2)}, u32[]{:S(2)}) collective-permute-start(f32[8,2,2,128]{3,0,2,1:T(8,128)S(1)} %log_add_fusion.3), channel_id=1, source_target_pairs={{0,1},{1,0},{2,3},{3,2},{4,5},{5,4},{6,7},{7,6},{8,9},{9,8},{10,11... | collective-permute-start | bytes 49160 | tf_op jit(solution)/shard_map/ppermute | solution.py:22
  94.1 3.6 %collective-permute-start.18 = (f32[8,2,2,128]{3,0,2,1:T(8,128)S(1)}, f32[8,2,2,128]{3,0,2,1:T(8,128)S(1)}, u32[]{:S(2)}, u32[]{:S(2)}) collective-permute-start(f32[8,2,2,128]{3,0,2,1:T(8,128)S(1)} %log_add_fusion.2), channel_id=1, source_target_pairs={{0,2},{1,7},{2,4},{3,1},{4,6},{5,3},{6,0},{7,5},{8,10},{9,15},{10,... | collective-permute-start | bytes 49160 | tf_op jit(solution)/shard_map/ppermute | solution.py:38
  96.8 4.1 %collective-permute-start.19 = (f32[8,2,2,128]{3,0,2,1:T(8,128)S(1)}, f32[8,2,2,128]{3,0,2,1:T(8,128)S(1)}, u32[]{:S(2)}, u32[]{:S(2)}) collective-permute-start(f32[8,2,2,128]{3,0,2,1:T(8,128)S(1)} %log_add_fusion.2), channel_id=1, source_target_pairs={{0,4},{1,5},{2,6},{3,7},{4,0},{5,1},{6,2},{7,3},{8,12},{9,13},{10,... | collective-permute-start | bytes 49160 | tf_op jit(solution)/shard_map/ppermute | solution.py:38
  101.0 1.3 collective-permute-start.20
  102.3 18.8 %copy-start.31 = (f32[1,2,2,128]{3,0,2,1:T(1,128)}, f32[1,2,2,128]{3,0,2,1:T(1,128)S(1)}, u32[]{:S(2)}) copy-start(f32[1,2,2,128]{3,0,2,1:T(1,128)S(1)} %get-tuple-element.28) | copy-start | bytes 6148
  121.1 3.4 %collective-permute-start.22 = (bf16[432,1024]{1,0:T(8,128)(2,1)S(1)}, bf16[432,1024]{1,0:T(8,128)(2,1)S(1)}, u32[]{:S(2)}, u32[]{:S(2)}) collective-permute-start(bf16[432,1024]{1,0:T(8,128)(2,1)S(1)} %get-tuple-element.17), channel_id=1, source_target_pairs={{0,1},{1,0},{2,3},{3,2},{4,5},{5,4},{6,7},{7,6},{8,9},{9,8},{10,11... | collective-permute-start | bytes 2654216 | tf_op jit(solution)/shard_map/ppermute | solution.py:22
  124.0 17.5 %copy-start.27 = (bf16[128,1024]{1,0:T(8,128)(2,1)S(1)}, bf16[128,1024]{1,0:T(8,128)(2,1)}, u32[]{:S(2)}) copy-start(bf16[128,1024]{1,0:T(8,128)(2,1)} %centroids.1) | copy-start | bytes 786436
  124.0 17.5 %copy-start.28 = (f32[128]{0:T(128)S(1)}, f32[128]{0:T(128)}, u32[]{:S(2)}) copy-start(f32[128]{0:T(128)} %param.5) | copy-start | bytes 1540
  124.0 6.0 %collective-permute-start.21 = (bf16[144,1024]{1,0:T(8,128)(2,1)S(1)}, bf16[144,1024]{1,0:T(8,128)(2,1)S(1)}, u32[]{:S(2)}, u32[]{:S(2)}) collective-permute-start(bf16[144,1024]{1,0:T(8,128)(2,1)S(1)} %get-tuple-element.16), channel_id=1, source_target_pairs={{0,1},{1,0},{2,3},{3,2},{4,5},{5,4},{6,7},{7,6},{8,9},{9,8},{10,11... | collective-permute-start | bytes 884744 | tf_op jit(solution)/shard_map/ppermute | solution.py:22
  124.7 10.1 %collective-permute-start.23 = (bf16[144,1024]{1,0:T(8,128)(2,1)S(1)}, bf16[144,1024]{1,0:T(8,128)(2,1)S(1)}, u32[]{:S(2)}, u32[]{:S(2)}) collective-permute-start(bf16[144,1024]{1,0:T(8,128)(2,1)S(1)} %get-tuple-element.20), channel_id=1, source_target_pairs={{0,128},{64,192},{128,0},{192,64},{1,129},{65,193},{129,1},{193,65... | collective-permute-start | bytes 884744 | tf_op jit(solution)/shard_map/ppermute | solution.py:18
  127.3 14.2 %collective-permute-start.24 = (bf16[144,1024]{1,0:T(8,128)(2,1)S(1)}, bf16[144,1024]{1,0:T(8,128)(2,1)S(1)}, u32[]{:S(2)}, u32[]{:S(2)}) collective-permute-start(bf16[144,1024]{1,0:T(8,128)(2,1)S(1)} %get-tuple-element.21), channel_id=1, source_target_pairs={{0,64},{64,128},{128,192},{192,0},{1,65},{65,129},{129,193},{193,1... | collective-permute-start | bytes 884744 | tf_op jit(solution)/shard_map/ppermute | solution.py:18
  127.7 13.8 %collective-permute-start.25 = (bf16[144,1024]{1,0:T(8,128)(2,1)S(1)}, bf16[144,1024]{1,0:T(8,128)(2,1)S(1)}, u32[]{:S(2)}, u32[]{:S(2)}) collective-permute-start(bf16[144,1024]{1,0:T(8,128)(2,1)S(1)} %get-tuple-element.22), channel_id=1, source_target_pairs={{0,192},{64,0},{128,64},{192,128},{1,193},{65,1},{129,65},{193,129... | collective-permute-start | bytes 884744 | tf_op jit(solution)/shard_map/ppermute | solution.py:18
  (26 other events, 49.8 us)

commit v2 on v1

--- a/solution.py
+++ b/solution.py
@@ -12,6 +12,7 @@
 TAIL = 16
 ORDER = (2, 1, 3, 0)
 VMEM_LIMIT = 30 * 1024 * 1024
+PIN = True
 
 
 def shift_x(value, by):
@@ -30,14 +31,6 @@
     return lax.ppermute(value, ("z", "c"), pairs)
 
 
-def along_y(value, by):
-    pairs = []
-    for y in range(NY):
-        pairs.append((y * NC, (y + by) % NY * NC))
-        pairs.append((y * NC + 1, (y - by) % NY * NC + 1))
-    return lax.ppermute(value, ("y", "c"), pairs)
-
-
 def swap_halves(value):
     pairs = []
     for y in range(NY):
@@ -55,44 +48,44 @@
     return high + jnp.log(sum(jnp.exp(p - high) for p in parts))
 
 
-def energies(local, h, y, z, c):
-    steps = [local[0]] + [pick(h, v, v[::-1]) for v in local[1:]]
-    mine = jnp.concatenate([v.reshape(-1, v.shape[-1]) for v in steps])
-    other = swap_cores(mine)
-
-    def split(flat):
-        out, at = [], 0
-        for v in steps:
-            n = v.shape[0] * v.shape[1]
-            out.append(flat[at : at + n].reshape(v.shape))
-            at += n
-        return out
-
-    back, ahead = split(pick(c, mine, other)), split(pick(c, other, mine))
+def energies(local, z, c, h):
+    rows = local.shape[1]
+    got = lax.all_to_all(jnp.broadcast_to(local[None], (NY * NC,) + local.shape), ("y", "c"), 0, 0, tiled=True)
+    got = got.reshape(NY, NC, *local.shape)
+
+    def in_order(v, odd):
+        steps = [v[0:2].reshape(2, 1, rows)]
+        steps += [v[2 + 4 * k : 6 + 4 * k].reshape(2, 2, rows) for k in range(3)]
+        steps += [v[14:16].reshape(2, 1, rows)]
+        return [steps[0]] + [pick(odd, s, s[::-1]) for s in steps[1:]]
+
+    def part(core):
+        parts = []
+        for y in range(NY):
+            v = got[y, core]
+            if y % 2:
+                v = jnp.concatenate([v[0:2]] + [v[a:b] for k in range(3) for a, b in ((4 + 4 * k, 6 + 4 * k), (2 + 4 * k, 4 + 4 * k))] + [v[15:16], v[14:15]])
+            parts.append(v)
+        return in_order(combine(parts), 0)
+
+    back, ahead = part(0), part(1)
     both = lambda k: jnp.concatenate([back[k], ahead[k]], axis=1)
-    block = jnp.stack([both(0), ahead[1], ahead[2], ahead[3], both(4), back[3], back[2], back[1]])
-
-    none = jnp.full_like(block, -1e30)
-    parts = [pick(c, block, none)]
-    for d in range(1, 4):
-        got = along_z(block, d)
-        parts.append(pick(c, jnp.roll(got, -d, axis=0), jnp.roll(got, d, axis=0)))
-    parts.append(pick(c, jnp.roll(along_z(block, 4), 4, axis=0), none))
-    part = combine(parts)
-    block = combine([part, swap_cores(part)])
-
-    parts = [pick(c, block, none), along_y(block, 1), pick(c, along_y(block, 2), none)]
-    part = combine(parts)
-    block = combine([part, swap_cores(part)])
-
-    own = lambda v: pick(c, v[:, :1], v[:, 1:])
-    out = [own(block[0])]
-    for k in range(1, 4):
-        v = pick(c, block[NZ - k], block[k])
-        out.append(pick(h, v, v[::-1]))
-    v = own(block[4])
-    out.append(pick(h, v, v[::-1]))
-    return jnp.concatenate([v.reshape(1, -1) for v in out], axis=1), block[0].reshape(-1)
+    blocks = [both(0), ahead[1], ahead[2], ahead[3], both(4), back[3], back[2], back[1]]
+
+    def wanted(by):
+        at = lambda k: blocks[(by + k) % NZ]
+        own = lambda v: pick(c, v[:, :1], v[:, 1:])
+        out = [own(at(0))] + [pick(c, at(-k), at(k)) for k in range(1, 4)] + [own(at(4))]
+        return jnp.concatenate([v.reshape(-1, rows) for v in out])
+
+    lots = jnp.stack([wanted(d) for d in range(NZ)])
+    lots = lax.dynamic_slice_in_dim(jnp.concatenate([lots, lots]), lax.rem(NZ - z, NZ), NZ, 0)
+    got = lax.all_to_all(lots, "z", 0, 0, tiled=True)
+    total = combine([got[i] for i in range(NZ)])
+    other = swap_cores(total[:2])
+    first, second = pick(c, total[:2], other), pick(c, other, total[:2])
+    row_energy = jnp.stack([first, second], axis=1).reshape(-1)
+    return jnp.concatenate([v.reshape(1, -1) for v in in_order(total, h)], axis=1), row_energy
 
 
 def turned(column):
@@ -116,32 +109,74 @@
     return total, tail[:, :n] + tail[:, n : 2 * n]
 
 
-def weigh_kernel(sizes, energy, *refs):
-    pieces = len(sizes)
-    logits, slab = refs[:pieces], refs[pieces : 2 * pieces]
-    message, keep, keep_count = refs[2 * pieces :]
+def score_kernel(table, *refs):
+    pieces, (logits, energy, high, total) = refs[:-4], refs[-4:]
+    first = pl.program_id(0) == 0
+    block = table[...]
+    wide = block.astype(F32)
+    squares = jnp.sum(wide * wide, axis=1, keepdims=True)
+    at = 0
+    for piece in pieces:
+        span = slice(at, at + piece.shape[0])
+        at += piece.shape[0]
+        product = lax.dot_general(block, piece[...], (((1,), (1,)), ((), ())), preferred_element_type=F32)
+        scores = 2.0 * product - squares
+        logits[:, span] = scores
+        top = jnp.max(scores, axis=0, keepdims=True)
+        old = jnp.where(first, top, high[:, span])
+        new = jnp.maximum(old, top)
+        kept = jnp.where(first, 0.0, total[:, span]) * jnp.exp(old - new)
+        added = kept + jnp.sum(jnp.exp(scores - new), axis=0, keepdims=True)
+        high[:, span] = new
+        total[:, span] = added
+        energy[:, span] = new + jnp.log(added)
+
+
+def score(table, pieces):
+    (count, width), rows = table.shape, sum(p.shape[0] for p in pieces)
+    tile = min(256, count)
+    whole = lambda v: pl.BlockSpec(v.shape, lambda i: (0, 0))
+    return pl.pallas_call(
+        score_kernel,
+        grid=(count // tile,),
+        in_specs=[pl.BlockSpec((tile, width), lambda i: (i, 0))] + [whole(p) for p in pieces],
+        out_specs=(pl.BlockSpec((tile, rows), lambda i: (i, 0)), pl.BlockSpec((1, rows), lambda i: (0, 0))),
+        out_shape=(jax.ShapeDtypeStruct((count, rows), F32), jax.ShapeDtypeStruct((1, rows), F32)),
+        scratch_shapes=[pltpu.VMEM((1, rows), F32), pltpu.VMEM((1, rows), F32)],
+        compiler_params=pltpu.CompilerParams(vmem_limit_bytes=VMEM_LIMIT),
+        cost_estimate=pl.CostEstimate(
+            flops=4 * count * rows * width,
+            bytes_accessed=4 * count * rows + 2 * (count + rows) * width,
+            transcendentals=count * rows,
+        ),
+    )(table, *pieces)
+
+
+def weigh_kernel(groups, sizes, energy, *refs):
+    logits, slab = refs[: len(groups)], refs[len(groups) : len(groups) + len(sizes)]
+    message, keep, keep_count = refs[len(groups) + len(sizes) :]
     n, width = keep.shape
+    step = min(sizes)
     counts, sets, at = None, [], 0
-    for p, size in enumerate(sizes):
+    for p, size in enumerate(groups):
         w = jnp.exp(logits[p][...] - energy[:, at : at + size])
         at += size
-        for cut in range(0, size, sizes[-1]):
-            part = w[:, cut : cut + sizes[-1]]
+        for cut in range(0, size, step):
+            part = w[:, cut : cut + step]
             counts = part if counts is None else counts + part
-        sets.append(w.astype(BF16))
+            sets.append(part.astype(BF16))
     column = jnp.sum(counts, axis=1, keepdims=True)
+    pairs = [jnp.concatenate(sets[p : p + 2], axis=1) for p in range(0, len(sets), 2)]
     tile = min(256, width)
     totals = []
     for at in range(0, width, tile):
         acc = None
-        for p in range(pieces):
-            if sizes[p] < sizes[1] and p == pieces - 1:
-                continue
-            w, rows = sets[p], slab[p][:, at : at + tile]
-            if sizes[p] < sizes[1]:
-                w = jnp.concatenate([w, sets[p + 1]], axis=1)
-                rows = jnp.concatenate([rows, slab[p + 1][:, at : at + tile]])
-            term = jnp.dot(w, rows, preferred_element_type=F32)
+        for p, pair in enumerate(pairs):
+            if p < len(sizes) - 2:
+                rows = slab[p][:, at : at + tile]
+            else:
+                rows = jnp.concatenate([slab[p][:, at : at + tile], slab[p + 1][:, at : at + tile]])
+            term = jnp.dot(pair, rows, preferred_element_type=F32)
             acc = term if acc is None else acc + term
         keep[:, at : at + tile] = acc[:n]
         totals.append(acc[n:])
@@ -156,10 +191,10 @@
     block = lambda rows, cols: pl.BlockSpec((rows, cols), lambda i: (i, 0))
     whole = lambda v: pl.BlockSpec(v.shape, lambda i: (0, 0))
     return pl.pallas_call(
-        functools.partial(weigh_kernel, sizes),
+        functools.partial(weigh_kernel, tuple(v.shape[1] for v in logits), sizes),
         grid=(count,),
         in_specs=[whole(energy)]
-        + [pl.BlockSpec((span, p.shape[1]), lambda i: (i + first, 0)) for p in logits]
+        + [pl.BlockSpec((span, v.shape[1]), lambda i: (i + first, 0)) for v in logits]
         + [whole(p) for p in slab],
         out_specs=(block(n + TAIL, width), block(n, width), block(TAIL, n)),
         out_shape=(
@@ -224,32 +259,29 @@
     h = lax.rem(y, 2)
 
     mine = lax.dynamic_slice_in_dim(embeddings, h * half, half, 0)
-    stream = along_z(mine, 1)
-    last = along_z(lax.dynamic_slice_in_dim(mine, c * sub, sub, 0), NZ // 2)
+    one = along_z(mine, 1)
     own = lax.dynamic_slice_in_dim(embeddings.reshape(2, 2, sub, width), c, 1, 1).reshape(half, width)
-    near = {d: shift_x(centroids, -d) for d in (1, 2, 3)}
-    pieces = [own, stream, swap_halves(stream)]
-    for step in range(2, NZ // 2):
-        stream = along_z(stream, 1)
-        pieces += [stream, swap_halves(stream)]
-    pieces += [last, swap_halves(last)]
-
+    two = along_z(one, 1)
+    three = along_z(two, 1)
+    four = along_z(lax.dynamic_slice_in_dim(three, c * sub, sub, 0), 1)
+
+    held, _ = lax.optimization_barrier((centroids, one))
+    near = {d: shift_x(held, -d) for d in (2, 1, 3)}
     near[0] = centroids
     mine = jnp.concatenate([near[d] for d in ORDER])
     other = swap_cores(mine)
     table = jnp.stack([mine.reshape(NX, -1, width), other.reshape(NX, -1, width)], axis=1).reshape(-1, width)
-    squares = jnp.sum(jnp.square(table.astype(F32)), axis=1)[:, None]
-
-    logits, local = [], []
-    for piece in pieces:
-        scores = 2.0 * lax.dot_general(table, piece, (((1,), (1,)), ((), ())), preferred_element_type=F32) - squares
-        high = jnp.max(scores, axis=0)
-        local.append(high + jnp.log(jnp.sum(jnp.exp(scores - high[None, :]), axis=0)))
-        logits.append(scores)
-    steps = [local[0].reshape(2, 1, sub)]
-    steps += [jnp.stack(local[k : k + 2]).reshape(2, 2, sub) for k in (1, 3, 5)]
-    steps += [jnp.stack(local[7:]).reshape(2, 1, sub)]
-    energy, row_energy = energies(steps, h, y, z, c)
+
+    in_vmem = lambda v: pltpu.with_memory_space_constraint(v, pltpu.VMEM) if PIN else v
+    pieces = [own, one, swap_halves(one), two, swap_halves(two), three, swap_halves(three), four, swap_halves(four)]
+    logits, local, at = [], [], 0
+    for count in (3, 2, 1, 2, 1):
+        scores, energy = score(table, pieces[at : at + count])
+        at += count
+        logits.append(in_vmem(scores))
+        local.append(energy)
+    energy, row_energy = energies(jnp.concatenate(local, axis=1).reshape(-1, sub), z, c, h)
+    pieces = [in_vmem(p) for p in pieces]
 
     message, keep, keep_count = weigh(0, NX - 1, logits, energy, pieces)
     sent = add(swap_cores(message), keep, keep_count)

time: 143 us -> 155 us (1.084)
  local copies, waits for them, and re-layouts: 18.2 us -> 39.9 us
  Pallas kernels: 9.28 us -> 21.9 us
  matrix products: 10.9 us -> 0 us
  starting transfers between devices: 53.1 us -> 48.2 us
  waiting for transfers between devices: 44.7 us -> 41 us
  other arithmetic: 5.33 us -> 1.89 us
    pallas_call x2 -> x7, Pallas kernels: 7.98 us -> 20.6 us  [the longest x5 13.3 us: score(): pl.pallas_call(score_kernel, grid=(count // tile,), in_specs=[pl.BlockSpe...]
    all_to_all x0 -> x2, waiting for transfers between devices: none -> 12.1 us  [the longest x1 7.23 us: energies(): got = lax.all_to_all(lots, 'z', 0, 0, tiled=True)]
    unnamed x70 -> x76, local copies, waits for them, and re-layouts: 17.1 us -> 28 us
    dot_general x9 -> x0, matrix products: 10.9 us -> none  [shards(): lax.dot_general(table, piece, (((1,), (1,)), ((), ())), preferred_element...]
    all_to_all x0 -> x2, starting transfers between devices: none -> 10.3 us  [the longest x1 5.66 us: energies(): lax.all_to_all(jnp.broadcast_to(local[None], (NY * NC,) + local.shape), (...]
    ppermute x8 -> x4, starting transfers between devices: 24.4 us -> 16 us  [along_z(): return lax.ppermute(value, ('z', 'c'), pairs)]
    ppermute x4, waiting for transfers between devices: 7.1 us -> 0.01 us  [swap_halves(): return lax.ppermute(value, ('y', 'c'), pairs)]
    concatenate x1 -> x17, local copies, waits for them, and re-layouts: 0.12 us -> 5.61 us  [the longest x4 4.14 us: part(): jnp.concatenate([v[0:2]] + [v[a:b] for k in range(3) for a, b in ((4 + 4...]
  transfers between devices with their start and end apart: 26 -> 20, of which waited for: 13 -> 10; matrix products, arithmetic and copies ran while one was open for 10% -> 4% of each run, Pallas kernels for 2% -> 8%
where the time goes in v2:
time: 155 us; the launch traced here: 154 us
  starting transfers between devices  48.2 us (31%)
  waiting for transfers between devices  41 us (26%)
  local copies, waits for them, and re-layouts  39.9 us (26%)
  Pallas kernels  21.9 us (14%)
  other arithmetic  1.89 us (1%)
    unnamed x76, local copies, waits for them, and re-layouts  28 us
    ppermute x6, waiting for transfers between devices, shift_x(): return lax.ppermute(value, 'x', [(i, (i + by) % NX) for i in range(NX)])  18.1 us
    ppermute x4, starting transfers between devices, along_z(): return lax.ppermute(value, ('z', 'c'), pairs)  16 us
    pallas_call x5, Pallas kernels, score(): pl.pallas_call(score_kernel, grid=(count // tile,), in_specs=[pl.BlockSpe...  13.3 us
    ppermute x4, waiting for transfers between devices, along_z(): return lax.ppermute(value, ('z', 'c'), pairs)  9.95 us
    ppermute x6, starting transfers between devices, shift_x(): return lax.ppermute(value, 'x', [(i, (i + by) % NX) for i in range(NX)])  8.86 us
    ppermute x4, starting transfers between devices, swap_halves(): return lax.ppermute(value, ('y', 'c'), pairs)  8.29 us
    pallas_call x2, Pallas kernels, weigh(): pl.pallas_call(functools.partial(weigh_kernel, tuple((v.shape[1] for v in...  7.39 us
  transfers between devices with their start and end apart: 20, of which 10 were waited for; matrix products, arithmetic and copies ran while one was open for 4% of the time, Pallas kernels for 8%

profile of v2, /device:TPU:1, one launch (start us, length us, event | category | flops | bytes accessed | tf_op | source)
XLA Modules:
  0.0 154.0 jit_solution(16958652171018980271)
XLA Ops:
  1.9 6.5 %collective-permute-start = (bf16[256,1024]{1,0:T(8,128)(2,1)S(1)}, bf16[256,1024]{1,0:T(8,128)(2,1)S(1)}, u32[]{:S(2)}, u32[]{:S(2)}) collective-permute-start(bf16[256,1024]{1,0:T(8,128)(2,1)S(1)} %constant_dynamic-slice_fusion.3), channel_id=1, source_target_pairs={{0,8},{1,57},{8,16},{9,1},{16,24},{17,9},{24,32},{25,17},{32,40},{... | collective-permute-start | bytes 1572872 | tf_op jit(solution)/shard_map/ppermute | solution.py:31
  8.4 6.1 %collective-permute-done.refs_1_.refs_6_ = bf16[256,1024]{1,0:T(8,128)(2,1)S(1)} collective-permute-done((bf16[256,1024]{1,0:T(8,128)(2,1)S(1)}, bf16[256,1024]{1,0:T(8,128)(2,1)S(1)}, u32[]{:S(2)}, u32[]{:S(2)}) %collective-permute-start) | collective-permute-done | bytes 524320 | tf_op jit(solution)/shard_map/ppermute | solution.py:31
  14.5 2.7 %collective-permute-start.1 = (bf16[128,1024]{1,0:T(8,128)(2,1)}, bf16[128,1024]{1,0:T(8,128)(2,1)S(1)}, u32[]{:S(2)}, u32[]{:S(2)}) collective-permute-start(bf16[128,1024]{1,0:T(8,128)(2,1)} %centroids.1), channel_id=1, source_target_pairs={{0,128},{64,192},{128,0},{192,64},{1,129},{65,193},{129,1},{193,65... | collective-permute-start | bytes 786440 | tf_op jit(solution)/shard_map/ppermute | solution.py:19
  18.7 3.1 %collective-permute-start.6 = (bf16[256,1024]{1,0:T(8,128)(2,1)S(1)}, bf16[256,1024]{1,0:T(8,128)(2,1)S(1)}, u32[]{:S(2)}, u32[]{:S(2)}) collective-permute-start(bf16[256,1024]{1,0:T(8,128)(2,1)S(1)} %collective-permute-done.refs_1_.refs_6_), channel_id=1, source_target_pairs={{0,8},{1,57},{8,16},{9,1},{16,24},{17,9},{24,32},{25,17},{32,40},{... | collective-permute-start | bytes 1572872 | tf_op jit(solution)/shard_map/ppermute | solution.py:31
  22.8 6.3 %collective-permute-done.2 = bf16[128,1024]{1,0:T(8,128)(2,1)S(1)} collective-permute-done((bf16[128,1024]{1,0:T(8,128)(2,1)}, bf16[128,1024]{1,0:T(8,128)(2,1)S(1)}, u32[]{:S(2)}, u32[]{:S(2)}) %collective-permute-start.2) | collective-permute-done | bytes 262176 | tf_op jit(solution)/shard_map/ppermute | solution.py:19
  31.3 1.6 %collective-permute-start.4 = (bf16[512,1024]{1,0:T(8,128)(2,1)}, bf16[512,1024]{1,0:T(8,128)(2,1)}, u32[]{:S(2)}, u32[]{:S(2)}) collective-permute-start(bf16[512,1024]{1,0:T(8,128)(2,1)} %constant_dynamic-update-slice_fusion), channel_id=1, source_target_pairs={{0,1},{1,0},{2,3},{3,2},{4,5},{5,4},{6,7},{7,6},{8,9},{9,8},{10,11... | collective-permute-start | bytes 3145736 | tf_op jit(solution)/shard_map/ppermute | solution.py:23
  32.9 3.1 %collective-permute-start.8 = (bf16[256,1024]{1,0:T(8,128)(2,1)S(1)}, bf16[256,1024]{1,0:T(8,128)(2,1)}, u32[]{:S(2)}, u32[]{:S(2)}) collective-permute-start(bf16[256,1024]{1,0:T(8,128)(2,1)S(1)} %collective-permute-done.6.refs_0_.refs_8_), channel_id=1, source_target_pairs={{0,8},{1,57},{8,16},{9,1},{16,24},{17,9},{24,32},{25,17},{32,40},{... | collective-permute-start | bytes 1572872 | tf_op jit(solution)/shard_map/ppermute | solution.py:31
  36.0 2.7 %collective-permute-start.5 = (bf16[256,1024]{1,0:T(8,128)(2,1)S(1)}, bf16[256,1024]{1,0:T(8,128)(2,1)S(1)}, u32[]{:S(2)}, u32[]{:S(2)}) collective-permute-start(bf16[256,1024]{1,0:T(8,128)(2,1)S(1)} %collective-permute-done.refs_1_.refs_6_), channel_id=1, source_target_pairs={{0,2},{1,7},{2,0},{3,5},{4,6},{5,3},{6,4},{7,1},{8,10},{9,15},{10,... | collective-permute-start | bytes 1572872 | tf_op jit(solution)/shard_map/ppermute | solution.py:39
  38.7 3.4 %collective-permute-done.8.refs_0_.refs_10_ = bf16[256,1024]{1,0:T(8,128)(2,1)} collective-permute-done((bf16[256,1024]{1,0:T(8,128)(2,1)S(1)}, bf16[256,1024]{1,0:T(8,128)(2,1)}, u32[]{:S(2)}, u32[]{:S(2)}) %collective-permute-start.8) | collective-permute-done | bytes 524320 | tf_op jit(solution)/shard_map/ppermute | solution.py:31
  43.1 3.3 %collective-permute-start.10 = (bf16[128,1024]{1,0:T(8,128)(2,1)S(1)}, bf16[128,1024]{1,0:T(8,128)(2,1)}, u32[]{:S(2)}, u32[]{:S(2)}) collective-permute-start(bf16[128,1024]{1,0:T(8,128)(2,1)S(1)} %constant_dynamic-slice_fusion.1), channel_id=1, source_target_pairs={{0,8},{1,57},{8,16},{9,1},{16,24},{17,9},{24,32},{25,17},{32,40},{... | collective-permute-start | bytes 786440 | tf_op jit(solution)/shard_map/ppermute | solution.py:31
  46.4 2.7 %collective-permute-start.7 = (bf16[256,1024]{1,0:T(8,128)(2,1)S(1)}, bf16[256,1024]{1,0:T(8,128)(2,1)S(1)}, u32[]{:S(2)}, u32[]{:S(2)}) collective-permute-start(bf16[256,1024]{1,0:T(8,128)(2,1)S(1)} %collective-permute-done.6.refs_0_.refs_8_), channel_id=1, source_target_pairs={{0,2},{1,7},{2,0},{3,5},{4,6},{5,3},{6,4},{7,1},{8,10},{9,15},{10,... | collective-permute-start | bytes 1572872 | tf_op jit(solution)/shard_map/ppermute | solution.py:39
  49.7 2.7 %collective-permute-start.11 = (bf16[128,1024]{1,0:T(8,128)(2,1)}, bf16[128,1024]{1,0:T(8,128)(2,1)S(1)}, u32[]{:S(2)}, u32[]{:S(2)}) collective-permute-start(bf16[128,1024]{1,0:T(8,128)(2,1)} %collective-permute-done.10.refs_1_.refs_12_), channel_id=1, source_target_pairs={{0,2},{1,7},{2,0},{3,5},{4,6},{5,3},{6,4},{7,1},{8,10},{9,15},{10,... | collective-permute-start | bytes 786440 | tf_op jit(solution)/shard_map/ppermute | solution.py:39
  52.4 1.7 %pad_maximum_fusion = bf16[4,2,128,1024]{3,2,1,0:T(8,128)(2,1)S(1)} fusion(bf16[4,1,128,1024]{3,2,1,0:T(8,128)(2,1)} %bitcast.3, bf16[4,1,128,1024]{3,2,1,0:T(8,128)(2,1)} %bitcast.1), kind=kLoop, calls=%fused_computation | loop fusion | flops 1048576 | bytes 4194304 | tf_op jit(solution)/shard_map/stack | solution.py:273
  54.2 3.1 %shard_map.58 = (f32[1024,768]{1,0:T(8,128)S(1)}, f32[1,768]{1,0:T(1,128)S(1)}) custom-call(bf16[1024,1024]{1,0:T(8,128)(2,1)S(1)} %bitcast.195, bf16[256,1024]{1,0:T(8,128)(2,1)S(1)} %bitcast.200, bf16[256,1024]{1,0:T(8,128)(2,1)S(1)} %collective-permute-done.refs_1_.refs_6_, bf16[256,1024]{1,0:T(8,128)(2,1)S(1)} %collective-permute-done.5.refs_2_.refs_7_), custom_call_target="tpu_custom_call" | custom-call | flops 3221225472 | bytes 6815744 | tf_op jit(solution)/shard_map/pallas_call | solution.py:139
  57.3 1.6 %copy-done.1 = f32[1024,768]{1,0:T(8,128)} copy-done((f32[1024,768]{1,0:T(8,128)}, f32[1024,768]{1,0:T(8,128)S(1)}, u32[]{:S(2)}) %copy-start.1) | copy-done | bytes 3145752
  58.9 2.4 %shard_map.59 = (f32[1024,512]{1,0:T(8,128)S(1)}, f32[1,512]{1,0:T(1,128)S(1)}) custom-call(bf16[1024,1024]{1,0:T(8,128)(2,1)S(1)} %bitcast.196, bf16[256,1024]{1,0:T(8,128)(2,1)S(1)} %copy-done.12, bf16[256,1024]{1,0:T(8,128)(2,1)S(1)} %collective-permute-done.7.refs_1_.refs_9_), custom_call_target="tpu_custom_call" | custom-call | flops 2147483648 | bytes 5242880 | tf_op jit(solution)/shard_map/pallas_call | solution.py:139
  61.3 2.8 %shard_map.60 = (f32[1024,256]{1,0:T(8,128)S(1)}, f32[1,256]{1,0:T(1,128)S(1)}) custom-call(bf16[1024,1024]{1,0:T(8,128)(2,1)S(1)} %bitcast.197, bf16[256,1024]{1,0:T(8,128)(2,1)} %collective-permute-done.8.refs_0_.refs_10_), custom_call_target="tpu_custom_call" | custom-call | flops 1073741824 | bytes 3670016 | tf_op jit(solution)/shard_map/pallas_call | solution.py:139
  65.2 1.6 %shard_map.62 = (f32[1024,128]{1,0:T(8,128)S(1)}, f32[1,128]{1,0:T(1,128)S(1)}) custom-call(bf16[1024,1024]{1,0:T(8,128)(2,1)S(1)} %bitcast.198, bf16[128,1024]{1,0:T(8,128)(2,1)S(1)} %collective-permute-done.11.refs_0_.refs_13_), custom_call_target="tpu_custom_call" | custom-call | flops 536870912 | bytes 2883584 | tf_op jit(solution)/shard_map/pallas_call | solution.py:139
  66.8 3.4 %shard_map.61 = (f32[1024,384]{1,0:T(8,128)S(1)}, f32[1,384]{1,0:T(1,128)S(1)}) custom-call(bf16[1024,1024]{1,0:T(8,128)(2,1)S(1)} %bitcast.199, bf16[256,1024]{1,0:T(8,128)(2,1)S(1)} %collective-permute-done.9.refs_0_.refs_11_, bf16[128,1024]{1,0:T(8,128)(2,1)} %collective-permute-done.10.refs_1_.refs_12_), custom_call_target="tpu_custom_call" | custom-call | flops 1610612736 | bytes 4456448 | tf_op jit(solution)/shard_map/pallas_call | solution.py:139
  72.1 5.7 %all-to-all-start = ((f32[8,16,128]{2,1,0:T(8,128)}), f32[8,16,128]{2,1,0:T(8,128)S(1)}, u32[]{:S(2)}, u32[]{:S(2)}) async-start(f32[8,16,128]{2,1,0:T(8,128)} %broadcast_in_dim.8), calls=%async_computation | async-start | bytes 131072 | tf_op jit(solution)/shard_map/all_to_all | solution.py:53
  77.7 4.9 %all-to-all-done = f32[8,16,128]{2,1,0:T(8,128)S(1)} async-done(((f32[8,16,128]{2,1,0:T(8,128)}), f32[8,16,128]{2,1,0:T(8,128)S(1)}, u32[]{:S(2)}, u32[]{:S(2)}) %all-to-all-start) | async-done | bytes 65568 | tf_op jit(solution)/shard_map/all_to_all | solution.py:53
  99.1 1.5 constant_dynamic-slice_fusion
  100.6 4.7 %all-to-all-start.1 = ((f32[8,16,128]{2,1,0:T(8,128)}), f32[8,16,128]{2,1,0:T(8,128)S(1)}, u32[]{:S(2)}, u32[]{:S(2)}) async-start(f32[8,16,128]{2,1,0:T(8,128)} %constant_dynamic-slice_fusion), calls=%async_computation.1 | async-start | bytes 131072 | tf_op jit(solution)/shard_map/all_to_all | solution.py:83
  105.3 7.2 %all-to-all-done.1 = f32[8,16,128]{2,1,0:T(8,128)S(1)} async-done(((f32[8,16,128]{2,1,0:T(8,128)}), f32[8,16,128]{2,1,0:T(8,128)S(1)}, u32[]{:S(2)}, u32[]{:S(2)}) %all-to-all-start.1) | async-done | bytes 65568 | tf_op jit(solution)/shard_map/all_to_all | solution.py:83
  112.6 2.5 %collective-permute-start.17 = (f32[2,128]{1,0:T(2,128)S(1)}, f32[2,128]{1,0:T(2,128)S(1)}, u32[]{:S(2)}, u32[]{:S(2)}) collective-permute-start(f32[2,128]{1,0:T(2,128)S(1)} %get-tuple-element.108), channel_id=1, source_target_pairs={{0,1},{1,0},{2,3},{3,2},{4,5},{5,4},{6,7},{7,6},{8,9},{9,8},{10,11... | collective-permute-start | bytes 3080 | tf_op jit(solution)/shard_map/ppermute | solution.py:23
  115.9 1.9 %copy-done.2 = f32[1024,768]{1,0:T(8,128)S(1)} copy-done((f32[1024,768]{1,0:T(8,128)S(1)}, f32[1024,768]{1,0:T(8,128)}, u32[]{:S(2)}) %copy-start.2) | copy-done | bytes 3145752
  127.7 5.0 %shard_map.64 = (bf16[432,1024]{1,0:T(8,128)(2,1)S(1)}, f32[384,1024]{1,0:T(8,128)S(1)}, f32[48,128]{1,0:T(8,128)S(1)}) custom-call(f32[1,2048]{1,0:T(1,128)S(1)} %constant_dynamic-update-slice_fusion.25.energy, f32[1024,768]{1,0:T(8,128)S(1)} %copy-done.2, f32[1024,512]{1,0:T(8,128)S(1)} %get-tuple-element.32.refs_1_, f32[1024,256]{1,0:T(8,128)S(1)} %copy-done.8, ...), custom_call_target="tpu_custom_call" | custom-call | flops 3221225472 | bytes 10485760 | tf_op jit(solution)/shard_map/pallas_call | solution.py:193
  133.1 2.4 %shard_map.63 = (bf16[144,1024]{1,0:T(8,128)(2,1)S(1)}, f32[128,1024]{1,0:T(8,128)S(1)}, f32[16,128]{1,0:T(8,128)S(1)}) custom-call(f32[1,2048]{1,0:T(1,128)S(1)} %constant_dynamic-update-slice_fusion.25.energy, f32[1024,768]{1,0:T(8,128)S(1)} %copy-done.2, f32[1024,512]{1,0:T(8,128)S(1)} %get-tuple-element.32.refs_1_, f32[1024,256]{1,0:T(8,128)S(1)} %copy-done.8, ...), custom_call_target="tpu_custom_call" | custom-call | flops 1073741824 | bytes 6291456 | tf_op jit(solution)/shard_map/pallas_call | solution.py:193
  136.0 2.0 %collective-permute-start.14 = (bf16[144,1024]{1,0:T(8,128)(2,1)S(1)}, bf16[144,1024]{1,0:T(8,128)(2,1)S(1)}, u32[]{:S(2)}, u32[]{:S(2)}) collective-permute-start(bf16[144,1024]{1,0:T(8,128)(2,1)S(1)} %get-tuple-element.42), channel_id=1, source_target_pairs={{0,128},{64,192},{128,0},{192,64},{1,129},{65,193},{129,1},{193,65... | collective-permute-start | bytes 884744 | tf_op jit(solution)/shard_map/ppermute | solution.py:19
  139.0 1.6 %collective-permute-start.16 = (bf16[144,1024]{1,0:T(8,128)(2,1)S(1)}, bf16[144,1024]{1,0:T(8,128)(2,1)S(1)}, u32[]{:S(2)}, u32[]{:S(2)}) collective-permute-start(bf16[144,1024]{1,0:T(8,128)(2,1)S(1)} %get-tuple-element.44), channel_id=1, source_target_pairs={{0,192},{64,0},{128,64},{192,128},{1,193},{65,1},{129,65},{193,129... | collective-permute-start | bytes 884744 | tf_op jit(solution)/shard_map/ppermute | solution.py:19
  141.3 4.7 %collective-permute-done.14.one = bf16[144,1024]{1,0:T(8,128)(2,1)S(1)} collective-permute-done((bf16[144,1024]{1,0:T(8,128)(2,1)S(1)}, bf16[144,1024]{1,0:T(8,128)(2,1)S(1)}, u32[]{:S(2)}, u32[]{:S(2)}) %collective-permute-start.14) | collective-permute-done | bytes 294944 | tf_op jit(solution)/shard_map/ppermute | solution.py:19
  145.9 6.9 %collective-permute-done.15.two = bf16[144,1024]{1,0:T(8,128)(2,1)S(1)} collective-permute-done((bf16[144,1024]{1,0:T(8,128)(2,1)S(1)}, bf16[144,1024]{1,0:T(8,128)(2,1)S(1)}, u32[]{:S(2)}, u32[]{:S(2)}) %collective-permute-start.15) | collective-permute-done | bytes 294944 | tf_op jit(solution)/shard_map/ppermute | solution.py:19
  (140 shorter events, 41.1 us)
Async XLA Ops:
  0.6 29.9 %copy-start.22 = (bf16[128,1024]{1,0:T(8,128)(2,1)S(1)}, bf16[128,1024]{1,0:T(8,128)(2,1)}, u32[]{:S(2)}) copy-start(bf16[128,1024]{1,0:T(8,128)(2,1)} %centroids.1) | copy-start | bytes 786436
  1.9 12.6 %collective-permute-start = (bf16[256,1024]{1,0:T(8,128)(2,1)S(1)}, bf16[256,1024]{1,0:T(8,128)(2,1)S(1)}, u32[]{:S(2)}, u32[]{:S(2)}) collective-permute-start(bf16[256,1024]{1,0:T(8,128)(2,1)S(1)} %constant_dynamic-slice_fusion.3), channel_id=1, source_target_pairs={{0,8},{1,57},{8,16},{9,1},{16,24},{17,9},{24,32},{25,17},{32,40},{... | collective-permute-start | bytes 1572872 | tf_op jit(solution)/shard_map/ppermute | solution.py:31
  14.5 39.7 %copy-start.9 = (bf16[256,1024]{1,0:T(8,128)(2,1)}, bf16[256,1024]{1,0:T(8,128)(2,1)S(1)}, u32[]{:S(2)}) copy-start(bf16[256,1024]{1,0:T(8,128)(2,1)S(1)} %collective-permute-done.refs_1_.refs_6_) | copy-start | bytes 1572868
  14.5 7.5 %collective-permute-start.1 = (bf16[128,1024]{1,0:T(8,128)(2,1)}, bf16[128,1024]{1,0:T(8,128)(2,1)S(1)}, u32[]{:S(2)}, u32[]{:S(2)}) collective-permute-start(bf16[128,1024]{1,0:T(8,128)(2,1)} %centroids.1), channel_id=1, source_target_pairs={{0,128},{64,192},{128,0},{192,64},{1,129},{65,193},{129,1},{193,65... | collective-permute-start | bytes 786440 | tf_op jit(solution)/shard_map/ppermute | solution.py:19
  17.3 11.8 %collective-permute-start.2 = (bf16[128,1024]{1,0:T(8,128)(2,1)}, bf16[128,1024]{1,0:T(8,128)(2,1)S(1)}, u32[]{:S(2)}, u32[]{:S(2)}) collective-permute-start(bf16[128,1024]{1,0:T(8,128)(2,1)} %centroids.1), channel_id=1, source_target_pairs={{0,192},{64,0},{128,64},{192,128},{1,193},{65,1},{129,65},{193,129... | collective-permute-start | bytes 786440 | tf_op jit(solution)/shard_map/ppermute | solution.py:19
  18.1 11.7 %collective-permute-start.3 = (bf16[128,1024]{1,0:T(8,128)(2,1)}, bf16[128,1024]{1,0:T(8,128)(2,1)S(1)}, u32[]{:S(2)}, u32[]{:S(2)}) collective-permute-start(bf16[128,1024]{1,0:T(8,128)(2,1)} %centroids.1), channel_id=1, source_target_pairs={{0,64},{64,128},{128,192},{192,0},{1,65},{65,129},{129,193},{193,1... | collective-permute-start | bytes 786440 | tf_op jit(solution)/shard_map/ppermute | solution.py:19
  18.7 14.2 %collective-permute-start.6 = (bf16[256,1024]{1,0:T(8,128)(2,1)S(1)}, bf16[256,1024]{1,0:T(8,128)(2,1)S(1)}, u32[]{:S(2)}, u32[]{:S(2)}) collective-permute-start(bf16[256,1024]{1,0:T(8,128)(2,1)S(1)} %collective-permute-done.refs_1_.refs_6_), channel_id=1, source_target_pairs={{0,8},{1,57},{8,16},{9,1},{16,24},{17,9},{24,32},{25,17},{32,40},{... | collective-permute-start | bytes 1572872 | tf_op jit(solution)/shard_map/ppermute | solution.py:31
  31.3 21.2 %collective-permute-start.4 = (bf16[512,1024]{1,0:T(8,128)(2,1)}, bf16[512,1024]{1,0:T(8,128)(2,1)}, u32[]{:S(2)}, u32[]{:S(2)}) collective-permute-start(bf16[512,1024]{1,0:T(8,128)(2,1)} %constant_dynamic-update-slice_fusion), channel_id=1, source_target_pairs={{0,1},{1,0},{2,3},{3,2},{4,5},{5,4},{6,7},{7,6},{8,9},{9,8},{10,11... | collective-permute-start | bytes 3145736 | tf_op jit(solution)/shard_map/ppermute | solution.py:23
  32.9 21.3 %copy-start.11 = (bf16[256,1024]{1,0:T(8,128)(2,1)}, bf16[256,1024]{1,0:T(8,128)(2,1)S(1)}, u32[]{:S(2)}) copy-start(bf16[256,1024]{1,0:T(8,128)(2,1)S(1)} %collective-permute-done.6.refs_0_.refs_8_) | copy-start | bytes 1572868
  32.9 9.2 %collective-permute-start.8 = (bf16[256,1024]{1,0:T(8,128)(2,1)S(1)}, bf16[256,1024]{1,0:T(8,128)(2,1)}, u32[]{:S(2)}, u32[]{:S(2)}) collective-permute-start(bf16[256,1024]{1,0:T(8,128)(2,1)S(1)} %collective-permute-done.6.refs_0_.refs_8_), channel_id=1, source_target_pairs={{0,8},{1,57},{8,16},{9,1},{16,24},{17,9},{24,32},{25,17},{32,40},{... | collective-permute-start | bytes 1572872 | tf_op jit(solution)/shard_map/ppermute | solution.py:31
  36.0 18.2 %collective-permute-start.5 = (bf16[256,1024]{1,0:T(8,128)(2,1)S(1)}, bf16[256,1024]{1,0:T(8,128)(2,1)S(1)}, u32[]{:S(2)}, u32[]{:S(2)}) collective-permute-start(bf16[256,1024]{1,0:T(8,128)(2,1)S(1)} %collective-permute-done.refs_1_.refs_6_), channel_id=1, source_target_pairs={{0,2},{1,7},{2,0},{3,5},{4,6},{5,3},{6,4},{7,1},{8,10},{9,15},{10,... | collective-permute-start | bytes 1572872 | tf_op jit(solution)/shard_map/ppermute | solution.py:39
  43.1 6.6 %collective-permute-start.10 = (bf16[128,1024]{1,0:T(8,128)(2,1)S(1)}, bf16[128,1024]{1,0:T(8,128)(2,1)}, u32[]{:S(2)}, u32[]{:S(2)}) collective-permute-start(bf16[128,1024]{1,0:T(8,128)(2,1)S(1)} %constant_dynamic-slice_fusion.1), channel_id=1, source_target_pairs={{0,8},{1,57},{8,16},{9,1},{16,24},{17,9},{24,32},{25,17},{32,40},{... | collective-permute-start | bytes 786440 | tf_op jit(solution)/shard_map/ppermute | solution.py:31
  46.4 12.5 %collective-permute-start.7 = (bf16[256,1024]{1,0:T(8,128)(2,1)S(1)}, bf16[256,1024]{1,0:T(8,128)(2,1)S(1)}, u32[]{:S(2)}, u32[]{:S(2)}) collective-permute-start(bf16[256,1024]{1,0:T(8,128)(2,1)S(1)} %collective-permute-done.6.refs_0_.refs_8_), channel_id=1, source_target_pairs={{0,2},{1,7},{2,0},{3,5},{4,6},{5,3},{6,4},{7,1},{8,10},{9,15},{10,... | collective-permute-start | bytes 1572872 | tf_op jit(solution)/shard_map/ppermute | solution.py:39
  49.2 5.1 %copy-start.5 = (bf16[2,1,128,1024]{3,2,1,0:T(8,128)(2,1)}, bf16[2,1,128,1024]{3,2,1,0:T(8,128)(2,1)S(1)}, u32[]{:S(2)}) copy-start(bf16[2,1,128,1024]{3,2,1,0:T(8,128)(2,1)S(1)} %constant_dynamic-slice_fusion.2) | copy-start | bytes 1572868
  49.2 17.6 %collective-permute-start.9 = (bf16[256,1024]{1,0:T(8,128)(2,1)}, bf16[256,1024]{1,0:T(8,128)(2,1)S(1)}, u32[]{:S(2)}, u32[]{:S(2)}) collective-permute-start(bf16[256,1024]{1,0:T(8,128)(2,1)} %collective-permute-done.8.refs_0_.refs_10_), channel_id=1, source_target_pairs={{0,2},{1,7},{2,0},{3,5},{4,6},{5,3},{6,4},{7,1},{8,10},{9,15},{10,... | collective-permute-start | bytes 1572872 | tf_op jit(solution)/shard_map/ppermute | solution.py:39
  49.7 15.5 %collective-permute-start.11 = (bf16[128,1024]{1,0:T(8,128)(2,1)}, bf16[128,1024]{1,0:T(8,128)(2,1)S(1)}, u32[]{:S(2)}, u32[]{:S(2)}) collective-permute-start(bf16[128,1024]{1,0:T(8,128)(2,1)} %collective-permute-done.10.refs_1_.refs_12_), channel_id=1, source_target_pairs={{0,2},{1,7},{2,0},{3,5},{4,6},{5,3},{6,4},{7,1},{8,10},{9,15},{10,... | collective-permute-start | bytes 786440 | tf_op jit(solution)/shard_map/ppermute | solution.py:39
  54.2 3.1 %copy-start.14 = (bf16[256,1024]{1,0:T(8,128)(2,1)}, bf16[256,1024]{1,0:T(8,128)(2,1)S(1)}, u32[]{:S(2)}) copy-start(bf16[256,1024]{1,0:T(8,128)(2,1)S(1)} %collective-permute-done.5.refs_2_.refs_7_) | copy-start | bytes 1572868
  54.2 4.7 %copy-start.12 = (bf16[256,1024]{1,0:T(8,128)(2,1)S(1)}, bf16[256,1024]{1,0:T(8,128)(2,1)}, u32[]{:S(2)}) copy-start(bf16[256,1024]{1,0:T(8,128)(2,1)} %copy-done.11) | copy-start | bytes 1572868
  58.9 2.4 %copy-start.16 = (bf16[256,1024]{1,0:T(8,128)(2,1)}, bf16[256,1024]{1,0:T(8,128)(2,1)S(1)}, u32[]{:S(2)}) copy-start(bf16[256,1024]{1,0:T(8,128)(2,1)S(1)} %collective-permute-done.7.refs_1_.refs_9_) | copy-start | bytes 1572868
  66.8 3.5 %copy-start.20 = (f32[1024,128]{1,0:T(8,128)}, f32[1024,128]{1,0:T(8,128)S(1)}, u32[]{:S(2)}) copy-start(f32[1024,128]{1,0:T(8,128)S(1)} %get-tuple-element.35.refs_4_) | copy-start | bytes 1572868
  66.8 3.5 %copy-start.18 = (bf16[256,1024]{1,0:T(8,128)(2,1)}, bf16[256,1024]{1,0:T(8,128)(2,1)S(1)}, u32[]{:S(2)}) copy-start(bf16[256,1024]{1,0:T(8,128)(2,1)S(1)} %collective-permute-done.9.refs_0_.refs_11_) | copy-start | bytes 1572868
  72.1 10.5 %all-to-all-start = ((f32[8,16,128]{2,1,0:T(8,128)}), f32[8,16,128]{2,1,0:T(8,128)S(1)}, u32[]{:S(2)}, u32[]{:S(2)}) async-start(f32[8,16,128]{2,1,0:T(8,128)} %broadcast_in_dim.8), calls=%async_computation | async-start | bytes 131072 | tf_op jit(solution)/shard_map/all_to_all | solution.py:53
  100.6 11.9 %all-to-all-start.1 = ((f32[8,16,128]{2,1,0:T(8,128)}), f32[8,16,128]{2,1,0:T(8,128)S(1)}, u32[]{:S(2)}, u32[]{:S(2)}) async-start(f32[8,16,128]{2,1,0:T(8,128)} %constant_dynamic-slice_fusion), calls=%async_computation.1 | async-start | bytes 131072 | tf_op jit(solution)/shard_map/all_to_all | solution.py:83
  112.6 3.3 %collective-permute-start.17 = (f32[2,128]{1,0:T(2,128)S(1)}, f32[2,128]{1,0:T(2,128)S(1)}, u32[]{:S(2)}, u32[]{:S(2)}) collective-permute-start(f32[2,128]{1,0:T(2,128)S(1)} %get-tuple-element.108), channel_id=1, source_target_pairs={{0,1},{1,0},{2,3},{3,2},{4,5},{5,4},{6,7},{7,6},{8,9},{9,8},{10,11... | collective-permute-start | bytes 3080 | tf_op jit(solution)/shard_map/ppermute | solution.py:23
  115.9 1.9 %copy-start.2 = (f32[1024,768]{1,0:T(8,128)S(1)}, f32[1024,768]{1,0:T(8,128)}, u32[]{:S(2)}) copy-start(f32[1024,768]{1,0:T(8,128)} %copy-done.1) | copy-start | bytes 9437188
  132.7 3.1 %collective-permute-start.13 = (bf16[432,1024]{1,0:T(8,128)(2,1)S(1)}, bf16[432,1024]{1,0:T(8,128)(2,1)S(1)}, u32[]{:S(2)}, u32[]{:S(2)}) collective-permute-start(bf16[432,1024]{1,0:T(8,128)(2,1)S(1)} %get-tuple-element.39), channel_id=1, source_target_pairs={{0,1},{1,0},{2,3},{3,2},{4,5},{5,4},{6,7},{7,6},{8,9},{9,8},{10,11... | collective-permute-start | bytes 2654216 | tf_op jit(solution)/shard_map/ppermute | solution.py:23
  135.5 17.4 %copy-start.23 = (bf16[128,1024]{1,0:T(8,128)(2,1)S(1)}, bf16[128,1024]{1,0:T(8,128)(2,1)}, u32[]{:S(2)}) copy-start(bf16[128,1024]{1,0:T(8,128)(2,1)} %centroids.1) | copy-start | bytes 786436
  135.5 17.3 %copy-start.24 = (f32[128]{0:T(128)S(1)}, f32[128]{0:T(128)}, u32[]{:S(2)}) copy-start(f32[128]{0:T(128)} %param.5) | copy-start | bytes 1540
  135.6 5.7 %collective-permute-start.12 = (bf16[144,1024]{1,0:T(8,128)(2,1)S(1)}, bf16[144,1024]{1,0:T(8,128)(2,1)S(1)}, u32[]{:S(2)}, u32[]{:S(2)}) collective-permute-start(bf16[144,1024]{1,0:T(8,128)(2,1)S(1)} %get-tuple-element.38), channel_id=1, source_target_pairs={{0,1},{1,0},{2,3},{3,2},{4,5},{5,4},{6,7},{7,6},{8,9},{9,8},{10,11... | collective-permute-start | bytes 884744 | tf_op jit(solution)/shard_map/ppermute | solution.py:23
  136.0 9.9 %collective-permute-start.14 = (bf16[144,1024]{1,0:T(8,128)(2,1)S(1)}, bf16[144,1024]{1,0:T(8,128)(2,1)S(1)}, u32[]{:S(2)}, u32[]{:S(2)}) collective-permute-start(bf16[144,1024]{1,0:T(8,128)(2,1)S(1)} %get-tuple-element.42), channel_id=1, source_target_pairs={{0,128},{64,192},{128,0},{192,64},{1,129},{65,193},{129,1},{193,65... | collective-permute-start | bytes 884744 | tf_op jit(solution)/shard_map/ppermute | solution.py:19
  138.0 14.9 %collective-permute-start.15 = (bf16[144,1024]{1,0:T(8,128)(2,1)S(1)}, bf16[144,1024]{1,0:T(8,128)(2,1)S(1)}, u32[]{:S(2)}, u32[]{:S(2)}) collective-permute-start(bf16[144,1024]{1,0:T(8,128)(2,1)S(1)} %get-tuple-element.43), channel_id=1, source_target_pairs={{0,64},{64,128},{128,192},{192,0},{1,65},{65,129},{129,193},{193,1... | collective-permute-start | bytes 884744 | tf_op jit(solution)/shard_map/ppermute | solution.py:19
  139.0 13.8 %collective-permute-start.16 = (bf16[144,1024]{1,0:T(8,128)(2,1)S(1)}, bf16[144,1024]{1,0:T(8,128)(2,1)S(1)}, u32[]{:S(2)}, u32[]{:S(2)}) collective-permute-start(bf16[144,1024]{1,0:T(8,128)(2,1)S(1)} %get-tuple-element.44), channel_id=1, source_target_pairs={{0,192},{64,0},{128,64},{192,128},{1,193},{65,1},{129,65},{193,129... | collective-permute-start | bytes 884744 | tf_op jit(solution)/shard_map/ppermute | solution.py:19
  (13 other events, 15.0 us)

commit v3 on v1

--- a/solution.py
+++ b/solution.py
@@ -12,6 +12,7 @@
 TAIL = 16
 ORDER = (2, 1, 3, 0)
 VMEM_LIMIT = 30 * 1024 * 1024
+PIN = True
 
 
 def shift_x(value, by):
@@ -72,15 +73,15 @@
     both = lambda k: jnp.concatenate([back[k], ahead[k]], axis=1)
     block = jnp.stack([both(0), ahead[1], ahead[2], ahead[3], both(4), back[3], back[2], back[1]])
 
+    near = along_z(block, 1)
+    near = pick(c, jnp.roll(near, -1, axis=0), jnp.roll(near, 1, axis=0))
+    far = swap_cores(near)
+    three = combine([block, near, far])
+    got = along_z(pick(c, three, combine([block, far])), 3)
+    got = pick(c, jnp.roll(got, -3, axis=0), jnp.roll(got, 3, axis=0))
+    block = combine([three, got, swap_cores(got)])
+
     none = jnp.full_like(block, -1e30)
-    parts = [pick(c, block, none)]
-    for d in range(1, 4):
-        got = along_z(block, d)
-        parts.append(pick(c, jnp.roll(got, -d, axis=0), jnp.roll(got, d, axis=0)))
-    parts.append(pick(c, jnp.roll(along_z(block, 4), 4, axis=0), none))
-    part = combine(parts)
-    block = combine([part, swap_cores(part)])
-
     parts = [pick(c, block, none), along_y(block, 1), pick(c, along_y(block, 2), none)]
     part = combine(parts)
     block = combine([part, swap_cores(part)])
@@ -116,32 +117,76 @@
     return total, tail[:, :n] + tail[:, n : 2 * n]
 
 
-def weigh_kernel(sizes, energy, *refs):
-    pieces = len(sizes)
-    logits, slab = refs[:pieces], refs[pieces : 2 * pieces]
-    message, keep, keep_count = refs[2 * pieces :]
+def score_kernel(parts, sizes, *refs):
+    table, pieces, (logits, energy) = refs[:parts], refs[parts:-2], refs[-2:]
+    chunks = []
+    for p in range(0, parts, NC):
+        block = jnp.concatenate([table[p + i][...] for i in range(NC)])
+        wide = block.astype(F32)
+        chunks.append((block, jnp.sum(wide * wide, axis=1, keepdims=True)))
+    span = chunks[0][0].shape[0]
+    at = 0
+    for piece, size in zip(pieces, sizes):
+        rows, lot = piece[...], slice(at, at + size)
+        at += size
+        high = None
+        for p, (block, squares) in enumerate(chunks):
+            product = lax.dot_general(block, rows, (((1,), (1,)), ((), ())), preferred_element_type=F32)
+            scores = 2.0 * product - squares
+            logits[p * span : (p + 1) * span, lot] = scores
+            top = jnp.max(scores, axis=0, keepdims=True)
+            high = top if high is None else jnp.maximum(high, top)
+        total = None
+        for p in range(len(chunks)):
+            part = jnp.sum(jnp.exp(logits[p * span : (p + 1) * span, lot] - high), axis=0, keepdims=True)
+            total = part if total is None else total + part
+        energy[:, lot] = high + jnp.log(total)
+
+
+def score(table, pieces):
+    count, width = sum(t.shape[0] for t in table), table[0].shape[1]
+    sizes = tuple(p.shape[0] for p in pieces)
+    rows = sum(sizes)
+    return pl.pallas_call(
+        functools.partial(score_kernel, len(table), sizes),
+        out_shape=(
+            pltpu.HBM((count, rows), F32) if PIN else jax.ShapeDtypeStruct((count, rows), F32),
+            jax.ShapeDtypeStruct((1, rows), F32),
+        ),
+        compiler_params=pltpu.CompilerParams(vmem_limit_bytes=VMEM_LIMIT),
+        cost_estimate=pl.CostEstimate(
+            flops=4 * count * rows * width,
+            bytes_accessed=4 * count * rows + 2 * (count + rows) * width,
+            transcendentals=count * rows,
+        ),
+    )(*table, *pieces)
+
+
+def weigh_kernel(groups, sizes, energy, *refs):
+    logits, slab = refs[: len(groups)], refs[len(groups) : len(groups) + len(sizes)]
+    message, keep, keep_count = refs[len(groups) + len(sizes) :]
     n, width = keep.shape
+    step = min(sizes)
     counts, sets, at = None, [], 0
-    for p, size in enumerate(sizes):
+    for p, size in enumerate(groups):
         w = jnp.exp(logits[p][...] - energy[:, at : at + size])
         at += size
-        for cut in range(0, size, sizes[-1]):
-            part = w[:, cut : cut + sizes[-1]]
+        for cut in range(0, size, step):
+            part = w[:, cut : cut + step]
             counts = part if counts is None else counts + part
-        sets.append(w.astype(BF16))
+            sets.append(part.astype(BF16))
     column = jnp.sum(counts, axis=1, keepdims=True)
+    pairs = [jnp.concatenate(sets[p : p + 2], axis=1) for p in range(0, len(sets), 2)]
     tile = min(256, width)
     totals = []
     for at in range(0, width, tile):
         acc = None
-        for p in range(pieces):
-            if sizes[p] < sizes[1] and p == pieces - 1:
-                continue
-            w, rows = sets[p], slab[p][:, at : at + tile]
-            if sizes[p] < sizes[1]:
-                w = jnp.concatenate([w, sets[p + 1]], axis=1)
-                rows = jnp.concatenate([rows, slab[p + 1][:, at : at + tile]])
-            term = jnp.dot(w, rows, preferred_element_type=F32)
+        for p, pair in enumerate(pairs):
+            if p < len(sizes) - 2:
+                rows = slab[p][:, at : at + tile]
+            else:
+                rows = jnp.concatenate([slab[p][:, at : at + tile], slab[p + 1][:, at : at + tile]])
+            term = jnp.dot(pair, rows, preferred_element_type=F32)
             acc = term if acc is None else acc + term
         keep[:, at : at + tile] = acc[:n]
         totals.append(acc[n:])
@@ -156,10 +201,10 @@
     block = lambda rows, cols: pl.BlockSpec((rows, cols), lambda i: (i, 0))
     whole = lambda v: pl.BlockSpec(v.shape, lambda i: (0, 0))
     return pl.pallas_call(
-        functools.partial(weigh_kernel, sizes),
+        functools.partial(weigh_kernel, tuple(v.shape[1] for v in logits), sizes),
         grid=(count,),
         in_specs=[whole(energy)]
-        + [pl.BlockSpec((span, p.shape[1]), lambda i: (i + first, 0)) for p in logits]
+        + [pl.BlockSpec((span, v.shape[1]), lambda i: (i + first, 0)) for v in logits]
         + [whole(p) for p in slab],
         out_specs=(block(n + TAIL, width), block(n, width), block(TAIL, n)),
         out_shape=(
@@ -223,33 +268,42 @@
     half, sub = rows // 2, rows // 4
     h = lax.rem(y, 2)
 
+    near = {d: shift_x(centroids, -d) for d in (2, 1, 3)}
+
     mine = lax.dynamic_slice_in_dim(embeddings, h * half, half, 0)
-    stream = along_z(mine, 1)
-    last = along_z(lax.dynamic_slice_in_dim(mine, c * sub, sub, 0), NZ // 2)
+    one = along_z(mine, 1)
     own = lax.dynamic_slice_in_dim(embeddings.reshape(2, 2, sub, width), c, 1, 1).reshape(half, width)
-    near = {d: shift_x(centroids, -d) for d in (1, 2, 3)}
-    pieces = [own, stream, swap_halves(stream)]
-    for step in range(2, NZ // 2):
-        stream = along_z(stream, 1)
-        pieces += [stream, swap_halves(stream)]
-    pieces += [last, swap_halves(last)]
-
-    near[0] = centroids
-    mine = jnp.concatenate([near[d] for d in ORDER])
-    other = swap_cores(mine)
-    table = jnp.stack([mine.reshape(NX, -1, width), other.reshape(NX, -1, width)], axis=1).reshape(-1, width)
-    squares = jnp.sum(jnp.square(table.astype(F32)), axis=1)[:, None]
-
-    logits, local = [], []
-    for piece in pieces:
-        scores = 2.0 * lax.dot_general(table, piece, (((1,), (1,)), ((), ())), preferred_element_type=F32) - squares
-        high = jnp.max(scores, axis=0)
-        local.append(high + jnp.log(jnp.sum(jnp.exp(scores - high[None, :]), axis=0)))
-        logits.append(scores)
-    steps = [local[0].reshape(2, 1, sub)]
-    steps += [jnp.stack(local[k : k + 2]).reshape(2, 2, sub) for k in (1, 3, 5)]
-    steps += [jnp.stack(local[7:]).reshape(2, 1, sub)]
+    two = along_z(one, 1)
+    three = along_z(two, 1)
+
+    late = lax.optimization_barrier([near[1], near[2], near[3], two])
+    near = {0: centroids, 1: late[0], 2: late[1], 3: late[2]}
+    table = [v for d in ORDER for v in (near[d], swap_cores(near[d]))]
+
+    fixed = lambda v: pltpu.with_memory_space_constraint(v, pltpu.HBM) if PIN else v
+    logits, local, pieces = [], [], []
+
+    def scored(*rows):
+        scores, energy = score(table, rows)
+        logits.append(fixed(scores))
+        local.append(energy)
+        pieces.extend(rows)
+        return energy
+
+    done = scored(own, one, swap_halves(one))
+    last, _ = lax.optimization_barrier((lax.dynamic_slice_in_dim(three, c * sub, sub, 0), done))
+    four = along_z(last, 1)
+    done = scored(two, swap_halves(two))
+    last, _ = lax.optimization_barrier((four, done))
+    scored(three)
+    scored(swap_halves(three), four)
+    scored(swap_halves(last))
+
+    local = jnp.concatenate(local, axis=1).reshape(-1, sub)
+    cut = lambda at, n, *shape: local[at : at + n].reshape(*shape, sub)
+    steps = [cut(0, 2, 2, 1)] + [cut(2 + 4 * k, 4, 2, 2) for k in range(3)] + [cut(14, 2, 2, 1)]
     energy, row_energy = energies(steps, h, y, z, c)
+    pieces = [fixed(p) for p in pieces]
 
     message, keep, keep_count = weigh(0, NX - 1, logits, energy, pieces)
     sent = add(swap_cores(message), keep, keep_count)

time: 143 us -> 124 us (0.87)
  Pallas kernels: 9.28 us -> 32.5 us
  local copies, waits for them, and re-layouts: 18.2 us -> 6.71 us
  matrix products: 10.9 us -> 0 us
  starting transfers between devices: 53.1 us -> 45.2 us
  waiting for transfers between devices: 44.7 us -> 37.7 us
  other arithmetic: 5.33 us -> 0.39 us
    pallas_call x2 -> x7, Pallas kernels: 7.98 us -> 31.2 us  [the longest x5 20 us: score(): pl.pallas_call(functools.partial(score_kernel, len(table), sizes), out_sh...]
    unnamed x70 -> x37, local copies, waits for them, and re-layouts: 17.1 us -> 4.86 us
    ppermute x8 -> x6, starting transfers between devices: 24.4 us -> 13.1 us  [along_z(): return lax.ppermute(value, ('z', 'c'), pairs)]
    dot_general x9 -> x0, matrix products: 10.9 us -> none  [shards(): lax.dot_general(table, piece, (((1,), (1,)), ((), ())), preferred_element...]
    ppermute x4, waiting for transfers between devices: 7.1 us -> 1.78 us  [swap_halves(): return lax.ppermute(value, ('y', 'c'), pairs)]
    ppermute x8 -> x6, waiting for transfers between devices: 15 us -> 11.4 us  [along_z(): return lax.ppermute(value, ('z', 'c'), pairs)]
    reduce_sum x10 -> x0, other arithmetic: 3.58 us -> none  [the longest x9 1.87 us: shards(): jnp.sum(jnp.exp(scores - high[None, :]), axis=0)]
    ppermute x6, waiting for transfers between devices: 15.7 us -> 18.8 us  [shift_x(): return lax.ppermute(value, 'x', [(i, (i + by) % NX) for i in range(NX)])]
  transfers between devices with their start and end apart: 26 -> 28, of which waited for: 13 -> 14; matrix products, arithmetic and copies ran while one was open for 10% -> 1% of each run, Pallas kernels for 2% -> 16%
where the time goes in v3:
time: 124 us; the launch traced here: 123 us
  starting transfers between devices  45.2 us (36%)
  waiting for transfers between devices  37.7 us (30%)
  Pallas kernels  32.5 us (26%)
  local copies, waits for them, and re-layouts  6.71 us (5%)
    pallas_call x5, Pallas kernels, score(): pl.pallas_call(functools.partial(score_kernel, len(table), sizes), out_sh...  20 us
    ppermute x6, waiting for transfers between devices, shift_x(): return lax.ppermute(value, 'x', [(i, (i + by) % NX) for i in range(NX)])  18.8 us
    ppermute x6, starting transfers between devices, along_z(): return lax.ppermute(value, ('z', 'c'), pairs)  13.1 us
    ppermute x6, waiting for transfers between devices, along_z(): return lax.ppermute(value, ('z', 'c'), pairs)  11.4 us
    pallas_call x2, Pallas kernels, weigh(): pl.pallas_call(functools.partial(weigh_kernel, tuple((v.shape[1] for v in...  11.2 us
    ppermute x6, starting transfers between devices, shift_x(): return lax.ppermute(value, 'x', [(i, (i + by) % NX) for i in range(NX)])  10.1 us
    ppermute x10, starting transfers between devices, swap_cores(): return lax.ppermute(value, 'c', [(0, 1), (1, 0)])  10.1 us
    ppermute x4, starting transfers between devices, swap_halves(): return lax.ppermute(value, ('y', 'c'), pairs)  8.58 us
  transfers between devices with their start and end apart: 28, of which 14 were waited for; matrix products, arithmetic and copies ran while one was open for 1% of the time, Pallas kernels for 16%

profile of v3, /device:TPU:1, one launch (start us, length us, event | category | flops | bytes accessed | tf_op | source)
XLA Modules:
  0.0 123.5 jit_solution(11695750891696898359)
XLA Ops:
  0.7 1.2 copy-done
  1.9 6.5 %collective-permute-start.3 = (bf16[256,1024]{1,0:T(8,128)(2,1)S(1)}, bf16[256,1024]{1,0:T(8,128)(2,1)S(1)}, u32[]{:S(2)}, u32[]{:S(2)}) collective-permute-start(bf16[256,1024]{1,0:T(8,128)(2,1)S(1)} %constant_dynamic-slice_fusion.2), channel_id=1, source_target_pairs={{0,8},{1,57},{8,16},{9,1},{16,24},{17,9},{24,32},{25,17},{32,40},{... | collective-permute-start | bytes 1572872 | tf_op jit(solution)/shard_map/ppermute | solution.py:31
  8.4 6.1 %collective-permute-done.3.refs_9_.refs_6_ = bf16[256,1024]{1,0:T(8,128)(2,1)S(1)} collective-permute-done((bf16[256,1024]{1,0:T(8,128)(2,1)S(1)}, bf16[256,1024]{1,0:T(8,128)(2,1)S(1)}, u32[]{:S(2)}, u32[]{:S(2)}) %collective-permute-start.3) | collective-permute-done | bytes 524320 | tf_op jit(solution)/shard_map/ppermute | solution.py:31
  14.5 3.1 %collective-permute-start.4 = (bf16[256,1024]{1,0:T(8,128)(2,1)S(1)}, bf16[256,1024]{1,0:T(8,128)(2,1)S(1)}, u32[]{:S(2)}, u32[]{:S(2)}) collective-permute-start(bf16[256,1024]{1,0:T(8,128)(2,1)S(1)} %collective-permute-done.3.refs_9_.refs_6_), channel_id=1, source_target_pairs={{0,8},{1,57},{8,16},{9,1},{16,24},{17,9},{24,32},{25,17},{32,40},{... | collective-permute-start | bytes 1572872 | tf_op jit(solution)/shard_map/ppermute | solution.py:31
  17.6 1.2 collective-permute-start.2
  18.8 2.5 %collective-permute-start.1 = (bf16[128,1024]{1,0:T(8,128)(2,1)}, bf16[128,1024]{1,0:T(8,128)(2,1)}, u32[]{:S(2)}, u32[]{:S(2)}) collective-permute-start(bf16[128,1024]{1,0:T(8,128)(2,1)} %centroids.1), channel_id=1, source_target_pairs={{0,128},{64,192},{128,0},{192,64},{1,129},{65,193},{129,1},{193,65... | collective-permute-start | bytes 786440 | tf_op jit(solution)/shard_map/ppermute | solution.py:19
  21.3 1.2 collective-permute-start
  22.4 2.7 %collective-permute-start.9 = (bf16[256,1024]{1,0:T(8,128)(2,1)S(1)}, bf16[256,1024]{1,0:T(8,128)(2,1)}, u32[]{:S(2)}, u32[]{:S(2)}) collective-permute-start(bf16[256,1024]{1,0:T(8,128)(2,1)S(1)} %collective-permute-done.3.refs_9_.refs_6_), channel_id=1, source_target_pairs={{0,2},{1,7},{2,0},{3,5},{4,6},{5,3},{6,4},{7,1},{8,10},{9,15},{10,... | collective-permute-start | bytes 1572872 | tf_op jit(solution)/shard_map/ppermute | solution.py:47
  25.2 1.3 %collective-permute-done.2.refs_4_ = bf16[128,1024]{1,0:T(8,128)(2,1)} collective-permute-done((bf16[128,1024]{1,0:T(8,128)(2,1)}, bf16[128,1024]{1,0:T(8,128)(2,1)}, u32[]{:S(2)}, u32[]{:S(2)}) %collective-permute-start.2) | collective-permute-done | bytes 262176 | tf_op jit(solution)/shard_map/ppermute | solution.py:19
  26.6 6.5 %collective-permute-done.1.refs_0_ = bf16[128,1024]{1,0:T(8,128)(2,1)} collective-permute-done((bf16[128,1024]{1,0:T(8,128)(2,1)}, bf16[128,1024]{1,0:T(8,128)(2,1)}, u32[]{:S(2)}, u32[]{:S(2)}) %collective-permute-start.1) | collective-permute-done | bytes 262176 | tf_op jit(solution)/shard_map/ppermute | solution.py:19
  34.7 1.1 collective-permute-start.11
  35.9 2.8 %collective-permute-start.10 = (bf16[256,1024]{1,0:T(8,128)(2,1)S(1)}, bf16[256,1024]{1,0:T(8,128)(2,1)}, u32[]{:S(2)}, u32[]{:S(2)}) collective-permute-start(bf16[256,1024]{1,0:T(8,128)(2,1)S(1)} %collective-permute-done.4.refs_8_), channel_id=1, source_target_pairs={{0,2},{1,7},{2,0},{3,5},{4,6},{5,3},{6,4},{7,1},{8,10},{9,15},{10,... | collective-permute-start | bytes 1572872 | tf_op jit(solution)/shard_map/ppermute | solution.py:47
  39.7 5.3 %shard_map.58 = (f32[1024,768]{1,0:T(8,128)}, f32[1,768]{1,0:T(1,128)S(1)}) custom-call(bf16[128,1024]{1,0:T(8,128)(2,1)} %collective-permute-done.1.refs_0_, bf16[128,1024]{1,0:T(8,128)(2,1)} %collective-permute-done.5.refs_1_, bf16[128,1024]{1,0:T(8,128)(2,1)} %collective-permute-done.refs_2_, bf16[128,1024]{1,0:T(8,128)(2,1)} %collective-permute-done.6.refs_3_, ...), custom_call_target="tpu_custom_call" | custom-call | flops 3221225472 | bytes 6815744 | tf_op jit(solution)/shard_map/pallas_call | solution.py:150
  46.3 2.4 %collective-permute-start.12 = (bf16[256,1024]{1,0:T(8,128)(2,1)S(1)}, bf16[256,1024]{1,0:T(8,128)(2,1)S(1)}, u32[]{:S(2)}, u32[]{:S(2)}) collective-permute-start(bf16[256,1024]{1,0:T(8,128)(2,1)S(1)} %collective-permute-done.11.refs_8_.refs_10_), channel_id=1, source_target_pairs={{0,2},{1,7},{2,0},{3,5},{4,6},{5,3},{6,4},{7,1},{8,10},{9,15},{10,... | collective-permute-start | bytes 1572872 | tf_op jit(solution)/shard_map/ppermute | solution.py:47
  49.8 4.3 %shard_map.59 = (f32[1024,512]{1,0:T(8,128)}, f32[1,512]{1,0:T(1,128)S(1)}) custom-call(bf16[128,1024]{1,0:T(8,128)(2,1)} %collective-permute-done.1.refs_0_, bf16[128,1024]{1,0:T(8,128)(2,1)} %collective-permute-done.5.refs_1_, bf16[128,1024]{1,0:T(8,128)(2,1)} %collective-permute-done.refs_2_, bf16[128,1024]{1,0:T(8,128)(2,1)} %collective-permute-done.6.refs_3_, ...), custom_call_target="tpu_custom_call" | custom-call | flops 2147483648 | bytes 5242880 | tf_op jit(solution)/shard_map/pallas_call | solution.py:150
  55.7 3.2 %shard_map.60 = (f32[1024,256]{1,0:T(8,128)}, f32[1,256]{1,0:T(1,128)S(1)}) custom-call(bf16[128,1024]{1,0:T(8,128)(2,1)} %collective-permute-done.1.refs_0_, bf16[128,1024]{1,0:T(8,128)(2,1)} %collective-permute-done.5.refs_1_, bf16[128,1024]{1,0:T(8,128)(2,1)} %collective-permute-done.refs_2_, bf16[128,1024]{1,0:T(8,128)(2,1)} %collective-permute-done.6.refs_3_, ...), custom_call_target="tpu_custom_call" | custom-call | flops 1073741824 | bytes 3670016 | tf_op jit(solution)/shard_map/pallas_call | solution.py:150
  58.9 1.8 %collective-permute-done.14.refs_8_.refs_13_ = bf16[128,1024]{1,0:T(8,128)(2,1)S(1)} collective-permute-done((bf16[128,1024]{1,0:T(8,128)(2,1)S(1)}, bf16[128,1024]{1,0:T(8,128)(2,1)S(1)}, u32[]{:S(2)}, u32[]{:S(2)}) %collective-permute-start.14) | collective-permute-done | bytes 262176 | tf_op jit(solution)/shard_map/ppermute | solution.py:47
  60.6 3.0 %shard_map.62 = (f32[1024,128]{1,0:T(8,128)}, f32[1,128]{1,0:T(1,128)S(1)}) custom-call(bf16[128,1024]{1,0:T(8,128)(2,1)} %collective-permute-done.1.refs_0_, bf16[128,1024]{1,0:T(8,128)(2,1)} %collective-permute-done.5.refs_1_, bf16[128,1024]{1,0:T(8,128)(2,1)} %collective-permute-done.refs_2_, bf16[128,1024]{1,0:T(8,128)(2,1)} %collective-permute-done.6.refs_3_, ...), custom_call_target="tpu_custom_call" | custom-call | flops 536870912 | bytes 2883584 | tf_op jit(solution)/shard_map/pallas_call | solution.py:150
  63.6 4.2 %shard_map.61 = (f32[1024,384]{1,0:T(8,128)}, f32[1,384]{1,0:T(1,128)S(1)}) custom-call(bf16[128,1024]{1,0:T(8,128)(2,1)} %collective-permute-done.1.refs_0_, bf16[128,1024]{1,0:T(8,128)(2,1)} %collective-permute-done.5.refs_1_, bf16[128,1024]{1,0:T(8,128)(2,1)} %collective-permute-done.refs_2_, bf16[128,1024]{1,0:T(8,128)(2,1)} %collective-permute-done.6.refs_3_, ...), custom_call_target="tpu_custom_call" | custom-call | flops 1610612736 | bytes 4456448 | tf_op jit(solution)/shard_map/pallas_call | solution.py:150
  68.1 1.2 collective-permute-done.15
  69.4 1.8 %collective-permute-start.16 = (f32[8,2,2,128]{3,1,2,0:T(2,128)S(1)}, f32[8,2,2,128]{3,1,2,0:T(2,128)S(1)}, u32[]{:S(2)}, u32[]{:S(2)}) collective-permute-start(f32[8,2,2,128]{3,1,2,0:T(2,128)S(1)} %constant_dynamic-update-slice_fusion), channel_id=1, source_target_pairs={{0,8},{1,57},{8,16},{9,1},{16,24},{17,9},{24,32},{25,17},{32,40},{... | collective-permute-start | bytes 49160 | tf_op jit(solution)/shard_map/ppermute | solution.py:31
  72.1 2.6 %collective-permute-start.17 = (f32[8,2,2,128]{3,1,2,0:T(2,128)S(1)}, f32[8,2,2,128]{3,1,2,0:T(2,128)S(1)}, u32[]{:S(2)}, u32[]{:S(2)}) collective-permute-start(f32[8,2,2,128]{3,1,2,0:T(2,128)S(1)} %maximum_select_fusion), channel_id=1, source_target_pairs={{0,1},{1,0},{2,3},{3,2},{4,5},{5,4},{6,7},{7,6},{8,9},{9,8},{10,11... | collective-permute-start | bytes 49160 | tf_op jit(solution)/shard_map/ppermute | solution.py:23
  75.7 4.4 %collective-permute-done.18 = f32[8,2,2,128]{3,1,2,0:T(2,128)S(1)} collective-permute-done((f32[8,2,2,128]{3,1,2,0:T(2,128)S(1)}, f32[8,2,2,128]{3,1,2,0:T(2,128)S(1)}, u32[]{:S(2)}, u32[]{:S(2)}) %collective-permute-start.18) | collective-permute-done | bytes 16416 | tf_op jit(solution)/shard_map/ppermute | solution.py:31
  80.1 2.8 %collective-permute-start.19 = (f32[8,2,2,128]{3,1,2,0:T(2,128)S(1)}, f32[8,2,2,128]{3,1,2,0:T(2,128)S(1)}, u32[]{:S(2)}, u32[]{:S(2)}) collective-permute-start(f32[8,2,2,128]{3,1,2,0:T(2,128)S(1)} %maximum_select_fusion.1), channel_id=1, source_target_pairs={{0,1},{1,0},{2,3},{3,2},{4,5},{5,4},{6,7},{7,6},{8,9},{9,8},{10,11... | collective-permute-start | bytes 49160 | tf_op jit(solution)/shard_map/ppermute | solution.py:23
  83.9 2.5 %collective-permute-start.21 = (f32[8,2,2,128]{3,1,2,0:T(2,128)S(1)}, f32[8,2,2,128]{3,1,2,0:T(2,128)S(1)}, u32[]{:S(2)}, u32[]{:S(2)}) collective-permute-start(f32[8,2,2,128]{3,1,2,0:T(2,128)S(1)} %log_add_fusion.2), channel_id=1, source_target_pairs={{0,4},{1,5},{2,6},{3,7},{4,0},{5,1},{6,2},{7,3},{8,12},{9,13},{10,... | collective-permute-start | bytes 49160 | tf_op jit(solution)/shard_map/ppermute | solution.py:39
  89.2 2.9 %collective-permute-start.22 = (f32[8,2,2,128]{3,1,2,0:T(2,128)S(1)}, f32[8,2,2,128]{3,1,2,0:T(2,128)S(1)}, u32[]{:S(2)}, u32[]{:S(2)}) collective-permute-start(f32[8,2,2,128]{3,1,2,0:T(2,128)S(1)} %log_add_fusion.1), channel_id=1, source_target_pairs={{0,1},{1,0},{2,3},{3,2},{4,5},{5,4},{6,7},{7,6},{8,9},{9,8},{10,11... | collective-permute-start | bytes 49160 | tf_op jit(solution)/shard_map/ppermute | solution.py:23
  93.2 7.2 %shard_map.64 = (bf16[432,1024]{1,0:T(8,128)(2,1)S(1)}, f32[384,1024]{1,0:T(8,128)S(1)}, f32[48,128]{1,0:T(8,128)S(1)}) custom-call(f32[1,2048]{1,0:T(1,128)S(1)} %constant_dynamic-update-slice_fusion.8.energy, f32[1024,768]{1,0:T(8,128)} %get-tuple-element.39.refs_0_, f32[1024,512]{1,0:T(8,128)} %get-tuple-element.40.refs_1_, ...), custom_call_target="tpu_custom_call" | custom-call | flops 3221225472 | bytes 10485760 | tf_op jit(solution)/shard_map/pallas_call | solution.py:203
  101.0 4.0 %shard_map.63 = (bf16[144,1024]{1,0:T(8,128)(2,1)S(1)}, f32[128,1024]{1,0:T(8,128)S(1)}, f32[16,128]{1,0:T(8,128)S(1)}) custom-call(f32[1,2048]{1,0:T(1,128)S(1)} %constant_dynamic-update-slice_fusion.8.energy, f32[1024,768]{1,0:T(8,128)} %get-tuple-element.39.refs_0_, f32[1024,512]{1,0:T(8,128)} %get-tuple-element.40.refs_1_, ...), custom_call_target="tpu_custom_call" | custom-call | flops 1073741824 | bytes 6291456 | tf_op jit(solution)/shard_map/pallas_call | solution.py:203
  105.5 2.7 %collective-permute-start.25 = (bf16[144,1024]{1,0:T(8,128)(2,1)S(1)}, bf16[144,1024]{1,0:T(8,128)(2,1)S(1)}, u32[]{:S(2)}, u32[]{:S(2)}) collective-permute-start(bf16[144,1024]{1,0:T(8,128)(2,1)S(1)} %get-tuple-element.50), channel_id=1, source_target_pairs={{0,128},{64,192},{128,0},{192,64},{1,129},{65,193},{129,1},{193,65... | collective-permute-start | bytes 884744 | tf_op jit(solution)/shard_map/ppermute | solution.py:19
  108.6 2.2 %collective-permute-start.27 = (bf16[144,1024]{1,0:T(8,128)(2,1)S(1)}, bf16[144,1024]{1,0:T(8,128)(2,1)S(1)}, u32[]{:S(2)}, u32[]{:S(2)}) collective-permute-start(bf16[144,1024]{1,0:T(8,128)(2,1)S(1)} %get-tuple-element.52), channel_id=1, source_target_pairs={{0,192},{64,0},{128,64},{192,128},{1,193},{65,1},{129,65},{193,129... | collective-permute-start | bytes 884744 | tf_op jit(solution)/shard_map/ppermute | solution.py:19
  111.4 4.0 %collective-permute-done.25.one = bf16[144,1024]{1,0:T(8,128)(2,1)S(1)} collective-permute-done((bf16[144,1024]{1,0:T(8,128)(2,1)S(1)}, bf16[144,1024]{1,0:T(8,128)(2,1)S(1)}, u32[]{:S(2)}, u32[]{:S(2)}) %collective-permute-start.25) | collective-permute-done | bytes 294944 | tf_op jit(solution)/shard_map/ppermute | solution.py:19
  115.4 7.0 %collective-permute-done.26.two = bf16[144,1024]{1,0:T(8,128)(2,1)S(1)} collective-permute-done((bf16[144,1024]{1,0:T(8,128)(2,1)S(1)}, bf16[144,1024]{1,0:T(8,128)(2,1)S(1)}, u32[]{:S(2)}, u32[]{:S(2)}) %collective-permute-start.26) | collective-permute-done | bytes 294944 | tf_op jit(solution)/shard_map/ppermute | solution.py:19
  (124 shorter events, 17.0 us)
Async XLA Ops:
  0.6 38.0 %copy-start.7 = (bf16[128,1024]{1,0:T(8,128)(2,1)S(1)}, bf16[128,1024]{1,0:T(8,128)(2,1)}, u32[]{:S(2)}) copy-start(bf16[128,1024]{1,0:T(8,128)(2,1)} %centroids.1) | copy-start | bytes 786436
  1.9 12.6 %collective-permute-start.3 = (bf16[256,1024]{1,0:T(8,128)(2,1)S(1)}, bf16[256,1024]{1,0:T(8,128)(2,1)S(1)}, u32[]{:S(2)}, u32[]{:S(2)}) collective-permute-start(bf16[256,1024]{1,0:T(8,128)(2,1)S(1)} %constant_dynamic-slice_fusion.2), channel_id=1, source_target_pairs={{0,8},{1,57},{8,16},{9,1},{16,24},{17,9},{24,32},{25,17},{32,40},{... | collective-permute-start | bytes 1572872 | tf_op jit(solution)/shard_map/ppermute | solution.py:31
  14.5 30.5 %copy-start.4 = (bf16[256,1024]{1,0:T(8,128)(2,1)}, bf16[256,1024]{1,0:T(8,128)(2,1)S(1)}, u32[]{:S(2)}) copy-start(bf16[256,1024]{1,0:T(8,128)(2,1)S(1)} %collective-permute-done.3.refs_9_.refs_6_) | copy-start | bytes 1572868
  14.5 18.6 %collective-permute-start.4 = (bf16[256,1024]{1,0:T(8,128)(2,1)S(1)}, bf16[256,1024]{1,0:T(8,128)(2,1)S(1)}, u32[]{:S(2)}, u32[]{:S(2)}) collective-permute-start(bf16[256,1024]{1,0:T(8,128)(2,1)S(1)} %collective-permute-done.3.refs_9_.refs_6_), channel_id=1, source_target_pairs={{0,8},{1,57},{8,16},{9,1},{16,24},{17,9},{24,32},{25,17},{32,40},{... | collective-permute-start | bytes 1572872 | tf_op jit(solution)/shard_map/ppermute | solution.py:31
  17.6 8.9 %collective-permute-start.2 = (bf16[128,1024]{1,0:T(8,128)(2,1)}, bf16[128,1024]{1,0:T(8,128)(2,1)}, u32[]{:S(2)}, u32[]{:S(2)}) collective-permute-start(bf16[128,1024]{1,0:T(8,128)(2,1)} %centroids.1), channel_id=1, source_target_pairs={{0,64},{64,128},{128,192},{192,0},{1,65},{65,129},{129,193},{193,1... | collective-permute-start | bytes 786440 | tf_op jit(solution)/shard_map/ppermute | solution.py:19
  18.8 14.3 %collective-permute-start.1 = (bf16[128,1024]{1,0:T(8,128)(2,1)}, bf16[128,1024]{1,0:T(8,128)(2,1)}, u32[]{:S(2)}, u32[]{:S(2)}) collective-permute-start(bf16[128,1024]{1,0:T(8,128)(2,1)} %centroids.1), channel_id=1, source_target_pairs={{0,128},{64,192},{128,0},{192,64},{1,129},{65,193},{129,1},{193,65... | collective-permute-start | bytes 786440 | tf_op jit(solution)/shard_map/ppermute | solution.py:19
  21.3 11.8 %collective-permute-start = (bf16[128,1024]{1,0:T(8,128)(2,1)}, bf16[128,1024]{1,0:T(8,128)(2,1)}, u32[]{:S(2)}, u32[]{:S(2)}) collective-permute-start(bf16[128,1024]{1,0:T(8,128)(2,1)} %centroids.1), channel_id=1, source_target_pairs={{0,192},{64,0},{128,64},{192,128},{1,193},{65,1},{129,65},{193,129... | collective-permute-start | bytes 786440 | tf_op jit(solution)/shard_map/ppermute | solution.py:19
  22.4 13.4 %collective-permute-start.9 = (bf16[256,1024]{1,0:T(8,128)(2,1)S(1)}, bf16[256,1024]{1,0:T(8,128)(2,1)}, u32[]{:S(2)}, u32[]{:S(2)}) collective-permute-start(bf16[256,1024]{1,0:T(8,128)(2,1)S(1)} %collective-permute-done.3.refs_9_.refs_6_), channel_id=1, source_target_pairs={{0,2},{1,7},{2,0},{3,5},{4,6},{5,3},{6,4},{7,1},{8,10},{9,15},{10,... | collective-permute-start | bytes 1572872 | tf_op jit(solution)/shard_map/ppermute | solution.py:47
  26.5 7.4 %collective-permute-start.8 = (bf16[128,1024]{1,0:T(8,128)(2,1)}, bf16[128,1024]{1,0:T(8,128)(2,1)S(1)}, u32[]{:S(2)}, u32[]{:S(2)}) collective-permute-start(bf16[128,1024]{1,0:T(8,128)(2,1)} %centroids.1), channel_id=1, source_target_pairs={{0,1},{1,0},{2,3},{3,2},{4,5},{5,4},{6,7},{7,6},{8,9},{9,8},{10,11... | collective-permute-start | bytes 786440 | tf_op jit(solution)/shard_map/ppermute | solution.py:23
  33.1 15.7 %copy-start.5 = (bf16[256,1024]{1,0:T(8,128)(2,1)}, bf16[256,1024]{1,0:T(8,128)(2,1)S(1)}, u32[]{:S(2)}) copy-start(bf16[256,1024]{1,0:T(8,128)(2,1)S(1)} %collective-permute-done.4.refs_8_) | copy-start | bytes 1572868
  33.1 5.5 %collective-permute-start.5 = (bf16[128,1024]{1,0:T(8,128)(2,1)}, bf16[128,1024]{1,0:T(8,128)(2,1)}, u32[]{:S(2)}, u32[]{:S(2)}) collective-permute-start(bf16[128,1024]{1,0:T(8,128)(2,1)} %collective-permute-done.1.refs_0_), channel_id=1, source_target_pairs={{0,1},{1,0},{2,3},{3,2},{4,5},{5,4},{6,7},{7,6},{8,9},{9,8},{10,11... | collective-permute-start | bytes 786440 | tf_op jit(solution)/shard_map/ppermute | solution.py:23
  33.4 5.2 %collective-permute-start.6 = (bf16[128,1024]{1,0:T(8,128)(2,1)}, bf16[128,1024]{1,0:T(8,128)(2,1)}, u32[]{:S(2)}, u32[]{:S(2)}) collective-permute-start(bf16[128,1024]{1,0:T(8,128)(2,1)} %collective-permute-done.refs_2_), channel_id=1, source_target_pairs={{0,1},{1,0},{2,3},{3,2},{4,5},{5,4},{6,7},{7,6},{8,9},{9,8},{10,11... | collective-permute-start | bytes 786440 | tf_op jit(solution)/shard_map/ppermute | solution.py:23
  33.7 5.0 %collective-permute-start.7 = (bf16[128,1024]{1,0:T(8,128)(2,1)}, bf16[128,1024]{1,0:T(8,128)(2,1)}, u32[]{:S(2)}, u32[]{:S(2)}) collective-permute-start(bf16[128,1024]{1,0:T(8,128)(2,1)} %collective-permute-done.2.refs_4_), channel_id=1, source_target_pairs={{0,1},{1,0},{2,3},{3,2},{4,5},{5,4},{6,7},{7,6},{8,9},{9,8},{10,11... | collective-permute-start | bytes 786440 | tf_op jit(solution)/shard_map/ppermute | solution.py:23
  34.7 10.4 %collective-permute-start.11 = (bf16[256,1024]{1,0:T(8,128)(2,1)S(1)}, bf16[256,1024]{1,0:T(8,128)(2,1)S(1)}, u32[]{:S(2)}, u32[]{:S(2)}) collective-permute-start(bf16[256,1024]{1,0:T(8,128)(2,1)S(1)} %collective-permute-done.4.refs_8_), channel_id=1, source_target_pairs={{0,8},{1,57},{8,16},{9,1},{16,24},{17,9},{24,32},{25,17},{32,40},{... | collective-permute-start | bytes 1572872 | tf_op jit(solution)/shard_map/ppermute | solution.py:31
  35.9 12.9 %collective-permute-start.10 = (bf16[256,1024]{1,0:T(8,128)(2,1)S(1)}, bf16[256,1024]{1,0:T(8,128)(2,1)}, u32[]{:S(2)}, u32[]{:S(2)}) collective-permute-start(bf16[256,1024]{1,0:T(8,128)(2,1)S(1)} %collective-permute-done.4.refs_8_), channel_id=1, source_target_pairs={{0,2},{1,7},{2,0},{3,5},{4,6},{5,3},{6,4},{7,1},{8,10},{9,15},{10,... | collective-permute-start | bytes 1572872 | tf_op jit(solution)/shard_map/ppermute | solution.py:47
  45.8 8.3 %collective-permute-start.13 = (bf16[128,1024]{1,0:T(8,128)(2,1)}, bf16[128,1024]{1,0:T(8,128)(2,1)S(1)}, u32[]{:S(2)}, u32[]{:S(2)}) collective-permute-start(bf16[128,1024]{1,0:T(8,128)(2,1)} %constant_dynamic-slice_fusion), channel_id=1, source_target_pairs={{0,8},{1,57},{8,16},{9,1},{16,24},{17,9},{24,32},{25,17},{32,40},{... | collective-permute-start | bytes 786440 | tf_op jit(solution)/shard_map/ppermute | solution.py:31
  46.3 17.3 %collective-permute-start.12 = (bf16[256,1024]{1,0:T(8,128)(2,1)S(1)}, bf16[256,1024]{1,0:T(8,128)(2,1)S(1)}, u32[]{:S(2)}, u32[]{:S(2)}) collective-permute-start(bf16[256,1024]{1,0:T(8,128)(2,1)S(1)} %collective-permute-done.11.refs_8_.refs_10_), channel_id=1, source_target_pairs={{0,2},{1,7},{2,0},{3,5},{4,6},{5,3},{6,4},{7,1},{8,10},{9,15},{10,... | collective-permute-start | bytes 1572872 | tf_op jit(solution)/shard_map/ppermute | solution.py:47
  54.1 6.5 %collective-permute-start.14 = (bf16[128,1024]{1,0:T(8,128)(2,1)S(1)}, bf16[128,1024]{1,0:T(8,128)(2,1)S(1)}, u32[]{:S(2)}, u32[]{:S(2)}) collective-permute-start(bf16[128,1024]{1,0:T(8,128)(2,1)S(1)} %collective-permute-done.13.refs_9_.refs_12_), channel_id=1, source_target_pairs={{0,2},{1,7},{2,0},{3,5},{4,6},{5,3},{6,4},{7,1},{8,10},{9,15},{10,... | collective-permute-start | bytes 786440 | tf_op jit(solution)/shard_map/ppermute | solution.py:47
  68.0 1.3 %collective-permute-start.15 = (f32[16,128]{1,0:T(8,128)S(1)}, f32[16,128]{1,0:T(8,128)S(1)}, u32[]{:S(2)}, u32[]{:S(2)}) collective-permute-start(f32[16,128]{1,0:T(8,128)S(1)} %concatenate.37), channel_id=1, source_target_pairs={{0,1},{1,0},{2,3},{3,2},{4,5},{5,4},{6,7},{7,6},{8,9},{9,8},{10,11... | collective-permute-start | bytes 24584 | tf_op jit(solution)/shard_map/ppermute | solution.py:23
  69.4 2.7 %collective-permute-start.16 = (f32[8,2,2,128]{3,1,2,0:T(2,128)S(1)}, f32[8,2,2,128]{3,1,2,0:T(2,128)S(1)}, u32[]{:S(2)}, u32[]{:S(2)}) collective-permute-start(f32[8,2,2,128]{3,1,2,0:T(2,128)S(1)} %constant_dynamic-update-slice_fusion), channel_id=1, source_target_pairs={{0,8},{1,57},{8,16},{9,1},{16,24},{17,9},{24,32},{25,17},{32,40},{... | collective-permute-start | bytes 49160 | tf_op jit(solution)/shard_map/ppermute | solution.py:31
  72.1 3.4 %collective-permute-start.17 = (f32[8,2,2,128]{3,1,2,0:T(2,128)S(1)}, f32[8,2,2,128]{3,1,2,0:T(2,128)S(1)}, u32[]{:S(2)}, u32[]{:S(2)}) collective-permute-start(f32[8,2,2,128]{3,1,2,0:T(2,128)S(1)} %maximum_select_fusion), channel_id=1, source_target_pairs={{0,1},{1,0},{2,3},{3,2},{4,5},{5,4},{6,7},{7,6},{8,9},{9,8},{10,11... | collective-permute-start | bytes 49160 | tf_op jit(solution)/shard_map/ppermute | solution.py:23
  75.6 4.5 %collective-permute-start.18 = (f32[8,2,2,128]{3,1,2,0:T(2,128)S(1)}, f32[8,2,2,128]{3,1,2,0:T(2,128)S(1)}, u32[]{:S(2)}, u32[]{:S(2)}) collective-permute-start(f32[8,2,2,128]{3,1,2,0:T(2,128)S(1)} %add_select_fusion), channel_id=1, source_target_pairs={{0,24},{1,41},{8,32},{9,49},{16,40},{17,57},{24,48},{25,1},{32,56}... | collective-permute-start | bytes 49160 | tf_op jit(solution)/shard_map/ppermute | solution.py:31
  80.1 3.6 %collective-permute-start.19 = (f32[8,2,2,128]{3,1,2,0:T(2,128)S(1)}, f32[8,2,2,128]{3,1,2,0:T(2,128)S(1)}, u32[]{:S(2)}, u32[]{:S(2)}) collective-permute-start(f32[8,2,2,128]{3,1,2,0:T(2,128)S(1)} %maximum_select_fusion.1), channel_id=1, source_target_pairs={{0,1},{1,0},{2,3},{3,2},{4,5},{5,4},{6,7},{7,6},{8,9},{9,8},{10,11... | collective-permute-start | bytes 49160 | tf_op jit(solution)/shard_map/ppermute | solution.py:23
  83.9 4.2 %collective-permute-start.21 = (f32[8,2,2,128]{3,1,2,0:T(2,128)S(1)}, f32[8,2,2,128]{3,1,2,0:T(2,128)S(1)}, u32[]{:S(2)}, u32[]{:S(2)}) collective-permute-start(f32[8,2,2,128]{3,1,2,0:T(2,128)S(1)} %log_add_fusion.2), channel_id=1, source_target_pairs={{0,4},{1,5},{2,6},{3,7},{4,0},{5,1},{6,2},{7,3},{8,12},{9,13},{10,... | collective-permute-start | bytes 49160 | tf_op jit(solution)/shard_map/ppermute | solution.py:39
  86.3 2.8 %collective-permute-start.20 = (f32[8,2,2,128]{3,1,2,0:T(2,128)S(1)}, f32[8,2,2,128]{3,1,2,0:T(2,128)S(1)}, u32[]{:S(2)}, u32[]{:S(2)}) collective-permute-start(f32[8,2,2,128]{3,1,2,0:T(2,128)S(1)} %log_add_fusion.2), channel_id=1, source_target_pairs={{0,2},{1,7},{2,4},{3,1},{4,6},{5,3},{6,0},{7,5},{8,10},{9,15},{10,... | collective-permute-start | bytes 49160 | tf_op jit(solution)/shard_map/ppermute | solution.py:39
  89.2 3.7 %collective-permute-start.22 = (f32[8,2,2,128]{3,1,2,0:T(2,128)S(1)}, f32[8,2,2,128]{3,1,2,0:T(2,128)S(1)}, u32[]{:S(2)}, u32[]{:S(2)}) collective-permute-start(f32[8,2,2,128]{3,1,2,0:T(2,128)S(1)} %log_add_fusion.1), channel_id=1, source_target_pairs={{0,1},{1,0},{2,3},{3,2},{4,5},{5,4},{6,7},{7,6},{8,9},{9,8},{10,11... | collective-permute-start | bytes 49160 | tf_op jit(solution)/shard_map/ppermute | solution.py:23
  100.3 5.0 %collective-permute-start.24 = (bf16[432,1024]{1,0:T(8,128)(2,1)S(1)}, bf16[432,1024]{1,0:T(8,128)(2,1)S(1)}, u32[]{:S(2)}, u32[]{:S(2)}) collective-permute-start(bf16[432,1024]{1,0:T(8,128)(2,1)S(1)} %get-tuple-element.47), channel_id=1, source_target_pairs={{0,1},{1,0},{2,3},{3,2},{4,5},{5,4},{6,7},{7,6},{8,9},{9,8},{10,11... | collective-permute-start | bytes 2654216 | tf_op jit(solution)/shard_map/ppermute | solution.py:23
  105.0 17.3 %copy-start.13 = (f32[128]{0:T(128)S(1)}, f32[128]{0:T(128)}, u32[]{:S(2)}) copy-start(f32[128]{0:T(128)} %param.5) | copy-start | bytes 1540
  105.0 6.4 %collective-permute-start.23 = (bf16[144,1024]{1,0:T(8,128)(2,1)S(1)}, bf16[144,1024]{1,0:T(8,128)(2,1)S(1)}, u32[]{:S(2)}, u32[]{:S(2)}) collective-permute-start(bf16[144,1024]{1,0:T(8,128)(2,1)S(1)} %get-tuple-element.46), channel_id=1, source_target_pairs={{0,1},{1,0},{2,3},{3,2},{4,5},{5,4},{6,7},{7,6},{8,9},{9,8},{10,11... | collective-permute-start | bytes 884744 | tf_op jit(solution)/shard_map/ppermute | solution.py:23
  105.5 9.9 %collective-permute-start.25 = (bf16[144,1024]{1,0:T(8,128)(2,1)S(1)}, bf16[144,1024]{1,0:T(8,128)(2,1)S(1)}, u32[]{:S(2)}, u32[]{:S(2)}) collective-permute-start(bf16[144,1024]{1,0:T(8,128)(2,1)S(1)} %get-tuple-element.50), channel_id=1, source_target_pairs={{0,128},{64,192},{128,0},{192,64},{1,129},{65,193},{129,1},{193,65... | collective-permute-start | bytes 884744 | tf_op jit(solution)/shard_map/ppermute | solution.py:19
  108.2 14.2 %collective-permute-start.26 = (bf16[144,1024]{1,0:T(8,128)(2,1)S(1)}, bf16[144,1024]{1,0:T(8,128)(2,1)S(1)}, u32[]{:S(2)}, u32[]{:S(2)}) collective-permute-start(bf16[144,1024]{1,0:T(8,128)(2,1)S(1)} %get-tuple-element.51), channel_id=1, source_target_pairs={{0,64},{64,128},{128,192},{192,0},{1,65},{65,129},{129,193},{193,1... | collective-permute-start | bytes 884744 | tf_op jit(solution)/shard_map/ppermute | solution.py:19
  108.6 13.7 %collective-permute-start.27 = (bf16[144,1024]{1,0:T(8,128)(2,1)S(1)}, bf16[144,1024]{1,0:T(8,128)(2,1)S(1)}, u32[]{:S(2)}, u32[]{:S(2)}) collective-permute-start(bf16[144,1024]{1,0:T(8,128)(2,1)S(1)} %get-tuple-element.52), channel_id=1, source_target_pairs={{0,192},{64,0},{128,64},{192,128},{1,193},{65,1},{129,65},{193,129... | collective-permute-start | bytes 884744 | tf_op jit(solution)/shard_map/ppermute | solution.py:19
  (10 other events, 44.4 us)

commit v4 on v3

--- a/solution.py
+++ b/solution.py
@@ -117,106 +117,131 @@
     return total, tail[:, :n] + tail[:, n : 2 * n]
 
 
-def score_kernel(parts, sizes, *refs):
-    table, pieces, (logits, energy) = refs[:parts], refs[parts:-2], refs[-2:]
-    chunks = []
-    for p in range(0, parts, NC):
-        block = jnp.concatenate([table[p + i][...] for i in range(NC)])
-        wide = block.astype(F32)
-        chunks.append((block, jnp.sum(wide * wide, axis=1, keepdims=True)))
-    span = chunks[0][0].shape[0]
+def score_kernel(parts, sizes, given, *refs):
+    table, refs = refs[:parts], refs[parts:]
+    pieces, refs = refs[: len(sizes)], refs[len(sizes) :]
+    squares, logits, energy = refs
+    n = table[0].shape[0]
+    span = n * NC
+    blocks = [jnp.concatenate([table[p + i][...] for i in range(NC)]) for p in range(0, parts, NC)]
+    if not given:
+        for p, block in enumerate(blocks):
+            wide = block.astype(F32)
+            total = jnp.sum(wide * wide, axis=1, keepdims=True)
+            squares[p * span : (p + 1) * span, :] = jnp.broadcast_to(total, (span, squares.shape[1]))
     at = 0
     for piece, size in zip(pieces, sizes):
         rows, lot = piece[...], slice(at, at + size)
         at += size
         high = None
-        for p, (block, squares) in enumerate(chunks):
+        for p, block in enumerate(blocks):
             product = lax.dot_general(block, rows, (((1,), (1,)), ((), ())), preferred_element_type=F32)
-            scores = 2.0 * product - squares
+            scores = 2.0 * product - squares[p * span : (p + 1) * span, :1]
             logits[p * span : (p + 1) * span, lot] = scores
             top = jnp.max(scores, axis=0, keepdims=True)
             high = top if high is None else jnp.maximum(high, top)
         total = None
-        for p in range(len(chunks)):
+        for p in range(len(blocks)):
             part = jnp.sum(jnp.exp(logits[p * span : (p + 1) * span, lot] - high), axis=0, keepdims=True)
             total = part if total is None else total + part
         energy[:, lot] = high + jnp.log(total)
 
 
-def score(table, pieces):
+def score(table, pieces, squares=None):
     count, width = sum(t.shape[0] for t in table), table[0].shape[1]
     sizes = tuple(p.shape[0] for p in pieces)
-    rows = sum(sizes)
-    return pl.pallas_call(
-        functools.partial(score_kernel, len(table), sizes),
-        out_shape=(
-            pltpu.HBM((count, rows), F32) if PIN else jax.ShapeDtypeStruct((count, rows), F32),
-            jax.ShapeDtypeStruct((1, rows), F32),
-        ),
+    rows, given = sum(sizes), squares is not None
+    out = [
+        pltpu.HBM((count, rows), F32) if PIN else jax.ShapeDtypeStruct((count, rows), F32),
+        jax.ShapeDtypeStruct((1, rows), F32),
+    ]
+    if not given:
+        out.insert(0, jax.ShapeDtypeStruct((count, 128), F32))
+    got = pl.pallas_call(
+        functools.partial(score_kernel, len(table), sizes, given),
+        out_shape=out,
         compiler_params=pltpu.CompilerParams(vmem_limit_bytes=VMEM_LIMIT),
         cost_estimate=pl.CostEstimate(
             flops=4 * count * rows * width,
             bytes_accessed=4 * count * rows + 2 * (count + rows) * width,
             transcendentals=count * rows,
         ),
-    )(*table, *pieces)
-
-
-def weigh_kernel(groups, sizes, energy, *refs):
-    logits, slab = refs[: len(groups)], refs[len(groups) : len(groups) + len(sizes)]
-    message, keep, keep_count = refs[len(groups) + len(sizes) :]
-    n, width = keep.shape
-    step = min(sizes)
-    counts, sets, at = None, [], 0
-    for p, size in enumerate(groups):
-        w = jnp.exp(logits[p][...] - energy[:, at : at + size])
-        at += size
-        for cut in range(0, size, step):
-            part = w[:, cut : cut + step]
-            counts = part if counts is None else counts + part
-            sets.append(part.astype(BF16))
-    column = jnp.sum(counts, axis=1, keepdims=True)
-    pairs = [jnp.concatenate(sets[p : p + 2], axis=1) for p in range(0, len(sets), 2)]
+    )(*table, *pieces, *([squares] if given else []))
+    return (squares, *got) if given else got
+
+
+def weigh_kernel(first, groups, sizes, energy, *refs):
+    logits, refs = refs[: len(groups)], refs[len(groups) :]
+    slab, refs = refs[: len(sizes)], refs[len(sizes) :]
+    message, keep, keep_count, scores, rows, sums, counts, sems = refs
+    height, width = sums.shape
+    n = keep_count.shape[1]
+    span = n * NC
+    starts = [sum(sizes[:p]) for p in range(len(sizes))]
+    edges = [sum(groups[:g]) for g in range(len(groups))]
+    copies = []
+    for p, (at, size) in enumerate(zip(starts, sizes)):
+        g = max(i for i, edge in enumerate(edges) if edge <= at)
+        part = logits[g].at[first * span : first * span + height, at - edges[g] : at - edges[g] + size]
+        pair = (
+            pltpu.make_async_copy(part, scores.at[:, at : at + size], sems.at[0, p]),
+            pltpu.make_async_copy(slab[p], rows.at[at : at + size, :], sems.at[1, p]),
+        )
+        for copy in pair:
+            copy.start()
+        copies.append(pair)
     tile = min(256, width)
-    totals = []
-    for at in range(0, width, tile):
-        acc = None
-        for p, pair in enumerate(pairs):
-            if p < len(sizes) - 2:
-                rows = slab[p][:, at : at + tile]
-            else:
-                rows = jnp.concatenate([slab[p][:, at : at + tile], slab[p + 1][:, at : at + tile]])
-            term = jnp.dot(pair, rows, preferred_element_type=F32)
-            acc = term if acc is None else acc + term
-        keep[:, at : at + tile] = acc[:n]
-        totals.append(acc[n:])
-    keep_count[...] = turned(column[:n])[:TAIL]
-    write_message(message, 0, jnp.concatenate(totals, axis=1), turned(column[n:])[:TAIL])
+    for step in range(0, len(sizes) - 1, 2):
+        last = step + 3 >= len(sizes)
+        stop = len(sizes) if last else step + 2
+        for p in range(step, stop):
+            for copy in copies[p]:
+                copy.wait()
+        at, end = starts[step], starts[stop - 1] + sizes[stop - 1]
+        for lot in range(0, height, span):
+            block = slice(lot, lot + span)
+            w = jnp.exp(scores[block, at:end] - energy[:, at:end])
+            part = functools.reduce(jnp.add, [w[:, k : k + 128] for k in range(0, end - at, 128)])
+            counts[block, :] = part if step == 0 else counts[block, :] + part
+            w = w.astype(BF16)
+            for col in range(0, width, tile):
+                term = jnp.dot(w, rows[at:end, col : col + tile], preferred_element_type=F32)
+                sums[block, col : col + tile] = term if step == 0 else sums[block, col : col + tile] + term
+        if last:
+            break
+    for i in range(height // span):
+        column = jnp.sum(counts[i * span : (i + 1) * span, :], axis=1, keepdims=True)
+        keep[i * n : (i + 1) * n, :] = sums[i * span : i * span + n, :]
+        keep_count[i * TAIL : (i + 1) * TAIL, :] = turned(column[:n])[:TAIL]
+        write_message(message, i * (n + TAIL), sums[i * span + n : (i + 1) * span, :], turned(column[n:])[:TAIL])
 
 
 def weigh(first, count, logits, energy, slab):
     span, width = logits[0].shape[0] // NX, slab[0].shape[1]
     n = span // NC
-    sizes = tuple(p.shape[0] for p in slab)
-    block = lambda rows, cols: pl.BlockSpec((rows, cols), lambda i: (i, 0))
-    whole = lambda v: pl.BlockSpec(v.shape, lambda i: (0, 0))
+    sizes, groups = tuple(p.shape[0] for p in slab), tuple(v.shape[1] for v in logits)
+    total, height = sum(sizes), count * span
+    away = pl.BlockSpec(memory_space=pl.ANY)
     return pl.pallas_call(
-        functools.partial(weigh_kernel, tuple(v.shape[1] for v in logits), sizes),
-        grid=(count,),
-        in_specs=[whole(energy)]
-        + [pl.BlockSpec((span, v.shape[1]), lambda i: (i + first, 0)) for v in logits]
-        + [whole(p) for p in slab],
-        out_specs=(block(n + TAIL, width), block(n, width), block(TAIL, n)),
+        functools.partial(weigh_kernel, first, groups, sizes),
+        in_specs=[pl.BlockSpec(memory_space=pltpu.VMEM)] + [away] * (len(groups) + len(sizes)),
         out_shape=(
             jax.ShapeDtypeStruct((count * (n + TAIL), width), BF16),
             jax.ShapeDtypeStruct((count * n, width), F32),
             jax.ShapeDtypeStruct((count * TAIL, n), F32),
         ),
+        scratch_shapes=[
+            pltpu.VMEM((height, total), F32),
+            pltpu.VMEM((total, width), BF16),
+            pltpu.VMEM((height, width), F32),
+            pltpu.VMEM((height, 128), F32),
+            pltpu.SemaphoreType.DMA((2, len(sizes))),
+        ],
         compiler_params=pltpu.CompilerParams(vmem_limit_bytes=VMEM_LIMIT),
         cost_estimate=pl.CostEstimate(
-            flops=2 * count * span * sum(sizes) * width,
-            bytes_accessed=4 * count * span * sum(sizes) + 2 * sum(sizes) * width,
-            transcendentals=count * span * sum(sizes),
+            flops=2 * height * total * width,
+            bytes_accessed=4 * height * total + 2 * total * width,
+            transcendentals=height * total,
         ),
     )(energy, *logits, *slab)
 
@@ -268,36 +293,37 @@
     half, sub = rows // 2, rows // 4
     h = lax.rem(y, 2)
 
-    near = {d: shift_x(centroids, -d) for d in (2, 1, 3)}
+    near = {0: centroids, 1: shift_x(centroids, -1), 3: shift_x(centroids, 1)}
 
     mine = lax.dynamic_slice_in_dim(embeddings, h * half, half, 0)
     one = along_z(mine, 1)
     own = lax.dynamic_slice_in_dim(embeddings.reshape(2, 2, sub, width), c, 1, 1).reshape(half, width)
+    one, near[1], near[3] = lax.optimization_barrier((one, near[1], near[3]))
     two = along_z(one, 1)
+    near[2] = shift_x(near[1], -1)
+    first = swap_halves(one)
+    two, near[2], first = lax.optimization_barrier((two, near[2], first))
     three = along_z(two, 1)
 
-    late = lax.optimization_barrier([near[1], near[2], near[3], two])
-    near = {0: centroids, 1: late[0], 2: late[1], 3: late[2]}
     table = [v for d in ORDER for v in (near[d], swap_cores(near[d]))]
 
     fixed = lambda v: pltpu.with_memory_space_constraint(v, pltpu.HBM) if PIN else v
-    logits, local, pieces = [], [], []
-
-    def scored(*rows):
-        scores, energy = score(table, rows)
-        logits.append(fixed(scores))
-        local.append(energy)
-        pieces.extend(rows)
-        return energy
-
-    done = scored(own, one, swap_halves(one))
-    last, _ = lax.optimization_barrier((lax.dynamic_slice_in_dim(three, c * sub, sub, 0), done))
-    four = along_z(last, 1)
-    done = scored(two, swap_halves(two))
-    last, _ = lax.optimization_barrier((four, done))
-    scored(three)
-    scored(swap_halves(three), four)
-    scored(swap_halves(last))
+    four = along_z(lax.dynamic_slice_in_dim(three, c * sub, sub, 0), 1)
+    lots = [(own, one, first, two, swap_halves(two))]
+    squares, scores, energy = score(table, lots[0])
+    logits, local = [scores], [energy]
+    last, _ = lax.optimization_barrier((four, energy))
+    last = swap_halves(last)
+    lots.append((three, swap_halves(three), four))
+    _, scores, energy = score(table, lots[1], squares)
+    last, _ = lax.optimization_barrier((last, energy))
+    logits.append(scores)
+    local.append(energy)
+    lots.append((last,))
+    _, scores, energy = score(table, lots[2], squares)
+    logits.append(scores)
+    local.append(energy)
+    logits, pieces = [fixed(v) for v in logits], [fixed(v) for lot in lots for v in lot]
 
     local = jnp.concatenate(local, axis=1).reshape(-1, sub)
     cut = lambda at, n, *shape: local[at : at + n].reshape(*shape, sub)

time: 124 us -> 119 us (0.960)
  Pallas kernels: 32.5 us -> 26.3 us
  local copies, waits for them, and re-layouts: 6.71 us -> 9.5 us
  waiting for transfers between devices: 37.7 us -> 35.3 us
    pallas_call x7 -> x5, Pallas kernels: 31.2 us -> 25.1 us  [the longest x3 15.8 us: score(): pl.pallas_call(functools.partial(score_kernel, len(table), sizes, given),...]
    ppermute x6, starting transfers between devices: 13.1 us -> 16.9 us  [along_z(): return lax.ppermute(value, ('z', 'c'), pairs)]
    ppermute x4, starting transfers between devices: 8.58 us -> 5.59 us  [swap_halves(): return lax.ppermute(value, ('y', 'c'), pairs)]
    unnamed x37 -> x41, local copies, waits for them, and re-layouts: 4.86 us -> 7.63 us
    ppermute x6, waiting for transfers between devices: 11.4 us -> 9.58 us  [along_z(): return lax.ppermute(value, ('z', 'c'), pairs)]
    ppermute x4, waiting for transfers between devices: 1.78 us -> 0.01 us  [swap_halves(): return lax.ppermute(value, ('y', 'c'), pairs)]
    ppermute x2, starting transfers between devices: 3.25 us -> 1.65 us  [along_y(): return lax.ppermute(value, ('y', 'c'), pairs)]
    ppermute x10, starting transfers between devices: 10.1 us -> 11.4 us  [swap_cores(): return lax.ppermute(value, 'c', [(0, 1), (1, 0)])]
  transfers between devices with their start and end apart: 28 -> 28, of which waited for: 14 -> 13; matrix products, arithmetic and copies ran while one was open for 1% -> 1% of each run, Pallas kernels for 16% -> 14%
where the time goes in v4:
time: 119 us; the launch traced here: 118 us
  starting transfers between devices  45.9 us (39%)
  waiting for transfers between devices  35.3 us (30%)
  Pallas kernels  26.3 us (22%)
  local copies, waits for them, and re-layouts  9.5 us (8%)
    ppermute x6, waiting for transfers between devices, shift_x(): return lax.ppermute(value, 'x', [(i, (i + by) % NX) for i in range(NX)])  19.5 us
    ppermute x6, starting transfers between devices, along_z(): return lax.ppermute(value, ('z', 'c'), pairs)  16.9 us
    pallas_call x3, Pallas kernels, score(): pl.pallas_call(functools.partial(score_kernel, len(table), sizes, given),...  15.8 us
    ppermute x10, starting transfers between devices, swap_cores(): return lax.ppermute(value, 'c', [(0, 1), (1, 0)])  11.4 us
    ppermute x6, starting transfers between devices, shift_x(): return lax.ppermute(value, 'x', [(i, (i + by) % NX) for i in range(NX)])  10.4 us
    ppermute x6, waiting for transfers between devices, along_z(): return lax.ppermute(value, ('z', 'c'), pairs)  9.58 us
    pallas_call x2, Pallas kernels, weigh(): pl.pallas_call(functools.partial(weigh_kernel, first, groups, sizes), in_...  9.21 us
    unnamed x41, local copies, waits for them, and re-layouts  7.63 us
  transfers between devices with their start and end apart: 28, of which 13 were waited for; matrix products, arithmetic and copies ran while one was open for 1% of the time, Pallas kernels for 14%

profile of v4, /device:TPU:1, one launch (start us, length us, event | category | flops | bytes accessed | tf_op | source)
XLA Modules:
  0.0 118.4 jit_solution(14464861438413983969)
XLA Ops:
  0.7 1.2 %copy-done = bf16[512,1024]{1,0:T(8,128)(2,1)S(1)} copy-done((bf16[512,1024]{1,0:T(8,128)(2,1)S(1)}, bf16[512,1024]{1,0:T(8,128)(2,1)}, u32[]{:S(2)}) %copy-start) | copy-done | bytes 1048600
  1.9 6.5 %collective-permute-start = (bf16[256,1024]{1,0:T(8,128)(2,1)S(1)}, bf16[256,1024]{1,0:T(8,128)(2,1)S(1)}, u32[]{:S(2)}, u32[]{:S(2)}) collective-permute-start(bf16[256,1024]{1,0:T(8,128)(2,1)S(1)} %constant_dynamic-slice_fusion.2), channel_id=1, source_target_pairs={{0,8},{1,57},{8,16},{9,1},{16,24},{17,9},{24,32},{25,17},{32,40},{... | collective-permute-start | bytes 1572872 | tf_op jit(solution)/shard_map/ppermute | solution.py:31
  8.4 1.2 %collective-permute-start.2 = (bf16[128,1024]{1,0:T(8,128)(2,1)}, bf16[128,1024]{1,0:T(8,128)(2,1)}, u32[]{:S(2)}, u32[]{:S(2)}) collective-permute-start(bf16[128,1024]{1,0:T(8,128)(2,1)} %centroids.1), channel_id=1, source_target_pairs={{0,64},{64,128},{128,192},{192,0},{1,65},{65,129},{129,193},{193,1... | collective-permute-start | bytes 786440 | tf_op jit(solution)/shard_map/ppermute | solution.py:19
  9.6 1.5 %collective-permute-start.1 = (bf16[128,1024]{1,0:T(8,128)(2,1)}, bf16[128,1024]{1,0:T(8,128)(2,1)}, u32[]{:S(2)}, u32[]{:S(2)}) collective-permute-start(bf16[128,1024]{1,0:T(8,128)(2,1)} %centroids.1), channel_id=1, source_target_pairs={{0,192},{64,0},{128,64},{192,128},{1,193},{65,1},{129,65},{193,129... | collective-permute-start | bytes 786440 | tf_op jit(solution)/shard_map/ppermute | solution.py:19
  11.1 4.5 %collective-permute-done.2.refs_4_ = bf16[128,1024]{1,0:T(8,128)(2,1)} collective-permute-done((bf16[128,1024]{1,0:T(8,128)(2,1)}, bf16[128,1024]{1,0:T(8,128)(2,1)}, u32[]{:S(2)}, u32[]{:S(2)}) %collective-permute-start.2) | collective-permute-done | bytes 262176 | tf_op jit(solution)/shard_map/ppermute | solution.py:19
  15.9 2.7 %collective-permute-start.5 = (bf16[256,1024]{1,0:T(8,128)(2,1)S(1)}, bf16[256,1024]{1,0:T(8,128)(2,1)S(1)}, u32[]{:S(2)}, u32[]{:S(2)}) collective-permute-start(bf16[256,1024]{1,0:T(8,128)(2,1)S(1)} %collective-permute-done.refs_9_.refs_4_), channel_id=1, source_target_pairs={{0,2},{1,7},{2,0},{3,5},{4,6},{5,3},{6,4},{7,1},{8,10},{9,15},{10,... | collective-permute-start | bytes 1572872 | tf_op jit(solution)/shard_map/ppermute | solution.py:47
  18.6 2.7 %collective-permute-start.3 = (bf16[256,1024]{1,0:T(8,128)(2,1)S(1)}, bf16[256,1024]{1,0:T(8,128)(2,1)}, u32[]{:S(2)}, u32[]{:S(2)}) collective-permute-start(bf16[256,1024]{1,0:T(8,128)(2,1)S(1)} %collective-permute-done.refs_9_.refs_4_), channel_id=1, source_target_pairs={{0,8},{1,57},{8,16},{9,1},{16,24},{17,9},{24,32},{25,17},{32,40},{... | collective-permute-start | bytes 1572872 | tf_op jit(solution)/shard_map/ppermute | solution.py:31
  21.4 2.3 %collective-permute-start.4 = (bf16[128,1024]{1,0:T(8,128)(2,1)}, bf16[128,1024]{1,0:T(8,128)(2,1)}, u32[]{:S(2)}, u32[]{:S(2)}) collective-permute-start(bf16[128,1024]{1,0:T(8,128)(2,1)} %collective-permute-done.1.refs_2_), channel_id=1, source_target_pairs={{0,192},{64,0},{128,64},{192,128},{1,193},{65,1},{129,65},{193,129... | collective-permute-start | bytes 786440 | tf_op jit(solution)/shard_map/ppermute | solution.py:19
  23.6 3.8 %collective-permute-done.4.refs_0_ = bf16[128,1024]{1,0:T(8,128)(2,1)} collective-permute-done((bf16[128,1024]{1,0:T(8,128)(2,1)}, bf16[128,1024]{1,0:T(8,128)(2,1)}, u32[]{:S(2)}, u32[]{:S(2)}) %collective-permute-start.4) | collective-permute-done | bytes 262176 | tf_op jit(solution)/shard_map/ppermute | solution.py:19
  27.5 3.2 %collective-permute-start.11 = (bf16[256,1024]{1,0:T(8,128)(2,1)}, bf16[256,1024]{1,0:T(8,128)(2,1)S(1)}, u32[]{:S(2)}, u32[]{:S(2)}) collective-permute-start(bf16[256,1024]{1,0:T(8,128)(2,1)} %collective-permute-done.3.refs_11_.refs_6_), channel_id=1, source_target_pairs={{0,8},{1,57},{8,16},{9,1},{16,24},{17,9},{24,32},{25,17},{32,40},{... | collective-permute-start | bytes 1572872 | tf_op jit(solution)/shard_map/ppermute | solution.py:31
  31.3 5.8 %collective-permute-done.11.refs_8_ = bf16[256,1024]{1,0:T(8,128)(2,1)S(1)} collective-permute-done((bf16[256,1024]{1,0:T(8,128)(2,1)}, bf16[256,1024]{1,0:T(8,128)(2,1)S(1)}, u32[]{:S(2)}, u32[]{:S(2)}) %collective-permute-start.11) | collective-permute-done | bytes 524320 | tf_op jit(solution)/shard_map/ppermute | solution.py:31
  37.2 2.0 %collective-permute-start.6 = (bf16[128,1024]{1,0:T(8,128)(2,1)}, bf16[128,1024]{1,0:T(8,128)(2,1)}, u32[]{:S(2)}, u32[]{:S(2)}) collective-permute-start(bf16[128,1024]{1,0:T(8,128)(2,1)} %collective-permute-done.4.refs_0_), channel_id=1, source_target_pairs={{0,1},{1,0},{2,3},{3,2},{4,5},{5,4},{6,7},{7,6},{8,9},{9,8},{10,11... | collective-permute-start | bytes 786440 | tf_op jit(solution)/shard_map/ppermute | solution.py:23
  41.8 1.4 %collective-permute-start.12 = (bf16[256,1024]{1,0:T(8,128)(2,1)S(1)}, bf16[256,1024]{1,0:T(8,128)(2,1)}, u32[]{:S(2)}, u32[]{:S(2)}) collective-permute-start(bf16[256,1024]{1,0:T(8,128)(2,1)S(1)} %collective-permute-done.11.refs_8_), channel_id=1, source_target_pairs={{0,2},{1,7},{2,0},{3,5},{4,6},{5,3},{6,4},{7,1},{8,10},{9,15},{10,... | collective-permute-start | bytes 1572872 | tf_op jit(solution)/shard_map/ppermute | solution.py:47
  45.1 7.7 %shard_map.58 = (f32[1024,128]{1,0:T(8,128)S(1)}, f32[1024,1280]{1,0:T(8,128)}, f32[1,1280]{1,0:T(1,128)S(1)}) custom-call(bf16[128,1024]{1,0:T(8,128)(2,1)} %collective-permute-done.4.refs_0_, bf16[128,1024]{1,0:T(8,128)(2,1)} %collective-permute-done.6.refs_1_, bf16[128,1024]{1,0:T(8,128)(2,1)} %collective-permute-done.1.refs_2_, ...), custom_call_target="tpu_custom_call" | custom-call | flops 5368709120 | bytes 9961472 | tf_op jit(solution)/shard_map/pallas_call | solution.py:160
  53.6 1.4 %collective-permute-start.14 = (bf16[128,1024]{1,0:T(8,128)(2,1)S(1)}, bf16[128,1024]{1,0:T(8,128)(2,1)S(1)}, u32[]{:S(2)}, u32[]{:S(2)}) collective-permute-start(bf16[128,1024]{1,0:T(8,128)(2,1)S(1)} %collective-permute-done.13.refs_10_), channel_id=1, source_target_pairs={{0,2},{1,7},{2,0},{3,5},{4,6},{5,3},{6,4},{7,1},{8,10},{9,15},{10,... | collective-permute-start | bytes 786440 | tf_op jit(solution)/shard_map/ppermute | solution.py:47
  58.0 5.2 %shard_map.59 = (f32[1024,640]{1,0:T(8,128)}, f32[1,640]{1,0:T(1,128)S(1)}) custom-call(bf16[128,1024]{1,0:T(8,128)(2,1)} %collective-permute-done.4.refs_0_, bf16[128,1024]{1,0:T(8,128)(2,1)} %collective-permute-done.6.refs_1_, bf16[128,1024]{1,0:T(8,128)(2,1)} %collective-permute-done.1.refs_2_, bf16[128,1024]{1,0:T(8,128)(2,1)} %collective-permute-done.7.refs_3_, ...), custom_call_target="tpu_custom_call" | custom-call | flops 2684354560 | bytes 6029312 | tf_op jit(solution)/shard_map/pallas_call | solution.py:160
  63.2 2.9 %shard_map.60 = (f32[1024,128]{1,0:T(8,128)}, f32[1,128]{1,0:T(1,128)S(1)}) custom-call(bf16[128,1024]{1,0:T(8,128)(2,1)} %collective-permute-done.4.refs_0_, bf16[128,1024]{1,0:T(8,128)(2,1)} %collective-permute-done.6.refs_1_, bf16[128,1024]{1,0:T(8,128)(2,1)} %collective-permute-done.1.refs_2_, bf16[128,1024]{1,0:T(8,128)(2,1)} %collective-permute-done.7.refs_3_, ...), custom_call_target="tpu_custom_call" | custom-call | flops 536870912 | bytes 2883584 | tf_op jit(solution)/shard_map/pallas_call | solution.py:160
  66.5 1.2 collective-permute-done.15
  68.8 1.6 %collective-permute-done.16 = f32[8,2,2,128]{3,1,2,0:T(2,128)S(1)} collective-permute-done((f32[8,2,2,128]{3,1,2,0:T(2,128)S(1)}, f32[8,2,2,128]{3,1,2,0:T(2,128)S(1)}, u32[]{:S(2)}, u32[]{:S(2)}) %collective-permute-start.16) | collective-permute-done | bytes 16416 | tf_op jit(solution)/shard_map/ppermute | solution.py:31
  70.5 2.6 %collective-permute-start.17 = (f32[8,2,2,128]{3,1,2,0:T(2,128)S(1)}, f32[8,2,2,128]{3,1,2,0:T(2,128)S(1)}, u32[]{:S(2)}, u32[]{:S(2)}) collective-permute-start(f32[8,2,2,128]{3,1,2,0:T(2,128)S(1)} %maximum_select_fusion), channel_id=1, source_target_pairs={{0,1},{1,0},{2,3},{3,2},{4,5},{5,4},{6,7},{7,6},{8,9},{9,8},{10,11... | collective-permute-start | bytes 49160 | tf_op jit(solution)/shard_map/ppermute | solution.py:23
  74.0 2.4 %collective-permute-start.18 = (f32[8,2,2,128]{3,1,2,0:T(2,128)S(1)}, f32[8,2,2,128]{3,1,2,0:T(2,128)S(1)}, u32[]{:S(2)}, u32[]{:S(2)}) collective-permute-start(f32[8,2,2,128]{3,1,2,0:T(2,128)S(1)} %add_select_fusion), channel_id=1, source_target_pairs={{0,24},{1,41},{8,32},{9,49},{16,40},{17,57},{24,48},{25,1},{32,56}... | collective-permute-start | bytes 49160 | tf_op jit(solution)/shard_map/ppermute | solution.py:31
  76.4 2.1 %collective-permute-done.18 = f32[8,2,2,128]{3,1,2,0:T(2,128)S(1)} collective-permute-done((f32[8,2,2,128]{3,1,2,0:T(2,128)S(1)}, f32[8,2,2,128]{3,1,2,0:T(2,128)S(1)}, u32[]{:S(2)}, u32[]{:S(2)}) %collective-permute-start.18) | collective-permute-done | bytes 16416 | tf_op jit(solution)/shard_map/ppermute | solution.py:31
  78.5 2.8 %collective-permute-start.19 = (f32[8,2,2,128]{3,1,2,0:T(2,128)S(1)}, f32[8,2,2,128]{3,1,2,0:T(2,128)S(1)}, u32[]{:S(2)}, u32[]{:S(2)}) collective-permute-start(f32[8,2,2,128]{3,1,2,0:T(2,128)S(1)} %maximum_select_fusion.1), channel_id=1, source_target_pairs={{0,1},{1,0},{2,3},{3,2},{4,5},{5,4},{6,7},{7,6},{8,9},{9,8},{10,11... | collective-permute-start | bytes 49160 | tf_op jit(solution)/shard_map/ppermute | solution.py:23
  83.9 2.5 %collective-permute-done.21 = f32[8,2,2,128]{3,1,2,0:T(2,128)S(1)} collective-permute-done((f32[8,2,2,128]{3,1,2,0:T(2,128)S(1)}, f32[8,2,2,128]{3,1,2,0:T(2,128)S(1)}, u32[]{:S(2)}, u32[]{:S(2)}) %collective-permute-start.21) | collective-permute-done | bytes 16416 | tf_op jit(solution)/shard_map/ppermute | solution.py:39
  86.5 2.7 %collective-permute-start.22 = (f32[8,2,2,128]{3,1,2,0:T(2,128)S(1)}, f32[8,2,2,128]{3,1,2,0:T(2,128)S(1)}, u32[]{:S(2)}, u32[]{:S(2)}) collective-permute-start(f32[8,2,2,128]{3,1,2,0:T(2,128)S(1)} %log_add_fusion.1), channel_id=1, source_target_pairs={{0,1},{1,0},{2,3},{3,2},{4,5},{5,4},{6,7},{7,6},{8,9},{9,8},{10,11... | collective-permute-start | bytes 49160 | tf_op jit(solution)/shard_map/ppermute | solution.py:23
  90.3 5.8 %shard_map.62 = (bf16[432,1024]{1,0:T(8,128)(2,1)S(1)}, f32[384,1024]{1,0:T(8,128)S(1)}, f32[48,128]{1,0:T(8,128)S(1)}) custom-call(f32[1,2048]{1,0:T(1,128)S(1)} %constant_dynamic-update-slice_fusion.8.energy, f32[1024,1280]{1,0:T(8,128)} %get-tuple-element.41.refs_0_, f32[1024,640]{1,0:T(8,128)} %get-tuple-element.42.refs_1_, ...), custom_call_target="tpu_custom_call" | custom-call | flops 3221225472 | bytes 10485760 | tf_op jit(solution)/shard_map/pallas_call | solution.py:225
  96.6 3.4 %shard_map.61 = (bf16[144,1024]{1,0:T(8,128)(2,1)S(1)}, f32[128,1024]{1,0:T(8,128)S(1)}, f32[16,128]{1,0:T(8,128)S(1)}) custom-call(f32[1,2048]{1,0:T(1,128)S(1)} %constant_dynamic-update-slice_fusion.8.energy, f32[1024,1280]{1,0:T(8,128)} %get-tuple-element.41.refs_0_, f32[1024,640]{1,0:T(8,128)} %get-tuple-element.42.refs_1_, ...), custom_call_target="tpu_custom_call" | custom-call | flops 1073741824 | bytes 6291456 | tf_op jit(solution)/shard_map/pallas_call | solution.py:225
  100.4 2.8 %collective-permute-start.25 = (bf16[144,1024]{1,0:T(8,128)(2,1)S(1)}, bf16[144,1024]{1,0:T(8,128)(2,1)S(1)}, u32[]{:S(2)}, u32[]{:S(2)}) collective-permute-start(bf16[144,1024]{1,0:T(8,128)(2,1)S(1)} %get-tuple-element.50), channel_id=1, source_target_pairs={{0,128},{64,192},{128,0},{192,64},{1,129},{65,193},{129,1},{193,65... | collective-permute-start | bytes 884744 | tf_op jit(solution)/shard_map/ppermute | solution.py:19
  103.6 2.2 %collective-permute-start.27 = (bf16[144,1024]{1,0:T(8,128)(2,1)S(1)}, bf16[144,1024]{1,0:T(8,128)(2,1)S(1)}, u32[]{:S(2)}, u32[]{:S(2)}) collective-permute-start(bf16[144,1024]{1,0:T(8,128)(2,1)S(1)} %get-tuple-element.52), channel_id=1, source_target_pairs={{0,192},{64,0},{128,64},{192,128},{1,193},{65,1},{129,65},{193,129... | collective-permute-start | bytes 884744 | tf_op jit(solution)/shard_map/ppermute | solution.py:19
  106.4 3.9 %collective-permute-done.25.one = bf16[144,1024]{1,0:T(8,128)(2,1)S(1)} collective-permute-done((bf16[144,1024]{1,0:T(8,128)(2,1)S(1)}, bf16[144,1024]{1,0:T(8,128)(2,1)S(1)}, u32[]{:S(2)}, u32[]{:S(2)}) %collective-permute-start.25) | collective-permute-done | bytes 294944 | tf_op jit(solution)/shard_map/ppermute | solution.py:19
  110.3 7.0 %collective-permute-done.26.two = bf16[144,1024]{1,0:T(8,128)(2,1)S(1)} collective-permute-done((bf16[144,1024]{1,0:T(8,128)(2,1)S(1)}, bf16[144,1024]{1,0:T(8,128)(2,1)S(1)}, u32[]{:S(2)}, u32[]{:S(2)}) %collective-permute-start.26) | collective-permute-done | bytes 294944 | tf_op jit(solution)/shard_map/ppermute | solution.py:19
  117.2 1.1 shard_map.64
  (126 shorter events, 17.3 us)
Async XLA Ops:
  1.9 14.0 %collective-permute-start = (bf16[256,1024]{1,0:T(8,128)(2,1)S(1)}, bf16[256,1024]{1,0:T(8,128)(2,1)S(1)}, u32[]{:S(2)}, u32[]{:S(2)}) collective-permute-start(bf16[256,1024]{1,0:T(8,128)(2,1)S(1)} %constant_dynamic-slice_fusion.2), channel_id=1, source_target_pairs={{0,8},{1,57},{8,16},{9,1},{16,24},{17,9},{24,32},{25,17},{32,40},{... | collective-permute-start | bytes 1572872 | tf_op jit(solution)/shard_map/ppermute | solution.py:31
  8.4 7.2 %collective-permute-start.2 = (bf16[128,1024]{1,0:T(8,128)(2,1)}, bf16[128,1024]{1,0:T(8,128)(2,1)}, u32[]{:S(2)}, u32[]{:S(2)}) collective-permute-start(bf16[128,1024]{1,0:T(8,128)(2,1)} %centroids.1), channel_id=1, source_target_pairs={{0,64},{64,128},{128,192},{192,0},{1,65},{65,129},{129,193},{193,1... | collective-permute-start | bytes 786440 | tf_op jit(solution)/shard_map/ppermute | solution.py:19
  9.6 6.3 %collective-permute-start.1 = (bf16[128,1024]{1,0:T(8,128)(2,1)}, bf16[128,1024]{1,0:T(8,128)(2,1)}, u32[]{:S(2)}, u32[]{:S(2)}) collective-permute-start(bf16[128,1024]{1,0:T(8,128)(2,1)} %centroids.1), channel_id=1, source_target_pairs={{0,192},{64,0},{128,64},{192,128},{1,193},{65,1},{129,65},{193,129... | collective-permute-start | bytes 786440 | tf_op jit(solution)/shard_map/ppermute | solution.py:19
  15.9 36.9 %copy-start.4 = (bf16[256,1024]{1,0:T(8,128)(2,1)}, bf16[256,1024]{1,0:T(8,128)(2,1)S(1)}, u32[]{:S(2)}) copy-start(bf16[256,1024]{1,0:T(8,128)(2,1)S(1)} %collective-permute-done.refs_9_.refs_4_) | copy-start | bytes 1572868
  15.9 11.6 %collective-permute-start.5 = (bf16[256,1024]{1,0:T(8,128)(2,1)S(1)}, bf16[256,1024]{1,0:T(8,128)(2,1)S(1)}, u32[]{:S(2)}, u32[]{:S(2)}) collective-permute-start(bf16[256,1024]{1,0:T(8,128)(2,1)S(1)} %collective-permute-done.refs_9_.refs_4_), channel_id=1, source_target_pairs={{0,2},{1,7},{2,0},{3,5},{4,6},{5,3},{6,4},{7,1},{8,10},{9,15},{10,... | collective-permute-start | bytes 1572872 | tf_op jit(solution)/shard_map/ppermute | solution.py:47
  18.6 8.9 %collective-permute-start.3 = (bf16[256,1024]{1,0:T(8,128)(2,1)S(1)}, bf16[256,1024]{1,0:T(8,128)(2,1)}, u32[]{:S(2)}, u32[]{:S(2)}) collective-permute-start(bf16[256,1024]{1,0:T(8,128)(2,1)S(1)} %collective-permute-done.refs_9_.refs_4_), channel_id=1, source_target_pairs={{0,8},{1,57},{8,16},{9,1},{16,24},{17,9},{24,32},{25,17},{32,40},{... | collective-permute-start | bytes 1572872 | tf_op jit(solution)/shard_map/ppermute | solution.py:31
  21.4 6.1 %collective-permute-start.4 = (bf16[128,1024]{1,0:T(8,128)(2,1)}, bf16[128,1024]{1,0:T(8,128)(2,1)}, u32[]{:S(2)}, u32[]{:S(2)}) collective-permute-start(bf16[128,1024]{1,0:T(8,128)(2,1)} %collective-permute-done.1.refs_2_), channel_id=1, source_target_pairs={{0,192},{64,0},{128,64},{192,128},{1,193},{65,1},{129,65},{193,129... | collective-permute-start | bytes 786440 | tf_op jit(solution)/shard_map/ppermute | solution.py:19
  27.5 25.3 %copy-start.5 = (bf16[256,1024]{1,0:T(8,128)(2,1)}, bf16[256,1024]{1,0:T(8,128)(2,1)S(1)}, u32[]{:S(2)}) copy-start(bf16[256,1024]{1,0:T(8,128)(2,1)S(1)} %collective-permute-done.5.refs_10_.refs_5_) | copy-start | bytes 1572868
  27.5 9.7 %collective-permute-start.11 = (bf16[256,1024]{1,0:T(8,128)(2,1)}, bf16[256,1024]{1,0:T(8,128)(2,1)S(1)}, u32[]{:S(2)}, u32[]{:S(2)}) collective-permute-start(bf16[256,1024]{1,0:T(8,128)(2,1)} %collective-permute-done.3.refs_11_.refs_6_), channel_id=1, source_target_pairs={{0,8},{1,57},{8,16},{9,1},{16,24},{17,9},{24,32},{25,17},{32,40},{... | collective-permute-start | bytes 1572872 | tf_op jit(solution)/shard_map/ppermute | solution.py:31
  30.7 12.4 %collective-permute-start.10 = (bf16[256,1024]{1,0:T(8,128)(2,1)}, bf16[256,1024]{1,0:T(8,128)(2,1)}, u32[]{:S(2)}, u32[]{:S(2)}) collective-permute-start(bf16[256,1024]{1,0:T(8,128)(2,1)} %collective-permute-done.3.refs_11_.refs_6_), channel_id=1, source_target_pairs={{0,2},{1,7},{2,0},{3,5},{4,6},{5,3},{6,4},{7,1},{8,10},{9,15},{10,... | collective-permute-start | bytes 1572872 | tf_op jit(solution)/shard_map/ppermute | solution.py:47
  30.8 9.2 %collective-permute-start.9 = (bf16[128,1024]{1,0:T(8,128)(2,1)}, bf16[128,1024]{1,0:T(8,128)(2,1)S(1)}, u32[]{:S(2)}, u32[]{:S(2)}) collective-permute-start(bf16[128,1024]{1,0:T(8,128)(2,1)} %centroids.1), channel_id=1, source_target_pairs={{0,1},{1,0},{2,3},{3,2},{4,5},{5,4},{6,7},{7,6},{8,9},{9,8},{10,11... | collective-permute-start | bytes 786440 | tf_op jit(solution)/shard_map/ppermute | solution.py:23
  30.8 12.3 %collective-permute-start.7 = (bf16[128,1024]{1,0:T(8,128)(2,1)}, bf16[128,1024]{1,0:T(8,128)(2,1)}, u32[]{:S(2)}, u32[]{:S(2)}) collective-permute-start(bf16[128,1024]{1,0:T(8,128)(2,1)} %collective-permute-done.1.refs_2_), channel_id=1, source_target_pairs={{0,1},{1,0},{2,3},{3,2},{4,5},{5,4},{6,7},{7,6},{8,9},{9,8},{10,11... | collective-permute-start | bytes 786440 | tf_op jit(solution)/shard_map/ppermute | solution.py:23
  31.3 10.4 %collective-permute-start.8 = (bf16[128,1024]{1,0:T(8,128)(2,1)}, bf16[128,1024]{1,0:T(8,128)(2,1)}, u32[]{:S(2)}, u32[]{:S(2)}) collective-permute-start(bf16[128,1024]{1,0:T(8,128)(2,1)} %collective-permute-done.2.refs_4_), channel_id=1, source_target_pairs={{0,1},{1,0},{2,3},{3,2},{4,5},{5,4},{6,7},{7,6},{8,9},{9,8},{10,11... | collective-permute-start | bytes 786440 | tf_op jit(solution)/shard_map/ppermute | solution.py:23
  37.2 6.0 %collective-permute-start.6 = (bf16[128,1024]{1,0:T(8,128)(2,1)}, bf16[128,1024]{1,0:T(8,128)(2,1)}, u32[]{:S(2)}, u32[]{:S(2)}) collective-permute-start(bf16[128,1024]{1,0:T(8,128)(2,1)} %collective-permute-done.4.refs_0_), channel_id=1, source_target_pairs={{0,1},{1,0},{2,3},{3,2},{4,5},{5,4},{6,7},{7,6},{8,9},{9,8},{10,11... | collective-permute-start | bytes 786440 | tf_op jit(solution)/shard_map/ppermute | solution.py:23
  40.7 12.9 %collective-permute-start.13 = (bf16[128,1024]{1,0:T(8,128)(2,1)}, bf16[128,1024]{1,0:T(8,128)(2,1)S(1)}, u32[]{:S(2)}, u32[]{:S(2)}) collective-permute-start(bf16[128,1024]{1,0:T(8,128)(2,1)} %constant_dynamic-slice_fusion), channel_id=1, source_target_pairs={{0,8},{1,57},{8,16},{9,1},{16,24},{17,9},{24,32},{25,17},{32,40},{... | collective-permute-start | bytes 786440 | tf_op jit(solution)/shard_map/ppermute | solution.py:31
  41.8 13.3 %collective-permute-start.12 = (bf16[256,1024]{1,0:T(8,128)(2,1)S(1)}, bf16[256,1024]{1,0:T(8,128)(2,1)}, u32[]{:S(2)}, u32[]{:S(2)}) collective-permute-start(bf16[256,1024]{1,0:T(8,128)(2,1)S(1)} %collective-permute-done.11.refs_8_), channel_id=1, source_target_pairs={{0,2},{1,7},{2,0},{3,5},{4,6},{5,3},{6,4},{7,1},{8,10},{9,15},{10,... | collective-permute-start | bytes 1572872 | tf_op jit(solution)/shard_map/ppermute | solution.py:47
  53.6 9.6 %collective-permute-start.14 = (bf16[128,1024]{1,0:T(8,128)(2,1)S(1)}, bf16[128,1024]{1,0:T(8,128)(2,1)S(1)}, u32[]{:S(2)}, u32[]{:S(2)}) collective-permute-start(bf16[128,1024]{1,0:T(8,128)(2,1)S(1)} %collective-permute-done.13.refs_10_), channel_id=1, source_target_pairs={{0,2},{1,7},{2,0},{3,5},{4,6},{5,3},{6,4},{7,1},{8,10},{9,15},{10,... | collective-permute-start | bytes 786440 | tf_op jit(solution)/shard_map/ppermute | solution.py:47
  63.2 27.1 %copy-start.3 = (bf16[128,1024]{1,0:T(8,128)(2,1)}, bf16[128,1024]{1,0:T(8,128)(2,1)S(1)}, u32[]{:S(2)}) copy-start(bf16[128,1024]{1,0:T(8,128)(2,1)S(1)} %collective-permute-done.14.refs_8_.refs_11_) | copy-start | bytes 786436
  66.4 1.3 %collective-permute-start.15 = (f32[16,128]{1,0:T(8,128)S(1)}, f32[16,128]{1,0:T(8,128)S(1)}, u32[]{:S(2)}, u32[]{:S(2)}) collective-permute-start(f32[16,128]{1,0:T(8,128)S(1)} %concatenate.33), channel_id=1, source_target_pairs={{0,1},{1,0},{2,3},{3,2},{4,5},{5,4},{6,7},{7,6},{8,9},{9,8},{10,11... | collective-permute-start | bytes 24584 | tf_op jit(solution)/shard_map/ppermute | solution.py:23
  67.8 2.7 %collective-permute-start.16 = (f32[8,2,2,128]{3,1,2,0:T(2,128)S(1)}, f32[8,2,2,128]{3,1,2,0:T(2,128)S(1)}, u32[]{:S(2)}, u32[]{:S(2)}) collective-permute-start(f32[8,2,2,128]{3,1,2,0:T(2,128)S(1)} %constant_dynamic-update-slice_fusion), channel_id=1, source_target_pairs={{0,8},{1,57},{8,16},{9,1},{16,24},{17,9},{24,32},{25,17},{32,40},{... | collective-permute-start | bytes 49160 | tf_op jit(solution)/shard_map/ppermute | solution.py:31
  70.5 3.4 %collective-permute-start.17 = (f32[8,2,2,128]{3,1,2,0:T(2,128)S(1)}, f32[8,2,2,128]{3,1,2,0:T(2,128)S(1)}, u32[]{:S(2)}, u32[]{:S(2)}) collective-permute-start(f32[8,2,2,128]{3,1,2,0:T(2,128)S(1)} %maximum_select_fusion), channel_id=1, source_target_pairs={{0,1},{1,0},{2,3},{3,2},{4,5},{5,4},{6,7},{7,6},{8,9},{9,8},{10,11... | collective-permute-start | bytes 49160 | tf_op jit(solution)/shard_map/ppermute | solution.py:23
  74.0 4.5 %collective-permute-start.18 = (f32[8,2,2,128]{3,1,2,0:T(2,128)S(1)}, f32[8,2,2,128]{3,1,2,0:T(2,128)S(1)}, u32[]{:S(2)}, u32[]{:S(2)}) collective-permute-start(f32[8,2,2,128]{3,1,2,0:T(2,128)S(1)} %add_select_fusion), channel_id=1, source_target_pairs={{0,24},{1,41},{8,32},{9,49},{16,40},{17,57},{24,48},{25,1},{32,56}... | collective-permute-start | bytes 49160 | tf_op jit(solution)/shard_map/ppermute | solution.py:31
  78.5 3.6 %collective-permute-start.19 = (f32[8,2,2,128]{3,1,2,0:T(2,128)S(1)}, f32[8,2,2,128]{3,1,2,0:T(2,128)S(1)}, u32[]{:S(2)}, u32[]{:S(2)}) collective-permute-start(f32[8,2,2,128]{3,1,2,0:T(2,128)S(1)} %maximum_select_fusion.1), channel_id=1, source_target_pairs={{0,1},{1,0},{2,3},{3,2},{4,5},{5,4},{6,7},{7,6},{8,9},{9,8},{10,11... | collective-permute-start | bytes 49160 | tf_op jit(solution)/shard_map/ppermute | solution.py:23
  82.2 4.2 %collective-permute-start.21 = (f32[8,2,2,128]{3,1,2,0:T(2,128)S(1)}, f32[8,2,2,128]{3,1,2,0:T(2,128)S(1)}, u32[]{:S(2)}, u32[]{:S(2)}) collective-permute-start(f32[8,2,2,128]{3,1,2,0:T(2,128)S(1)} %log_add_fusion.2), channel_id=1, source_target_pairs={{0,4},{1,5},{2,6},{3,7},{4,0},{5,1},{6,2},{7,3},{8,12},{9,13},{10,... | collective-permute-start | bytes 49160 | tf_op jit(solution)/shard_map/ppermute | solution.py:39
  83.2 3.2 %collective-permute-start.20 = (f32[8,2,2,128]{3,1,2,0:T(2,128)S(1)}, f32[8,2,2,128]{3,1,2,0:T(2,128)S(1)}, u32[]{:S(2)}, u32[]{:S(2)}) collective-permute-start(f32[8,2,2,128]{3,1,2,0:T(2,128)S(1)} %log_add_fusion.2), channel_id=1, source_target_pairs={{0,2},{1,7},{2,4},{3,1},{4,6},{5,3},{6,0},{7,5},{8,10},{9,15},{10,... | collective-permute-start | bytes 49160 | tf_op jit(solution)/shard_map/ppermute | solution.py:39
  86.5 3.5 %collective-permute-start.22 = (f32[8,2,2,128]{3,1,2,0:T(2,128)S(1)}, f32[8,2,2,128]{3,1,2,0:T(2,128)S(1)}, u32[]{:S(2)}, u32[]{:S(2)}) collective-permute-start(f32[8,2,2,128]{3,1,2,0:T(2,128)S(1)} %log_add_fusion.1), channel_id=1, source_target_pairs={{0,1},{1,0},{2,3},{3,2},{4,5},{5,4},{6,7},{7,6},{8,9},{9,8},{10,11... | collective-permute-start | bytes 49160 | tf_op jit(solution)/shard_map/ppermute | solution.py:23
  96.1 21.1 %copy-start.15 = (f32[128]{0:T(128)S(1)}, f32[128]{0:T(128)}, u32[]{:S(2)}) copy-start(f32[128]{0:T(128)} %param.5) | copy-start | bytes 1540
  96.2 4.1 %collective-permute-start.24 = (bf16[432,1024]{1,0:T(8,128)(2,1)S(1)}, bf16[432,1024]{1,0:T(8,128)(2,1)S(1)}, u32[]{:S(2)}, u32[]{:S(2)}) collective-permute-start(bf16[432,1024]{1,0:T(8,128)(2,1)S(1)} %get-tuple-element.47), channel_id=1, source_target_pairs={{0,1},{1,0},{2,3},{3,2},{4,5},{5,4},{6,7},{7,6},{8,9},{9,8},{10,11... | collective-permute-start | bytes 2654216 | tf_op jit(solution)/shard_map/ppermute | solution.py:23
  100.0 6.4 %collective-permute-start.23 = (bf16[144,1024]{1,0:T(8,128)(2,1)S(1)}, bf16[144,1024]{1,0:T(8,128)(2,1)S(1)}, u32[]{:S(2)}, u32[]{:S(2)}) collective-permute-start(bf16[144,1024]{1,0:T(8,128)(2,1)S(1)} %get-tuple-element.46), channel_id=1, source_target_pairs={{0,1},{1,0},{2,3},{3,2},{4,5},{5,4},{6,7},{7,6},{8,9},{9,8},{10,11... | collective-permute-start | bytes 884744 | tf_op jit(solution)/shard_map/ppermute | solution.py:23
  100.4 9.9 %collective-permute-start.25 = (bf16[144,1024]{1,0:T(8,128)(2,1)S(1)}, bf16[144,1024]{1,0:T(8,128)(2,1)S(1)}, u32[]{:S(2)}, u32[]{:S(2)}) collective-permute-start(bf16[144,1024]{1,0:T(8,128)(2,1)S(1)} %get-tuple-element.50), channel_id=1, source_target_pairs={{0,128},{64,192},{128,0},{192,64},{1,129},{65,193},{129,1},{193,65... | collective-permute-start | bytes 884744 | tf_op jit(solution)/shard_map/ppermute | solution.py:19
  103.2 14.1 %collective-permute-start.26 = (bf16[144,1024]{1,0:T(8,128)(2,1)S(1)}, bf16[144,1024]{1,0:T(8,128)(2,1)S(1)}, u32[]{:S(2)}, u32[]{:S(2)}) collective-permute-start(bf16[144,1024]{1,0:T(8,128)(2,1)S(1)} %get-tuple-element.51), channel_id=1, source_target_pairs={{0,64},{64,128},{128,192},{192,0},{1,65},{65,129},{129,193},{193,1... | collective-permute-start | bytes 884744 | tf_op jit(solution)/shard_map/ppermute | solution.py:19
  103.6 13.6 %collective-permute-start.27 = (bf16[144,1024]{1,0:T(8,128)(2,1)S(1)}, bf16[144,1024]{1,0:T(8,128)(2,1)S(1)}, u32[]{:S(2)}, u32[]{:S(2)}) collective-permute-start(bf16[144,1024]{1,0:T(8,128)(2,1)S(1)} %get-tuple-element.52), channel_id=1, source_target_pairs={{0,192},{64,0},{128,64},{192,128},{1,193},{65,1},{129,65},{193,129... | collective-permute-start | bytes 884744 | tf_op jit(solution)/shard_map/ppermute | solution.py:19
  (12 other events, 65.8 us)

commit v5 on v4

--- a/solution.py
+++ b/solution.py
@@ -120,37 +120,60 @@
 def score_kernel(parts, sizes, given, *refs):
     table, refs = refs[:parts], refs[parts:]
     pieces, refs = refs[: len(sizes)], refs[len(sizes) :]
-    squares, logits, energy = refs
+    if given:
+        known, logits, energy, block, squares, rows, scores, sems = refs
+    else:
+        squares, logits, energy, block, rows, scores, sems = refs
     n = table[0].shape[0]
+    starts = [sum(sizes[:p]) for p in range(len(sizes))]
+    loads = [pltpu.make_async_copy(t, block.at[p * n : (p + 1) * n, :], sems.at[p]) for p, t in enumerate(table)]
+    if given:
+        loads.append(pltpu.make_async_copy(known, squares, sems.at[parts]))
+    arrivals = [
+        pltpu.make_async_copy(piece, rows.at[at : at + size, :], sems.at[parts + 1 + p])
+        for p, (piece, at, size) in enumerate(zip(pieces, starts, sizes))
+    ]
+    for copy in loads + arrivals:
+        copy.start()
+    for copy in loads:
+        copy.wait()
     span = n * NC
-    blocks = [jnp.concatenate([table[p + i][...] for i in range(NC)]) for p in range(0, parts, NC)]
+    height = parts * n
     if not given:
-        for p, block in enumerate(blocks):
-            wide = block.astype(F32)
+        for at in range(0, height, span):
+            wide = block[at : at + span, :].astype(F32)
             total = jnp.sum(wide * wide, axis=1, keepdims=True)
-            squares[p * span : (p + 1) * span, :] = jnp.broadcast_to(total, (span, squares.shape[1]))
-    at = 0
-    for piece, size in zip(pieces, sizes):
-        rows, lot = piece[...], slice(at, at + size)
-        at += size
+            squares[at : at + span, :] = jnp.broadcast_to(total, (span, squares.shape[1]))
+    leaving = []
+    for p, (at, size) in enumerate(zip(starts, sizes)):
+        arrivals[p].wait()
+        lot = slice(at, at + size)
         high = None
-        for p, block in enumerate(blocks):
-            product = lax.dot_general(block, rows, (((1,), (1,)), ((), ())), preferred_element_type=F32)
-            scores = 2.0 * product - squares[p * span : (p + 1) * span, :1]
-            logits[p * span : (p + 1) * span, lot] = scores
-            top = jnp.max(scores, axis=0, keepdims=True)
+        for k in range(0, height, span):
+            product = lax.dot_general(
+                block[k : k + span, :], rows[lot, :], (((1,), (1,)), ((), ())), preferred_element_type=F32
+            )
+            part = 2.0 * product - squares[k : k + span, :1]
+            scores[k : k + span, lot] = part
+            top = jnp.max(part, axis=0, keepdims=True)
             high = top if high is None else jnp.maximum(high, top)
+        copy = pltpu.make_async_copy(scores.at[:, lot], logits.at[:, lot], sems.at[parts + 1 + len(sizes) + p])
+        copy.start()
+        leaving.append(copy)
         total = None
-        for p in range(len(blocks)):
-            part = jnp.sum(jnp.exp(logits[p * span : (p + 1) * span, lot] - high), axis=0, keepdims=True)
+        for k in range(0, height, span):
+            part = jnp.sum(jnp.exp(scores[k : k + span, lot] - high), axis=0, keepdims=True)
             total = part if total is None else total + part
         energy[:, lot] = high + jnp.log(total)
+    for copy in leaving:
+        copy.wait()
 
 
 def score(table, pieces, squares=None):
     count, width = sum(t.shape[0] for t in table), table[0].shape[1]
     sizes = tuple(p.shape[0] for p in pieces)
     rows, given = sum(sizes), squares is not None
+    away, near = pl.BlockSpec(memory_space=pl.ANY), pl.BlockSpec(memory_space=pltpu.VMEM)
     out = [
         pltpu.HBM((count, rows), F32) if PIN else jax.ShapeDtypeStruct((count, rows), F32),
         jax.ShapeDtypeStruct((1, rows), F32),
@@ -159,7 +182,16 @@
         out.insert(0, jax.ShapeDtypeStruct((count, 128), F32))
     got = pl.pallas_call(
         functools.partial(score_kernel, len(table), sizes, given),
+        in_specs=[away] * (len(table) + len(sizes) + given),
+        out_specs=[away, near] if given else [near, away, near],
         out_shape=out,
+        scratch_shapes=[pltpu.VMEM((count, width), BF16)]
+        + [pltpu.VMEM((count, 128), F32)] * given
+        + [
+            pltpu.VMEM((rows, width), BF16),
+            pltpu.VMEM((count, rows), F32),
+            pltpu.SemaphoreType.DMA((len(table) + 1 + 2 * len(sizes),)),
+        ],
         compiler_params=pltpu.CompilerParams(vmem_limit_bytes=VMEM_LIMIT),
         cost_estimate=pl.CostEstimate(
             flops=4 * count * rows * width,
@@ -305,22 +337,23 @@
     two, near[2], first = lax.optimization_barrier((two, near[2], first))
     three = along_z(two, 1)
 
-    table = [v for d in ORDER for v in (near[d], swap_cores(near[d]))]
-
     fixed = lambda v: pltpu.with_memory_space_constraint(v, pltpu.HBM) if PIN else v
+    table = [fixed(v) for d in ORDER for v in (near[d], swap_cores(near[d]))]
+
     four = along_z(lax.dynamic_slice_in_dim(three, c * sub, sub, 0), 1)
     lots = [(own, one, first, two, swap_halves(two))]
-    squares, scores, energy = score(table, lots[0])
+    squares, scores, energy = score(table, [fixed(v) for v in lots[0]])
+    squares = fixed(squares)
     logits, local = [scores], [energy]
     last, _ = lax.optimization_barrier((four, energy))
     last = swap_halves(last)
     lots.append((three, swap_halves(three), four))
-    _, scores, energy = score(table, lots[1], squares)
+    _, scores, energy = score(table, [fixed(v) for v in lots[1]], squares)
     last, _ = lax.optimization_barrier((last, energy))
     logits.append(scores)
     local.append(energy)
     lots.append((last,))
-    _, scores, energy = score(table, lots[2], squares)
+    _, scores, energy = score(table, [fixed(v) for v in lots[2]], squares)
     logits.append(scores)
     local.append(energy)
     logits, pieces = [fixed(v) for v in logits], [fixed(v) for lot in lots for v in lot]

time: 119 us -> 114 us (0.958)
  local copies, waits for them, and re-layouts: 9.5 us -> 4.69 us
    unnamed x41 -> x27, local copies, waits for them, and re-layouts: 7.63 us -> 2.81 us
  transfers between devices with their start and end apart: 28 -> 28, of which waited for: 13 -> 14; matrix products, arithmetic and copies ran while one was open for 1% -> 1% of each run, Pallas kernels for 14% -> 15%
where the time goes in v5:
time: 114 us
  starting transfers between devices  46.9 us (41%)
  waiting for transfers between devices  34.2 us (30%)
  Pallas kernels  26.8 us (24%)
  local copies, waits for them, and re-layouts  4.69 us (4%)
    ppermute x6, waiting for transfers between devices, shift_x(): return lax.ppermute(value, 'x', [(i, (i + by) % NX) for i in range(NX)])  19.4 us
    ppermute x6, starting transfers between devices, along_z(): return lax.ppermute(value, ('z', 'c'), pairs)  17.4 us
    pallas_call x3, Pallas kernels, score(): pl.pallas_call(functools.partial(score_kernel, len(table), sizes, given),...  16.4 us
    ppermute x10, starting transfers between devices, swap_cores(): return lax.ppermute(value, 'c', [(0, 1), (1, 0)])  11.5 us
    ppermute x6, starting transfers between devices, shift_x(): return lax.ppermute(value, 'x', [(i, (i + by) % NX) for i in range(NX)])  10.4 us
    pallas_call x2, Pallas kernels, weigh(): pl.pallas_call(functools.partial(weigh_kernel, first, groups, sizes), in_...  9.22 us
    ppermute x6, waiting for transfers between devices, along_z(): return lax.ppermute(value, ('z', 'c'), pairs)  8.78 us
    ppermute x4, starting transfers between devices, swap_halves(): return lax.ppermute(value, ('y', 'c'), pairs)  5.59 us
  transfers between devices with their start and end apart: 28, of which 14 were waited for; matrix products, arithmetic and copies ran while one was open for 1% of the time, Pallas kernels for 15%

profile of v5, /device:TPU:1, one launch (start us, length us, event | category | flops | bytes accessed | tf_op | source)
XLA Modules:
  0.0 114.0 jit_solution(11833786268847576684)
XLA Ops:
  0.7 1.2 %copy-done = bf16[512,1024]{1,0:T(8,128)(2,1)S(1)} copy-done((bf16[512,1024]{1,0:T(8,128)(2,1)S(1)}, bf16[512,1024]{1,0:T(8,128)(2,1)}, u32[]{:S(2)}) %copy-start) | copy-done | bytes 1048600
  1.9 6.5 %collective-permute-start = (bf16[256,1024]{1,0:T(8,128)(2,1)S(1)}, bf16[256,1024]{1,0:T(8,128)(2,1)S(1)}, u32[]{:S(2)}, u32[]{:S(2)}) collective-permute-start(bf16[256,1024]{1,0:T(8,128)(2,1)S(1)} %constant_dynamic-slice_fusion.2), channel_id=1, source_target_pairs={{0,8},{1,57},{8,16},{9,1},{16,24},{17,9},{24,32},{25,17},{32,40},{... | collective-permute-start | bytes 1572872 | tf_op jit(solution)/shard_map/ppermute | solution.py:31
  8.4 1.2 %collective-permute-start.2 = (bf16[128,1024]{1,0:T(8,128)(2,1)}, bf16[128,1024]{1,0:T(8,128)(2,1)}, u32[]{:S(2)}, u32[]{:S(2)}) collective-permute-start(bf16[128,1024]{1,0:T(8,128)(2,1)} %centroids.1), channel_id=1, source_target_pairs={{0,64},{64,128},{128,192},{192,0},{1,65},{65,129},{129,193},{193,1... | collective-permute-start | bytes 786440 | tf_op jit(solution)/shard_map/ppermute | solution.py:19
  9.6 1.5 %collective-permute-start.1 = (bf16[128,1024]{1,0:T(8,128)(2,1)}, bf16[128,1024]{1,0:T(8,128)(2,1)}, u32[]{:S(2)}, u32[]{:S(2)}) collective-permute-start(bf16[128,1024]{1,0:T(8,128)(2,1)} %centroids.1), channel_id=1, source_target_pairs={{0,192},{64,0},{128,64},{192,128},{1,193},{65,1},{129,65},{193,129... | collective-permute-start | bytes 786440 | tf_op jit(solution)/shard_map/ppermute | solution.py:19
  11.1 4.5 %collective-permute-done.2.refs_4_ = bf16[128,1024]{1,0:T(8,128)(2,1)} collective-permute-done((bf16[128,1024]{1,0:T(8,128)(2,1)}, bf16[128,1024]{1,0:T(8,128)(2,1)}, u32[]{:S(2)}, u32[]{:S(2)}) %collective-permute-start.2) | collective-permute-done | bytes 262176 | tf_op jit(solution)/shard_map/ppermute | solution.py:19
  15.9 2.7 %collective-permute-start.5 = (bf16[256,1024]{1,0:T(8,128)(2,1)S(1)}, bf16[256,1024]{1,0:T(8,128)(2,1)S(1)}, u32[]{:S(2)}, u32[]{:S(2)}) collective-permute-start(bf16[256,1024]{1,0:T(8,128)(2,1)S(1)} %collective-permute-done.refs_9_.refs_4_), channel_id=1, source_target_pairs={{0,2},{1,7},{2,0},{3,5},{4,6},{5,3},{6,4},{7,1},{8,10},{9,15},{10,... | collective-permute-start | bytes 1572872 | tf_op jit(solution)/shard_map/ppermute | solution.py:47
  18.6 2.7 %collective-permute-start.3 = (bf16[256,1024]{1,0:T(8,128)(2,1)S(1)}, bf16[256,1024]{1,0:T(8,128)(2,1)S(1)}, u32[]{:S(2)}, u32[]{:S(2)}) collective-permute-start(bf16[256,1024]{1,0:T(8,128)(2,1)S(1)} %collective-permute-done.refs_9_.refs_4_), channel_id=1, source_target_pairs={{0,8},{1,57},{8,16},{9,1},{16,24},{17,9},{24,32},{25,17},{32,40},{... | collective-permute-start | bytes 1572872 | tf_op jit(solution)/shard_map/ppermute | solution.py:31
  21.4 2.3 %collective-permute-start.4 = (bf16[128,1024]{1,0:T(8,128)(2,1)}, bf16[128,1024]{1,0:T(8,128)(2,1)}, u32[]{:S(2)}, u32[]{:S(2)}) collective-permute-start(bf16[128,1024]{1,0:T(8,128)(2,1)} %collective-permute-done.1.refs_2_), channel_id=1, source_target_pairs={{0,192},{64,0},{128,64},{192,128},{1,193},{65,1},{129,65},{193,129... | collective-permute-start | bytes 786440 | tf_op jit(solution)/shard_map/ppermute | solution.py:19
  23.6 3.8 %collective-permute-done.4.refs_0_ = bf16[128,1024]{1,0:T(8,128)(2,1)} collective-permute-done((bf16[128,1024]{1,0:T(8,128)(2,1)}, bf16[128,1024]{1,0:T(8,128)(2,1)}, u32[]{:S(2)}, u32[]{:S(2)}) %collective-permute-start.4) | collective-permute-done | bytes 262176 | tf_op jit(solution)/shard_map/ppermute | solution.py:19
  27.5 3.1 %collective-permute-start.11 = (bf16[256,1024]{1,0:T(8,128)(2,1)S(1)}, bf16[256,1024]{1,0:T(8,128)(2,1)S(1)}, u32[]{:S(2)}, u32[]{:S(2)}) collective-permute-start(bf16[256,1024]{1,0:T(8,128)(2,1)S(1)} %collective-permute-done.3.refs_11_.refs_6_), channel_id=1, source_target_pairs={{0,8},{1,57},{8,16},{9,1},{16,24},{17,9},{24,32},{25,17},{32,40},{... | collective-permute-start | bytes 1572872 | tf_op jit(solution)/shard_map/ppermute | solution.py:31
  31.2 5.5 %collective-permute-done.11.refs_8_ = bf16[256,1024]{1,0:T(8,128)(2,1)S(1)} collective-permute-done((bf16[256,1024]{1,0:T(8,128)(2,1)S(1)}, bf16[256,1024]{1,0:T(8,128)(2,1)S(1)}, u32[]{:S(2)}, u32[]{:S(2)}) %collective-permute-start.11) | collective-permute-done | bytes 524320 | tf_op jit(solution)/shard_map/ppermute | solution.py:31
  36.7 2.1 %collective-permute-start.6 = (bf16[128,1024]{1,0:T(8,128)(2,1)}, bf16[128,1024]{1,0:T(8,128)(2,1)}, u32[]{:S(2)}, u32[]{:S(2)}) collective-permute-start(bf16[128,1024]{1,0:T(8,128)(2,1)} %collective-permute-done.4.refs_0_), channel_id=1, source_target_pairs={{0,1},{1,0},{2,3},{3,2},{4,5},{5,4},{6,7},{7,6},{8,9},{9,8},{10,11... | collective-permute-start | bytes 786440 | tf_op jit(solution)/shard_map/ppermute | solution.py:23
  40.9 1.4 %collective-permute-start.12 = (bf16[256,1024]{1,0:T(8,128)(2,1)S(1)}, bf16[256,1024]{1,0:T(8,128)(2,1)}, u32[]{:S(2)}, u32[]{:S(2)}) collective-permute-start(bf16[256,1024]{1,0:T(8,128)(2,1)S(1)} %collective-permute-done.11.refs_8_), channel_id=1, source_target_pairs={{0,2},{1,7},{2,0},{3,5},{4,6},{5,3},{6,4},{7,1},{8,10},{9,15},{10,... | collective-permute-start | bytes 1572872 | tf_op jit(solution)/shard_map/ppermute | solution.py:47
  42.3 7.7 %shard_map.58 = (f32[1024,128]{1,0:T(8,128)S(1)}, f32[1024,1280]{1,0:T(8,128)}, f32[1,1280]{1,0:T(1,128)S(1)}) custom-call(bf16[128,1024]{1,0:T(8,128)(2,1)} %collective-permute-done.4.refs_0_, bf16[128,1024]{1,0:T(8,128)(2,1)} %collective-permute-done.6.refs_1_, bf16[128,1024]{1,0:T(8,128)(2,1)} %collective-permute-done.1.refs_2_, ...), custom_call_target="tpu_custom_call" | custom-call | flops 5368709120 | bytes 9961472 | tf_op jit(solution)/shard_map/pallas_call | solution.py:183
  50.8 1.4 %collective-permute-start.14 = (bf16[128,1024]{1,0:T(8,128)(2,1)}, bf16[128,1024]{1,0:T(8,128)(2,1)S(1)}, u32[]{:S(2)}, u32[]{:S(2)}) collective-permute-start(bf16[128,1024]{1,0:T(8,128)(2,1)} %collective-permute-done.13.refs_10_), channel_id=1, source_target_pairs={{0,2},{1,7},{2,0},{3,5},{4,6},{5,3},{6,4},{7,1},{8,10},{9,15},{10,... | collective-permute-start | bytes 786440 | tf_op jit(solution)/shard_map/ppermute | solution.py:47
  52.2 5.4 %shard_map.59 = (f32[1024,640]{1,0:T(8,128)}, f32[1,640]{1,0:T(1,128)S(1)}) custom-call(bf16[128,1024]{1,0:T(8,128)(2,1)} %collective-permute-done.4.refs_0_, bf16[128,1024]{1,0:T(8,128)(2,1)} %collective-permute-done.6.refs_1_, bf16[128,1024]{1,0:T(8,128)(2,1)} %collective-permute-done.1.refs_2_, bf16[128,1024]{1,0:T(8,128)(2,1)} %collective-permute-done.7.refs_3_, ...), custom_call_target="tpu_custom_call" | custom-call | flops 2684354560 | bytes 6029312 | tf_op jit(solution)/shard_map/pallas_call | solution.py:183
  58.3 3.3 %shard_map.60 = (f32[1024,128]{1,0:T(8,128)}, f32[1,128]{1,0:T(1,128)S(1)}) custom-call(bf16[128,1024]{1,0:T(8,128)(2,1)} %collective-permute-done.4.refs_0_, bf16[128,1024]{1,0:T(8,128)(2,1)} %collective-permute-done.6.refs_1_, bf16[128,1024]{1,0:T(8,128)(2,1)} %collective-permute-done.1.refs_2_, bf16[128,1024]{1,0:T(8,128)(2,1)} %collective-permute-done.7.refs_3_, ...), custom_call_target="tpu_custom_call" | custom-call | flops 536870912 | bytes 2883584 | tf_op jit(solution)/shard_map/pallas_call | solution.py:183
  62.0 1.2 %collective-permute-done.15 = f32[16,128]{1,0:T(8,128)S(1)} collective-permute-done((f32[16,128]{1,0:T(8,128)S(1)}, f32[16,128]{1,0:T(8,128)S(1)}, u32[]{:S(2)}, u32[]{:S(2)}) %collective-permute-start.15) | collective-permute-done | bytes 8224 | tf_op jit(solution)/shard_map/ppermute | solution.py:23
  64.4 1.6 %collective-permute-done.16 = f32[8,2,2,128]{3,1,2,0:T(2,128)S(1)} collective-permute-done((f32[8,2,2,128]{3,1,2,0:T(2,128)S(1)}, f32[8,2,2,128]{3,1,2,0:T(2,128)S(1)}, u32[]{:S(2)}, u32[]{:S(2)}) %collective-permute-start.16) | collective-permute-done | bytes 16416 | tf_op jit(solution)/shard_map/ppermute | solution.py:31
  66.0 2.6 %collective-permute-start.17 = (f32[8,2,2,128]{3,1,2,0:T(2,128)S(1)}, f32[8,2,2,128]{3,1,2,0:T(2,128)S(1)}, u32[]{:S(2)}, u32[]{:S(2)}) collective-permute-start(f32[8,2,2,128]{3,1,2,0:T(2,128)S(1)} %maximum_select_fusion), channel_id=1, source_target_pairs={{0,1},{1,0},{2,3},{3,2},{4,5},{5,4},{6,7},{7,6},{8,9},{9,8},{10,11... | collective-permute-start | bytes 49160 | tf_op jit(solution)/shard_map/ppermute | solution.py:23
  69.5 2.8 %collective-permute-start.18 = (f32[8,2,2,128]{3,1,2,0:T(2,128)S(1)}, f32[8,2,2,128]{3,1,2,0:T(2,128)S(1)}, u32[]{:S(2)}, u32[]{:S(2)}) collective-permute-start(f32[8,2,2,128]{3,1,2,0:T(2,128)S(1)} %add_select_fusion), channel_id=1, source_target_pairs={{0,24},{1,41},{8,32},{9,49},{16,40},{17,57},{24,48},{25,1},{32,56}... | collective-permute-start | bytes 49160 | tf_op jit(solution)/shard_map/ppermute | solution.py:31
  72.3 1.6 %collective-permute-done.18 = f32[8,2,2,128]{3,1,2,0:T(2,128)S(1)} collective-permute-done((f32[8,2,2,128]{3,1,2,0:T(2,128)S(1)}, f32[8,2,2,128]{3,1,2,0:T(2,128)S(1)}, u32[]{:S(2)}, u32[]{:S(2)}) %collective-permute-start.18) | collective-permute-done | bytes 16416 | tf_op jit(solution)/shard_map/ppermute | solution.py:31
  74.0 2.8 %collective-permute-start.19 = (f32[8,2,2,128]{3,1,2,0:T(2,128)S(1)}, f32[8,2,2,128]{3,1,2,0:T(2,128)S(1)}, u32[]{:S(2)}, u32[]{:S(2)}) collective-permute-start(f32[8,2,2,128]{3,1,2,0:T(2,128)S(1)} %maximum_select_fusion.1), channel_id=1, source_target_pairs={{0,1},{1,0},{2,3},{3,2},{4,5},{5,4},{6,7},{7,6},{8,9},{9,8},{10,11... | collective-permute-start | bytes 49160 | tf_op jit(solution)/shard_map/ppermute | solution.py:23
  77.7 1.3 %collective-permute-start.21 = (f32[8,2,2,128]{3,1,2,0:T(2,128)S(1)}, f32[8,2,2,128]{3,1,2,0:T(2,128)S(1)}, u32[]{:S(2)}, u32[]{:S(2)}) collective-permute-start(f32[8,2,2,128]{3,1,2,0:T(2,128)S(1)} %log_add_fusion.2), channel_id=1, source_target_pairs={{0,4},{1,5},{2,6},{3,7},{4,0},{5,1},{6,2},{7,3},{8,12},{9,13},{10,... | collective-permute-start | bytes 49160 | tf_op jit(solution)/shard_map/ppermute | solution.py:39
  79.8 2.2 %collective-permute-done.21 = f32[8,2,2,128]{3,1,2,0:T(2,128)S(1)} collective-permute-done((f32[8,2,2,128]{3,1,2,0:T(2,128)S(1)}, f32[8,2,2,128]{3,1,2,0:T(2,128)S(1)}, u32[]{:S(2)}, u32[]{:S(2)}) %collective-permute-start.21) | collective-permute-done | bytes 16416 | tf_op jit(solution)/shard_map/ppermute | solution.py:39
  82.1 2.7 %collective-permute-start.22 = (f32[8,2,2,128]{3,1,2,0:T(2,128)S(1)}, f32[8,2,2,128]{3,1,2,0:T(2,128)S(1)}, u32[]{:S(2)}, u32[]{:S(2)}) collective-permute-start(f32[8,2,2,128]{3,1,2,0:T(2,128)S(1)} %log_add_fusion.1), channel_id=1, source_target_pairs={{0,1},{1,0},{2,3},{3,2},{4,5},{5,4},{6,7},{7,6},{8,9},{9,8},{10,11... | collective-permute-start | bytes 49160 | tf_op jit(solution)/shard_map/ppermute | solution.py:23
  85.9 5.8 %shard_map.62 = (bf16[432,1024]{1,0:T(8,128)(2,1)S(1)}, f32[384,1024]{1,0:T(8,128)S(1)}, f32[48,128]{1,0:T(8,128)S(1)}) custom-call(f32[1,2048]{1,0:T(1,128)S(1)} %constant_dynamic-update-slice_fusion.8.energy, f32[1024,1280]{1,0:T(8,128)} %get-tuple-element.41.refs_0_, f32[1024,640]{1,0:T(8,128)} %get-tuple-element.42.refs_1_, ...), custom_call_target="tpu_custom_call" | custom-call | flops 3221225472 | bytes 10485760 | tf_op jit(solution)/shard_map/pallas_call | solution.py:257
  92.2 3.4 %shard_map.61 = (bf16[144,1024]{1,0:T(8,128)(2,1)S(1)}, f32[128,1024]{1,0:T(8,128)S(1)}, f32[16,128]{1,0:T(8,128)S(1)}) custom-call(f32[1,2048]{1,0:T(1,128)S(1)} %constant_dynamic-update-slice_fusion.8.energy, f32[1024,1280]{1,0:T(8,128)} %get-tuple-element.41.refs_0_, f32[1024,640]{1,0:T(8,128)} %get-tuple-element.42.refs_1_, ...), custom_call_target="tpu_custom_call" | custom-call | flops 1073741824 | bytes 6291456 | tf_op jit(solution)/shard_map/pallas_call | solution.py:257
  96.0 2.8 %collective-permute-start.25 = (bf16[144,1024]{1,0:T(8,128)(2,1)S(1)}, bf16[144,1024]{1,0:T(8,128)(2,1)S(1)}, u32[]{:S(2)}, u32[]{:S(2)}) collective-permute-start(bf16[144,1024]{1,0:T(8,128)(2,1)S(1)} %get-tuple-element.50), channel_id=1, source_target_pairs={{0,128},{64,192},{128,0},{192,64},{1,129},{65,193},{129,1},{193,65... | collective-permute-start | bytes 884744 | tf_op jit(solution)/shard_map/ppermute | solution.py:19
  99.3 2.2 %collective-permute-start.27 = (bf16[144,1024]{1,0:T(8,128)(2,1)S(1)}, bf16[144,1024]{1,0:T(8,128)(2,1)S(1)}, u32[]{:S(2)}, u32[]{:S(2)}) collective-permute-start(bf16[144,1024]{1,0:T(8,128)(2,1)S(1)} %get-tuple-element.52), channel_id=1, source_target_pairs={{0,192},{64,0},{128,64},{192,128},{1,193},{65,1},{129,65},{193,129... | collective-permute-start | bytes 884744 | tf_op jit(solution)/shard_map/ppermute | solution.py:19
  102.1 3.8 %collective-permute-done.25.one = bf16[144,1024]{1,0:T(8,128)(2,1)S(1)} collective-permute-done((bf16[144,1024]{1,0:T(8,128)(2,1)S(1)}, bf16[144,1024]{1,0:T(8,128)(2,1)S(1)}, u32[]{:S(2)}, u32[]{:S(2)}) %collective-permute-start.25) | collective-permute-done | bytes 294944 | tf_op jit(solution)/shard_map/ppermute | solution.py:19
  105.9 7.0 %collective-permute-done.26.two = bf16[144,1024]{1,0:T(8,128)(2,1)S(1)} collective-permute-done((bf16[144,1024]{1,0:T(8,128)(2,1)S(1)}, bf16[144,1024]{1,0:T(8,128)(2,1)S(1)}, u32[]{:S(2)}, u32[]{:S(2)}) %collective-permute-start.26) | collective-permute-done | bytes 294944 | tf_op jit(solution)/shard_map/ppermute | solution.py:19
  (112 shorter events, 12.9 us)
Async XLA Ops:
  1.9 14.0 %collective-permute-start = (bf16[256,1024]{1,0:T(8,128)(2,1)S(1)}, bf16[256,1024]{1,0:T(8,128)(2,1)S(1)}, u32[]{:S(2)}, u32[]{:S(2)}) collective-permute-start(bf16[256,1024]{1,0:T(8,128)(2,1)S(1)} %constant_dynamic-slice_fusion.2), channel_id=1, source_target_pairs={{0,8},{1,57},{8,16},{9,1},{16,24},{17,9},{24,32},{25,17},{32,40},{... | collective-permute-start | bytes 1572872 | tf_op jit(solution)/shard_map/ppermute | solution.py:31
  8.4 7.2 %collective-permute-start.2 = (bf16[128,1024]{1,0:T(8,128)(2,1)}, bf16[128,1024]{1,0:T(8,128)(2,1)}, u32[]{:S(2)}, u32[]{:S(2)}) collective-permute-start(bf16[128,1024]{1,0:T(8,128)(2,1)} %centroids.1), channel_id=1, source_target_pairs={{0,64},{64,128},{128,192},{192,0},{1,65},{65,129},{129,193},{193,1... | collective-permute-start | bytes 786440 | tf_op jit(solution)/shard_map/ppermute | solution.py:19
  9.6 6.3 %collective-permute-start.1 = (bf16[128,1024]{1,0:T(8,128)(2,1)}, bf16[128,1024]{1,0:T(8,128)(2,1)}, u32[]{:S(2)}, u32[]{:S(2)}) collective-permute-start(bf16[128,1024]{1,0:T(8,128)(2,1)} %centroids.1), channel_id=1, source_target_pairs={{0,192},{64,0},{128,64},{192,128},{1,193},{65,1},{129,65},{193,129... | collective-permute-start | bytes 786440 | tf_op jit(solution)/shard_map/ppermute | solution.py:19
  15.9 26.4 %copy-start.6 = (bf16[256,1024]{1,0:T(8,128)(2,1)}, bf16[256,1024]{1,0:T(8,128)(2,1)S(1)}, u32[]{:S(2)}) copy-start(bf16[256,1024]{1,0:T(8,128)(2,1)S(1)} %collective-permute-done.refs_9_.refs_4_) | copy-start | bytes 1572868
  15.9 11.6 %collective-permute-start.5 = (bf16[256,1024]{1,0:T(8,128)(2,1)S(1)}, bf16[256,1024]{1,0:T(8,128)(2,1)S(1)}, u32[]{:S(2)}, u32[]{:S(2)}) collective-permute-start(bf16[256,1024]{1,0:T(8,128)(2,1)S(1)} %collective-permute-done.refs_9_.refs_4_), channel_id=1, source_target_pairs={{0,2},{1,7},{2,0},{3,5},{4,6},{5,3},{6,4},{7,1},{8,10},{9,15},{10,... | collective-permute-start | bytes 1572872 | tf_op jit(solution)/shard_map/ppermute | solution.py:47
  18.6 8.9 %collective-permute-start.3 = (bf16[256,1024]{1,0:T(8,128)(2,1)S(1)}, bf16[256,1024]{1,0:T(8,128)(2,1)S(1)}, u32[]{:S(2)}, u32[]{:S(2)}) collective-permute-start(bf16[256,1024]{1,0:T(8,128)(2,1)S(1)} %collective-permute-done.refs_9_.refs_4_), channel_id=1, source_target_pairs={{0,8},{1,57},{8,16},{9,1},{16,24},{17,9},{24,32},{25,17},{32,40},{... | collective-permute-start | bytes 1572872 | tf_op jit(solution)/shard_map/ppermute | solution.py:31
  21.4 6.1 %collective-permute-start.4 = (bf16[128,1024]{1,0:T(8,128)(2,1)}, bf16[128,1024]{1,0:T(8,128)(2,1)}, u32[]{:S(2)}, u32[]{:S(2)}) collective-permute-start(bf16[128,1024]{1,0:T(8,128)(2,1)} %collective-permute-done.1.refs_2_), channel_id=1, source_target_pairs={{0,192},{64,0},{128,64},{192,128},{1,193},{65,1},{129,65},{193,129... | collective-permute-start | bytes 786440 | tf_op jit(solution)/shard_map/ppermute | solution.py:19
  27.5 14.8 %copy-start.7 = (bf16[256,1024]{1,0:T(8,128)(2,1)}, bf16[256,1024]{1,0:T(8,128)(2,1)S(1)}, u32[]{:S(2)}) copy-start(bf16[256,1024]{1,0:T(8,128)(2,1)S(1)} %collective-permute-done.5.refs_10_.refs_5_) | copy-start | bytes 1572868
  27.5 9.2 %collective-permute-start.11 = (bf16[256,1024]{1,0:T(8,128)(2,1)S(1)}, bf16[256,1024]{1,0:T(8,128)(2,1)S(1)}, u32[]{:S(2)}, u32[]{:S(2)}) collective-permute-start(bf16[256,1024]{1,0:T(8,128)(2,1)S(1)} %collective-permute-done.3.refs_11_.refs_6_), channel_id=1, source_target_pairs={{0,8},{1,57},{8,16},{9,1},{16,24},{17,9},{24,32},{25,17},{32,40},{... | collective-permute-start | bytes 1572872 | tf_op jit(solution)/shard_map/ppermute | solution.py:31
  30.6 11.6 %collective-permute-start.10 = (bf16[256,1024]{1,0:T(8,128)(2,1)S(1)}, bf16[256,1024]{1,0:T(8,128)(2,1)}, u32[]{:S(2)}, u32[]{:S(2)}) collective-permute-start(bf16[256,1024]{1,0:T(8,128)(2,1)S(1)} %collective-permute-done.3.refs_11_.refs_6_), channel_id=1, source_target_pairs={{0,2},{1,7},{2,0},{3,5},{4,6},{5,3},{6,4},{7,1},{8,10},{9,15},{10,... | collective-permute-start | bytes 1572872 | tf_op jit(solution)/shard_map/ppermute | solution.py:47
  30.7 9.0 %collective-permute-start.9 = (bf16[128,1024]{1,0:T(8,128)(2,1)}, bf16[128,1024]{1,0:T(8,128)(2,1)}, u32[]{:S(2)}, u32[]{:S(2)}) collective-permute-start(bf16[128,1024]{1,0:T(8,128)(2,1)} %centroids.1), channel_id=1, source_target_pairs={{0,1},{1,0},{2,3},{3,2},{4,5},{5,4},{6,7},{7,6},{8,9},{9,8},{10,11... | collective-permute-start | bytes 786440 | tf_op jit(solution)/shard_map/ppermute | solution.py:23
  30.7 11.5 %collective-permute-start.7 = (bf16[128,1024]{1,0:T(8,128)(2,1)}, bf16[128,1024]{1,0:T(8,128)(2,1)}, u32[]{:S(2)}, u32[]{:S(2)}) collective-permute-start(bf16[128,1024]{1,0:T(8,128)(2,1)} %collective-permute-done.1.refs_2_), channel_id=1, source_target_pairs={{0,1},{1,0},{2,3},{3,2},{4,5},{5,4},{6,7},{7,6},{8,9},{9,8},{10,11... | collective-permute-start | bytes 786440 | tf_op jit(solution)/shard_map/ppermute | solution.py:23
  31.2 9.6 %collective-permute-start.8 = (bf16[128,1024]{1,0:T(8,128)(2,1)}, bf16[128,1024]{1,0:T(8,128)(2,1)}, u32[]{:S(2)}, u32[]{:S(2)}) collective-permute-start(bf16[128,1024]{1,0:T(8,128)(2,1)} %collective-permute-done.2.refs_4_), channel_id=1, source_target_pairs={{0,1},{1,0},{2,3},{3,2},{4,5},{5,4},{6,7},{7,6},{8,9},{9,8},{10,11... | collective-permute-start | bytes 786440 | tf_op jit(solution)/shard_map/ppermute | solution.py:23
  36.7 5.5 %collective-permute-start.6 = (bf16[128,1024]{1,0:T(8,128)(2,1)}, bf16[128,1024]{1,0:T(8,128)(2,1)}, u32[]{:S(2)}, u32[]{:S(2)}) collective-permute-start(bf16[128,1024]{1,0:T(8,128)(2,1)} %collective-permute-done.4.refs_0_), channel_id=1, source_target_pairs={{0,1},{1,0},{2,3},{3,2},{4,5},{5,4},{6,7},{7,6},{8,9},{9,8},{10,11... | collective-permute-start | bytes 786440 | tf_op jit(solution)/shard_map/ppermute | solution.py:23
  39.7 11.1 %collective-permute-start.13 = (bf16[128,1024]{1,0:T(8,128)(2,1)S(1)}, bf16[128,1024]{1,0:T(8,128)(2,1)}, u32[]{:S(2)}, u32[]{:S(2)}) collective-permute-start(bf16[128,1024]{1,0:T(8,128)(2,1)S(1)} %constant_dynamic-slice_fusion), channel_id=1, source_target_pairs={{0,8},{1,57},{8,16},{9,1},{16,24},{17,9},{24,32},{25,17},{32,40},{... | collective-permute-start | bytes 786440 | tf_op jit(solution)/shard_map/ppermute | solution.py:31
  40.9 11.4 %collective-permute-start.12 = (bf16[256,1024]{1,0:T(8,128)(2,1)S(1)}, bf16[256,1024]{1,0:T(8,128)(2,1)}, u32[]{:S(2)}, u32[]{:S(2)}) collective-permute-start(bf16[256,1024]{1,0:T(8,128)(2,1)S(1)} %collective-permute-done.11.refs_8_), channel_id=1, source_target_pairs={{0,2},{1,7},{2,0},{3,5},{4,6},{5,3},{6,4},{7,1},{8,10},{9,15},{10,... | collective-permute-start | bytes 1572872 | tf_op jit(solution)/shard_map/ppermute | solution.py:47
  50.8 6.8 %collective-permute-start.14 = (bf16[128,1024]{1,0:T(8,128)(2,1)}, bf16[128,1024]{1,0:T(8,128)(2,1)S(1)}, u32[]{:S(2)}, u32[]{:S(2)}) collective-permute-start(bf16[128,1024]{1,0:T(8,128)(2,1)} %collective-permute-done.13.refs_10_), channel_id=1, source_target_pairs={{0,2},{1,7},{2,0},{3,5},{4,6},{5,3},{6,4},{7,1},{8,10},{9,15},{10,... | collective-permute-start | bytes 786440 | tf_op jit(solution)/shard_map/ppermute | solution.py:47
  61.9 1.3 %collective-permute-start.15 = (f32[16,128]{1,0:T(8,128)S(1)}, f32[16,128]{1,0:T(8,128)S(1)}, u32[]{:S(2)}, u32[]{:S(2)}) collective-permute-start(f32[16,128]{1,0:T(8,128)S(1)} %concatenate.33), channel_id=1, source_target_pairs={{0,1},{1,0},{2,3},{3,2},{4,5},{5,4},{6,7},{7,6},{8,9},{9,8},{10,11... | collective-permute-start | bytes 24584 | tf_op jit(solution)/shard_map/ppermute | solution.py:23
  63.3 2.7 %collective-permute-start.16 = (f32[8,2,2,128]{3,1,2,0:T(2,128)S(1)}, f32[8,2,2,128]{3,1,2,0:T(2,128)S(1)}, u32[]{:S(2)}, u32[]{:S(2)}) collective-permute-start(f32[8,2,2,128]{3,1,2,0:T(2,128)S(1)} %constant_dynamic-update-slice_fusion), channel_id=1, source_target_pairs={{0,8},{1,57},{8,16},{9,1},{16,24},{17,9},{24,32},{25,17},{32,40},{... | collective-permute-start | bytes 49160 | tf_op jit(solution)/shard_map/ppermute | solution.py:31
  66.0 3.4 %collective-permute-start.17 = (f32[8,2,2,128]{3,1,2,0:T(2,128)S(1)}, f32[8,2,2,128]{3,1,2,0:T(2,128)S(1)}, u32[]{:S(2)}, u32[]{:S(2)}) collective-permute-start(f32[8,2,2,128]{3,1,2,0:T(2,128)S(1)} %maximum_select_fusion), channel_id=1, source_target_pairs={{0,1},{1,0},{2,3},{3,2},{4,5},{5,4},{6,7},{7,6},{8,9},{9,8},{10,11... | collective-permute-start | bytes 49160 | tf_op jit(solution)/shard_map/ppermute | solution.py:23
  69.5 4.5 %collective-permute-start.18 = (f32[8,2,2,128]{3,1,2,0:T(2,128)S(1)}, f32[8,2,2,128]{3,1,2,0:T(2,128)S(1)}, u32[]{:S(2)}, u32[]{:S(2)}) collective-permute-start(f32[8,2,2,128]{3,1,2,0:T(2,128)S(1)} %add_select_fusion), channel_id=1, source_target_pairs={{0,24},{1,41},{8,32},{9,49},{16,40},{17,57},{24,48},{25,1},{32,56}... | collective-permute-start | bytes 49160 | tf_op jit(solution)/shard_map/ppermute | solution.py:31
  74.0 3.6 %collective-permute-start.19 = (f32[8,2,2,128]{3,1,2,0:T(2,128)S(1)}, f32[8,2,2,128]{3,1,2,0:T(2,128)S(1)}, u32[]{:S(2)}, u32[]{:S(2)}) collective-permute-start(f32[8,2,2,128]{3,1,2,0:T(2,128)S(1)} %maximum_select_fusion.1), channel_id=1, source_target_pairs={{0,1},{1,0},{2,3},{3,2},{4,5},{5,4},{6,7},{7,6},{8,9},{9,8},{10,11... | collective-permute-start | bytes 49160 | tf_op jit(solution)/shard_map/ppermute | solution.py:23
  77.7 4.2 %collective-permute-start.21 = (f32[8,2,2,128]{3,1,2,0:T(2,128)S(1)}, f32[8,2,2,128]{3,1,2,0:T(2,128)S(1)}, u32[]{:S(2)}, u32[]{:S(2)}) collective-permute-start(f32[8,2,2,128]{3,1,2,0:T(2,128)S(1)} %log_add_fusion.2), channel_id=1, source_target_pairs={{0,4},{1,5},{2,6},{3,7},{4,0},{5,1},{6,2},{7,3},{8,12},{9,13},{10,... | collective-permute-start | bytes 49160 | tf_op jit(solution)/shard_map/ppermute | solution.py:39
  79.1 3.0 %collective-permute-start.20 = (f32[8,2,2,128]{3,1,2,0:T(2,128)S(1)}, f32[8,2,2,128]{3,1,2,0:T(2,128)S(1)}, u32[]{:S(2)}, u32[]{:S(2)}) collective-permute-start(f32[8,2,2,128]{3,1,2,0:T(2,128)S(1)} %log_add_fusion.2), channel_id=1, source_target_pairs={{0,2},{1,7},{2,4},{3,1},{4,6},{5,3},{6,0},{7,5},{8,10},{9,15},{10,... | collective-permute-start | bytes 49160 | tf_op jit(solution)/shard_map/ppermute | solution.py:39
  82.1 3.5 %collective-permute-start.22 = (f32[8,2,2,128]{3,1,2,0:T(2,128)S(1)}, f32[8,2,2,128]{3,1,2,0:T(2,128)S(1)}, u32[]{:S(2)}, u32[]{:S(2)}) collective-permute-start(f32[8,2,2,128]{3,1,2,0:T(2,128)S(1)} %log_add_fusion.1), channel_id=1, source_target_pairs={{0,1},{1,0},{2,3},{3,2},{4,5},{5,4},{6,7},{7,6},{8,9},{9,8},{10,11... | collective-permute-start | bytes 49160 | tf_op jit(solution)/shard_map/ppermute | solution.py:23
  91.8 21.1 %copy-start.3 = (f32[128]{0:T(128)S(1)}, f32[128]{0:T(128)}, u32[]{:S(2)}) copy-start(f32[128]{0:T(128)} %param.5) | copy-start | bytes 1540
  91.8 4.1 %collective-permute-start.24 = (bf16[432,1024]{1,0:T(8,128)(2,1)S(1)}, bf16[432,1024]{1,0:T(8,128)(2,1)S(1)}, u32[]{:S(2)}, u32[]{:S(2)}) collective-permute-start(bf16[432,1024]{1,0:T(8,128)(2,1)S(1)} %get-tuple-element.47), channel_id=1, source_target_pairs={{0,1},{1,0},{2,3},{3,2},{4,5},{5,4},{6,7},{7,6},{8,9},{9,8},{10,11... | collective-permute-start | bytes 2654216 | tf_op jit(solution)/shard_map/ppermute | solution.py:23
  95.6 17.3 %copy-start.1 = (bf16[128,1024]{1,0:T(8,128)(2,1)S(1)}, bf16[128,1024]{1,0:T(8,128)(2,1)}, u32[]{:S(2)}) copy-start(bf16[128,1024]{1,0:T(8,128)(2,1)} %centroids.1) | copy-start | bytes 786436
  95.6 6.5 %collective-permute-start.23 = (bf16[144,1024]{1,0:T(8,128)(2,1)S(1)}, bf16[144,1024]{1,0:T(8,128)(2,1)S(1)}, u32[]{:S(2)}, u32[]{:S(2)}) collective-permute-start(bf16[144,1024]{1,0:T(8,128)(2,1)S(1)} %get-tuple-element.46), channel_id=1, source_target_pairs={{0,1},{1,0},{2,3},{3,2},{4,5},{5,4},{6,7},{7,6},{8,9},{9,8},{10,11... | collective-permute-start | bytes 884744 | tf_op jit(solution)/shard_map/ppermute | solution.py:23
  96.0 9.9 %collective-permute-start.25 = (bf16[144,1024]{1,0:T(8,128)(2,1)S(1)}, bf16[144,1024]{1,0:T(8,128)(2,1)S(1)}, u32[]{:S(2)}, u32[]{:S(2)}) collective-permute-start(bf16[144,1024]{1,0:T(8,128)(2,1)S(1)} %get-tuple-element.50), channel_id=1, source_target_pairs={{0,128},{64,192},{128,0},{192,64},{1,129},{65,193},{129,1},{193,65... | collective-permute-start | bytes 884744 | tf_op jit(solution)/shard_map/ppermute | solution.py:19
  98.8 14.0 %collective-permute-start.26 = (bf16[144,1024]{1,0:T(8,128)(2,1)S(1)}, bf16[144,1024]{1,0:T(8,128)(2,1)S(1)}, u32[]{:S(2)}, u32[]{:S(2)}) collective-permute-start(bf16[144,1024]{1,0:T(8,128)(2,1)S(1)} %get-tuple-element.51), channel_id=1, source_target_pairs={{0,64},{64,128},{128,192},{192,0},{1,65},{65,129},{129,193},{193,1... | collective-permute-start | bytes 884744 | tf_op jit(solution)/shard_map/ppermute | solution.py:19
  99.3 13.5 %collective-permute-start.27 = (bf16[144,1024]{1,0:T(8,128)(2,1)S(1)}, bf16[144,1024]{1,0:T(8,128)(2,1)S(1)}, u32[]{:S(2)}, u32[]{:S(2)}) collective-permute-start(bf16[144,1024]{1,0:T(8,128)(2,1)S(1)} %get-tuple-element.52), channel_id=1, source_target_pairs={{0,192},{64,0},{128,64},{192,128},{1,193},{65,1},{129,65},{193,129... | collective-permute-start | bytes 884744 | tf_op jit(solution)/shard_map/ppermute | solution.py:19
  (5 other events, 30.7 us)

commit v6 on v4

--- a/solution.py
+++ b/solution.py
@@ -11,7 +11,8 @@
 BF16, F32 = jnp.bfloat16, jnp.float32
 TAIL = 16
 ORDER = (2, 1, 3, 0)
-VMEM_LIMIT = 30 * 1024 * 1024
+VMEM_LIMIT = 20 * 1024 * 1024
+SMALL_LIMIT = 4 * 1024 * 1024
 PIN = True
 
 
@@ -47,53 +48,109 @@
     return lax.ppermute(value, ("y", "c"), pairs)
 
 
-def pick(place, first, second):
-    return jnp.where(place == 0, first, second)
-
-
 def combine(parts):
     high = functools.reduce(jnp.maximum, parts)
     return high + jnp.log(sum(jnp.exp(p - high) for p in parts))
 
 
-def energies(local, h, y, z, c):
-    steps = [local[0]] + [pick(h, v, v[::-1]) for v in local[1:]]
-    mine = jnp.concatenate([v.reshape(-1, v.shape[-1]) for v in steps])
-    other = swap_cores(mine)
-
-    def split(flat):
-        out, at = [], 0
-        for v in steps:
-            n = v.shape[0] * v.shape[1]
-            out.append(flat[at : at + n].reshape(v.shape))
-            at += n
-        return out
-
-    back, ahead = split(pick(c, mine, other)), split(pick(c, other, mine))
-    both = lambda k: jnp.concatenate([back[k], ahead[k]], axis=1)
-    block = jnp.stack([both(0), ahead[1], ahead[2], ahead[3], both(4), back[3], back[2], back[1]])
-
+def pick(place, first, second):
+    return jnp.where(place == 0, first, second)
+
+
+def small(kernel, place, out, *args):
+    return pl.pallas_call(
+        kernel,
+        in_specs=[pl.BlockSpec(memory_space=pltpu.SMEM)] + [pl.BlockSpec(memory_space=pltpu.VMEM)] * len(args),
+        out_shape=[jax.ShapeDtypeStruct(shape, F32) for shape in out],
+        compiler_params=pltpu.CompilerParams(vmem_limit_bytes=SMALL_LIMIT),
+    )(place, *args)
+
+
+def turn(v, by):
+    by %= NZ
+    return jnp.concatenate([v[:, NZ - by :], v[:, : NZ - by]], axis=1)
+
+
+def pack_kernel(place, first, second, third, out):
+    sub = out.shape[1]
+    given = [v[:, k : k + sub] for v in (first, second, third) for k in range(0, v.shape[1], sub)]
+    h = place[1]
+    out[0:1, :] = given[0]
+    out[1:2, :] = given[1]
+    at = 2
+    for mine, other in ((given[2:4], given[4:6]), (given[6:8], given[8:10]), (given[10:12], given[12:14]), (given[14:15], given[15:16])):
+        for v, w in ((mine, other), (other, mine)):
+            for i in range(len(v)):
+                out[at : at + 1, :] = pick(h, v[i], w[i])
+                at += 1
+
+
+def block_kernel(place, mine, other, out):
+    c = place[0]
+    back = lambda i: pick(c, mine[i : i + 1, :], other[i : i + 1, :])
+    ahead = lambda i: pick(c, other[i : i + 1, :], mine[i : i + 1, :])
+    for half in range(2):
+        for sub in range(2):
+            q = 2 * half + sub
+            side = ahead if sub else back
+            out[q, 0:1, :] = side(half)
+            out[q, 4:5, :] = side(14 + half)
+            for k in range(1, 4):
+                out[q, k : k + 1, :] = ahead(4 * k - 2 + q)
+                out[q, NZ - k : NZ - k + 1, :] = back(4 * k - 2 + q)
+
+
+def near_kernel(place, block, near, far, three, message):
+    c = place[0]
+    own = block[...]
+    from_back = turn(pick(c, near[...], far[...]), -1)
+    from_ahead = turn(pick(c, far[...], near[...]), 1)
+    both = combine([own, from_back, from_ahead])
+    three[...] = both
+    message[...] = pick(c, both, combine([own, from_back]))
+
+
+def far_kernel(place, three, got, other, out):
+    c = place[0]
+    from_back = turn(pick(c, got[...], other[...]), -3)
+    from_ahead = turn(pick(c, other[...], got[...]), 3)
+    out[...] = combine([three[...], from_back, from_ahead])
+
+
+def side_kernel(place, block, one, two, out):
+    out[...] = pick(place[0], combine([block[...], one[...], two[...]]), one[...])
+
+
+def last_kernel(place, part, other, energy, own):
+    c, h = place[0], place[1]
+    block = combine([part[...], other[...]])
+    n = block.shape[2]
+    own[...] = block[:, 0]
+
+    def steps(half, step):
+        return [pick(c, block[2 * half + i, NZ - step : NZ - step + 1], block[2 * half + i, step : step + 1]) for i in range(2)]
+
+    out = [pick(c, block[2 * half, 0:1], block[2 * half + 1, 0:1]) for half in range(2)]
+    for step in range(1, 4):
+        low, top = steps(0, step), steps(1, step)
+        out += [pick(h, low[i], top[i]) for i in range(2)] + [pick(h, top[i], low[i]) for i in range(2)]
+    low, top = (pick(c, block[2 * half, 4:5], block[2 * half + 1, 4:5]) for half in range(2))
+    out += [pick(h, low, top), pick(h, top, low)]
+    for i, v in enumerate(out):
+        energy[:, i * n : (i + 1) * n] = v
+
+
+def energies(local, place, sub):
+    (mine,) = small(pack_kernel, place, [(16, sub)], *local)
+    shape = (4, NZ, sub)
+    (block,) = small(block_kernel, place, [shape], mine, swap_cores(mine))
     near = along_z(block, 1)
-    near = pick(c, jnp.roll(near, -1, axis=0), jnp.roll(near, 1, axis=0))
-    far = swap_cores(near)
-    three = combine([block, near, far])
-    got = along_z(pick(c, three, combine([block, far])), 3)
-    got = pick(c, jnp.roll(got, -3, axis=0), jnp.roll(got, 3, axis=0))
-    block = combine([three, got, swap_cores(got)])
-
-    none = jnp.full_like(block, -1e30)
-    parts = [pick(c, block, none), along_y(block, 1), pick(c, along_y(block, 2), none)]
-    part = combine(parts)
-    block = combine([part, swap_cores(part)])
-
-    own = lambda v: pick(c, v[:, :1], v[:, 1:])
-    out = [own(block[0])]
-    for k in range(1, 4):
-        v = pick(c, block[NZ - k], block[k])
-        out.append(pick(h, v, v[::-1]))
-    v = own(block[4])
-    out.append(pick(h, v, v[::-1]))
-    return jnp.concatenate([v.reshape(1, -1) for v in out], axis=1), block[0].reshape(-1)
+    three, message = small(near_kernel, place, [shape] * 2, block, near, swap_cores(near))
+    got = along_z(message, 3)
+    (block,) = small(far_kernel, place, [shape], three, got, swap_cores(got))
+    (part,) = small(side_kernel, place, [shape], block, along_y(block, 1), along_y(block, 2))
+    energy, own = small(last_kernel, place, [(1, 16 * sub), (4, sub)], part, swap_cores(part))
+    return energy, own.reshape(-1)
 
 
 def turned(column):
@@ -152,7 +209,7 @@
     sizes = tuple(p.shape[0] for p in pieces)
     rows, given = sum(sizes), squares is not None
     out = [
-        pltpu.HBM((count, rows), F32) if PIN else jax.ShapeDtypeStruct((count, rows), F32),
+        pltpu.VMEM((count, rows), F32) if PIN else jax.ShapeDtypeStruct((count, rows), F32),
         jax.ShapeDtypeStruct((1, rows), F32),
     ]
     if not given:
@@ -172,48 +229,34 @@
 
 def weigh_kernel(first, groups, sizes, energy, *refs):
     logits, refs = refs[: len(groups)], refs[len(groups) :]
-    slab, refs = refs[: len(sizes)], refs[len(sizes) :]
-    message, keep, keep_count, scores, rows, sums, counts, sems = refs
-    height, width = sums.shape
-    n = keep_count.shape[1]
-    span = n * NC
-    starts = [sum(sizes[:p]) for p in range(len(sizes))]
-    edges = [sum(groups[:g]) for g in range(len(groups))]
-    copies = []
-    for p, (at, size) in enumerate(zip(starts, sizes)):
-        g = max(i for i, edge in enumerate(edges) if edge <= at)
-        part = logits[g].at[first * span : first * span + height, at - edges[g] : at - edges[g] + size]
-        pair = (
-            pltpu.make_async_copy(part, scores.at[:, at : at + size], sems.at[0, p]),
-            pltpu.make_async_copy(slab[p], rows.at[at : at + size, :], sems.at[1, p]),
-        )
-        for copy in pair:
-            copy.start()
-        copies.append(pair)
+    slab, (message, keep, keep_count) = refs[: len(sizes)], refs[len(sizes) :]
+    n, width = keep_count.shape[1], keep.shape[1]
+    span, step = n * NC, min(sizes)
     tile = min(256, width)
-    for step in range(0, len(sizes) - 1, 2):
-        last = step + 3 >= len(sizes)
-        stop = len(sizes) if last else step + 2
-        for p in range(step, stop):
-            for copy in copies[p]:
-                copy.wait()
-        at, end = starts[step], starts[stop - 1] + sizes[stop - 1]
-        for lot in range(0, height, span):
-            block = slice(lot, lot + span)
-            w = jnp.exp(scores[block, at:end] - energy[:, at:end])
-            part = functools.reduce(jnp.add, [w[:, k : k + 128] for k in range(0, end - at, 128)])
-            counts[block, :] = part if step == 0 else counts[block, :] + part
-            w = w.astype(BF16)
-            for col in range(0, width, tile):
-                term = jnp.dot(w, rows[at:end, col : col + tile], preferred_element_type=F32)
-                sums[block, col : col + tile] = term if step == 0 else sums[block, col : col + tile] + term
-        if last:
-            break
-    for i in range(height // span):
-        column = jnp.sum(counts[i * span : (i + 1) * span, :], axis=1, keepdims=True)
-        keep[i * n : (i + 1) * n, :] = sums[i * span : i * span + n, :]
+    for i in range(keep.shape[0] // n):
+        lot = slice((first + i) * span, (first + i + 1) * span)
+        counts, sets, at = None, [], 0
+        for p, size in enumerate(groups):
+            for cut in range(0, size, step):
+                w = jnp.exp(logits[p][lot, cut : cut + step] - energy[:, at + cut : at + cut + step])
+                counts = w if counts is None else counts + w
+                sets.append(w.astype(BF16))
+            at += size
+        column = jnp.sum(counts, axis=1, keepdims=True)
+        pairs = [jnp.concatenate(sets[p : p + 2], axis=1) for p in range(0, len(sets), 2)]
+        totals = []
+        for at in range(0, width, tile):
+            acc = None
+            for p, pair in enumerate(pairs):
+                rows = slab[p][:, at : at + tile]
+                if rows.shape[0] < pair.shape[1]:
+                    rows = jnp.concatenate([rows, slab[p + 1][:, at : at + tile]])
+                term = jnp.dot(pair, rows, preferred_element_type=F32)
+                acc = term if acc is None else acc + term
+            keep[i * n : (i + 1) * n, at : at + tile] = acc[:n]
+            totals.append(acc[n:])
         keep_count[i * TAIL : (i + 1) * TAIL, :] = turned(column[:n])[:TAIL]
-        write_message(message, i * (n + TAIL), sums[i * span + n : (i + 1) * span, :], turned(column[n:])[:TAIL])
+        write_message(message, i * (n + TAIL), jnp.concatenate(totals, axis=1), turned(column[n:])[:TAIL])
 
 
 def weigh(first, count, logits, energy, slab):
@@ -221,22 +264,13 @@
     n = span // NC
     sizes, groups = tuple(p.shape[0] for p in slab), tuple(v.shape[1] for v in logits)
     total, height = sum(sizes), count * span
-    away = pl.BlockSpec(memory_space=pl.ANY)
     return pl.pallas_call(
         functools.partial(weigh_kernel, first, groups, sizes),
-        in_specs=[pl.BlockSpec(memory_space=pltpu.VMEM)] + [away] * (len(groups) + len(sizes)),
         out_shape=(
             jax.ShapeDtypeStruct((count * (n + TAIL), width), BF16),
             jax.ShapeDtypeStruct((count * n, width), F32),
             jax.ShapeDtypeStruct((count * TAIL, n), F32),
         ),
-        scratch_shapes=[
-            pltpu.VMEM((height, total), F32),
-            pltpu.VMEM((total, width), BF16),
-            pltpu.VMEM((height, width), F32),
-            pltpu.VMEM((height, 128), F32),
-            pltpu.SemaphoreType.DMA((2, len(sizes))),
-        ],
         compiler_params=pltpu.CompilerParams(vmem_limit_bytes=VMEM_LIMIT),
         cost_estimate=pl.CostEstimate(
             flops=2 * height * total * width,
@@ -288,10 +322,11 @@
 
 
 def shards(embeddings, centroids, masses):
-    z, y, c = (lax.axis_index(a) for a in ("z", "y", "c"))
+    y, c = lax.axis_index("y"), lax.axis_index("c")
     rows, width = embeddings.shape
     half, sub = rows // 2, rows // 4
     h = lax.rem(y, 2)
+    place, embeddings = lax.optimization_barrier((jnp.stack([c, h]), embeddings))
 
     near = {0: centroids, 1: shift_x(centroids, -1), 3: shift_x(centroids, 1)}
 
@@ -305,31 +340,26 @@
     two, near[2], first = lax.optimization_barrier((two, near[2], first))
     three = along_z(two, 1)
 
-    table = [v for d in ORDER for v in (near[d], swap_cores(near[d]))]
-
-    fixed = lambda v: pltpu.with_memory_space_constraint(v, pltpu.HBM) if PIN else v
+    fixed = lambda v: pltpu.with_memory_space_constraint(v, pltpu.VMEM) if PIN else v
+    table = [fixed(v) for d in ORDER for v in (near[d], swap_cores(near[d]))]
+
     four = along_z(lax.dynamic_slice_in_dim(three, c * sub, sub, 0), 1)
-    lots = [(own, one, first, two, swap_halves(two))]
+    lots = [[fixed(v) for v in (own, one, first, two, swap_halves(two))]]
     squares, scores, energy = score(table, lots[0])
-    logits, local = [scores], [energy]
+    squares, logits, local = fixed(squares), [scores], [energy]
     last, _ = lax.optimization_barrier((four, energy))
     last = swap_halves(last)
-    lots.append((three, swap_halves(three), four))
+    lots.append([fixed(v) for v in (three, swap_halves(three), four)])
     _, scores, energy = score(table, lots[1], squares)
     last, _ = lax.optimization_barrier((last, energy))
     logits.append(scores)
     local.append(energy)
-    lots.append((last,))
+    lots.append([fixed(last)])
     _, scores, energy = score(table, lots[2], squares)
     logits.append(scores)
     local.append(energy)
-    logits, pieces = [fixed(v) for v in logits], [fixed(v) for lot in lots for v in lot]
-
-    local = jnp.concatenate(local, axis=1).reshape(-1, sub)
-    cut = lambda at, n, *shape: local[at : at + n].reshape(*shape, sub)
-    steps = [cut(0, 2, 2, 1)] + [cut(2 + 4 * k, 4, 2, 2) for k in range(3)] + [cut(14, 2, 2, 1)]
-    energy, row_energy = energies(steps, h, y, z, c)
-    pieces = [fixed(p) for p in pieces]
+    energy, row_energy = energies(local, place, sub)
+    logits, pieces = [fixed(v) for v in logits], [v for lot in lots for v in lot]
 
     message, keep, keep_count = weigh(0, NX - 1, logits, energy, pieces)
     sent = add(swap_cores(message), keep, keep_count)

time: 119 us -> 111 us (0.933)
  local copies, waits for them, and re-layouts: 9.5 us -> 2.88 us
  starting transfers between devices: 45.9 us -> 49.7 us
  Pallas kernels: 26.3 us -> 23.5 us
  waiting for transfers between devices: 35.3 us -> 33.6 us
    unnamed x41 -> x12, local copies, waits for them, and re-layouts: 7.63 us -> 2.79 us
    pallas_call x3, Pallas kernels: 15.8 us -> 11.2 us  [score(): pl.pallas_call(functools.partial(score_kernel, len(table), sizes, given),...]
    ppermute x6, waiting for transfers between devices: 9.58 us -> 7.15 us  [along_z(): return lax.ppermute(value, ('z', 'c'), pairs)]
    ppermute x2, starting transfers between devices: 1.65 us -> 3.78 us  [along_y(): return lax.ppermute(value, ('y', 'c'), pairs)]
    pallas_call x2 -> x8, Pallas kernels: 9.21 us -> 11 us  [the longest x2 7 us: weigh(): pl.pallas_call(functools.partial(weigh_kernel, first, groups, sizes), out...]
    ppermute x6, starting transfers between devices: 16.9 us -> 18.2 us  [along_z(): return lax.ppermute(value, ('z', 'c'), pairs)]
  transfers between devices with their start and end apart: 28 -> 28, of which waited for: 13 -> 16; matrix products, arithmetic and copies ran while one was open for 1% -> 0% of each run, Pallas kernels for 14% -> 10%
where the time goes in v6:
time: 111 us
  starting transfers between devices  49.7 us (45%)
  waiting for transfers between devices  33.6 us (30%)
  Pallas kernels  23.5 us (21%)
  local copies, waits for them, and re-layouts  2.88 us (3%)
    ppermute x6, waiting for transfers between devices, shift_x(): return lax.ppermute(value, 'x', [(i, (i + by) % NX) for i in range(NX)])  20 us
    ppermute x6, starting transfers between devices, along_z(): return lax.ppermute(value, ('z', 'c'), pairs)  18.2 us
    pallas_call x3, Pallas kernels, score(): pl.pallas_call(functools.partial(score_kernel, len(table), sizes, given),...  11.2 us
    ppermute x6, starting transfers between devices, shift_x(): return lax.ppermute(value, 'x', [(i, (i + by) % NX) for i in range(NX)])  10.6 us
    ppermute x10, starting transfers between devices, swap_cores(): return lax.ppermute(value, 'c', [(0, 1), (1, 0)])  10.5 us
    ppermute x6, waiting for transfers between devices, along_z(): return lax.ppermute(value, ('z', 'c'), pairs)  7.15 us
    pallas_call x2, Pallas kernels, weigh(): pl.pallas_call(functools.partial(weigh_kernel, first, groups, sizes), out...  7 us
    ppermute x4, starting transfers between devices, swap_halves(): return lax.ppermute(value, ('y', 'c'), pairs)  6.65 us
  transfers between devices with their start and end apart: 28, of which 16 were waited for; matrix products, arithmetic and copies ran while one was open for 0% of the time, Pallas kernels for 10%

profile of v6, /device:TPU:1, one launch (start us, length us, event | category | flops | bytes accessed | tf_op | source)
XLA Modules:
  0.0 110.5 jit_solution(4247194007933345112)
XLA Ops:
  0.7 1.1 %copy-done = bf16[512,1024]{1,0:T(8,128)(2,1)S(1)} copy-done((bf16[512,1024]{1,0:T(8,128)(2,1)S(1)}, bf16[512,1024]{1,0:T(8,128)(2,1)}, u32[]{:S(2)}) %copy-start) | copy-done | bytes 1048600
  1.9 6.5 %collective-permute-start = (bf16[256,1024]{1,0:T(8,128)(2,1)S(1)}, bf16[256,1024]{1,0:T(8,128)(2,1)S(1)}, u32[]{:S(2)}, u32[]{:S(2)}) collective-permute-start(bf16[256,1024]{1,0:T(8,128)(2,1)S(1)} %constant_dynamic-slice_fusion.2), channel_id=1, source_target_pairs={{0,8},{1,57},{8,16},{9,1},{16,24},{17,9},{24,32},{25,17},{32,40},{... | collective-permute-start | bytes 1572872 | tf_op jit(solution)/shard_map/ppermute | solution.py:32
  8.4 1.2 %collective-permute-start.2 = (bf16[128,1024]{1,0:T(8,128)(2,1)}, bf16[128,1024]{1,0:T(8,128)(2,1)}, u32[]{:S(2)}, u32[]{:S(2)}) collective-permute-start(bf16[128,1024]{1,0:T(8,128)(2,1)} %centroids.1), channel_id=1, source_target_pairs={{0,64},{64,128},{128,192},{192,0},{1,65},{65,129},{129,193},{193,1... | collective-permute-start | bytes 786440 | tf_op jit(solution)/shard_map/ppermute | solution.py:20
  9.6 1.5 %collective-permute-start.1 = (bf16[128,1024]{1,0:T(8,128)(2,1)}, bf16[128,1024]{1,0:T(8,128)(2,1)}, u32[]{:S(2)}, u32[]{:S(2)}) collective-permute-start(bf16[128,1024]{1,0:T(8,128)(2,1)} %centroids.1), channel_id=1, source_target_pairs={{0,192},{64,0},{128,64},{192,128},{1,193},{65,1},{129,65},{193,129... | collective-permute-start | bytes 786440 | tf_op jit(solution)/shard_map/ppermute | solution.py:20
  11.1 4.5 %collective-permute-done.2.refs_4_ = bf16[128,1024]{1,0:T(8,128)(2,1)} collective-permute-done((bf16[128,1024]{1,0:T(8,128)(2,1)}, bf16[128,1024]{1,0:T(8,128)(2,1)}, u32[]{:S(2)}, u32[]{:S(2)}) %collective-permute-start.2) | collective-permute-done | bytes 262176 | tf_op jit(solution)/shard_map/ppermute | solution.py:20
  15.9 2.7 %collective-permute-start.5 = (bf16[256,1024]{1,0:T(8,128)(2,1)S(1)}, bf16[256,1024]{1,0:T(8,128)(2,1)S(1)}, u32[]{:S(2)}, u32[]{:S(2)}) collective-permute-start(bf16[256,1024]{1,0:T(8,128)(2,1)S(1)} %collective-permute-done.refs_9_.refs_4_), channel_id=1, source_target_pairs={{0,2},{1,7},{2,0},{3,5},{4,6},{5,3},{6,4},{7,1},{8,10},{9,15},{10,... | collective-permute-start | bytes 1572872 | tf_op jit(solution)/shard_map/ppermute | solution.py:48
  18.6 2.7 %collective-permute-start.3 = (bf16[256,1024]{1,0:T(8,128)(2,1)S(1)}, bf16[256,1024]{1,0:T(8,128)(2,1)S(1)}, u32[]{:S(2)}, u32[]{:S(2)}) collective-permute-start(bf16[256,1024]{1,0:T(8,128)(2,1)S(1)} %collective-permute-done.refs_9_.refs_4_), channel_id=1, source_target_pairs={{0,8},{1,57},{8,16},{9,1},{16,24},{17,9},{24,32},{25,17},{32,40},{... | collective-permute-start | bytes 1572872 | tf_op jit(solution)/shard_map/ppermute | solution.py:32
  21.3 2.4 %collective-permute-start.4 = (bf16[128,1024]{1,0:T(8,128)(2,1)}, bf16[128,1024]{1,0:T(8,128)(2,1)}, u32[]{:S(2)}, u32[]{:S(2)}) collective-permute-start(bf16[128,1024]{1,0:T(8,128)(2,1)} %collective-permute-done.1.refs_2_), channel_id=1, source_target_pairs={{0,192},{64,0},{128,64},{192,128},{1,193},{65,1},{129,65},{193,129... | collective-permute-start | bytes 786440 | tf_op jit(solution)/shard_map/ppermute | solution.py:20
  23.6 3.8 %collective-permute-done.4.refs_0_ = bf16[128,1024]{1,0:T(8,128)(2,1)} collective-permute-done((bf16[128,1024]{1,0:T(8,128)(2,1)}, bf16[128,1024]{1,0:T(8,128)(2,1)}, u32[]{:S(2)}, u32[]{:S(2)}) %collective-permute-start.4) | collective-permute-done | bytes 262176 | tf_op jit(solution)/shard_map/ppermute | solution.py:20
  27.5 3.1 %collective-permute-start.11 = (bf16[256,1024]{1,0:T(8,128)(2,1)S(1)}, bf16[256,1024]{1,0:T(8,128)(2,1)S(1)}, u32[]{:S(2)}, u32[]{:S(2)}) collective-permute-start(bf16[256,1024]{1,0:T(8,128)(2,1)S(1)} %collective-permute-done.3.refs_11_.refs_6_), channel_id=1, source_target_pairs={{0,8},{1,57},{8,16},{9,1},{16,24},{17,9},{24,32},{25,17},{32,40},{... | collective-permute-start | bytes 1572872 | tf_op jit(solution)/shard_map/ppermute | solution.py:32
  33.1 3.5 %collective-permute-done.11.refs_8_ = bf16[256,1024]{1,0:T(8,128)(2,1)S(1)} collective-permute-done((bf16[256,1024]{1,0:T(8,128)(2,1)S(1)}, bf16[256,1024]{1,0:T(8,128)(2,1)S(1)}, u32[]{:S(2)}, u32[]{:S(2)}) %collective-permute-start.11) | collective-permute-done | bytes 524320 | tf_op jit(solution)/shard_map/ppermute | solution.py:32
  36.6 1.2 %collective-permute-start.12 = (bf16[256,1024]{1,0:T(8,128)(2,1)S(1)}, bf16[256,1024]{1,0:T(8,128)(2,1)S(1)}, u32[]{:S(2)}, u32[]{:S(2)}) collective-permute-start(bf16[256,1024]{1,0:T(8,128)(2,1)S(1)} %collective-permute-done.11.refs_8_), channel_id=1, source_target_pairs={{0,2},{1,7},{2,0},{3,5},{4,6},{5,3},{6,4},{7,1},{8,10},{9,15},{10,... | collective-permute-start | bytes 1572872 | tf_op jit(solution)/shard_map/ppermute | solution.py:48
  37.8 2.3 %collective-permute-start.13 = (bf16[128,1024]{1,0:T(8,128)(2,1)S(1)}, bf16[128,1024]{1,0:T(8,128)(2,1)S(1)}, u32[]{:S(2)}, u32[]{:S(2)}) collective-permute-start(bf16[128,1024]{1,0:T(8,128)(2,1)S(1)} %constant_dynamic-slice_fusion), channel_id=1, source_target_pairs={{0,8},{1,57},{8,16},{9,1},{16,24},{17,9},{24,32},{25,17},{32,40},{... | collective-permute-start | bytes 786440 | tf_op jit(solution)/shard_map/ppermute | solution.py:32
  41.1 5.4 %shard_map.58 = (f32[1024,128]{1,0:T(8,128)S(1)}, f32[1024,1280]{1,0:T(8,128)S(1)}, f32[1,1280]{1,0:T(1,128)S(1)}) custom-call(bf16[128,1024]{1,0:T(8,128)(2,1)} %collective-permute-done.4.refs_0_, bf16[128,1024]{1,0:T(8,128)(2,1)} %collective-permute-done.6.refs_1_, bf16[128,1024]{1,0:T(8,128)(2,1)} %collective-permute-done.1.refs_2_, ...), custom_call_target="tpu_custom_call" | custom-call | flops 5368709120 | bytes 9961472 | tf_op jit(solution)/shard_map/pallas_call | solution.py:217
  46.6 2.7 %collective-permute-start.14 = (bf16[128,1024]{1,0:T(8,128)(2,1)S(1)}, bf16[128,1024]{1,0:T(8,128)(2,1)S(1)}, u32[]{:S(2)}, u32[]{:S(2)}) collective-permute-start(bf16[128,1024]{1,0:T(8,128)(2,1)S(1)} %collective-permute-done.13.refs_10_), channel_id=1, source_target_pairs={{0,2},{1,7},{2,0},{3,5},{4,6},{5,3},{6,4},{7,1},{8,10},{9,15},{10,... | collective-permute-start | bytes 786440 | tf_op jit(solution)/shard_map/ppermute | solution.py:48
  49.3 3.6 %shard_map.59 = (f32[1024,640]{1,0:T(8,128)S(1)}, f32[1,640]{1,0:T(1,128)S(1)}) custom-call(bf16[128,1024]{1,0:T(8,128)(2,1)} %collective-permute-done.4.refs_0_, bf16[128,1024]{1,0:T(8,128)(2,1)} %collective-permute-done.6.refs_1_, bf16[128,1024]{1,0:T(8,128)(2,1)} %collective-permute-done.1.refs_2_, bf16[128,1024]{1,0:T(8,128)(2,1)} %collective-permute-done.7.refs_3_, ...), custom_call_target="tpu_custom_call" | custom-call | flops 2684354560 | bytes 6029312 | tf_op jit(solution)/shard_map/pallas_call | solution.py:217
  53.1 2.2 %shard_map.60 = (f32[1024,128]{1,0:T(8,128)S(1)}, f32[1,128]{1,0:T(1,128)S(1)}) custom-call(bf16[128,1024]{1,0:T(8,128)(2,1)} %collective-permute-done.4.refs_0_, bf16[128,1024]{1,0:T(8,128)(2,1)} %collective-permute-done.6.refs_1_, bf16[128,1024]{1,0:T(8,128)(2,1)} %collective-permute-done.1.refs_2_, bf16[128,1024]{1,0:T(8,128)(2,1)} %collective-permute-done.7.refs_3_, ...), custom_call_target="tpu_custom_call" | custom-call | flops 536870912 | bytes 2883584 | tf_op jit(solution)/shard_map/pallas_call | solution.py:217
  57.8 2.0 %collective-permute-start.16 = (f32[4,8,128]{2,1,0:T(8,128)S(1)}, f32[4,8,128]{2,1,0:T(8,128)S(1)}, u32[]{:S(2)}, u32[]{:S(2)}) collective-permute-start(f32[4,8,128]{2,1,0:T(8,128)S(1)} %shard_map.62.block), channel_id=1, source_target_pairs={{0,8},{1,57},{8,16},{9,1},{16,24},{17,9},{24,32},{25,17},{32,40},{... | collective-permute-start | bytes 49160 | tf_op jit(solution)/shard_map/ppermute | solution.py:32
  60.6 2.5 %collective-permute-start.17 = (f32[4,8,128]{2,1,0:T(8,128)S(1)}, f32[4,8,128]{2,1,0:T(8,128)S(1)}, u32[]{:S(2)}, u32[]{:S(2)}) collective-permute-start(f32[4,8,128]{2,1,0:T(8,128)S(1)} %collective-permute-done.16.near), channel_id=1, source_target_pairs={{0,1},{1,0},{2,3},{3,2},{4,5},{5,4},{6,7},{7,6},{8,9},{9,8},{10,11... | collective-permute-start | bytes 49160 | tf_op jit(solution)/shard_map/ppermute | solution.py:24
  64.6 1.7 %collective-permute-start.18 = (f32[4,8,128]{2,1,0:T(8,128)S(1)}, f32[4,8,128]{2,1,0:T(8,128)S(1)}, u32[]{:S(2)}, u32[]{:S(2)}) collective-permute-start(f32[4,8,128]{2,1,0:T(8,128)S(1)} %get-tuple-element.50), channel_id=1, source_target_pairs={{0,24},{1,41},{8,32},{9,49},{16,40},{17,57},{24,48},{25,1},{32,56}... | collective-permute-start | bytes 49160 | tf_op jit(solution)/shard_map/ppermute | solution.py:32
  66.3 2.8 %collective-permute-done.18.got = f32[4,8,128]{2,1,0:T(8,128)S(1)} collective-permute-done((f32[4,8,128]{2,1,0:T(8,128)S(1)}, f32[4,8,128]{2,1,0:T(8,128)S(1)}, u32[]{:S(2)}, u32[]{:S(2)}) %collective-permute-start.18) | collective-permute-done | bytes 16416 | tf_op jit(solution)/shard_map/ppermute | solution.py:32
  69.0 2.8 %collective-permute-start.19 = (f32[4,8,128]{2,1,0:T(8,128)S(1)}, f32[4,8,128]{2,1,0:T(8,128)S(1)}, u32[]{:S(2)}, u32[]{:S(2)}) collective-permute-start(f32[4,8,128]{2,1,0:T(8,128)S(1)} %collective-permute-done.18.got), channel_id=1, source_target_pairs={{0,1},{1,0},{2,3},{3,2},{4,5},{5,4},{6,7},{7,6},{8,9},{9,8},{10,11... | collective-permute-start | bytes 49160 | tf_op jit(solution)/shard_map/ppermute | solution.py:24
  73.2 3.0 %collective-permute-start.21 = (f32[4,8,128]{2,1,0:T(8,128)S(1)}, f32[4,8,128]{2,1,0:T(8,128)S(1)}, u32[]{:S(2)}, u32[]{:S(2)}) collective-permute-start(f32[4,8,128]{2,1,0:T(8,128)S(1)} %shard_map.64.block), channel_id=1, source_target_pairs={{0,4},{1,5},{2,6},{3,7},{4,0},{5,1},{6,2},{7,3},{8,12},{9,13},{10,... | collective-permute-start | bytes 49160 | tf_op jit(solution)/shard_map/ppermute | solution.py:40
  77.4 1.4 %collective-permute-done.20.one = f32[4,8,128]{2,1,0:T(8,128)S(1)} collective-permute-done((f32[4,8,128]{2,1,0:T(8,128)S(1)}, f32[4,8,128]{2,1,0:T(8,128)S(1)}, u32[]{:S(2)}, u32[]{:S(2)}) %collective-permute-start.20) | collective-permute-done | bytes 16416 | tf_op jit(solution)/shard_map/ppermute | solution.py:40
  79.4 3.3 %collective-permute-start.22 = (f32[4,8,128]{2,1,0:T(8,128)S(1)}, f32[4,8,128]{2,1,0:T(8,128)S(1)}, u32[]{:S(2)}, u32[]{:S(2)}) collective-permute-start(f32[4,8,128]{2,1,0:T(8,128)S(1)} %shard_map.65.part), channel_id=1, source_target_pairs={{0,1},{1,0},{2,3},{3,2},{4,5},{5,4},{6,7},{7,6},{8,9},{9,8},{10,11... | collective-permute-start | bytes 49160 | tf_op jit(solution)/shard_map/ppermute | solution.py:24
  83.5 1.1 %shard_map.66 = (f32[1,2048]{1,0:T(1,128)S(1)}, f32[4,128]{1,0:T(4,128)}) custom-call(s32[2]{0:T(128)S(1)} %pad_add_fusion.place, f32[4,8,128]{2,1,0:T(8,128)S(1)} %shard_map.65.part, f32[4,8,128]{2,1,0:T(8,128)S(1)} %collective-permute-done.22.other), custom_call_target="tpu_custom_call" | custom-call | tf_op jit(solution)/shard_map/pallas_call | solution.py:61
  84.7 4.6 %shard_map.68 = (bf16[432,1024]{1,0:T(8,128)(2,1)S(1)}, f32[384,1024]{1,0:T(8,128)S(1)}, f32[48,128]{1,0:T(8,128)S(1)}) custom-call(f32[1,2048]{1,0:T(1,128)S(1)} %get-tuple-element.51.energy, f32[1024,1280]{1,0:T(8,128)S(1)} %get-tuple-element.52.refs_0_, f32[1024,640]{1,0:T(8,128)S(1)} %get-tuple-element.53.refs_1_, ...), custom_call_target="tpu_custom_call" | custom-call | flops 3221225472 | bytes 10485760 | tf_op jit(solution)/shard_map/pallas_call | solution.py:267
  89.8 2.4 %shard_map.67 = (bf16[144,1024]{1,0:T(8,128)(2,1)S(1)}, f32[128,1024]{1,0:T(8,128)S(1)}, f32[16,128]{1,0:T(8,128)S(1)}) custom-call(f32[1,2048]{1,0:T(1,128)S(1)} %get-tuple-element.51.energy, f32[1024,1280]{1,0:T(8,128)S(1)} %get-tuple-element.52.refs_0_, f32[1024,640]{1,0:T(8,128)S(1)} %get-tuple-element.53.refs_1_, ...), custom_call_target="tpu_custom_call" | custom-call | flops 1073741824 | bytes 6291456 | tf_op jit(solution)/shard_map/pallas_call | solution.py:267
  92.5 2.8 %collective-permute-start.25 = (bf16[144,1024]{1,0:T(8,128)(2,1)S(1)}, bf16[144,1024]{1,0:T(8,128)(2,1)S(1)}, u32[]{:S(2)}, u32[]{:S(2)}) collective-permute-start(bf16[144,1024]{1,0:T(8,128)(2,1)S(1)} %get-tuple-element.61), channel_id=1, source_target_pairs={{0,128},{64,192},{128,0},{192,64},{1,129},{65,193},{129,1},{193,65... | collective-permute-start | bytes 884744 | tf_op jit(solution)/shard_map/ppermute | solution.py:20
  95.7 2.4 %collective-permute-start.27 = (bf16[144,1024]{1,0:T(8,128)(2,1)S(1)}, bf16[144,1024]{1,0:T(8,128)(2,1)S(1)}, u32[]{:S(2)}, u32[]{:S(2)}) collective-permute-start(bf16[144,1024]{1,0:T(8,128)(2,1)S(1)} %get-tuple-element.63), channel_id=1, source_target_pairs={{0,192},{64,0},{128,64},{192,128},{1,193},{65,1},{129,65},{193,129... | collective-permute-start | bytes 884744 | tf_op jit(solution)/shard_map/ppermute | solution.py:20
  98.1 4.3 %collective-permute-done.25.one = bf16[144,1024]{1,0:T(8,128)(2,1)S(1)} collective-permute-done((bf16[144,1024]{1,0:T(8,128)(2,1)S(1)}, bf16[144,1024]{1,0:T(8,128)(2,1)S(1)}, u32[]{:S(2)}, u32[]{:S(2)}) %collective-permute-start.25) | collective-permute-done | bytes 294944 | tf_op jit(solution)/shard_map/ppermute | solution.py:20
  102.4 7.0 %collective-permute-done.26.two = bf16[144,1024]{1,0:T(8,128)(2,1)S(1)} collective-permute-done((bf16[144,1024]{1,0:T(8,128)(2,1)S(1)}, bf16[144,1024]{1,0:T(8,128)(2,1)S(1)}, u32[]{:S(2)}, u32[]{:S(2)}) %collective-permute-start.26) | collective-permute-done | bytes 294944 | tf_op jit(solution)/shard_map/ppermute | solution.py:20
  (53 shorter events, 15.2 us)
Async XLA Ops:
  0.6 1.2 %copy-start = (bf16[512,1024]{1,0:T(8,128)(2,1)S(1)}, bf16[512,1024]{1,0:T(8,128)(2,1)}, u32[]{:S(2)}) copy-start(bf16[512,1024]{1,0:T(8,128)(2,1)} %param.3) | copy-start | bytes 3145732
  0.6 39.5 %copy-start.1 = (bf16[128,1024]{1,0:T(8,128)(2,1)S(1)}, bf16[128,1024]{1,0:T(8,128)(2,1)}, u32[]{:S(2)}) copy-start(bf16[128,1024]{1,0:T(8,128)(2,1)} %centroids.1) | copy-start | bytes 786436
  1.9 14.0 %collective-permute-start = (bf16[256,1024]{1,0:T(8,128)(2,1)S(1)}, bf16[256,1024]{1,0:T(8,128)(2,1)S(1)}, u32[]{:S(2)}, u32[]{:S(2)}) collective-permute-start(bf16[256,1024]{1,0:T(8,128)(2,1)S(1)} %constant_dynamic-slice_fusion.2), channel_id=1, source_target_pairs={{0,8},{1,57},{8,16},{9,1},{16,24},{17,9},{24,32},{25,17},{32,40},{... | collective-permute-start | bytes 1572872 | tf_op jit(solution)/shard_map/ppermute | solution.py:32
  8.4 7.2 %collective-permute-start.2 = (bf16[128,1024]{1,0:T(8,128)(2,1)}, bf16[128,1024]{1,0:T(8,128)(2,1)}, u32[]{:S(2)}, u32[]{:S(2)}) collective-permute-start(bf16[128,1024]{1,0:T(8,128)(2,1)} %centroids.1), channel_id=1, source_target_pairs={{0,64},{64,128},{128,192},{192,0},{1,65},{65,129},{129,193},{193,1... | collective-permute-start | bytes 786440 | tf_op jit(solution)/shard_map/ppermute | solution.py:20
  9.6 6.3 %collective-permute-start.1 = (bf16[128,1024]{1,0:T(8,128)(2,1)}, bf16[128,1024]{1,0:T(8,128)(2,1)}, u32[]{:S(2)}, u32[]{:S(2)}) collective-permute-start(bf16[128,1024]{1,0:T(8,128)(2,1)} %centroids.1), channel_id=1, source_target_pairs={{0,192},{64,0},{128,64},{192,128},{1,193},{65,1},{129,65},{193,129... | collective-permute-start | bytes 786440 | tf_op jit(solution)/shard_map/ppermute | solution.py:20
  15.9 11.6 %collective-permute-start.5 = (bf16[256,1024]{1,0:T(8,128)(2,1)S(1)}, bf16[256,1024]{1,0:T(8,128)(2,1)S(1)}, u32[]{:S(2)}, u32[]{:S(2)}) collective-permute-start(bf16[256,1024]{1,0:T(8,128)(2,1)S(1)} %collective-permute-done.refs_9_.refs_4_), channel_id=1, source_target_pairs={{0,2},{1,7},{2,0},{3,5},{4,6},{5,3},{6,4},{7,1},{8,10},{9,15},{10,... | collective-permute-start | bytes 1572872 | tf_op jit(solution)/shard_map/ppermute | solution.py:48
  18.6 8.8 %collective-permute-start.3 = (bf16[256,1024]{1,0:T(8,128)(2,1)S(1)}, bf16[256,1024]{1,0:T(8,128)(2,1)S(1)}, u32[]{:S(2)}, u32[]{:S(2)}) collective-permute-start(bf16[256,1024]{1,0:T(8,128)(2,1)S(1)} %collective-permute-done.refs_9_.refs_4_), channel_id=1, source_target_pairs={{0,8},{1,57},{8,16},{9,1},{16,24},{17,9},{24,32},{25,17},{32,40},{... | collective-permute-start | bytes 1572872 | tf_op jit(solution)/shard_map/ppermute | solution.py:32
  21.3 6.2 %collective-permute-start.4 = (bf16[128,1024]{1,0:T(8,128)(2,1)}, bf16[128,1024]{1,0:T(8,128)(2,1)}, u32[]{:S(2)}, u32[]{:S(2)}) collective-permute-start(bf16[128,1024]{1,0:T(8,128)(2,1)} %collective-permute-done.1.refs_2_), channel_id=1, source_target_pairs={{0,192},{64,0},{128,64},{192,128},{1,193},{65,1},{129,65},{193,129... | collective-permute-start | bytes 786440 | tf_op jit(solution)/shard_map/ppermute | solution.py:20
  27.5 9.2 %collective-permute-start.11 = (bf16[256,1024]{1,0:T(8,128)(2,1)S(1)}, bf16[256,1024]{1,0:T(8,128)(2,1)S(1)}, u32[]{:S(2)}, u32[]{:S(2)}) collective-permute-start(bf16[256,1024]{1,0:T(8,128)(2,1)S(1)} %collective-permute-done.3.refs_11_.refs_6_), channel_id=1, source_target_pairs={{0,8},{1,57},{8,16},{9,1},{16,24},{17,9},{24,32},{25,17},{32,40},{... | collective-permute-start | bytes 1572872 | tf_op jit(solution)/shard_map/ppermute | solution.py:32
  30.5 1.7 %collective-permute-start.9 = (bf16[128,1024]{1,0:T(8,128)(2,1)}, bf16[128,1024]{1,0:T(8,128)(2,1)S(1)}, u32[]{:S(2)}, u32[]{:S(2)}) collective-permute-start(bf16[128,1024]{1,0:T(8,128)(2,1)} %centroids.1), channel_id=1, source_target_pairs={{0,1},{1,0},{2,3},{3,2},{4,5},{5,4},{6,7},{7,6},{8,9},{9,8},{10,11... | collective-permute-start | bytes 786440 | tf_op jit(solution)/shard_map/ppermute | solution.py:24
  30.5 9.6 %collective-permute-start.10 = (bf16[256,1024]{1,0:T(8,128)(2,1)S(1)}, bf16[256,1024]{1,0:T(8,128)(2,1)}, u32[]{:S(2)}, u32[]{:S(2)}) collective-permute-start(bf16[256,1024]{1,0:T(8,128)(2,1)S(1)} %collective-permute-done.3.refs_11_.refs_6_), channel_id=1, source_target_pairs={{0,2},{1,7},{2,0},{3,5},{4,6},{5,3},{6,4},{7,1},{8,10},{9,15},{10,... | collective-permute-start | bytes 1572872 | tf_op jit(solution)/shard_map/ppermute | solution.py:48
  30.6 9.5 %collective-permute-start.7 = (bf16[128,1024]{1,0:T(8,128)(2,1)}, bf16[128,1024]{1,0:T(8,128)(2,1)}, u32[]{:S(2)}, u32[]{:S(2)}) collective-permute-start(bf16[128,1024]{1,0:T(8,128)(2,1)} %collective-permute-done.1.refs_2_), channel_id=1, source_target_pairs={{0,1},{1,0},{2,3},{3,2},{4,5},{5,4},{6,7},{7,6},{8,9},{9,8},{10,11... | collective-permute-start | bytes 786440 | tf_op jit(solution)/shard_map/ppermute | solution.py:24
  31.2 6.7 %collective-permute-start.8 = (bf16[128,1024]{1,0:T(8,128)(2,1)}, bf16[128,1024]{1,0:T(8,128)(2,1)}, u32[]{:S(2)}, u32[]{:S(2)}) collective-permute-start(bf16[128,1024]{1,0:T(8,128)(2,1)} %collective-permute-done.2.refs_4_), channel_id=1, source_target_pairs={{0,1},{1,0},{2,3},{3,2},{4,5},{5,4},{6,7},{7,6},{8,9},{9,8},{10,11... | collective-permute-start | bytes 786440 | tf_op jit(solution)/shard_map/ppermute | solution.py:24
  33.0 7.2 %collective-permute-start.6 = (bf16[128,1024]{1,0:T(8,128)(2,1)}, bf16[128,1024]{1,0:T(8,128)(2,1)}, u32[]{:S(2)}, u32[]{:S(2)}) collective-permute-start(bf16[128,1024]{1,0:T(8,128)(2,1)} %collective-permute-done.4.refs_0_), channel_id=1, source_target_pairs={{0,1},{1,0},{2,3},{3,2},{4,5},{5,4},{6,7},{7,6},{8,9},{9,8},{10,11... | collective-permute-start | bytes 786440 | tf_op jit(solution)/shard_map/ppermute | solution.py:24
  36.6 12.6 %collective-permute-start.12 = (bf16[256,1024]{1,0:T(8,128)(2,1)S(1)}, bf16[256,1024]{1,0:T(8,128)(2,1)S(1)}, u32[]{:S(2)}, u32[]{:S(2)}) collective-permute-start(bf16[256,1024]{1,0:T(8,128)(2,1)S(1)} %collective-permute-done.11.refs_8_), channel_id=1, source_target_pairs={{0,2},{1,7},{2,0},{3,5},{4,6},{5,3},{6,4},{7,1},{8,10},{9,15},{10,... | collective-permute-start | bytes 1572872 | tf_op jit(solution)/shard_map/ppermute | solution.py:48
  37.8 8.7 %collective-permute-start.13 = (bf16[128,1024]{1,0:T(8,128)(2,1)S(1)}, bf16[128,1024]{1,0:T(8,128)(2,1)S(1)}, u32[]{:S(2)}, u32[]{:S(2)}) collective-permute-start(bf16[128,1024]{1,0:T(8,128)(2,1)S(1)} %constant_dynamic-slice_fusion), channel_id=1, source_target_pairs={{0,8},{1,57},{8,16},{9,1},{16,24},{17,9},{24,32},{25,17},{32,40},{... | collective-permute-start | bytes 786440 | tf_op jit(solution)/shard_map/ppermute | solution.py:32
  41.1 8.1 %copy-start.4 = (bf16[128,1024]{1,0:T(8,128)(2,1)S(1)}, bf16[128,1024]{1,0:T(8,128)(2,1)}, u32[]{:S(2)}) copy-start(bf16[128,1024]{1,0:T(8,128)(2,1)} %copy-done.2) | copy-start | bytes 786436
  46.6 6.5 %collective-permute-start.14 = (bf16[128,1024]{1,0:T(8,128)(2,1)S(1)}, bf16[128,1024]{1,0:T(8,128)(2,1)S(1)}, u32[]{:S(2)}, u32[]{:S(2)}) collective-permute-start(bf16[128,1024]{1,0:T(8,128)(2,1)S(1)} %collective-permute-done.13.refs_10_), channel_id=1, source_target_pairs={{0,2},{1,7},{2,0},{3,5},{4,6},{5,3},{6,4},{7,1},{8,10},{9,15},{10,... | collective-permute-start | bytes 786440 | tf_op jit(solution)/shard_map/ppermute | solution.py:48
  55.8 1.4 %collective-permute-start.15 = (f32[16,128]{1,0:T(8,128)S(1)}, f32[16,128]{1,0:T(8,128)S(1)}, u32[]{:S(2)}, u32[]{:S(2)}) collective-permute-start(f32[16,128]{1,0:T(8,128)S(1)} %shard_map.61.mine), channel_id=1, source_target_pairs={{0,1},{1,0},{2,3},{3,2},{4,5},{5,4},{6,7},{7,6},{8,9},{9,8},{10,11... | collective-permute-start | bytes 24584 | tf_op jit(solution)/shard_map/ppermute | solution.py:24
  57.8 2.8 %collective-permute-start.16 = (f32[4,8,128]{2,1,0:T(8,128)S(1)}, f32[4,8,128]{2,1,0:T(8,128)S(1)}, u32[]{:S(2)}, u32[]{:S(2)}) collective-permute-start(f32[4,8,128]{2,1,0:T(8,128)S(1)} %shard_map.62.block), channel_id=1, source_target_pairs={{0,8},{1,57},{8,16},{9,1},{16,24},{17,9},{24,32},{25,17},{32,40},{... | collective-permute-start | bytes 49160 | tf_op jit(solution)/shard_map/ppermute | solution.py:32
  60.6 3.4 %collective-permute-start.17 = (f32[4,8,128]{2,1,0:T(8,128)S(1)}, f32[4,8,128]{2,1,0:T(8,128)S(1)}, u32[]{:S(2)}, u32[]{:S(2)}) collective-permute-start(f32[4,8,128]{2,1,0:T(8,128)S(1)} %collective-permute-done.16.near), channel_id=1, source_target_pairs={{0,1},{1,0},{2,3},{3,2},{4,5},{5,4},{6,7},{7,6},{8,9},{9,8},{10,11... | collective-permute-start | bytes 49160 | tf_op jit(solution)/shard_map/ppermute | solution.py:24
  64.6 4.5 %collective-permute-start.18 = (f32[4,8,128]{2,1,0:T(8,128)S(1)}, f32[4,8,128]{2,1,0:T(8,128)S(1)}, u32[]{:S(2)}, u32[]{:S(2)}) collective-permute-start(f32[4,8,128]{2,1,0:T(8,128)S(1)} %get-tuple-element.50), channel_id=1, source_target_pairs={{0,24},{1,41},{8,32},{9,49},{16,40},{17,57},{24,48},{25,1},{32,56}... | collective-permute-start | bytes 49160 | tf_op jit(solution)/shard_map/ppermute | solution.py:32
  69.0 3.6 %collective-permute-start.19 = (f32[4,8,128]{2,1,0:T(8,128)S(1)}, f32[4,8,128]{2,1,0:T(8,128)S(1)}, u32[]{:S(2)}, u32[]{:S(2)}) collective-permute-start(f32[4,8,128]{2,1,0:T(8,128)S(1)} %collective-permute-done.18.got), channel_id=1, source_target_pairs={{0,1},{1,0},{2,3},{3,2},{4,5},{5,4},{6,7},{7,6},{8,9},{9,8},{10,11... | collective-permute-start | bytes 49160 | tf_op jit(solution)/shard_map/ppermute | solution.py:24
  73.2 4.2 %collective-permute-start.21 = (f32[4,8,128]{2,1,0:T(8,128)S(1)}, f32[4,8,128]{2,1,0:T(8,128)S(1)}, u32[]{:S(2)}, u32[]{:S(2)}) collective-permute-start(f32[4,8,128]{2,1,0:T(8,128)S(1)} %shard_map.64.block), channel_id=1, source_target_pairs={{0,4},{1,5},{2,6},{3,7},{4,0},{5,1},{6,2},{7,3},{8,12},{9,13},{10,... | collective-permute-start | bytes 49160 | tf_op jit(solution)/shard_map/ppermute | solution.py:40
  76.3 2.6 %collective-permute-start.20 = (f32[4,8,128]{2,1,0:T(8,128)S(1)}, f32[4,8,128]{2,1,0:T(8,128)S(1)}, u32[]{:S(2)}, u32[]{:S(2)}) collective-permute-start(f32[4,8,128]{2,1,0:T(8,128)S(1)} %shard_map.64.block), channel_id=1, source_target_pairs={{0,2},{1,7},{2,4},{3,1},{4,6},{5,3},{6,0},{7,5},{8,10},{9,15},{10,... | collective-permute-start | bytes 49160 | tf_op jit(solution)/shard_map/ppermute | solution.py:40
  79.4 4.1 %collective-permute-start.22 = (f32[4,8,128]{2,1,0:T(8,128)S(1)}, f32[4,8,128]{2,1,0:T(8,128)S(1)}, u32[]{:S(2)}, u32[]{:S(2)}) collective-permute-start(f32[4,8,128]{2,1,0:T(8,128)S(1)} %shard_map.65.part), channel_id=1, source_target_pairs={{0,1},{1,0},{2,3},{3,2},{4,5},{5,4},{6,7},{7,6},{8,9},{9,8},{10,11... | collective-permute-start | bytes 49160 | tf_op jit(solution)/shard_map/ppermute | solution.py:24
  89.3 20.0 %copy-start.5 = (f32[128]{0:T(128)S(1)}, f32[128]{0:T(128)}, u32[]{:S(2)}) copy-start(f32[128]{0:T(128)} %param.5) | copy-start | bytes 1540
  89.4 3.0 %collective-permute-start.24 = (bf16[432,1024]{1,0:T(8,128)(2,1)S(1)}, bf16[432,1024]{1,0:T(8,128)(2,1)S(1)}, u32[]{:S(2)}, u32[]{:S(2)}) collective-permute-start(bf16[432,1024]{1,0:T(8,128)(2,1)S(1)} %get-tuple-element.58), channel_id=1, source_target_pairs={{0,1},{1,0},{2,3},{3,2},{4,5},{5,4},{6,7},{7,6},{8,9},{9,8},{10,11... | collective-permute-start | bytes 2654216 | tf_op jit(solution)/shard_map/ppermute | solution.py:24
  92.2 5.9 %collective-permute-start.23 = (bf16[144,1024]{1,0:T(8,128)(2,1)S(1)}, bf16[144,1024]{1,0:T(8,128)(2,1)S(1)}, u32[]{:S(2)}, u32[]{:S(2)}) collective-permute-start(bf16[144,1024]{1,0:T(8,128)(2,1)S(1)} %get-tuple-element.57), channel_id=1, source_target_pairs={{0,1},{1,0},{2,3},{3,2},{4,5},{5,4},{6,7},{7,6},{8,9},{9,8},{10,11... | collective-permute-start | bytes 884744 | tf_op jit(solution)/shard_map/ppermute | solution.py:24
  92.5 9.9 %collective-permute-start.25 = (bf16[144,1024]{1,0:T(8,128)(2,1)S(1)}, bf16[144,1024]{1,0:T(8,128)(2,1)S(1)}, u32[]{:S(2)}, u32[]{:S(2)}) collective-permute-start(bf16[144,1024]{1,0:T(8,128)(2,1)S(1)} %get-tuple-element.61), channel_id=1, source_target_pairs={{0,128},{64,192},{128,0},{192,64},{1,129},{65,193},{129,1},{193,65... | collective-permute-start | bytes 884744 | tf_op jit(solution)/shard_map/ppermute | solution.py:20
  95.4 14.0 %collective-permute-start.26 = (bf16[144,1024]{1,0:T(8,128)(2,1)S(1)}, bf16[144,1024]{1,0:T(8,128)(2,1)S(1)}, u32[]{:S(2)}, u32[]{:S(2)}) collective-permute-start(bf16[144,1024]{1,0:T(8,128)(2,1)S(1)} %get-tuple-element.62), channel_id=1, source_target_pairs={{0,64},{64,128},{128,192},{192,0},{1,65},{65,129},{129,193},{193,1... | collective-permute-start | bytes 884744 | tf_op jit(solution)/shard_map/ppermute | solution.py:20
  95.7 13.7 %collective-permute-start.27 = (bf16[144,1024]{1,0:T(8,128)(2,1)S(1)}, bf16[144,1024]{1,0:T(8,128)(2,1)S(1)}, u32[]{:S(2)}, u32[]{:S(2)}) collective-permute-start(bf16[144,1024]{1,0:T(8,128)(2,1)S(1)} %get-tuple-element.63), channel_id=1, source_target_pairs={{0,192},{64,0},{128,64},{192,128},{1,193},{65,1},{129,65},{193,129... | collective-permute-start | bytes 884744 | tf_op jit(solution)/shard_map/ppermute | solution.py:20
  (2 other events, 1.7 us)

commit v7 on v6

--- a/solution.py
+++ b/solution.py
@@ -11,6 +11,7 @@
 BF16, F32 = jnp.bfloat16, jnp.float32
 TAIL = 16
 ORDER = (2, 1, 3, 0)
+BATCH = 512
 VMEM_LIMIT = 20 * 1024 * 1024
 SMALL_LIMIT = 4 * 1024 * 1024
 PIN = True
@@ -60,7 +61,6 @@
 def small(kernel, place, out, *args):
     return pl.pallas_call(
         kernel,
-        in_specs=[pl.BlockSpec(memory_space=pltpu.SMEM)] + [pl.BlockSpec(memory_space=pltpu.VMEM)] * len(args),
         out_shape=[jax.ShapeDtypeStruct(shape, F32) for shape in out],
         compiler_params=pltpu.CompilerParams(vmem_limit_bytes=SMALL_LIMIT),
     )(place, *args)
@@ -74,7 +74,7 @@
 def pack_kernel(place, first, second, third, out):
     sub = out.shape[1]
     given = [v[:, k : k + sub] for v in (first, second, third) for k in range(0, v.shape[1], sub)]
-    h = place[1]
+    h = place[4:5, :]
     out[0:1, :] = given[0]
     out[1:2, :] = given[1]
     at = 2
@@ -86,7 +86,7 @@
 
 
 def block_kernel(place, mine, other, out):
-    c = place[0]
+    c = place[0:1, :]
     back = lambda i: pick(c, mine[i : i + 1, :], other[i : i + 1, :])
     ahead = lambda i: pick(c, other[i : i + 1, :], mine[i : i + 1, :])
     for half in range(2):
@@ -101,7 +101,7 @@
 
 
 def near_kernel(place, block, near, far, three, message):
-    c = place[0]
+    c = place[0:1, :]
     own = block[...]
     from_back = turn(pick(c, near[...], far[...]), -1)
     from_ahead = turn(pick(c, far[...], near[...]), 1)
@@ -111,18 +111,18 @@
 
 
 def far_kernel(place, three, got, other, out):
-    c = place[0]
+    c = place[0:1, :]
     from_back = turn(pick(c, got[...], other[...]), -3)
     from_ahead = turn(pick(c, other[...], got[...]), 3)
     out[...] = combine([three[...], from_back, from_ahead])
 
 
 def side_kernel(place, block, one, two, out):
-    out[...] = pick(place[0], combine([block[...], one[...], two[...]]), one[...])
+    out[...] = pick(place[0:1, :], combine([block[...], one[...], two[...]]), one[...])
 
 
 def last_kernel(place, part, other, energy, own):
-    c, h = place[0], place[1]
+    c, h = place[0:1, :], place[4:5, :]
     block = combine([part[...], other[...]])
     n = block.shape[2]
     own[...] = block[:, 0]
@@ -186,10 +186,15 @@
             wide = block.astype(F32)
             total = jnp.sum(wide * wide, axis=1, keepdims=True)
             squares[p * span : (p + 1) * span, :] = jnp.broadcast_to(total, (span, squares.shape[1]))
-    at = 0
+    batches, at = [[]], 0
     for piece, size in zip(pieces, sizes):
-        rows, lot = piece[...], slice(at, at + size)
-        at += size
+        if sum(k for _, k in batches[-1]) >= BATCH:
+            batches.append([])
+        batches[-1].append((piece, size))
+    for batch in batches:
+        rows = jnp.concatenate([piece[...] for piece, _ in batch])
+        lot = slice(at, at + rows.shape[0])
+        at += rows.shape[0]
         high = None
         for p, block in enumerate(blocks):
             product = lax.dot_general(block, rows, (((1,), (1,)), ((), ())), preferred_element_type=F32)
@@ -288,26 +293,30 @@
     )(*args)
 
 
-def add_kernel(n, got, keep, keep_count, *messages):
-    for i, message in enumerate(messages):
+def add_kernel(n, got, keep, keep_count, *out):
+    messages, counts = out[: len(out) // 2], out[len(out) // 2 :]
+    for i, (message, count) in enumerate(zip(messages, counts)):
         total, row = read_message(got, i * (n + TAIL), n)
-        total = total + keep[i * n : (i + 1) * n, :]
-        write_message(message, 0, total, row + keep_count[i * TAIL : (i + 1) * TAIL, :])
+        message[...] = (total + keep[i * n : (i + 1) * n, :]).astype(BF16)
+        count[...] = (row + keep_count[i * TAIL : (i + 1) * TAIL, :])[:8]
 
 
 def add(got, keep, keep_count):
     n = keep_count.shape[1]
-    shape = jax.ShapeDtypeStruct((n + TAIL, got.shape[1]), BF16)
-    return call(functools.partial(add_kernel, n), (shape,) * (NX - 1), got, keep, keep_count)
-
-
-def update_kernel(n, keep, keep_count, got, one, two, three, masses, centroids, new_centroids, new_masses):
-    total, row = keep[...], keep_count[...]
-    for message in (got, one, two, three):
-        t, r = read_message(message, 0, n)
-        total, row = total + t, row + r
+    k = keep.shape[0] // n
+    shapes = [jax.ShapeDtypeStruct((n, keep.shape[1]), BF16)] * k + [jax.ShapeDtypeStruct((8, n), F32)] * k
+    out = call(functools.partial(add_kernel, n), shapes, got, keep, keep_count)
+    return out[:k], out[k:]
+
+
+def update_kernel(n, keep, keep_count, got, masses, centroids, *refs):
+    others, (new_centroids, new_masses) = refs[:-2], refs[-2:]
+    total, row = read_message(got, 0, n)
+    total, row = total + keep[...], (row + keep_count[...])[:1]
+    for message, count in zip(others[: NX - 1], others[NX - 1 :]):
+        total, row = total + message[...].astype(F32), row + count[:1, :]
     mass = masses[...]
-    new = mass + row[:1]
+    new = mass + row
     new_masses[...] = new
     column = lambda v: jnp.transpose(jnp.broadcast_to(v, (n, n)))[:, :1]
     new_centroids[...] = (column(mass) * centroids[...].astype(F32) + total) / column(new)
@@ -317,7 +326,7 @@
     n, width = centroids.shape
     out = (jax.ShapeDtypeStruct((n, width), F32), jax.ShapeDtypeStruct((1, n), F32))
     return call(
-        functools.partial(update_kernel, n), out, keep, keep_count, got, *others, masses.reshape(1, n), centroids
+        functools.partial(update_kernel, n), out, keep, keep_count, got, masses.reshape(1, n), centroids, *others
     )
 
 
@@ -326,7 +335,8 @@
     rows, width = embeddings.shape
     half, sub = rows // 2, rows // 4
     h = lax.rem(y, 2)
-    place, embeddings = lax.optimization_barrier((jnp.stack([c, h]), embeddings))
+    place = jnp.concatenate([jnp.full((4, sub), c, F32), jnp.full((4, sub), h, F32)])
+    place, embeddings = lax.optimization_barrier((place, embeddings))
 
     near = {0: centroids, 1: shift_x(centroids, -1), 3: shift_x(centroids, 1)}
 
@@ -349,12 +359,12 @@
     squares, logits, local = fixed(squares), [scores], [energy]
     last, _ = lax.optimization_barrier((four, energy))
     last = swap_halves(last)
-    lots.append([fixed(v) for v in (three, swap_halves(three), four)])
+    lots.append([fixed(v) for v in (three, swap_halves(three))])
     _, scores, energy = score(table, lots[1], squares)
     last, _ = lax.optimization_barrier((last, energy))
     logits.append(scores)
     local.append(energy)
-    lots.append([fixed(last)])
+    lots.append([fixed(four), fixed(last)])
     _, scores, energy = score(table, lots[2], squares)
     logits.append(scores)
     local.append(energy)
@@ -362,10 +372,12 @@
     logits, pieces = [fixed(v) for v in logits], [v for lot in lots for v in lot]
 
     message, keep, keep_count = weigh(0, NX - 1, logits, energy, pieces)
-    sent = add(swap_cores(message), keep, keep_count)
+    sums, counts = add(swap_cores(message), keep, keep_count)
+    sums = [shift_x(m, d) for m, d in zip(sums, ORDER)]
     message, keep, keep_count = weigh(NX - 1, 1, logits, energy, pieces)
-    others = [shift_x(m, d) for m, d in zip(sent, ORDER)]
-    new_centroids, new_masses = update(keep, keep_count, swap_cores(message), others, masses, centroids)
+    keep_count, *counts = lax.optimization_barrier([keep_count, *counts])
+    counts = [shift_x(m, d) for m, d in zip(counts, ORDER)]
+    new_centroids, new_masses = update(keep, keep_count, swap_cores(message), [*sums, *counts], masses, centroids)
     return new_centroids, new_masses.reshape(-1), row_energy
 
 

time: 111 us -> 109 us (0.982)
  Pallas kernels: 23.5 us -> 19.8 us
  waiting for transfers between devices: 33.6 us -> 35.5 us
  local copies, waits for them, and re-layouts: 2.88 us -> 1.29 us
    pallas_call x6, Pallas kernels: 3.97 us -> 0.72 us  [small(): pl.pallas_call(kernel, out_shape=[jax.ShapeDtypeStruct(shape, F32) for sh...]
    ppermute x6 -> x9, starting transfers between devices: 10.6 us -> 13.7 us  [shift_x(): return lax.ppermute(value, 'x', [(i, (i + by) % NX) for i in range(NX)])]
    ppermute x6 -> x9, waiting for transfers between devices: 20 us -> 17.9 us  [shift_x(): return lax.ppermute(value, 'x', [(i, (i + by) % NX) for i in range(NX)])]
    ppermute x4, waiting for transfers between devices: 0.21 us -> 2.15 us  [swap_halves(): return lax.ppermute(value, ('y', 'c'), pairs)]
    ppermute x6, waiting for transfers between devices: 7.15 us -> 8.9 us  [along_z(): return lax.ppermute(value, ('z', 'c'), pairs)]
    ppermute x2, starting transfers between devices: 3.78 us -> 2.07 us  [along_y(): return lax.ppermute(value, ('y', 'c'), pairs)]
    unnamed x12 -> x6, local copies, waits for them, and re-layouts: 2.79 us -> 1.12 us
    ppermute x6, starting transfers between devices: 18.2 us -> 16.9 us  [along_z(): return lax.ppermute(value, ('z', 'c'), pairs)]
  transfers between devices with their start and end apart: 28 -> 31, of which waited for: 16 -> 16; matrix products, arithmetic and copies ran while one was open for 0% -> 0% of each run, Pallas kernels for 10% -> 10%
where the time goes in v7:
time: 109 us; the launch traced here: 108 us
  starting transfers between devices  50 us (46%)
  waiting for transfers between devices  35.5 us (33%)
  Pallas kernels  19.8 us (18%)
  local copies, waits for them, and re-layouts  1.29 us (1%)
    ppermute x9, waiting for transfers between devices, shift_x(): return lax.ppermute(value, 'x', [(i, (i + by) % NX) for i in range(NX)])  17.9 us
    ppermute x6, starting transfers between devices, along_z(): return lax.ppermute(value, ('z', 'c'), pairs)  16.9 us
    ppermute x9, starting transfers between devices, shift_x(): return lax.ppermute(value, 'x', [(i, (i + by) % NX) for i in range(NX)])  13.7 us
    ppermute x10, starting transfers between devices, swap_cores(): return lax.ppermute(value, 'c', [(0, 1), (1, 0)])  11.7 us
    pallas_call x3, Pallas kernels, score(): pl.pallas_call(functools.partial(score_kernel, len(table), sizes, given),...  10.9 us
    ppermute x6, waiting for transfers between devices, along_z(): return lax.ppermute(value, ('z', 'c'), pairs)  8.9 us
    pallas_call x2, Pallas kernels, weigh(): pl.pallas_call(functools.partial(weigh_kernel, first, groups, sizes), out...  6.93 us
    ppermute x4, starting transfers between devices, swap_halves(): return lax.ppermute(value, ('y', 'c'), pairs)  5.58 us
  transfers between devices with their start and end apart: 31, of which 16 were waited for; matrix products, arithmetic and copies ran while one was open for 0% of the time, Pallas kernels for 10%

profile of v7, /device:TPU:1, one launch (start us, length us, event | category | flops | bytes accessed | tf_op | source)
XLA Modules:
  0.0 107.5 jit_solution(5302669338433616694)
XLA Ops:
  1.9 6.5 %collective-permute-start = (bf16[256,1024]{1,0:T(8,128)(2,1)S(1)}, bf16[256,1024]{1,0:T(8,128)(2,1)S(1)}, u32[]{:S(2)}, u32[]{:S(2)}) collective-permute-start(bf16[256,1024]{1,0:T(8,128)(2,1)S(1)} %constant_dynamic-slice_fusion.2), channel_id=1, source_target_pairs={{0,8},{1,57},{8,16},{9,1},{16,24},{17,9},{24,32},{25,17},{32,40},{... | collective-permute-start | bytes 1572872 | tf_op jit(solution)/shard_map/ppermute | solution.py:33
  8.4 1.2 %collective-permute-start.2 = (bf16[128,1024]{1,0:T(8,128)(2,1)}, bf16[128,1024]{1,0:T(8,128)(2,1)}, u32[]{:S(2)}, u32[]{:S(2)}) collective-permute-start(bf16[128,1024]{1,0:T(8,128)(2,1)} %centroids.1), channel_id=1, source_target_pairs={{0,64},{64,128},{128,192},{192,0},{1,65},{65,129},{129,193},{193,1... | collective-permute-start | bytes 786440 | tf_op jit(solution)/shard_map/ppermute | solution.py:21
  9.6 1.5 %collective-permute-start.1 = (bf16[128,1024]{1,0:T(8,128)(2,1)}, bf16[128,1024]{1,0:T(8,128)(2,1)}, u32[]{:S(2)}, u32[]{:S(2)}) collective-permute-start(bf16[128,1024]{1,0:T(8,128)(2,1)} %centroids.1), channel_id=1, source_target_pairs={{0,192},{64,0},{128,64},{192,128},{1,193},{65,1},{129,65},{193,129... | collective-permute-start | bytes 786440 | tf_op jit(solution)/shard_map/ppermute | solution.py:21
  11.1 4.5 %collective-permute-done.2.refs_4_ = bf16[128,1024]{1,0:T(8,128)(2,1)} collective-permute-done((bf16[128,1024]{1,0:T(8,128)(2,1)}, bf16[128,1024]{1,0:T(8,128)(2,1)}, u32[]{:S(2)}, u32[]{:S(2)}) %collective-permute-start.2) | collective-permute-done | bytes 262176 | tf_op jit(solution)/shard_map/ppermute | solution.py:21
  15.9 2.7 %collective-permute-start.5 = (bf16[256,1024]{1,0:T(8,128)(2,1)S(1)}, bf16[256,1024]{1,0:T(8,128)(2,1)S(1)}, u32[]{:S(2)}, u32[]{:S(2)}) collective-permute-start(bf16[256,1024]{1,0:T(8,128)(2,1)S(1)} %collective-permute-done.refs_9_.refs_4_), channel_id=1, source_target_pairs={{0,2},{1,7},{2,0},{3,5},{4,6},{5,3},{6,4},{7,1},{8,10},{9,15},{10,... | collective-permute-start | bytes 1572872 | tf_op jit(solution)/shard_map/ppermute | solution.py:49
  18.6 2.7 %collective-permute-start.3 = (bf16[256,1024]{1,0:T(8,128)(2,1)S(1)}, bf16[256,1024]{1,0:T(8,128)(2,1)S(1)}, u32[]{:S(2)}, u32[]{:S(2)}) collective-permute-start(bf16[256,1024]{1,0:T(8,128)(2,1)S(1)} %collective-permute-done.refs_9_.refs_4_), channel_id=1, source_target_pairs={{0,8},{1,57},{8,16},{9,1},{16,24},{17,9},{24,32},{25,17},{32,40},{... | collective-permute-start | bytes 1572872 | tf_op jit(solution)/shard_map/ppermute | solution.py:33
  21.3 2.4 %collective-permute-start.4 = (bf16[128,1024]{1,0:T(8,128)(2,1)}, bf16[128,1024]{1,0:T(8,128)(2,1)}, u32[]{:S(2)}, u32[]{:S(2)}) collective-permute-start(bf16[128,1024]{1,0:T(8,128)(2,1)} %collective-permute-done.1.refs_2_), channel_id=1, source_target_pairs={{0,192},{64,0},{128,64},{192,128},{1,193},{65,1},{129,65},{193,129... | collective-permute-start | bytes 786440 | tf_op jit(solution)/shard_map/ppermute | solution.py:21
  23.6 3.8 %collective-permute-done.4.refs_0_ = bf16[128,1024]{1,0:T(8,128)(2,1)} collective-permute-done((bf16[128,1024]{1,0:T(8,128)(2,1)}, bf16[128,1024]{1,0:T(8,128)(2,1)}, u32[]{:S(2)}, u32[]{:S(2)}) %collective-permute-start.4) | collective-permute-done | bytes 262176 | tf_op jit(solution)/shard_map/ppermute | solution.py:21
  27.5 3.1 %collective-permute-start.11 = (bf16[256,1024]{1,0:T(8,128)(2,1)S(1)}, bf16[256,1024]{1,0:T(8,128)(2,1)S(1)}, u32[]{:S(2)}, u32[]{:S(2)}) collective-permute-start(bf16[256,1024]{1,0:T(8,128)(2,1)S(1)} %collective-permute-done.3.refs_11_.refs_6_), channel_id=1, source_target_pairs={{0,8},{1,57},{8,16},{9,1},{16,24},{17,9},{24,32},{25,17},{32,40},{... | collective-permute-start | bytes 1572872 | tf_op jit(solution)/shard_map/ppermute | solution.py:33
  31.1 5.5 %collective-permute-done.11.refs_8_ = bf16[256,1024]{1,0:T(8,128)(2,1)S(1)} collective-permute-done((bf16[256,1024]{1,0:T(8,128)(2,1)S(1)}, bf16[256,1024]{1,0:T(8,128)(2,1)S(1)}, u32[]{:S(2)}, u32[]{:S(2)}) %collective-permute-start.11) | collective-permute-done | bytes 524320 | tf_op jit(solution)/shard_map/ppermute | solution.py:33
  36.6 2.2 %collective-permute-start.6 = (bf16[128,1024]{1,0:T(8,128)(2,1)}, bf16[128,1024]{1,0:T(8,128)(2,1)}, u32[]{:S(2)}, u32[]{:S(2)}) collective-permute-start(bf16[128,1024]{1,0:T(8,128)(2,1)} %collective-permute-done.4.refs_0_), channel_id=1, source_target_pairs={{0,1},{1,0},{2,3},{3,2},{4,5},{5,4},{6,7},{7,6},{8,9},{9,8},{10,11... | collective-permute-start | bytes 786440 | tf_op jit(solution)/shard_map/ppermute | solution.py:25
  39.9 1.4 %collective-permute-start.12 = (bf16[256,1024]{1,0:T(8,128)(2,1)S(1)}, bf16[256,1024]{1,0:T(8,128)(2,1)S(1)}, u32[]{:S(2)}, u32[]{:S(2)}) collective-permute-start(bf16[256,1024]{1,0:T(8,128)(2,1)S(1)} %collective-permute-done.11.refs_8_), channel_id=1, source_target_pairs={{0,2},{1,7},{2,0},{3,5},{4,6},{5,3},{6,4},{7,1},{8,10},{9,15},{10,... | collective-permute-start | bytes 1572872 | tf_op jit(solution)/shard_map/ppermute | solution.py:49
  41.4 5.5 %shard_map.58 = (f32[1024,128]{1,0:T(8,128)S(1)}, f32[1024,1280]{1,0:T(8,128)S(1)}, f32[1,1280]{1,0:T(1,128)S(1)}) custom-call(bf16[128,1024]{1,0:T(8,128)(2,1)} %collective-permute-done.4.refs_0_, bf16[128,1024]{1,0:T(8,128)(2,1)} %collective-permute-done.6.refs_1_, bf16[128,1024]{1,0:T(8,128)(2,1)} %collective-permute-done.1.refs_2_, ...), custom_call_target="tpu_custom_call" | custom-call | flops 5368709120 | bytes 9961472 | tf_op jit(solution)/shard_map/pallas_call | solution.py:222
  47.0 1.3 %collective-permute-start.14 = (bf16[128,1024]{1,0:T(8,128)(2,1)S(1)}, bf16[128,1024]{1,0:T(8,128)(2,1)S(1)}, u32[]{:S(2)}, u32[]{:S(2)}) collective-permute-start(bf16[128,1024]{1,0:T(8,128)(2,1)S(1)} %collective-permute-done.13.refs_8_.refs_10_), channel_id=1, source_target_pairs={{0,2},{1,7},{2,0},{3,5},{4,6},{5,3},{6,4},{7,1},{8,10},{9,15},{10,... | collective-permute-start | bytes 786440 | tf_op jit(solution)/shard_map/ppermute | solution.py:49
  49.2 3.0 %shard_map.59 = (f32[1024,512]{1,0:T(8,128)S(1)}, f32[1,512]{1,0:T(1,128)S(1)}) custom-call(bf16[128,1024]{1,0:T(8,128)(2,1)} %collective-permute-done.4.refs_0_, bf16[128,1024]{1,0:T(8,128)(2,1)} %collective-permute-done.6.refs_1_, bf16[128,1024]{1,0:T(8,128)(2,1)} %collective-permute-done.1.refs_2_, bf16[128,1024]{1,0:T(8,128)(2,1)} %collective-permute-done.7.refs_3_, ...), custom_call_target="tpu_custom_call" | custom-call | flops 2147483648 | bytes 5242880 | tf_op jit(solution)/shard_map/pallas_call | solution.py:222
  52.2 1.2 %collective-permute-done.14.refs_9_.refs_11_ = bf16[128,1024]{1,0:T(8,128)(2,1)S(1)} collective-permute-done((bf16[128,1024]{1,0:T(8,128)(2,1)S(1)}, bf16[128,1024]{1,0:T(8,128)(2,1)S(1)}, u32[]{:S(2)}, u32[]{:S(2)}) %collective-permute-start.14) | collective-permute-done | bytes 262176 | tf_op jit(solution)/shard_map/ppermute | solution.py:49
  53.5 2.4 %shard_map.60 = (f32[1024,256]{1,0:T(8,128)S(1)}, f32[1,256]{1,0:T(1,128)S(1)}) custom-call(bf16[128,1024]{1,0:T(8,128)(2,1)} %collective-permute-done.4.refs_0_, bf16[128,1024]{1,0:T(8,128)(2,1)} %collective-permute-done.6.refs_1_, bf16[128,1024]{1,0:T(8,128)(2,1)} %collective-permute-done.1.refs_2_, bf16[128,1024]{1,0:T(8,128)(2,1)} %collective-permute-done.7.refs_3_, ...), custom_call_target="tpu_custom_call" | custom-call | flops 1073741824 | bytes 3670016 | tf_op jit(solution)/shard_map/pallas_call | solution.py:222
  55.9 1.2 %collective-permute-done.15.other = f32[16,128]{1,0:T(8,128)S(1)} collective-permute-done((f32[16,128]{1,0:T(8,128)S(1)}, f32[16,128]{1,0:T(8,128)S(1)}, u32[]{:S(2)}, u32[]{:S(2)}) %collective-permute-start.15) | collective-permute-done | bytes 8224 | tf_op jit(solution)/shard_map/ppermute | solution.py:25
  57.9 1.9 %collective-permute-done.16.near = f32[4,8,128]{2,1,0:T(8,128)S(1)} collective-permute-done((f32[4,8,128]{2,1,0:T(8,128)S(1)}, f32[4,8,128]{2,1,0:T(8,128)S(1)}, u32[]{:S(2)}, u32[]{:S(2)}) %collective-permute-start.16) | collective-permute-done | bytes 16416 | tf_op jit(solution)/shard_map/ppermute | solution.py:33
  59.8 2.5 %collective-permute-start.17 = (f32[4,8,128]{2,1,0:T(8,128)S(1)}, f32[4,8,128]{2,1,0:T(8,128)S(1)}, u32[]{:S(2)}, u32[]{:S(2)}) collective-permute-start(f32[4,8,128]{2,1,0:T(8,128)S(1)} %collective-permute-done.16.near), channel_id=1, source_target_pairs={{0,1},{1,0},{2,3},{3,2},{4,5},{5,4},{6,7},{7,6},{8,9},{9,8},{10,11... | collective-permute-start | bytes 49160 | tf_op jit(solution)/shard_map/ppermute | solution.py:25
  63.2 3.0 %collective-permute-start.18 = (f32[4,8,128]{2,1,0:T(8,128)S(1)}, f32[4,8,128]{2,1,0:T(8,128)S(1)}, u32[]{:S(2)}, u32[]{:S(2)}) collective-permute-start(f32[4,8,128]{2,1,0:T(8,128)S(1)} %get-tuple-element.57), channel_id=1, source_target_pairs={{0,24},{1,41},{8,32},{9,49},{16,40},{17,57},{24,48},{25,1},{32,56}... | collective-permute-start | bytes 49160 | tf_op jit(solution)/shard_map/ppermute | solution.py:33
  66.2 1.5 %collective-permute-done.18.got = f32[4,8,128]{2,1,0:T(8,128)S(1)} collective-permute-done((f32[4,8,128]{2,1,0:T(8,128)S(1)}, f32[4,8,128]{2,1,0:T(8,128)S(1)}, u32[]{:S(2)}, u32[]{:S(2)}) %collective-permute-start.18) | collective-permute-done | bytes 16416 | tf_op jit(solution)/shard_map/ppermute | solution.py:33
  67.7 2.7 %collective-permute-start.19 = (f32[4,8,128]{2,1,0:T(8,128)S(1)}, f32[4,8,128]{2,1,0:T(8,128)S(1)}, u32[]{:S(2)}, u32[]{:S(2)}) collective-permute-start(f32[4,8,128]{2,1,0:T(8,128)S(1)} %collective-permute-done.18.got), channel_id=1, source_target_pairs={{0,1},{1,0},{2,3},{3,2},{4,5},{5,4},{6,7},{7,6},{8,9},{9,8},{10,11... | collective-permute-start | bytes 49160 | tf_op jit(solution)/shard_map/ppermute | solution.py:25
  71.2 2.1 %collective-permute-start.21 = (f32[4,8,128]{2,1,0:T(8,128)S(1)}, f32[4,8,128]{2,1,0:T(8,128)S(1)}, u32[]{:S(2)}, u32[]{:S(2)}) collective-permute-start(f32[4,8,128]{2,1,0:T(8,128)S(1)} %shard_map.64.block), channel_id=1, source_target_pairs={{0,4},{1,5},{2,6},{3,7},{4,0},{5,1},{6,2},{7,3},{8,12},{9,13},{10,... | collective-permute-start | bytes 49160 | tf_op jit(solution)/shard_map/ppermute | solution.py:41
  73.3 2.1 %collective-permute-done.21.two = f32[4,8,128]{2,1,0:T(8,128)S(1)} collective-permute-done((f32[4,8,128]{2,1,0:T(8,128)S(1)}, f32[4,8,128]{2,1,0:T(8,128)S(1)}, u32[]{:S(2)}, u32[]{:S(2)}) %collective-permute-start.21) | collective-permute-done | bytes 16416 | tf_op jit(solution)/shard_map/ppermute | solution.py:41
  76.2 3.0 %collective-permute-start.22 = (f32[4,8,128]{2,1,0:T(8,128)S(1)}, f32[4,8,128]{2,1,0:T(8,128)S(1)}, u32[]{:S(2)}, u32[]{:S(2)}) collective-permute-start(f32[4,8,128]{2,1,0:T(8,128)S(1)} %shard_map.65.part), channel_id=1, source_target_pairs={{0,1},{1,0},{2,3},{3,2},{4,5},{5,4},{6,7},{7,6},{8,9},{9,8},{10,11... | collective-permute-start | bytes 49160 | tf_op jit(solution)/shard_map/ppermute | solution.py:25
  80.6 4.6 %shard_map.68 = (bf16[432,1024]{1,0:T(8,128)(2,1)S(1)}, f32[384,1024]{1,0:T(8,128)S(1)}, f32[48,128]{1,0:T(8,128)S(1)}) custom-call(f32[1,2048]{1,0:T(1,128)S(1)} %get-tuple-element.58.energy, f32[1024,1280]{1,0:T(8,128)S(1)} %get-tuple-element.59.refs_0_, f32[1024,512]{1,0:T(8,128)S(1)} %get-tuple-element.60.refs_1_, ...), custom_call_target="tpu_custom_call" | custom-call | flops 3221225472 | bytes 10485760 | tf_op jit(solution)/shard_map/pallas_call | solution.py:272
  85.7 2.3 %shard_map.67 = (bf16[144,1024]{1,0:T(8,128)(2,1)S(1)}, f32[128,1024]{1,0:T(8,128)S(1)}, f32[16,128]{1,0:T(8,128)S(1)}) custom-call(f32[1,2048]{1,0:T(1,128)S(1)} %get-tuple-element.58.energy, f32[1024,1280]{1,0:T(8,128)S(1)} %get-tuple-element.59.refs_0_, f32[1024,512]{1,0:T(8,128)S(1)} %get-tuple-element.60.refs_1_, ...), custom_call_target="tpu_custom_call" | custom-call | flops 1073741824 | bytes 6291456 | tf_op jit(solution)/shard_map/pallas_call | solution.py:272
  88.4 2.8 %collective-permute-start.25 = (bf16[128,1024]{1,0:T(8,128)(2,1)S(1)}, bf16[128,1024]{1,0:T(8,128)(2,1)S(1)}, u32[]{:S(2)}, u32[]{:S(2)}) collective-permute-start(bf16[128,1024]{1,0:T(8,128)(2,1)S(1)} %get-tuple-element.72), channel_id=1, source_target_pairs={{0,128},{64,192},{128,0},{192,64},{1,129},{65,193},{129,1},{193,65... | collective-permute-start | bytes 786440 | tf_op jit(solution)/shard_map/ppermute | solution.py:21
  91.7 2.3 %collective-permute-start.27 = (bf16[128,1024]{1,0:T(8,128)(2,1)S(1)}, bf16[128,1024]{1,0:T(8,128)(2,1)S(1)}, u32[]{:S(2)}, u32[]{:S(2)}) collective-permute-start(bf16[128,1024]{1,0:T(8,128)(2,1)S(1)} %get-tuple-element.74), channel_id=1, source_target_pairs={{0,192},{64,0},{128,64},{192,128},{1,193},{65,1},{129,65},{193,129... | collective-permute-start | bytes 786440 | tf_op jit(solution)/shard_map/ppermute | solution.py:21
  94.5 8.5 %collective-permute-done.28.refs_3_ = f32[8,128]{1,0:T(8,128)S(1)} collective-permute-done((f32[8,128]{1,0:T(8,128)S(1)}, f32[8,128]{1,0:T(8,128)S(1)}, u32[]{:S(2)}, u32[]{:S(2)}) %collective-permute-start.28) | collective-permute-done | bytes 4128 | tf_op jit(solution)/shard_map/ppermute | solution.py:21
  103.0 2.6 %collective-permute-start.30 = (f32[8,128]{1,0:T(8,128)S(1)}, f32[8,128]{1,0:T(8,128)S(1)}, u32[]{:S(2)}, u32[]{:S(2)}) collective-permute-start(f32[8,128]{1,0:T(8,128)S(1)} %get-tuple-element.77), channel_id=1, source_target_pairs={{0,192},{64,0},{128,64},{192,128},{1,193},{65,1},{129,65},{193,129... | collective-permute-start | bytes 12296 | tf_op jit(solution)/shard_map/ppermute | solution.py:21
  (55 shorter events, 12.7 us)
Async XLA Ops:
  0.6 40.7 %copy-start.1 = (bf16[128,1024]{1,0:T(8,128)(2,1)S(1)}, bf16[128,1024]{1,0:T(8,128)(2,1)}, u32[]{:S(2)}) copy-start(bf16[128,1024]{1,0:T(8,128)(2,1)} %centroids.1) | copy-start | bytes 786436
  1.9 14.0 %collective-permute-start = (bf16[256,1024]{1,0:T(8,128)(2,1)S(1)}, bf16[256,1024]{1,0:T(8,128)(2,1)S(1)}, u32[]{:S(2)}, u32[]{:S(2)}) collective-permute-start(bf16[256,1024]{1,0:T(8,128)(2,1)S(1)} %constant_dynamic-slice_fusion.2), channel_id=1, source_target_pairs={{0,8},{1,57},{8,16},{9,1},{16,24},{17,9},{24,32},{25,17},{32,40},{... | collective-permute-start | bytes 1572872 | tf_op jit(solution)/shard_map/ppermute | solution.py:33
  8.4 7.2 %collective-permute-start.2 = (bf16[128,1024]{1,0:T(8,128)(2,1)}, bf16[128,1024]{1,0:T(8,128)(2,1)}, u32[]{:S(2)}, u32[]{:S(2)}) collective-permute-start(bf16[128,1024]{1,0:T(8,128)(2,1)} %centroids.1), channel_id=1, source_target_pairs={{0,64},{64,128},{128,192},{192,0},{1,65},{65,129},{129,193},{193,1... | collective-permute-start | bytes 786440 | tf_op jit(solution)/shard_map/ppermute | solution.py:21
  9.6 6.3 %collective-permute-start.1 = (bf16[128,1024]{1,0:T(8,128)(2,1)}, bf16[128,1024]{1,0:T(8,128)(2,1)}, u32[]{:S(2)}, u32[]{:S(2)}) collective-permute-start(bf16[128,1024]{1,0:T(8,128)(2,1)} %centroids.1), channel_id=1, source_target_pairs={{0,192},{64,0},{128,64},{192,128},{1,193},{65,1},{129,65},{193,129... | collective-permute-start | bytes 786440 | tf_op jit(solution)/shard_map/ppermute | solution.py:21
  15.9 11.6 %collective-permute-start.5 = (bf16[256,1024]{1,0:T(8,128)(2,1)S(1)}, bf16[256,1024]{1,0:T(8,128)(2,1)S(1)}, u32[]{:S(2)}, u32[]{:S(2)}) collective-permute-start(bf16[256,1024]{1,0:T(8,128)(2,1)S(1)} %collective-permute-done.refs_9_.refs_4_), channel_id=1, source_target_pairs={{0,2},{1,7},{2,0},{3,5},{4,6},{5,3},{6,4},{7,1},{8,10},{9,15},{10,... | collective-permute-start | bytes 1572872 | tf_op jit(solution)/shard_map/ppermute | solution.py:49
  18.6 8.8 %collective-permute-start.3 = (bf16[256,1024]{1,0:T(8,128)(2,1)S(1)}, bf16[256,1024]{1,0:T(8,128)(2,1)S(1)}, u32[]{:S(2)}, u32[]{:S(2)}) collective-permute-start(bf16[256,1024]{1,0:T(8,128)(2,1)S(1)} %collective-permute-done.refs_9_.refs_4_), channel_id=1, source_target_pairs={{0,8},{1,57},{8,16},{9,1},{16,24},{17,9},{24,32},{25,17},{32,40},{... | collective-permute-start | bytes 1572872 | tf_op jit(solution)/shard_map/ppermute | solution.py:33
  21.3 6.2 %collective-permute-start.4 = (bf16[128,1024]{1,0:T(8,128)(2,1)}, bf16[128,1024]{1,0:T(8,128)(2,1)}, u32[]{:S(2)}, u32[]{:S(2)}) collective-permute-start(bf16[128,1024]{1,0:T(8,128)(2,1)} %collective-permute-done.1.refs_2_), channel_id=1, source_target_pairs={{0,192},{64,0},{128,64},{192,128},{1,193},{65,1},{129,65},{193,129... | collective-permute-start | bytes 786440 | tf_op jit(solution)/shard_map/ppermute | solution.py:21
  27.5 9.2 %collective-permute-start.11 = (bf16[256,1024]{1,0:T(8,128)(2,1)S(1)}, bf16[256,1024]{1,0:T(8,128)(2,1)S(1)}, u32[]{:S(2)}, u32[]{:S(2)}) collective-permute-start(bf16[256,1024]{1,0:T(8,128)(2,1)S(1)} %collective-permute-done.3.refs_11_.refs_6_), channel_id=1, source_target_pairs={{0,8},{1,57},{8,16},{9,1},{16,24},{17,9},{24,32},{25,17},{32,40},{... | collective-permute-start | bytes 1572872 | tf_op jit(solution)/shard_map/ppermute | solution.py:33
  30.5 10.9 %collective-permute-start.10 = (bf16[256,1024]{1,0:T(8,128)(2,1)S(1)}, bf16[256,1024]{1,0:T(8,128)(2,1)}, u32[]{:S(2)}, u32[]{:S(2)}) collective-permute-start(bf16[256,1024]{1,0:T(8,128)(2,1)S(1)} %collective-permute-done.3.refs_11_.refs_6_), channel_id=1, source_target_pairs={{0,2},{1,7},{2,0},{3,5},{4,6},{5,3},{6,4},{7,1},{8,10},{9,15},{10,... | collective-permute-start | bytes 1572872 | tf_op jit(solution)/shard_map/ppermute | solution.py:49
  30.6 8.3 %collective-permute-start.9 = (bf16[128,1024]{1,0:T(8,128)(2,1)}, bf16[128,1024]{1,0:T(8,128)(2,1)}, u32[]{:S(2)}, u32[]{:S(2)}) collective-permute-start(bf16[128,1024]{1,0:T(8,128)(2,1)} %centroids.1), channel_id=1, source_target_pairs={{0,1},{1,0},{2,3},{3,2},{4,5},{5,4},{6,7},{7,6},{8,9},{9,8},{10,11... | collective-permute-start | bytes 786440 | tf_op jit(solution)/shard_map/ppermute | solution.py:25
  30.6 10.8 %collective-permute-start.7 = (bf16[128,1024]{1,0:T(8,128)(2,1)}, bf16[128,1024]{1,0:T(8,128)(2,1)}, u32[]{:S(2)}, u32[]{:S(2)}) collective-permute-start(bf16[128,1024]{1,0:T(8,128)(2,1)} %collective-permute-done.1.refs_2_), channel_id=1, source_target_pairs={{0,1},{1,0},{2,3},{3,2},{4,5},{5,4},{6,7},{7,6},{8,9},{9,8},{10,11... | collective-permute-start | bytes 786440 | tf_op jit(solution)/shard_map/ppermute | solution.py:25
  31.1 8.8 %collective-permute-start.8 = (bf16[128,1024]{1,0:T(8,128)(2,1)}, bf16[128,1024]{1,0:T(8,128)(2,1)}, u32[]{:S(2)}, u32[]{:S(2)}) collective-permute-start(bf16[128,1024]{1,0:T(8,128)(2,1)} %collective-permute-done.2.refs_4_), channel_id=1, source_target_pairs={{0,1},{1,0},{2,3},{3,2},{4,5},{5,4},{6,7},{7,6},{8,9},{9,8},{10,11... | collective-permute-start | bytes 786440 | tf_op jit(solution)/shard_map/ppermute | solution.py:25
  36.6 4.7 %collective-permute-start.6 = (bf16[128,1024]{1,0:T(8,128)(2,1)}, bf16[128,1024]{1,0:T(8,128)(2,1)}, u32[]{:S(2)}, u32[]{:S(2)}) collective-permute-start(bf16[128,1024]{1,0:T(8,128)(2,1)} %collective-permute-done.4.refs_0_), channel_id=1, source_target_pairs={{0,1},{1,0},{2,3},{3,2},{4,5},{5,4},{6,7},{7,6},{8,9},{9,8},{10,11... | collective-permute-start | bytes 786440 | tf_op jit(solution)/shard_map/ppermute | solution.py:25
  38.9 8.0 %collective-permute-start.13 = (bf16[128,1024]{1,0:T(8,128)(2,1)S(1)}, bf16[128,1024]{1,0:T(8,128)(2,1)S(1)}, u32[]{:S(2)}, u32[]{:S(2)}) collective-permute-start(bf16[128,1024]{1,0:T(8,128)(2,1)S(1)} %constant_dynamic-slice_fusion), channel_id=1, source_target_pairs={{0,8},{1,57},{8,16},{9,1},{16,24},{17,9},{24,32},{25,17},{32,40},{... | collective-permute-start | bytes 786440 | tf_op jit(solution)/shard_map/ppermute | solution.py:33
  39.9 9.2 %collective-permute-start.12 = (bf16[256,1024]{1,0:T(8,128)(2,1)S(1)}, bf16[256,1024]{1,0:T(8,128)(2,1)S(1)}, u32[]{:S(2)}, u32[]{:S(2)}) collective-permute-start(bf16[256,1024]{1,0:T(8,128)(2,1)S(1)} %collective-permute-done.11.refs_8_), channel_id=1, source_target_pairs={{0,2},{1,7},{2,0},{3,5},{4,6},{5,3},{6,4},{7,1},{8,10},{9,15},{10,... | collective-permute-start | bytes 1572872 | tf_op jit(solution)/shard_map/ppermute | solution.py:49
  47.0 6.5 %collective-permute-start.14 = (bf16[128,1024]{1,0:T(8,128)(2,1)S(1)}, bf16[128,1024]{1,0:T(8,128)(2,1)S(1)}, u32[]{:S(2)}, u32[]{:S(2)}) collective-permute-start(bf16[128,1024]{1,0:T(8,128)(2,1)S(1)} %collective-permute-done.13.refs_8_.refs_10_), channel_id=1, source_target_pairs={{0,2},{1,7},{2,0},{3,5},{4,6},{5,3},{6,4},{7,1},{8,10},{9,15},{10,... | collective-permute-start | bytes 786440 | tf_op jit(solution)/shard_map/ppermute | solution.py:49
  55.8 1.3 %collective-permute-start.15 = (f32[16,128]{1,0:T(8,128)S(1)}, f32[16,128]{1,0:T(8,128)S(1)}, u32[]{:S(2)}, u32[]{:S(2)}) collective-permute-start(f32[16,128]{1,0:T(8,128)S(1)} %shard_map.61.mine), channel_id=1, source_target_pairs={{0,1},{1,0},{2,3},{3,2},{4,5},{5,4},{6,7},{7,6},{8,9},{9,8},{10,11... | collective-permute-start | bytes 24584 | tf_op jit(solution)/shard_map/ppermute | solution.py:25
  57.1 2.7 %collective-permute-start.16 = (f32[4,8,128]{2,1,0:T(8,128)S(1)}, f32[4,8,128]{2,1,0:T(8,128)S(1)}, u32[]{:S(2)}, u32[]{:S(2)}) collective-permute-start(f32[4,8,128]{2,1,0:T(8,128)S(1)} %shard_map.62.block), channel_id=1, source_target_pairs={{0,8},{1,57},{8,16},{9,1},{16,24},{17,9},{24,32},{25,17},{32,40},{... | collective-permute-start | bytes 49160 | tf_op jit(solution)/shard_map/ppermute | solution.py:33
  59.8 3.4 %collective-permute-start.17 = (f32[4,8,128]{2,1,0:T(8,128)S(1)}, f32[4,8,128]{2,1,0:T(8,128)S(1)}, u32[]{:S(2)}, u32[]{:S(2)}) collective-permute-start(f32[4,8,128]{2,1,0:T(8,128)S(1)} %collective-permute-done.16.near), channel_id=1, source_target_pairs={{0,1},{1,0},{2,3},{3,2},{4,5},{5,4},{6,7},{7,6},{8,9},{9,8},{10,11... | collective-permute-start | bytes 49160 | tf_op jit(solution)/shard_map/ppermute | solution.py:25
  63.2 4.5 %collective-permute-start.18 = (f32[4,8,128]{2,1,0:T(8,128)S(1)}, f32[4,8,128]{2,1,0:T(8,128)S(1)}, u32[]{:S(2)}, u32[]{:S(2)}) collective-permute-start(f32[4,8,128]{2,1,0:T(8,128)S(1)} %get-tuple-element.57), channel_id=1, source_target_pairs={{0,24},{1,41},{8,32},{9,49},{16,40},{17,57},{24,48},{25,1},{32,56}... | collective-permute-start | bytes 49160 | tf_op jit(solution)/shard_map/ppermute | solution.py:33
  67.7 3.5 %collective-permute-start.19 = (f32[4,8,128]{2,1,0:T(8,128)S(1)}, f32[4,8,128]{2,1,0:T(8,128)S(1)}, u32[]{:S(2)}, u32[]{:S(2)}) collective-permute-start(f32[4,8,128]{2,1,0:T(8,128)S(1)} %collective-permute-done.18.got), channel_id=1, source_target_pairs={{0,1},{1,0},{2,3},{3,2},{4,5},{5,4},{6,7},{7,6},{8,9},{9,8},{10,11... | collective-permute-start | bytes 49160 | tf_op jit(solution)/shard_map/ppermute | solution.py:25
  71.2 4.2 %collective-permute-start.21 = (f32[4,8,128]{2,1,0:T(8,128)S(1)}, f32[4,8,128]{2,1,0:T(8,128)S(1)}, u32[]{:S(2)}, u32[]{:S(2)}) collective-permute-start(f32[4,8,128]{2,1,0:T(8,128)S(1)} %shard_map.64.block), channel_id=1, source_target_pairs={{0,4},{1,5},{2,6},{3,7},{4,0},{5,1},{6,2},{7,3},{8,12},{9,13},{10,... | collective-permute-start | bytes 49160 | tf_op jit(solution)/shard_map/ppermute | solution.py:41
  73.3 2.9 %collective-permute-start.20 = (f32[4,8,128]{2,1,0:T(8,128)S(1)}, f32[4,8,128]{2,1,0:T(8,128)S(1)}, u32[]{:S(2)}, u32[]{:S(2)}) collective-permute-start(f32[4,8,128]{2,1,0:T(8,128)S(1)} %shard_map.64.block), channel_id=1, source_target_pairs={{0,2},{1,7},{2,4},{3,1},{4,6},{5,3},{6,0},{7,5},{8,10},{9,15},{10,... | collective-permute-start | bytes 49160 | tf_op jit(solution)/shard_map/ppermute | solution.py:41
  76.2 3.8 %collective-permute-start.22 = (f32[4,8,128]{2,1,0:T(8,128)S(1)}, f32[4,8,128]{2,1,0:T(8,128)S(1)}, u32[]{:S(2)}, u32[]{:S(2)}) collective-permute-start(f32[4,8,128]{2,1,0:T(8,128)S(1)} %shard_map.65.part), channel_id=1, source_target_pairs={{0,1},{1,0},{2,3},{3,2},{4,5},{5,4},{6,7},{7,6},{8,9},{9,8},{10,11... | collective-permute-start | bytes 49160 | tf_op jit(solution)/shard_map/ppermute | solution.py:25
  85.3 3.0 %collective-permute-start.23 = (bf16[432,1024]{1,0:T(8,128)(2,1)S(1)}, bf16[432,1024]{1,0:T(8,128)(2,1)S(1)}, u32[]{:S(2)}, u32[]{:S(2)}) collective-permute-start(bf16[432,1024]{1,0:T(8,128)(2,1)S(1)} %get-tuple-element.64), channel_id=1, source_target_pairs={{0,1},{1,0},{2,3},{3,2},{4,5},{5,4},{6,7},{7,6},{8,9},{9,8},{10,11... | collective-permute-start | bytes 2654216 | tf_op jit(solution)/shard_map/ppermute | solution.py:25
  88.0 5.9 %collective-permute-start.24 = (bf16[144,1024]{1,0:T(8,128)(2,1)S(1)}, bf16[144,1024]{1,0:T(8,128)(2,1)S(1)}, u32[]{:S(2)}, u32[]{:S(2)}) collective-permute-start(bf16[144,1024]{1,0:T(8,128)(2,1)S(1)} %get-tuple-element.71), channel_id=1, source_target_pairs={{0,1},{1,0},{2,3},{3,2},{4,5},{5,4},{6,7},{7,6},{8,9},{9,8},{10,11... | collective-permute-start | bytes 884744 | tf_op jit(solution)/shard_map/ppermute | solution.py:25
  88.4 17.9 %collective-permute-start.25 = (bf16[128,1024]{1,0:T(8,128)(2,1)S(1)}, bf16[128,1024]{1,0:T(8,128)(2,1)S(1)}, u32[]{:S(2)}, u32[]{:S(2)}) collective-permute-start(bf16[128,1024]{1,0:T(8,128)(2,1)S(1)} %get-tuple-element.72), channel_id=1, source_target_pairs={{0,128},{64,192},{128,0},{192,64},{1,129},{65,193},{129,1},{193,65... | collective-permute-start | bytes 786440 | tf_op jit(solution)/shard_map/ppermute | solution.py:21
  91.3 15.1 %collective-permute-start.26 = (bf16[128,1024]{1,0:T(8,128)(2,1)S(1)}, bf16[128,1024]{1,0:T(8,128)(2,1)S(1)}, u32[]{:S(2)}, u32[]{:S(2)}) collective-permute-start(bf16[128,1024]{1,0:T(8,128)(2,1)S(1)} %get-tuple-element.73), channel_id=1, source_target_pairs={{0,64},{64,128},{128,192},{192,0},{1,65},{65,129},{129,193},{193,1... | collective-permute-start | bytes 786440 | tf_op jit(solution)/shard_map/ppermute | solution.py:21
  91.7 14.7 %collective-permute-start.27 = (bf16[128,1024]{1,0:T(8,128)(2,1)S(1)}, bf16[128,1024]{1,0:T(8,128)(2,1)S(1)}, u32[]{:S(2)}, u32[]{:S(2)}) collective-permute-start(bf16[128,1024]{1,0:T(8,128)(2,1)S(1)} %get-tuple-element.74), channel_id=1, source_target_pairs={{0,192},{64,0},{128,64},{192,128},{1,193},{65,1},{129,65},{193,129... | collective-permute-start | bytes 786440 | tf_op jit(solution)/shard_map/ppermute | solution.py:21
  93.9 9.1 %collective-permute-start.28 = (f32[8,128]{1,0:T(8,128)S(1)}, f32[8,128]{1,0:T(8,128)S(1)}, u32[]{:S(2)}, u32[]{:S(2)}) collective-permute-start(f32[8,128]{1,0:T(8,128)S(1)} %get-tuple-element.75), channel_id=1, source_target_pairs={{0,128},{64,192},{128,0},{192,64},{1,129},{65,193},{129,1},{193,65... | collective-permute-start | bytes 12296 | tf_op jit(solution)/shard_map/ppermute | solution.py:21
  94.0 11.7 %collective-permute-start.29 = (f32[8,128]{1,0:T(8,128)S(1)}, f32[8,128]{1,0:T(8,128)S(1)}, u32[]{:S(2)}, u32[]{:S(2)}) collective-permute-start(f32[8,128]{1,0:T(8,128)S(1)} %get-tuple-element.76), channel_id=1, source_target_pairs={{0,64},{64,128},{128,192},{192,0},{1,65},{65,129},{129,193},{193,1... | collective-permute-start | bytes 12296 | tf_op jit(solution)/shard_map/ppermute | solution.py:21
  103.0 3.3 %collective-permute-start.30 = (f32[8,128]{1,0:T(8,128)S(1)}, f32[8,128]{1,0:T(8,128)S(1)}, u32[]{:S(2)}, u32[]{:S(2)}) collective-permute-start(f32[8,128]{1,0:T(8,128)S(1)} %get-tuple-element.77), channel_id=1, source_target_pairs={{0,192},{64,0},{128,64},{192,128},{1,193},{65,1},{129,65},{193,129... | collective-permute-start | bytes 12296 | tf_op jit(solution)/shard_map/ppermute | solution.py:21
  (2 other events, 19.6 us)

commit v8 on v7

--- a/solution.py
+++ b/solution.py
@@ -33,12 +33,8 @@
     return lax.ppermute(value, ("z", "c"), pairs)
 
 
-def along_y(value, by):
-    pairs = []
-    for y in range(NY):
-        pairs.append((y * NC, (y + by) % NY * NC))
-        pairs.append((y * NC + 1, (y - by) % NY * NC + 1))
-    return lax.ppermute(value, ("y", "c"), pairs)
+def shift_y(value, by):
+    return lax.ppermute(value, "y", [(i, (i + by) % NY) for i in range(NY)])
 
 
 def swap_halves(value):
@@ -83,6 +79,10 @@
             for i in range(len(v)):
                 out[at : at + 1, :] = pick(h, v[i], w[i])
                 at += 1
+
+
+def sum_kernel(place, own, *refs):
+    refs[-1][...] = combine([own[...]] + [v[...] for v in refs[:-1]])
 
 
 def block_kernel(place, mine, other, out):
@@ -110,20 +110,11 @@
     message[...] = pick(c, both, combine([own, from_back]))
 
 
-def far_kernel(place, three, got, other, out):
-    c = place[0:1, :]
+def last_kernel(place, three, got, other, energy, own):
+    c, h = place[0:1, :], place[4:5, :]
     from_back = turn(pick(c, got[...], other[...]), -3)
     from_ahead = turn(pick(c, other[...], got[...]), 3)
-    out[...] = combine([three[...], from_back, from_ahead])
-
-
-def side_kernel(place, block, one, two, out):
-    out[...] = pick(place[0:1, :], combine([block[...], one[...], two[...]]), one[...])
-
-
-def last_kernel(place, part, other, energy, own):
-    c, h = place[0:1, :], place[4:5, :]
-    block = combine([part[...], other[...]])
+    block = combine([three[...], from_back, from_ahead])
     n = block.shape[2]
     own[...] = block[:, 0]
 
@@ -142,14 +133,13 @@
 
 def energies(local, place, sub):
     (mine,) = small(pack_kernel, place, [(16, sub)], *local)
+    (mine,) = small(sum_kernel, place, [(16, sub)], mine, *[shift_y(mine, d) for d in (1, 2, 3)])
     shape = (4, NZ, sub)
     (block,) = small(block_kernel, place, [shape], mine, swap_cores(mine))
     near = along_z(block, 1)
     three, message = small(near_kernel, place, [shape] * 2, block, near, swap_cores(near))
     got = along_z(message, 3)
-    (block,) = small(far_kernel, place, [shape], three, got, swap_cores(got))
-    (part,) = small(side_kernel, place, [shape], block, along_y(block, 1), along_y(block, 2))
-    energy, own = small(last_kernel, place, [(1, 16 * sub), (4, sub)], part, swap_cores(part))
+    energy, own = small(last_kernel, place, [(1, 16 * sub), (4, sub)], three, got, swap_cores(got))
     return energy, own.reshape(-1)
 
 
@@ -293,28 +283,31 @@
     )(*args)
 
 
-def add_kernel(n, got, keep, keep_count, *out):
-    messages, counts = out[: len(out) // 2], out[len(out) // 2 :]
-    for i, (message, count) in enumerate(zip(messages, counts)):
+def add_kernel(n, got, keep, keep_count, count, *messages):
+    count[...] = jnp.zeros(count.shape, F32)
+    for i, message in enumerate(messages):
         total, row = read_message(got, i * (n + TAIL), n)
         message[...] = (total + keep[i * n : (i + 1) * n, :]).astype(BF16)
-        count[...] = (row + keep_count[i * TAIL : (i + 1) * TAIL, :])[:8]
+        count[i : i + 1, :] = row[:1] + keep_count[i * TAIL : i * TAIL + 1, :]
 
 
 def add(got, keep, keep_count):
     n = keep_count.shape[1]
     k = keep.shape[0] // n
-    shapes = [jax.ShapeDtypeStruct((n, keep.shape[1]), BF16)] * k + [jax.ShapeDtypeStruct((8, n), F32)] * k
-    out = call(functools.partial(add_kernel, n), shapes, got, keep, keep_count)
-    return out[:k], out[k:]
-
-
-def update_kernel(n, keep, keep_count, got, masses, centroids, *refs):
+    shapes = [jax.ShapeDtypeStruct((8, n), F32)] + [jax.ShapeDtypeStruct((n, keep.shape[1]), BF16)] * k
+    return call(functools.partial(add_kernel, n), shapes, got, keep, keep_count)
+
+
+def hand_on_kernel(count, one, out):
+    out[...] = jnp.broadcast_to(count[0:1, :] + one[2:3, :], out.shape)
+
+
+def update_kernel(n, keep, keep_count, got, one, two, masses, centroids, *refs):
     others, (new_centroids, new_masses) = refs[:-2], refs[-2:]
     total, row = read_message(got, 0, n)
-    total, row = total + keep[...], (row + keep_count[...])[:1]
-    for message, count in zip(others[: NX - 1], others[NX - 1 :]):
-        total, row = total + message[...].astype(F32), row + count[:1, :]
+    total, row = total + keep[...], (row + keep_count[...])[:1] + one[1:2, :] + two[:1, :]
+    for message in others:
+        total = total + message[...].astype(F32)
     mass = masses[...]
     new = mass + row
     new_masses[...] = new
@@ -322,12 +315,11 @@
     new_centroids[...] = (column(mass) * centroids[...].astype(F32) + total) / column(new)
 
 
-def update(keep, keep_count, got, others, masses, centroids):
+def update(keep, keep_count, got, counts, others, masses, centroids):
     n, width = centroids.shape
     out = (jax.ShapeDtypeStruct((n, width), F32), jax.ShapeDtypeStruct((1, n), F32))
-    return call(
-        functools.partial(update_kernel, n), out, keep, keep_count, got, masses.reshape(1, n), centroids, *others
-    )
+    args = (keep, keep_count, got, *counts, masses.reshape(1, n), centroids, *others)
+    return call(functools.partial(update_kernel, n), out, *args)
 
 
 def shards(embeddings, centroids, masses):
@@ -343,15 +335,19 @@
     mine = lax.dynamic_slice_in_dim(embeddings, h * half, half, 0)
     one = along_z(mine, 1)
     own = lax.dynamic_slice_in_dim(embeddings.reshape(2, 2, sub, width), c, 1, 1).reshape(half, width)
-    one, near[1], near[3] = lax.optimization_barrier((one, near[1], near[3]))
-    two = along_z(one, 1)
+    swapped = {0: swap_cores(centroids)}
+    one, near[1], near[3], swapped[0] = lax.optimization_barrier((one, near[1], near[3], swapped[0]))
+    swapped |= {1: swap_cores(near[1]), 3: swap_cores(near[3])}
     near[2] = shift_x(near[1], -1)
     first = swap_halves(one)
-    two, near[2], first = lax.optimization_barrier((two, near[2], first))
+    two = along_z(one, 1)
+    two, near[2], swapped[1], swapped[3] = lax.optimization_barrier((two, near[2], swapped[1], swapped[3]))
+    swapped[2] = swap_cores(near[2])
     three = along_z(two, 1)
+    two, first = lax.optimization_barrier((two, first))
 
     fixed = lambda v: pltpu.with_memory_space_constraint(v, pltpu.VMEM) if PIN else v
-    table = [fixed(v) for d in ORDER for v in (near[d], swap_cores(near[d]))]
+    table = [fixed(v) for d in ORDER for v in (near[d], swapped[d])]
 
     four = along_z(lax.dynamic_slice_in_dim(three, c * sub, sub, 0), 1)
     lots = [[fixed(v) for v in (own, one, first, two, swap_halves(two))]]
@@ -372,12 +368,13 @@
     logits, pieces = [fixed(v) for v in logits], [v for lot in lots for v in lot]
 
     message, keep, keep_count = weigh(0, NX - 1, logits, energy, pieces)
-    sums, counts = add(swap_cores(message), keep, keep_count)
+    count, *sums = add(swap_cores(message), keep, keep_count)
     sums = [shift_x(m, d) for m, d in zip(sums, ORDER)]
     message, keep, keep_count = weigh(NX - 1, 1, logits, energy, pieces)
-    keep_count, *counts = lax.optimization_barrier([keep_count, *counts])
-    counts = [shift_x(m, d) for m, d in zip(counts, ORDER)]
-    new_centroids, new_masses = update(keep, keep_count, swap_cores(message), [*sums, *counts], masses, centroids)
+    keep_count, count = lax.optimization_barrier((keep_count, count))
+    one = shift_x(count, 1)
+    two = shift_x(call(hand_on_kernel, jax.ShapeDtypeStruct(count.shape, F32), count, one), 2)
+    new_centroids, new_masses = update(keep, keep_count, swap_cores(message), (one, two), sums, masses, centroids)
     return new_centroids, new_masses.reshape(-1), row_energy
 
 

time: 109 us -> 114 us (1.046)
  local copies, waits for them, and re-layouts: 1.29 us -> 9.53 us
  starting transfers between devices: 50 us -> 46.6 us
  waiting for transfers between devices: 35.5 us -> 37.8 us
  Pallas kernels: 19.8 us -> 18.6 us
    unnamed x6 -> x26, local copies, waits for them, and re-layouts: 1.12 us -> 9.37 us
    ppermute x10 -> x9, starting transfers between devices: 11.7 us -> 7.86 us  [swap_cores(): return lax.ppermute(value, 'c', [(0, 1), (1, 0)])]
    ppermute x9 -> x8, waiting for transfers between devices: 17.9 us -> 20.6 us  [shift_x(): return lax.ppermute(value, 'x', [(i, (i + by) % NX) for i in range(NX)])]
    ppermute x4, starting transfers between devices: 5.58 us -> 7.03 us  [swap_halves(): return lax.ppermute(value, ('y', 'c'), pairs)]
    pallas_call x3, Pallas kernels: 10.9 us -> 9.77 us  [score(): pl.pallas_call(functools.partial(score_kernel, len(table), sizes, given),...]
    ppermute x10 -> x9, waiting for transfers between devices: 3.69 us -> 2.52 us  [swap_cores(): return lax.ppermute(value, 'c', [(0, 1), (1, 0)])]
    ppermute x9 -> x8, starting transfers between devices: 13.7 us -> 13 us  [shift_x(): return lax.ppermute(value, 'x', [(i, (i + by) % NX) for i in range(NX)])]
    ppermute x2 -> x3, waiting for transfers between devices: 2.86 us -> 3.33 us  [shift_y(): return lax.ppermute(value, 'y', [(i, (i + by) % NY) for i in range(NY)])]
  transfers between devices with their start and end apart: 31 -> 30, of which waited for: 16 -> 13; matrix products, arithmetic and copies ran while one was open for 0% -> 0% of each run, Pallas kernels for 10% -> 9%
where the time goes in v8:
time: 114 us; the launch traced here: 113 us
  starting transfers between devices  46.6 us (41%)
  waiting for transfers between devices  37.8 us (33%)
  Pallas kernels  18.6 us (16%)
  local copies, waits for them, and re-layouts  9.53 us (8%)
    ppermute x8, waiting for transfers between devices, shift_x(): return lax.ppermute(value, 'x', [(i, (i + by) % NX) for i in range(NX)])  20.6 us
    ppermute x6, starting transfers between devices, along_z(): return lax.ppermute(value, ('z', 'c'), pairs)  16.8 us
    ppermute x8, starting transfers between devices, shift_x(): return lax.ppermute(value, 'x', [(i, (i + by) % NX) for i in range(NX)])  13 us
    pallas_call x3, Pallas kernels, score(): pl.pallas_call(functools.partial(score_kernel, len(table), sizes, given),...  9.77 us
    unnamed x26, local copies, waits for them, and re-layouts  9.37 us
    ppermute x6, waiting for transfers between devices, along_z(): return lax.ppermute(value, ('z', 'c'), pairs)  8.76 us
    ppermute x9, starting transfers between devices, swap_cores(): return lax.ppermute(value, 'c', [(0, 1), (1, 0)])  7.86 us
    ppermute x4, starting transfers between devices, swap_halves(): return lax.ppermute(value, ('y', 'c'), pairs)  7.03 us
  transfers between devices with their start and end apart: 30, of which 13 were waited for; matrix products, arithmetic and copies ran while one was open for 0% of the time, Pallas kernels for 9%

profile of v8, /device:TPU:1, one launch (start us, length us, event | category | flops | bytes accessed | tf_op | source)
XLA Modules:
  0.0 113.4 jit_solution(12483379571559442710)
XLA Ops:
  1.9 6.5 %collective-permute-start = (bf16[256,1024]{1,0:T(8,128)(2,1)S(1)}, bf16[256,1024]{1,0:T(8,128)(2,1)S(1)}, u32[]{:S(2)}, u32[]{:S(2)}) collective-permute-start(bf16[256,1024]{1,0:T(8,128)(2,1)S(1)} %constant_dynamic-slice_fusion.2), channel_id=1, source_target_pairs={{0,8},{1,57},{8,16},{9,1},{16,24},{17,9},{24,32},{25,17},{32,40},{... | collective-permute-start | bytes 1572872 | tf_op jit(solution)/shard_map/ppermute | solution.py:33
  8.4 1.2 %collective-permute-start.2 = (bf16[128,1024]{1,0:T(8,128)(2,1)}, bf16[128,1024]{1,0:T(8,128)(2,1)S(1)}, u32[]{:S(2)}, u32[]{:S(2)}) collective-permute-start(bf16[128,1024]{1,0:T(8,128)(2,1)} %centroids.1), channel_id=1, source_target_pairs={{0,64},{64,128},{128,192},{192,0},{1,65},{65,129},{129,193},{193,1... | collective-permute-start | bytes 786440 | tf_op jit(solution)/shard_map/ppermute | solution.py:21
  9.6 1.5 %collective-permute-start.1 = (bf16[128,1024]{1,0:T(8,128)(2,1)}, bf16[128,1024]{1,0:T(8,128)(2,1)S(1)}, u32[]{:S(2)}, u32[]{:S(2)}) collective-permute-start(bf16[128,1024]{1,0:T(8,128)(2,1)} %centroids.1), channel_id=1, source_target_pairs={{0,192},{64,0},{128,64},{192,128},{1,193},{65,1},{129,65},{193,129... | collective-permute-start | bytes 786440 | tf_op jit(solution)/shard_map/ppermute | solution.py:21
  11.8 5.4 %collective-permute-done.2.refs_4_ = bf16[128,1024]{1,0:T(8,128)(2,1)S(1)} collective-permute-done((bf16[128,1024]{1,0:T(8,128)(2,1)}, bf16[128,1024]{1,0:T(8,128)(2,1)S(1)}, u32[]{:S(2)}, u32[]{:S(2)}) %collective-permute-start.2) | collective-permute-done | bytes 262176 | tf_op jit(solution)/shard_map/ppermute | solution.py:21
  18.0 2.7 %collective-permute-start.9 = (bf16[256,1024]{1,0:T(8,128)(2,1)S(1)}, bf16[256,1024]{1,0:T(8,128)(2,1)S(1)}, u32[]{:S(2)}, u32[]{:S(2)}) collective-permute-start(bf16[256,1024]{1,0:T(8,128)(2,1)S(1)} %collective-permute-done.refs_9_.refs_4_), channel_id=1, source_target_pairs={{0,2},{1,7},{2,0},{3,5},{4,6},{5,3},{6,4},{7,1},{8,10},{9,15},{10,... | collective-permute-start | bytes 1572872 | tf_op jit(solution)/shard_map/ppermute | solution.py:45
  21.9 2.4 %collective-permute-start.5 = (bf16[128,1024]{1,0:T(8,128)(2,1)S(1)}, bf16[128,1024]{1,0:T(8,128)(2,1)}, u32[]{:S(2)}, u32[]{:S(2)}) collective-permute-start(bf16[128,1024]{1,0:T(8,128)(2,1)S(1)} %collective-permute-done.1.refs_2_), channel_id=1, source_target_pairs={{0,192},{64,0},{128,64},{192,128},{1,193},{65,1},{129,65},{193,129... | collective-permute-start | bytes 786440 | tf_op jit(solution)/shard_map/ppermute | solution.py:21
  26.5 3.6 %collective-permute-done.5.refs_0_ = bf16[128,1024]{1,0:T(8,128)(2,1)} collective-permute-done((bf16[128,1024]{1,0:T(8,128)(2,1)S(1)}, bf16[128,1024]{1,0:T(8,128)(2,1)}, u32[]{:S(2)}, u32[]{:S(2)}) %collective-permute-start.5) | collective-permute-done | bytes 262176 | tf_op jit(solution)/shard_map/ppermute | solution.py:21
  30.1 1.9 %collective-permute-start.11 = (bf16[256,1024]{1,0:T(8,128)(2,1)S(1)}, bf16[256,1024]{1,0:T(8,128)(2,1)S(1)}, u32[]{:S(2)}, u32[]{:S(2)}) collective-permute-start(bf16[256,1024]{1,0:T(8,128)(2,1)S(1)} %collective-permute-done.4.refs_11_.refs_6_), channel_id=1, source_target_pairs={{0,8},{1,57},{8,16},{9,1},{16,24},{17,9},{24,32},{25,17},{32,40},{... | collective-permute-start | bytes 1572872 | tf_op jit(solution)/shard_map/ppermute | solution.py:33
  32.0 1.5 %collective-permute-start.10 = (bf16[256,1024]{1,0:T(8,128)(2,1)S(1)}, bf16[256,1024]{1,0:T(8,128)(2,1)}, u32[]{:S(2)}, u32[]{:S(2)}) collective-permute-start(bf16[256,1024]{1,0:T(8,128)(2,1)S(1)} %collective-permute-done.4.refs_11_.refs_6_), channel_id=1, source_target_pairs={{0,2},{1,7},{2,0},{3,5},{4,6},{5,3},{6,4},{7,1},{8,10},{9,15},{10,... | collective-permute-start | bytes 1572872 | tf_op jit(solution)/shard_map/ppermute | solution.py:45
  33.6 5.0 %collective-permute-done.11.refs_8_ = bf16[256,1024]{1,0:T(8,128)(2,1)S(1)} collective-permute-done((bf16[256,1024]{1,0:T(8,128)(2,1)S(1)}, bf16[256,1024]{1,0:T(8,128)(2,1)S(1)}, u32[]{:S(2)}, u32[]{:S(2)}) %collective-permute-start.11) | collective-permute-done | bytes 524320 | tf_op jit(solution)/shard_map/ppermute | solution.py:33
  38.5 2.8 %collective-permute-start.13 = (bf16[128,1024]{1,0:T(8,128)(2,1)S(1)}, bf16[128,1024]{1,0:T(8,128)(2,1)S(1)}, u32[]{:S(2)}, u32[]{:S(2)}) collective-permute-start(bf16[128,1024]{1,0:T(8,128)(2,1)S(1)} %constant_dynamic-slice_fusion), channel_id=1, source_target_pairs={{0,8},{1,57},{8,16},{9,1},{16,24},{17,9},{24,32},{25,17},{32,40},{... | collective-permute-start | bytes 786440 | tf_op jit(solution)/shard_map/ppermute | solution.py:33
  41.3 1.5 %collective-permute-start.12 = (bf16[256,1024]{1,0:T(8,128)(2,1)S(1)}, bf16[256,1024]{1,0:T(8,128)(2,1)S(1)}, u32[]{:S(2)}, u32[]{:S(2)}) collective-permute-start(bf16[256,1024]{1,0:T(8,128)(2,1)S(1)} %collective-permute-done.11.refs_8_), channel_id=1, source_target_pairs={{0,2},{1,7},{2,0},{3,5},{4,6},{5,3},{6,4},{7,1},{8,10},{9,15},{10,... | collective-permute-start | bytes 1572872 | tf_op jit(solution)/shard_map/ppermute | solution.py:45
  47.6 5.2 %shard_map.58 = (f32[1024,128]{1,0:T(8,128)S(1)}, f32[1024,1280]{1,0:T(8,128)S(1)}, f32[1,1280]{1,0:T(1,128)S(1)}) custom-call(bf16[128,1024]{1,0:T(8,128)(2,1)} %collective-permute-done.5.refs_0_, bf16[128,1024]{1,0:T(8,128)(2,1)} %collective-permute-done.8.refs_1_, bf16[128,1024]{1,0:T(8,128)(2,1)S(1)} %copy-done.8, bf16[128,1024]{1,0:T(8,128)(2,1)S(1)} %copy-done.12, ...), custom_call_target="tpu_custom_call" | custom-call | flops 5368709120 | bytes 9961472 | tf_op jit(solution)/shard_map/pallas_call | solution.py:212
  52.8 1.2 %collective-permute-start.14 = (bf16[128,1024]{1,0:T(8,128)(2,1)S(1)}, bf16[128,1024]{1,0:T(8,128)(2,1)S(1)}, u32[]{:S(2)}, u32[]{:S(2)}) collective-permute-start(bf16[128,1024]{1,0:T(8,128)(2,1)S(1)} %collective-permute-done.13.refs_8_.refs_10_), channel_id=1, source_target_pairs={{0,2},{1,7},{2,0},{3,5},{4,6},{5,3},{6,4},{7,1},{8,10},{9,15},{10,... | collective-permute-start | bytes 786440 | tf_op jit(solution)/shard_map/ppermute | solution.py:45
  54.0 2.7 %shard_map.59 = (f32[1024,512]{1,0:T(8,128)S(1)}, f32[1,512]{1,0:T(1,128)S(1)}) custom-call(bf16[128,1024]{1,0:T(8,128)(2,1)} %collective-permute-done.5.refs_0_, bf16[128,1024]{1,0:T(8,128)(2,1)} %collective-permute-done.8.refs_1_, bf16[128,1024]{1,0:T(8,128)(2,1)S(1)} %copy-done.8, bf16[128,1024]{1,0:T(8,128)(2,1)S(1)} %copy-done.12, ...), custom_call_target="tpu_custom_call" | custom-call | flops 2147483648 | bytes 5242880 | tf_op jit(solution)/shard_map/pallas_call | solution.py:212
  56.7 2.6 %collective-permute-done.14.refs_9_.refs_11_ = bf16[128,1024]{1,0:T(8,128)(2,1)S(1)} collective-permute-done((bf16[128,1024]{1,0:T(8,128)(2,1)S(1)}, bf16[128,1024]{1,0:T(8,128)(2,1)S(1)}, u32[]{:S(2)}, u32[]{:S(2)}) %collective-permute-start.14) | collective-permute-done | bytes 262176 | tf_op jit(solution)/shard_map/ppermute | solution.py:45
  59.3 2.0 %shard_map.60 = (f32[1024,256]{1,0:T(8,128)S(1)}, f32[1,256]{1,0:T(1,128)S(1)}) custom-call(bf16[128,1024]{1,0:T(8,128)(2,1)} %collective-permute-done.5.refs_0_, bf16[128,1024]{1,0:T(8,128)(2,1)} %collective-permute-done.8.refs_1_, bf16[128,1024]{1,0:T(8,128)(2,1)S(1)} %copy-done.8, bf16[128,1024]{1,0:T(8,128)(2,1)S(1)} %copy-done.12, ...), custom_call_target="tpu_custom_call" | custom-call | flops 1073741824 | bytes 3670016 | tf_op jit(solution)/shard_map/pallas_call | solution.py:212
  61.3 1.2 %collective-permute-start.17 = (f32[16,128]{1,0:T(8,128)S(1)}, f32[16,128]{1,0:T(8,128)S(1)}, u32[]{:S(2)}, u32[]{:S(2)}) collective-permute-start(f32[16,128]{1,0:T(8,128)S(1)} %shard_map.61.own), channel_id=1, source_target_pairs={{0,6},{2,0},{4,2},{6,4},{1,7},{3,1},{5,3},{7,5},{8,14},{10,8},{12,... | collective-permute-start | bytes 24584 | tf_op jit(solution)/shard_map/ppermute | solution.py:37
  63.9 2.6 %collective-permute-done.16.refs_1_ = f32[16,128]{1,0:T(8,128)S(1)} collective-permute-done((f32[16,128]{1,0:T(8,128)S(1)}, f32[16,128]{1,0:T(8,128)S(1)}, u32[]{:S(2)}, u32[]{:S(2)}) %collective-permute-start.16) | collective-permute-done | bytes 8224 | tf_op jit(solution)/shard_map/ppermute | solution.py:37
  66.5 2.6 %collective-permute-start.18 = (f32[16,128]{1,0:T(8,128)S(1)}, f32[16,128]{1,0:T(8,128)S(1)}, u32[]{:S(2)}, u32[]{:S(2)}) collective-permute-start(f32[16,128]{1,0:T(8,128)S(1)} %shard_map.62.mine), channel_id=1, source_target_pairs={{0,1},{1,0},{2,3},{3,2},{4,5},{5,4},{6,7},{7,6},{8,9},{9,8},{10,11... | collective-permute-start | bytes 24584 | tf_op jit(solution)/shard_map/ppermute | solution.py:25
  70.0 2.8 %collective-permute-start.19 = (f32[4,8,128]{2,1,0:T(8,128)S(1)}, f32[4,8,128]{2,1,0:T(8,128)S(1)}, u32[]{:S(2)}, u32[]{:S(2)}) collective-permute-start(f32[4,8,128]{2,1,0:T(8,128)S(1)} %shard_map.63.block), channel_id=1, source_target_pairs={{0,8},{1,57},{8,16},{9,1},{16,24},{17,9},{24,32},{25,17},{32,40},{... | collective-permute-start | bytes 49160 | tf_op jit(solution)/shard_map/ppermute | solution.py:33
  73.6 1.7 %collective-permute-start.20 = (f32[4,8,128]{2,1,0:T(8,128)S(1)}, f32[4,8,128]{2,1,0:T(8,128)S(1)}, u32[]{:S(2)}, u32[]{:S(2)}) collective-permute-start(f32[4,8,128]{2,1,0:T(8,128)S(1)} %collective-permute-done.19.near), channel_id=1, source_target_pairs={{0,1},{1,0},{2,3},{3,2},{4,5},{5,4},{6,7},{7,6},{8,9},{9,8},{10,11... | collective-permute-start | bytes 49160 | tf_op jit(solution)/shard_map/ppermute | solution.py:25
  76.2 2.1 %collective-permute-start.21 = (f32[4,8,128]{2,1,0:T(8,128)S(1)}, f32[4,8,128]{2,1,0:T(8,128)S(1)}, u32[]{:S(2)}, u32[]{:S(2)}) collective-permute-start(f32[4,8,128]{2,1,0:T(8,128)S(1)} %get-tuple-element.61), channel_id=1, source_target_pairs={{0,24},{1,41},{8,32},{9,49},{16,40},{17,57},{24,48},{25,1},{32,56}... | collective-permute-start | bytes 49160 | tf_op jit(solution)/shard_map/ppermute | solution.py:33
  78.3 2.9 %collective-permute-done.21.got = f32[4,8,128]{2,1,0:T(8,128)S(1)} collective-permute-done((f32[4,8,128]{2,1,0:T(8,128)S(1)}, f32[4,8,128]{2,1,0:T(8,128)S(1)}, u32[]{:S(2)}, u32[]{:S(2)}) %collective-permute-start.21) | collective-permute-done | bytes 16416 | tf_op jit(solution)/shard_map/ppermute | solution.py:33
  81.3 2.3 %collective-permute-start.22 = (f32[4,8,128]{2,1,0:T(8,128)S(1)}, f32[4,8,128]{2,1,0:T(8,128)S(1)}, u32[]{:S(2)}, u32[]{:S(2)}) collective-permute-start(f32[4,8,128]{2,1,0:T(8,128)S(1)} %collective-permute-done.21.got), channel_id=1, source_target_pairs={{0,1},{1,0},{2,3},{3,2},{4,5},{5,4},{6,7},{7,6},{8,9},{9,8},{10,11... | collective-permute-start | bytes 49160 | tf_op jit(solution)/shard_map/ppermute | solution.py:25
  85.0 4.6 %shard_map.67 = (bf16[432,1024]{1,0:T(8,128)(2,1)S(1)}, f32[384,1024]{1,0:T(8,128)S(1)}, f32[48,128]{1,0:T(8,128)S(1)}) custom-call(f32[1,2048]{1,0:T(1,128)S(1)} %get-tuple-element.62.energy, f32[1024,1280]{1,0:T(8,128)S(1)} %get-tuple-element.63.refs_0_, f32[1024,512]{1,0:T(8,128)S(1)} %get-tuple-element.64.refs_1_, ...), custom_call_target="tpu_custom_call" | custom-call | flops 3221225472 | bytes 10485760 | tf_op jit(solution)/shard_map/pallas_call | solution.py:262
  90.1 2.3 %shard_map.66 = (bf16[144,1024]{1,0:T(8,128)(2,1)S(1)}, f32[128,1024]{1,0:T(8,128)S(1)}, f32[16,128]{1,0:T(8,128)S(1)}) custom-call(f32[1,2048]{1,0:T(1,128)S(1)} %get-tuple-element.62.energy, f32[1024,1280]{1,0:T(8,128)S(1)} %get-tuple-element.63.refs_0_, f32[1024,512]{1,0:T(8,128)S(1)} %get-tuple-element.64.refs_1_, ...), custom_call_target="tpu_custom_call" | custom-call | flops 1073741824 | bytes 6291456 | tf_op jit(solution)/shard_map/pallas_call | solution.py:262
  92.8 2.4 %collective-permute-start.27 = (bf16[128,1024]{1,0:T(8,128)(2,1)S(1)}, bf16[128,1024]{1,0:T(8,128)(2,1)S(1)}, u32[]{:S(2)}, u32[]{:S(2)}) collective-permute-start(bf16[128,1024]{1,0:T(8,128)(2,1)S(1)} %get-tuple-element.75), channel_id=1, source_target_pairs={{0,128},{64,192},{128,0},{192,64},{1,129},{65,193},{129,1},{193,65... | collective-permute-start | bytes 786440 | tf_op jit(solution)/shard_map/ppermute | solution.py:21
  95.2 1.8 %collective-permute-start.28 = (bf16[128,1024]{1,0:T(8,128)(2,1)S(1)}, bf16[128,1024]{1,0:T(8,128)(2,1)S(1)}, u32[]{:S(2)}, u32[]{:S(2)}) collective-permute-start(bf16[128,1024]{1,0:T(8,128)(2,1)S(1)} %get-tuple-element.76), channel_id=1, source_target_pairs={{0,64},{64,128},{128,192},{192,0},{1,65},{65,129},{129,193},{193,1... | collective-permute-start | bytes 786440 | tf_op jit(solution)/shard_map/ppermute | solution.py:21
  98.4 9.9 %collective-permute-done.25.one = f32[8,128]{1,0:T(8,128)S(1)} collective-permute-done((f32[8,128]{1,0:T(8,128)S(1)}, f32[8,128]{1,0:T(8,128)S(1)}, u32[]{:S(2)}, u32[]{:S(2)}) %collective-permute-start.25) | collective-permute-done | bytes 4128 | tf_op jit(solution)/shard_map/ppermute | solution.py:21
  108.3 2.3 %collective-permute-start.26 = (f32[8,128]{1,0:T(8,128)S(1)}, f32[8,128]{1,0:T(8,128)S(1)}, u32[]{:S(2)}, u32[]{:S(2)}) collective-permute-start(f32[8,128]{1,0:T(8,128)S(1)} %shard_map.69), channel_id=1, source_target_pairs={{0,128},{64,192},{128,0},{192,64},{1,129},{65,193},{129,1},{193,65... | collective-permute-start | bytes 12296 | tf_op jit(solution)/shard_map/ppermute | solution.py:21
  110.6 1.7 %collective-permute-done.26.two = f32[8,128]{1,0:T(8,128)S(1)} collective-permute-done((f32[8,128]{1,0:T(8,128)S(1)}, f32[8,128]{1,0:T(8,128)S(1)}, u32[]{:S(2)}, u32[]{:S(2)}) %collective-permute-start.26) | collective-permute-done | bytes 4128 | tf_op jit(solution)/shard_map/ppermute | solution.py:21
  (73 shorter events, 19.7 us)
Async XLA Ops:
  0.6 42.2 %copy-start.1 = (bf16[128,1024]{1,0:T(8,128)(2,1)S(1)}, bf16[128,1024]{1,0:T(8,128)(2,1)}, u32[]{:S(2)}) copy-start(bf16[128,1024]{1,0:T(8,128)(2,1)} %centroids.1) | copy-start | bytes 786436
  1.9 15.3 %collective-permute-start = (bf16[256,1024]{1,0:T(8,128)(2,1)S(1)}, bf16[256,1024]{1,0:T(8,128)(2,1)S(1)}, u32[]{:S(2)}, u32[]{:S(2)}) collective-permute-start(bf16[256,1024]{1,0:T(8,128)(2,1)S(1)} %constant_dynamic-slice_fusion.2), channel_id=1, source_target_pairs={{0,8},{1,57},{8,16},{9,1},{16,24},{17,9},{24,32},{25,17},{32,40},{... | collective-permute-start | bytes 1572872 | tf_op jit(solution)/shard_map/ppermute | solution.py:33
  8.4 2.7 %collective-permute-start.3 = (bf16[128,1024]{1,0:T(8,128)(2,1)}, bf16[128,1024]{1,0:T(8,128)(2,1)S(1)}, u32[]{:S(2)}, u32[]{:S(2)}) collective-permute-start(bf16[128,1024]{1,0:T(8,128)(2,1)} %centroids.1), channel_id=1, source_target_pairs={{0,1},{1,0},{2,3},{3,2},{4,5},{5,4},{6,7},{7,6},{8,9},{9,8},{10,11... | collective-permute-start | bytes 786440 | tf_op jit(solution)/shard_map/ppermute | solution.py:25
  8.4 8.8 %collective-permute-start.2 = (bf16[128,1024]{1,0:T(8,128)(2,1)}, bf16[128,1024]{1,0:T(8,128)(2,1)S(1)}, u32[]{:S(2)}, u32[]{:S(2)}) collective-permute-start(bf16[128,1024]{1,0:T(8,128)(2,1)} %centroids.1), channel_id=1, source_target_pairs={{0,64},{64,128},{128,192},{192,0},{1,65},{65,129},{129,193},{193,1... | collective-permute-start | bytes 786440 | tf_op jit(solution)/shard_map/ppermute | solution.py:21
  9.6 7.6 %collective-permute-start.1 = (bf16[128,1024]{1,0:T(8,128)(2,1)}, bf16[128,1024]{1,0:T(8,128)(2,1)S(1)}, u32[]{:S(2)}, u32[]{:S(2)}) collective-permute-start(bf16[128,1024]{1,0:T(8,128)(2,1)} %centroids.1), channel_id=1, source_target_pairs={{0,192},{64,0},{128,64},{192,128},{1,193},{65,1},{129,65},{193,129... | collective-permute-start | bytes 786440 | tf_op jit(solution)/shard_map/ppermute | solution.py:21
  17.2 12.9 %collective-permute-start.4 = (bf16[256,1024]{1,0:T(8,128)(2,1)S(1)}, bf16[256,1024]{1,0:T(8,128)(2,1)S(1)}, u32[]{:S(2)}, u32[]{:S(2)}) collective-permute-start(bf16[256,1024]{1,0:T(8,128)(2,1)S(1)} %collective-permute-done.refs_9_.refs_4_), channel_id=1, source_target_pairs={{0,8},{1,57},{8,16},{9,1},{16,24},{17,9},{24,32},{25,17},{32,40},{... | collective-permute-start | bytes 1572872 | tf_op jit(solution)/shard_map/ppermute | solution.py:33
  18.0 14.0 %collective-permute-start.9 = (bf16[256,1024]{1,0:T(8,128)(2,1)S(1)}, bf16[256,1024]{1,0:T(8,128)(2,1)S(1)}, u32[]{:S(2)}, u32[]{:S(2)}) collective-permute-start(bf16[256,1024]{1,0:T(8,128)(2,1)S(1)} %collective-permute-done.refs_9_.refs_4_), channel_id=1, source_target_pairs={{0,2},{1,7},{2,0},{3,5},{4,6},{5,3},{6,4},{7,1},{8,10},{9,15},{10,... | collective-permute-start | bytes 1572872 | tf_op jit(solution)/shard_map/ppermute | solution.py:45
  20.7 4.3 %collective-permute-start.7 = (bf16[128,1024]{1,0:T(8,128)(2,1)S(1)}, bf16[128,1024]{1,0:T(8,128)(2,1)S(1)}, u32[]{:S(2)}, u32[]{:S(2)}) collective-permute-start(bf16[128,1024]{1,0:T(8,128)(2,1)S(1)} %collective-permute-done.2.refs_4_), channel_id=1, source_target_pairs={{0,1},{1,0},{2,3},{3,2},{4,5},{5,4},{6,7},{7,6},{8,9},{9,8},{10,11... | collective-permute-start | bytes 786440 | tf_op jit(solution)/shard_map/ppermute | solution.py:25
  21.4 4.3 %collective-permute-start.6 = (bf16[128,1024]{1,0:T(8,128)(2,1)S(1)}, bf16[128,1024]{1,0:T(8,128)(2,1)S(1)}, u32[]{:S(2)}, u32[]{:S(2)}) collective-permute-start(bf16[128,1024]{1,0:T(8,128)(2,1)S(1)} %collective-permute-done.1.refs_2_), channel_id=1, source_target_pairs={{0,1},{1,0},{2,3},{3,2},{4,5},{5,4},{6,7},{7,6},{8,9},{9,8},{10,11... | collective-permute-start | bytes 786440 | tf_op jit(solution)/shard_map/ppermute | solution.py:25
  21.9 8.1 %collective-permute-start.5 = (bf16[128,1024]{1,0:T(8,128)(2,1)S(1)}, bf16[128,1024]{1,0:T(8,128)(2,1)}, u32[]{:S(2)}, u32[]{:S(2)}) collective-permute-start(bf16[128,1024]{1,0:T(8,128)(2,1)S(1)} %collective-permute-done.1.refs_2_), channel_id=1, source_target_pairs={{0,192},{64,0},{128,64},{192,128},{1,193},{65,1},{129,65},{193,129... | collective-permute-start | bytes 786440 | tf_op jit(solution)/shard_map/ppermute | solution.py:21
  30.1 8.4 %collective-permute-start.11 = (bf16[256,1024]{1,0:T(8,128)(2,1)S(1)}, bf16[256,1024]{1,0:T(8,128)(2,1)S(1)}, u32[]{:S(2)}, u32[]{:S(2)}) collective-permute-start(bf16[256,1024]{1,0:T(8,128)(2,1)S(1)} %collective-permute-done.4.refs_11_.refs_6_), channel_id=1, source_target_pairs={{0,8},{1,57},{8,16},{9,1},{16,24},{17,9},{24,32},{25,17},{32,40},{... | collective-permute-start | bytes 1572872 | tf_op jit(solution)/shard_map/ppermute | solution.py:33
  32.0 10.9 %collective-permute-start.10 = (bf16[256,1024]{1,0:T(8,128)(2,1)S(1)}, bf16[256,1024]{1,0:T(8,128)(2,1)}, u32[]{:S(2)}, u32[]{:S(2)}) collective-permute-start(bf16[256,1024]{1,0:T(8,128)(2,1)S(1)} %collective-permute-done.4.refs_11_.refs_6_), channel_id=1, source_target_pairs={{0,2},{1,7},{2,0},{3,5},{4,6},{5,3},{6,4},{7,1},{8,10},{9,15},{10,... | collective-permute-start | bytes 1572872 | tf_op jit(solution)/shard_map/ppermute | solution.py:45
  33.5 9.3 %collective-permute-start.8 = (bf16[128,1024]{1,0:T(8,128)(2,1)}, bf16[128,1024]{1,0:T(8,128)(2,1)}, u32[]{:S(2)}, u32[]{:S(2)}) collective-permute-start(bf16[128,1024]{1,0:T(8,128)(2,1)} %collective-permute-done.5.refs_0_), channel_id=1, source_target_pairs={{0,1},{1,0},{2,3},{3,2},{4,5},{5,4},{6,7},{7,6},{8,9},{9,8},{10,11... | collective-permute-start | bytes 786440 | tf_op jit(solution)/shard_map/ppermute | solution.py:25
  38.5 14.2 %collective-permute-start.13 = (bf16[128,1024]{1,0:T(8,128)(2,1)S(1)}, bf16[128,1024]{1,0:T(8,128)(2,1)S(1)}, u32[]{:S(2)}, u32[]{:S(2)}) collective-permute-start(bf16[128,1024]{1,0:T(8,128)(2,1)S(1)} %constant_dynamic-slice_fusion), channel_id=1, source_target_pairs={{0,8},{1,57},{8,16},{9,1},{16,24},{17,9},{24,32},{25,17},{32,40},{... | collective-permute-start | bytes 786440 | tf_op jit(solution)/shard_map/ppermute | solution.py:33
  41.3 12.7 %collective-permute-start.12 = (bf16[256,1024]{1,0:T(8,128)(2,1)S(1)}, bf16[256,1024]{1,0:T(8,128)(2,1)S(1)}, u32[]{:S(2)}, u32[]{:S(2)}) collective-permute-start(bf16[256,1024]{1,0:T(8,128)(2,1)S(1)} %collective-permute-done.11.refs_8_), channel_id=1, source_target_pairs={{0,2},{1,7},{2,0},{3,5},{4,6},{5,3},{6,4},{7,1},{8,10},{9,15},{10,... | collective-permute-start | bytes 1572872 | tf_op jit(solution)/shard_map/ppermute | solution.py:45
  52.8 6.5 %collective-permute-start.14 = (bf16[128,1024]{1,0:T(8,128)(2,1)S(1)}, bf16[128,1024]{1,0:T(8,128)(2,1)S(1)}, u32[]{:S(2)}, u32[]{:S(2)}) collective-permute-start(bf16[128,1024]{1,0:T(8,128)(2,1)S(1)} %collective-permute-done.13.refs_8_.refs_10_), channel_id=1, source_target_pairs={{0,2},{1,7},{2,0},{3,5},{4,6},{5,3},{6,4},{7,1},{8,10},{9,15},{10,... | collective-permute-start | bytes 786440 | tf_op jit(solution)/shard_map/ppermute | solution.py:45
  61.3 2.6 %collective-permute-start.17 = (f32[16,128]{1,0:T(8,128)S(1)}, f32[16,128]{1,0:T(8,128)S(1)}, u32[]{:S(2)}, u32[]{:S(2)}) collective-permute-start(f32[16,128]{1,0:T(8,128)S(1)} %shard_map.61.own), channel_id=1, source_target_pairs={{0,6},{2,0},{4,2},{6,4},{1,7},{3,1},{5,3},{7,5},{8,14},{10,8},{12,... | collective-permute-start | bytes 24584 | tf_op jit(solution)/shard_map/ppermute | solution.py:37
  62.5 4.0 %collective-permute-start.16 = (f32[16,128]{1,0:T(8,128)S(1)}, f32[16,128]{1,0:T(8,128)S(1)}, u32[]{:S(2)}, u32[]{:S(2)}) collective-permute-start(f32[16,128]{1,0:T(8,128)S(1)} %shard_map.61.own), channel_id=1, source_target_pairs={{0,4},{2,6},{4,0},{6,2},{1,5},{3,7},{5,1},{7,3},{8,12},{10,14},{12... | collective-permute-start | bytes 24584 | tf_op jit(solution)/shard_map/ppermute | solution.py:37
  62.6 3.9 %collective-permute-start.15 = (f32[16,128]{1,0:T(8,128)S(1)}, f32[16,128]{1,0:T(8,128)S(1)}, u32[]{:S(2)}, u32[]{:S(2)}) collective-permute-start(f32[16,128]{1,0:T(8,128)S(1)} %shard_map.61.own), channel_id=1, source_target_pairs={{0,2},{2,4},{4,6},{6,0},{1,3},{3,5},{5,7},{7,1},{8,10},{10,12},{12... | collective-permute-start | bytes 24584 | tf_op jit(solution)/shard_map/ppermute | solution.py:37
  66.5 3.4 %collective-permute-start.18 = (f32[16,128]{1,0:T(8,128)S(1)}, f32[16,128]{1,0:T(8,128)S(1)}, u32[]{:S(2)}, u32[]{:S(2)}) collective-permute-start(f32[16,128]{1,0:T(8,128)S(1)} %shard_map.62.mine), channel_id=1, source_target_pairs={{0,1},{1,0},{2,3},{3,2},{4,5},{5,4},{6,7},{7,6},{8,9},{9,8},{10,11... | collective-permute-start | bytes 24584 | tf_op jit(solution)/shard_map/ppermute | solution.py:25
  70.0 3.6 %collective-permute-start.19 = (f32[4,8,128]{2,1,0:T(8,128)S(1)}, f32[4,8,128]{2,1,0:T(8,128)S(1)}, u32[]{:S(2)}, u32[]{:S(2)}) collective-permute-start(f32[4,8,128]{2,1,0:T(8,128)S(1)} %shard_map.63.block), channel_id=1, source_target_pairs={{0,8},{1,57},{8,16},{9,1},{16,24},{17,9},{24,32},{25,17},{32,40},{... | collective-permute-start | bytes 49160 | tf_op jit(solution)/shard_map/ppermute | solution.py:33
  73.6 2.6 %collective-permute-start.20 = (f32[4,8,128]{2,1,0:T(8,128)S(1)}, f32[4,8,128]{2,1,0:T(8,128)S(1)}, u32[]{:S(2)}, u32[]{:S(2)}) collective-permute-start(f32[4,8,128]{2,1,0:T(8,128)S(1)} %collective-permute-done.19.near), channel_id=1, source_target_pairs={{0,1},{1,0},{2,3},{3,2},{4,5},{5,4},{6,7},{7,6},{8,9},{9,8},{10,11... | collective-permute-start | bytes 49160 | tf_op jit(solution)/shard_map/ppermute | solution.py:25
  76.2 5.0 %collective-permute-start.21 = (f32[4,8,128]{2,1,0:T(8,128)S(1)}, f32[4,8,128]{2,1,0:T(8,128)S(1)}, u32[]{:S(2)}, u32[]{:S(2)}) collective-permute-start(f32[4,8,128]{2,1,0:T(8,128)S(1)} %get-tuple-element.61), channel_id=1, source_target_pairs={{0,24},{1,41},{8,32},{9,49},{16,40},{17,57},{24,48},{25,1},{32,56}... | collective-permute-start | bytes 49160 | tf_op jit(solution)/shard_map/ppermute | solution.py:33
  81.3 3.1 %collective-permute-start.22 = (f32[4,8,128]{2,1,0:T(8,128)S(1)}, f32[4,8,128]{2,1,0:T(8,128)S(1)}, u32[]{:S(2)}, u32[]{:S(2)}) collective-permute-start(f32[4,8,128]{2,1,0:T(8,128)S(1)} %collective-permute-done.21.got), channel_id=1, source_target_pairs={{0,1},{1,0},{2,3},{3,2},{4,5},{5,4},{6,7},{7,6},{8,9},{9,8},{10,11... | collective-permute-start | bytes 49160 | tf_op jit(solution)/shard_map/ppermute | solution.py:25
  89.6 3.0 %collective-permute-start.23 = (bf16[432,1024]{1,0:T(8,128)(2,1)S(1)}, bf16[432,1024]{1,0:T(8,128)(2,1)S(1)}, u32[]{:S(2)}, u32[]{:S(2)}) collective-permute-start(bf16[432,1024]{1,0:T(8,128)(2,1)S(1)} %get-tuple-element.68), channel_id=1, source_target_pairs={{0,1},{1,0},{2,3},{3,2},{4,5},{5,4},{6,7},{7,6},{8,9},{9,8},{10,11... | collective-permute-start | bytes 2654216 | tf_op jit(solution)/shard_map/ppermute | solution.py:25
  92.4 19.9 %copy-start.2 = (f32[128]{0:T(128)S(1)}, f32[128]{0:T(128)}, u32[]{:S(2)}) copy-start(f32[128]{0:T(128)} %param.5) | copy-start | bytes 1540
  92.4 18.2 %collective-permute-start.24 = (bf16[144,1024]{1,0:T(8,128)(2,1)S(1)}, bf16[144,1024]{1,0:T(8,128)(2,1)S(1)}, u32[]{:S(2)}, u32[]{:S(2)}) collective-permute-start(bf16[144,1024]{1,0:T(8,128)(2,1)S(1)} %get-tuple-element.73), channel_id=1, source_target_pairs={{0,1},{1,0},{2,3},{3,2},{4,5},{5,4},{6,7},{7,6},{8,9},{9,8},{10,11... | collective-permute-start | bytes 884744 | tf_op jit(solution)/shard_map/ppermute | solution.py:25
  92.8 19.5 %collective-permute-start.27 = (bf16[128,1024]{1,0:T(8,128)(2,1)S(1)}, bf16[128,1024]{1,0:T(8,128)(2,1)S(1)}, u32[]{:S(2)}, u32[]{:S(2)}) collective-permute-start(bf16[128,1024]{1,0:T(8,128)(2,1)S(1)} %get-tuple-element.75), channel_id=1, source_target_pairs={{0,128},{64,192},{128,0},{192,64},{1,129},{65,193},{129,1},{193,65... | collective-permute-start | bytes 786440 | tf_op jit(solution)/shard_map/ppermute | solution.py:21
  95.2 17.1 %collective-permute-start.28 = (bf16[128,1024]{1,0:T(8,128)(2,1)S(1)}, bf16[128,1024]{1,0:T(8,128)(2,1)S(1)}, u32[]{:S(2)}, u32[]{:S(2)}) collective-permute-start(bf16[128,1024]{1,0:T(8,128)(2,1)S(1)} %get-tuple-element.76), channel_id=1, source_target_pairs={{0,64},{64,128},{128,192},{192,0},{1,65},{65,129},{129,193},{193,1... | collective-permute-start | bytes 786440 | tf_op jit(solution)/shard_map/ppermute | solution.py:21
  97.0 15.3 %collective-permute-start.29 = (bf16[128,1024]{1,0:T(8,128)(2,1)S(1)}, bf16[128,1024]{1,0:T(8,128)(2,1)S(1)}, u32[]{:S(2)}, u32[]{:S(2)}) collective-permute-start(bf16[128,1024]{1,0:T(8,128)(2,1)S(1)} %get-tuple-element.77), channel_id=1, source_target_pairs={{0,192},{64,0},{128,64},{192,128},{1,193},{65,1},{129,65},{193,129... | collective-permute-start | bytes 786440 | tf_op jit(solution)/shard_map/ppermute | solution.py:21
  97.8 10.5 %collective-permute-start.25 = (f32[8,128]{1,0:T(8,128)S(1)}, f32[8,128]{1,0:T(8,128)S(1)}, u32[]{:S(2)}, u32[]{:S(2)}) collective-permute-start(f32[8,128]{1,0:T(8,128)S(1)} %get-tuple-element.74.count), channel_id=1, source_target_pairs={{0,64},{64,128},{128,192},{192,0},{1,65},{65,129},{129,193},{193,1... | collective-permute-start | bytes 12296 | tf_op jit(solution)/shard_map/ppermute | solution.py:21
  108.3 4.0 %collective-permute-start.26 = (f32[8,128]{1,0:T(8,128)S(1)}, f32[8,128]{1,0:T(8,128)S(1)}, u32[]{:S(2)}, u32[]{:S(2)}) collective-permute-start(f32[8,128]{1,0:T(8,128)S(1)} %shard_map.69), channel_id=1, source_target_pairs={{0,128},{64,192},{128,0},{192,64},{1,129},{65,193},{129,1},{193,65... | collective-permute-start | bytes 12296 | tf_op jit(solution)/shard_map/ppermute | solution.py:21
  (11 other events, 9.5 us)

commit v9 on v8

--- a/solution.py
+++ b/solution.py
@@ -283,43 +283,37 @@
     )(*args)
 
 
-def add_kernel(n, got, keep, keep_count, count, *messages):
-    count[...] = jnp.zeros(count.shape, F32)
+def add_kernel(n, got, keep, keep_count, *messages):
     for i, message in enumerate(messages):
         total, row = read_message(got, i * (n + TAIL), n)
-        message[...] = (total + keep[i * n : (i + 1) * n, :]).astype(BF16)
-        count[i : i + 1, :] = row[:1] + keep_count[i * TAIL : i * TAIL + 1, :]
+        total = total + keep[i * n : (i + 1) * n, :]
+        write_message(message, 0, total, row + keep_count[i * TAIL : (i + 1) * TAIL, :])
 
 
 def add(got, keep, keep_count):
     n = keep_count.shape[1]
-    k = keep.shape[0] // n
-    shapes = [jax.ShapeDtypeStruct((8, n), F32)] + [jax.ShapeDtypeStruct((n, keep.shape[1]), BF16)] * k
-    return call(functools.partial(add_kernel, n), shapes, got, keep, keep_count)
-
-
-def hand_on_kernel(count, one, out):
-    out[...] = jnp.broadcast_to(count[0:1, :] + one[2:3, :], out.shape)
-
-
-def update_kernel(n, keep, keep_count, got, one, two, masses, centroids, *refs):
-    others, (new_centroids, new_masses) = refs[:-2], refs[-2:]
-    total, row = read_message(got, 0, n)
-    total, row = total + keep[...], (row + keep_count[...])[:1] + one[1:2, :] + two[:1, :]
-    for message in others:
-        total = total + message[...].astype(F32)
+    shape = jax.ShapeDtypeStruct((n + TAIL, got.shape[1]), BF16)
+    return call(functools.partial(add_kernel, n), (shape,) * (NX - 1), got, keep, keep_count)
+
+
+def update_kernel(n, keep, keep_count, got, one, two, three, masses, centroids, new_centroids, new_masses):
+    total, row = keep[...], keep_count[...]
+    for message in (got, one, two, three):
+        t, r = read_message(message, 0, n)
+        total, row = total + t, row + r
     mass = masses[...]
-    new = mass + row
+    new = mass + row[:1]
     new_masses[...] = new
     column = lambda v: jnp.transpose(jnp.broadcast_to(v, (n, n)))[:, :1]
     new_centroids[...] = (column(mass) * centroids[...].astype(F32) + total) / column(new)
 
 
-def update(keep, keep_count, got, counts, others, masses, centroids):
+def update(keep, keep_count, got, others, masses, centroids):
     n, width = centroids.shape
     out = (jax.ShapeDtypeStruct((n, width), F32), jax.ShapeDtypeStruct((1, n), F32))
-    args = (keep, keep_count, got, *counts, masses.reshape(1, n), centroids, *others)
-    return call(functools.partial(update_kernel, n), out, *args)
+    return call(
+        functools.partial(update_kernel, n), out, keep, keep_count, got, *others, masses.reshape(1, n), centroids
+    )
 
 
 def shards(embeddings, centroids, masses):
@@ -335,19 +329,16 @@
     mine = lax.dynamic_slice_in_dim(embeddings, h * half, half, 0)
     one = along_z(mine, 1)
     own = lax.dynamic_slice_in_dim(embeddings.reshape(2, 2, sub, width), c, 1, 1).reshape(half, width)
-    swapped = {0: swap_cores(centroids)}
-    one, near[1], near[3], swapped[0] = lax.optimization_barrier((one, near[1], near[3], swapped[0]))
-    swapped |= {1: swap_cores(near[1]), 3: swap_cores(near[3])}
+    one, near[1], near[3] = lax.optimization_barrier((one, near[1], near[3]))
     near[2] = shift_x(near[1], -1)
     first = swap_halves(one)
     two = along_z(one, 1)
-    two, near[2], swapped[1], swapped[3] = lax.optimization_barrier((two, near[2], swapped[1], swapped[3]))
-    swapped[2] = swap_cores(near[2])
+    two, near[2] = lax.optimization_barrier((two, near[2]))
     three = along_z(two, 1)
     two, first = lax.optimization_barrier((two, first))
 
     fixed = lambda v: pltpu.with_memory_space_constraint(v, pltpu.VMEM) if PIN else v
-    table = [fixed(v) for d in ORDER for v in (near[d], swapped[d])]
+    table = [fixed(v) for d in ORDER for v in (near[d], swap_cores(near[d]))]
 
     four = along_z(lax.dynamic_slice_in_dim(three, c * sub, sub, 0), 1)
     lots = [[fixed(v) for v in (own, one, first, two, swap_halves(two))]]
@@ -368,13 +359,10 @@
     logits, pieces = [fixed(v) for v in logits], [v for lot in lots for v in lot]
 
     message, keep, keep_count = weigh(0, NX - 1, logits, energy, pieces)
-    count, *sums = add(swap_cores(message), keep, keep_count)
-    sums = [shift_x(m, d) for m, d in zip(sums, ORDER)]
+    sent = add(swap_cores(message), keep, keep_count)
     message, keep, keep_count = weigh(NX - 1, 1, logits, energy, pieces)
-    keep_count, count = lax.optimization_barrier((keep_count, count))
-    one = shift_x(count, 1)
-    two = shift_x(call(hand_on_kernel, jax.ShapeDtypeStruct(count.shape, F32), count, one), 2)
-    new_centroids, new_masses = update(keep, keep_count, swap_cores(message), (one, two), sums, masses, centroids)
+    others = [shift_x(m, d) for m, d in zip(sent, ORDER)]
+    new_centroids, new_masses = update(keep, keep_count, swap_cores(message), others, masses, centroids)
     return new_centroids, new_masses.reshape(-1), row_energy
 
 

time: 114 us -> 104 us (0.912)
  local copies, waits for them, and re-layouts: 9.53 us -> 1.29 us
  waiting for transfers between devices: 37.8 us -> 32.4 us
  starting transfers between devices: 46.6 us -> 49.6 us
  Pallas kernels: 18.6 us -> 19.8 us
    unnamed x26 -> x6, local copies, waits for them, and re-layouts: 9.37 us -> 1.12 us
    ppermute x6, waiting for transfers between devices: 8.76 us -> 4.1 us  [along_z(): return lax.ppermute(value, ('z', 'c'), pairs)]
    ppermute x9, starting transfers between devices: 7.86 us -> 11 us  [swap_cores(): return lax.ppermute(value, 'c', [(0, 1), (1, 0)])]
    ppermute x4, starting transfers between devices: 7.03 us -> 9.8 us  [swap_halves(): return lax.ppermute(value, ('y', 'c'), pairs)]
    ppermute x8 -> x6, waiting for transfers between devices: 20.6 us -> 18.2 us  [shift_x(): return lax.ppermute(value, 'x', [(i, (i + by) % NX) for i in range(NX)])]
    ppermute x8 -> x6, starting transfers between devices: 13 us -> 10.7 us  [shift_x(): return lax.ppermute(value, 'x', [(i, (i + by) % NX) for i in range(NX)])]
    ppermute x4, waiting for transfers between devices: 2.62 us -> 4.22 us  [swap_halves(): return lax.ppermute(value, ('y', 'c'), pairs)]
    pallas_call x3, Pallas kernels: 9.77 us -> 10.9 us  [score(): pl.pallas_call(functools.partial(score_kernel, len(table), sizes, given),...]
  transfers between devices with their start and end apart: 30 -> 28, of which waited for: 13 -> 15; matrix products, arithmetic and copies ran while one was open for 0% -> 0% of each run, Pallas kernels for 9% -> 11%
where the time goes in v9:
time: 104 us
  starting transfers between devices  49.6 us (48%)
  waiting for transfers between devices  32.4 us (31%)
  Pallas kernels  19.8 us (19%)
  local copies, waits for them, and re-layouts  1.29 us (1%)
    ppermute x6, waiting for transfers between devices, shift_x(): return lax.ppermute(value, 'x', [(i, (i + by) % NX) for i in range(NX)])  18.2 us
    ppermute x6, starting transfers between devices, along_z(): return lax.ppermute(value, ('z', 'c'), pairs)  15.8 us
    ppermute x9, starting transfers between devices, swap_cores(): return lax.ppermute(value, 'c', [(0, 1), (1, 0)])  11 us
    pallas_call x3, Pallas kernels, score(): pl.pallas_call(functools.partial(score_kernel, len(table), sizes, given),...  10.9 us
    ppermute x6, starting transfers between devices, shift_x(): return lax.ppermute(value, 'x', [(i, (i + by) % NX) for i in range(NX)])  10.7 us
    ppermute x4, starting transfers between devices, swap_halves(): return lax.ppermute(value, ('y', 'c'), pairs)  9.8 us
    pallas_call x2, Pallas kernels, weigh(): pl.pallas_call(functools.partial(weigh_kernel, first, groups, sizes), out...  6.94 us
    ppermute x4, waiting for transfers between devices, swap_halves(): return lax.ppermute(value, ('y', 'c'), pairs)  4.22 us
  transfers between devices with their start and end apart: 28, of which 15 were waited for; matrix products, arithmetic and copies ran while one was open for 0% of the time, Pallas kernels for 11%

profile of v9, /device:TPU:1, one launch (start us, length us, event | category | flops | bytes accessed | tf_op | source)
XLA Modules:
  0.0 103.9 jit_solution(15445009336660425266)
XLA Ops:
  1.9 6.5 %collective-permute-start = (bf16[256,1024]{1,0:T(8,128)(2,1)S(1)}, bf16[256,1024]{1,0:T(8,128)(2,1)S(1)}, u32[]{:S(2)}, u32[]{:S(2)}) collective-permute-start(bf16[256,1024]{1,0:T(8,128)(2,1)S(1)} %constant_dynamic-slice_fusion.2), channel_id=1, source_target_pairs={{0,8},{1,57},{8,16},{9,1},{16,24},{17,9},{24,32},{25,17},{32,40},{... | collective-permute-start | bytes 1572872 | tf_op jit(solution)/shard_map/ppermute | solution.py:33
  8.4 1.2 %collective-permute-start.2 = (bf16[128,1024]{1,0:T(8,128)(2,1)}, bf16[128,1024]{1,0:T(8,128)(2,1)}, u32[]{:S(2)}, u32[]{:S(2)}) collective-permute-start(bf16[128,1024]{1,0:T(8,128)(2,1)} %centroids.1), channel_id=1, source_target_pairs={{0,64},{64,128},{128,192},{192,0},{1,65},{65,129},{129,193},{193,1... | collective-permute-start | bytes 786440 | tf_op jit(solution)/shard_map/ppermute | solution.py:21
  9.6 1.5 %collective-permute-start.1 = (bf16[128,1024]{1,0:T(8,128)(2,1)}, bf16[128,1024]{1,0:T(8,128)(2,1)}, u32[]{:S(2)}, u32[]{:S(2)}) collective-permute-start(bf16[128,1024]{1,0:T(8,128)(2,1)} %centroids.1), channel_id=1, source_target_pairs={{0,192},{64,0},{128,64},{192,128},{1,193},{65,1},{129,65},{193,129... | collective-permute-start | bytes 786440 | tf_op jit(solution)/shard_map/ppermute | solution.py:21
  11.1 4.5 %collective-permute-done.2.refs_4_ = bf16[128,1024]{1,0:T(8,128)(2,1)} collective-permute-done((bf16[128,1024]{1,0:T(8,128)(2,1)}, bf16[128,1024]{1,0:T(8,128)(2,1)}, u32[]{:S(2)}, u32[]{:S(2)}) %collective-permute-start.2) | collective-permute-done | bytes 262176 | tf_op jit(solution)/shard_map/ppermute | solution.py:21
  15.9 2.7 %collective-permute-start.3 = (bf16[256,1024]{1,0:T(8,128)(2,1)S(1)}, bf16[256,1024]{1,0:T(8,128)(2,1)S(1)}, u32[]{:S(2)}, u32[]{:S(2)}) collective-permute-start(bf16[256,1024]{1,0:T(8,128)(2,1)S(1)} %collective-permute-done.refs_9_.refs_4_), channel_id=1, source_target_pairs={{0,8},{1,57},{8,16},{9,1},{16,24},{17,9},{24,32},{25,17},{32,40},{... | collective-permute-start | bytes 1572872 | tf_op jit(solution)/shard_map/ppermute | solution.py:33
  18.5 2.4 %collective-permute-start.4 = (bf16[128,1024]{1,0:T(8,128)(2,1)}, bf16[128,1024]{1,0:T(8,128)(2,1)}, u32[]{:S(2)}, u32[]{:S(2)}) collective-permute-start(bf16[128,1024]{1,0:T(8,128)(2,1)} %collective-permute-done.1.refs_2_), channel_id=1, source_target_pairs={{0,192},{64,0},{128,64},{192,128},{1,193},{65,1},{129,65},{193,129... | collective-permute-start | bytes 786440 | tf_op jit(solution)/shard_map/ppermute | solution.py:21
  20.9 2.7 %collective-permute-start.9 = (bf16[256,1024]{1,0:T(8,128)(2,1)S(1)}, bf16[256,1024]{1,0:T(8,128)(2,1)S(1)}, u32[]{:S(2)}, u32[]{:S(2)}) collective-permute-start(bf16[256,1024]{1,0:T(8,128)(2,1)S(1)} %collective-permute-done.refs_9_.refs_4_), channel_id=1, source_target_pairs={{0,2},{1,7},{2,0},{3,5},{4,6},{5,3},{6,4},{7,1},{8,10},{9,15},{10,... | collective-permute-start | bytes 1572872 | tf_op jit(solution)/shard_map/ppermute | solution.py:45
  23.6 2.2 %collective-permute-done.4.refs_0_ = bf16[128,1024]{1,0:T(8,128)(2,1)} collective-permute-done((bf16[128,1024]{1,0:T(8,128)(2,1)}, bf16[128,1024]{1,0:T(8,128)(2,1)}, u32[]{:S(2)}, u32[]{:S(2)}) %collective-permute-start.4) | collective-permute-done | bytes 262176 | tf_op jit(solution)/shard_map/ppermute | solution.py:21
  25.9 1.9 %collective-permute-start.11 = (bf16[256,1024]{1,0:T(8,128)(2,1)S(1)}, bf16[256,1024]{1,0:T(8,128)(2,1)S(1)}, u32[]{:S(2)}, u32[]{:S(2)}) collective-permute-start(bf16[256,1024]{1,0:T(8,128)(2,1)S(1)} %collective-permute-done.3.refs_11_.refs_6_), channel_id=1, source_target_pairs={{0,8},{1,57},{8,16},{9,1},{16,24},{17,9},{24,32},{25,17},{32,40},{... | collective-permute-start | bytes 1572872 | tf_op jit(solution)/shard_map/ppermute | solution.py:33
  27.8 2.4 %collective-permute-done.9.refs_10_.refs_5_ = bf16[256,1024]{1,0:T(8,128)(2,1)S(1)} collective-permute-done((bf16[256,1024]{1,0:T(8,128)(2,1)S(1)}, bf16[256,1024]{1,0:T(8,128)(2,1)S(1)}, u32[]{:S(2)}, u32[]{:S(2)}) %collective-permute-start.9) | collective-permute-done | bytes 524320 | tf_op jit(solution)/shard_map/ppermute | solution.py:45
  30.2 2.7 %collective-permute-start.10 = (bf16[256,1024]{1,0:T(8,128)(2,1)S(1)}, bf16[256,1024]{1,0:T(8,128)(2,1)}, u32[]{:S(2)}, u32[]{:S(2)}) collective-permute-start(bf16[256,1024]{1,0:T(8,128)(2,1)S(1)} %collective-permute-done.3.refs_11_.refs_6_), channel_id=1, source_target_pairs={{0,2},{1,7},{2,0},{3,5},{4,6},{5,3},{6,4},{7,1},{8,10},{9,15},{10,... | collective-permute-start | bytes 1572872 | tf_op jit(solution)/shard_map/ppermute | solution.py:45
  34.3 3.0 %collective-permute-start.5 = (bf16[128,1024]{1,0:T(8,128)(2,1)}, bf16[128,1024]{1,0:T(8,128)(2,1)}, u32[]{:S(2)}, u32[]{:S(2)}) collective-permute-start(bf16[128,1024]{1,0:T(8,128)(2,1)} %collective-permute-done.4.refs_0_), channel_id=1, source_target_pairs={{0,1},{1,0},{2,3},{3,2},{4,5},{5,4},{6,7},{7,6},{8,9},{9,8},{10,11... | collective-permute-start | bytes 786440 | tf_op jit(solution)/shard_map/ppermute | solution.py:25
  37.9 2.7 %collective-permute-start.12 = (bf16[256,1024]{1,0:T(8,128)(2,1)S(1)}, bf16[256,1024]{1,0:T(8,128)(2,1)S(1)}, u32[]{:S(2)}, u32[]{:S(2)}) collective-permute-start(bf16[256,1024]{1,0:T(8,128)(2,1)S(1)} %collective-permute-done.11.refs_8_), channel_id=1, source_target_pairs={{0,2},{1,7},{2,0},{3,5},{4,6},{5,3},{6,4},{7,1},{8,10},{9,15},{10,... | collective-permute-start | bytes 1572872 | tf_op jit(solution)/shard_map/ppermute | solution.py:45
  40.7 5.5 %shard_map.58 = (f32[1024,128]{1,0:T(8,128)S(1)}, f32[1024,1280]{1,0:T(8,128)S(1)}, f32[1,1280]{1,0:T(1,128)S(1)}) custom-call(bf16[128,1024]{1,0:T(8,128)(2,1)} %collective-permute-done.4.refs_0_, bf16[128,1024]{1,0:T(8,128)(2,1)} %collective-permute-done.5.refs_1_, bf16[128,1024]{1,0:T(8,128)(2,1)} %collective-permute-done.1.refs_2_, ...), custom_call_target="tpu_custom_call" | custom-call | flops 5368709120 | bytes 9961472 | tf_op jit(solution)/shard_map/pallas_call | solution.py:212
  46.2 1.7 %collective-permute-start.14 = (bf16[128,1024]{1,0:T(8,128)(2,1)S(1)}, bf16[128,1024]{1,0:T(8,128)(2,1)S(1)}, u32[]{:S(2)}, u32[]{:S(2)}) collective-permute-start(bf16[128,1024]{1,0:T(8,128)(2,1)S(1)} %collective-permute-done.13.refs_8_.refs_10_), channel_id=1, source_target_pairs={{0,2},{1,7},{2,0},{3,5},{4,6},{5,3},{6,4},{7,1},{8,10},{9,15},{10,... | collective-permute-start | bytes 786440 | tf_op jit(solution)/shard_map/ppermute | solution.py:45
  47.9 3.1 %shard_map.59 = (f32[1024,512]{1,0:T(8,128)S(1)}, f32[1,512]{1,0:T(1,128)S(1)}) custom-call(bf16[128,1024]{1,0:T(8,128)(2,1)} %collective-permute-done.4.refs_0_, bf16[128,1024]{1,0:T(8,128)(2,1)} %collective-permute-done.5.refs_1_, bf16[128,1024]{1,0:T(8,128)(2,1)} %collective-permute-done.1.refs_2_, bf16[128,1024]{1,0:T(8,128)(2,1)} %collective-permute-done.6.refs_3_, ...), custom_call_target="tpu_custom_call" | custom-call | flops 2147483648 | bytes 5242880 | tf_op jit(solution)/shard_map/pallas_call | solution.py:212
  50.9 1.8 %collective-permute-done.14.refs_9_.refs_11_ = bf16[128,1024]{1,0:T(8,128)(2,1)S(1)} collective-permute-done((bf16[128,1024]{1,0:T(8,128)(2,1)S(1)}, bf16[128,1024]{1,0:T(8,128)(2,1)S(1)}, u32[]{:S(2)}, u32[]{:S(2)}) %collective-permute-start.14) | collective-permute-done | bytes 262176 | tf_op jit(solution)/shard_map/ppermute | solution.py:45
  52.7 2.3 %shard_map.60 = (f32[1024,256]{1,0:T(8,128)S(1)}, f32[1,256]{1,0:T(1,128)S(1)}) custom-call(bf16[128,1024]{1,0:T(8,128)(2,1)} %collective-permute-done.4.refs_0_, bf16[128,1024]{1,0:T(8,128)(2,1)} %collective-permute-done.5.refs_1_, bf16[128,1024]{1,0:T(8,128)(2,1)} %collective-permute-done.1.refs_2_, bf16[128,1024]{1,0:T(8,128)(2,1)} %collective-permute-done.6.refs_3_, ...), custom_call_target="tpu_custom_call" | custom-call | flops 1073741824 | bytes 3670016 | tf_op jit(solution)/shard_map/pallas_call | solution.py:212
  55.1 1.6 %collective-permute-start.17 = (f32[16,128]{1,0:T(8,128)S(1)}, f32[16,128]{1,0:T(8,128)S(1)}, u32[]{:S(2)}, u32[]{:S(2)}) collective-permute-start(f32[16,128]{1,0:T(8,128)S(1)} %shard_map.61.own), channel_id=1, source_target_pairs={{0,6},{2,0},{4,2},{6,4},{1,7},{3,1},{5,3},{7,5},{8,14},{10,8},{12,... | collective-permute-start | bytes 24584 | tf_op jit(solution)/shard_map/ppermute | solution.py:37
  57.7 3.1 %collective-permute-done.16.refs_1_ = f32[16,128]{1,0:T(8,128)S(1)} collective-permute-done((f32[16,128]{1,0:T(8,128)S(1)}, f32[16,128]{1,0:T(8,128)S(1)}, u32[]{:S(2)}, u32[]{:S(2)}) %collective-permute-start.16) | collective-permute-done | bytes 8224 | tf_op jit(solution)/shard_map/ppermute | solution.py:37
  60.8 1.7 %collective-permute-start.18 = (f32[16,128]{1,0:T(8,128)S(1)}, f32[16,128]{1,0:T(8,128)S(1)}, u32[]{:S(2)}, u32[]{:S(2)}) collective-permute-start(f32[16,128]{1,0:T(8,128)S(1)} %shard_map.62.mine), channel_id=1, source_target_pairs={{0,1},{1,0},{2,3},{3,2},{4,5},{5,4},{6,7},{7,6},{8,9},{9,8},{10,11... | collective-permute-start | bytes 24584 | tf_op jit(solution)/shard_map/ppermute | solution.py:25
  63.3 2.1 %collective-permute-start.19 = (f32[4,8,128]{2,1,0:T(8,128)S(1)}, f32[4,8,128]{2,1,0:T(8,128)S(1)}, u32[]{:S(2)}, u32[]{:S(2)}) collective-permute-start(f32[4,8,128]{2,1,0:T(8,128)S(1)} %shard_map.63.block), channel_id=1, source_target_pairs={{0,8},{1,57},{8,16},{9,1},{16,24},{17,9},{24,32},{25,17},{32,40},{... | collective-permute-start | bytes 49160 | tf_op jit(solution)/shard_map/ppermute | solution.py:33
  66.2 2.4 %collective-permute-start.20 = (f32[4,8,128]{2,1,0:T(8,128)S(1)}, f32[4,8,128]{2,1,0:T(8,128)S(1)}, u32[]{:S(2)}, u32[]{:S(2)}) collective-permute-start(f32[4,8,128]{2,1,0:T(8,128)S(1)} %collective-permute-done.19.near), channel_id=1, source_target_pairs={{0,1},{1,0},{2,3},{3,2},{4,5},{5,4},{6,7},{7,6},{8,9},{9,8},{10,11... | collective-permute-start | bytes 49160 | tf_op jit(solution)/shard_map/ppermute | solution.py:25
  69.6 2.2 %collective-permute-start.21 = (f32[4,8,128]{2,1,0:T(8,128)S(1)}, f32[4,8,128]{2,1,0:T(8,128)S(1)}, u32[]{:S(2)}, u32[]{:S(2)}) collective-permute-start(f32[4,8,128]{2,1,0:T(8,128)S(1)} %get-tuple-element.52), channel_id=1, source_target_pairs={{0,24},{1,41},{8,32},{9,49},{16,40},{17,57},{24,48},{25,1},{32,56}... | collective-permute-start | bytes 49160 | tf_op jit(solution)/shard_map/ppermute | solution.py:33
  71.7 2.3 %collective-permute-done.21.got = f32[4,8,128]{2,1,0:T(8,128)S(1)} collective-permute-done((f32[4,8,128]{2,1,0:T(8,128)S(1)}, f32[4,8,128]{2,1,0:T(8,128)S(1)}, u32[]{:S(2)}, u32[]{:S(2)}) %collective-permute-start.21) | collective-permute-done | bytes 16416 | tf_op jit(solution)/shard_map/ppermute | solution.py:33
  74.0 2.7 %collective-permute-start.22 = (f32[4,8,128]{2,1,0:T(8,128)S(1)}, f32[4,8,128]{2,1,0:T(8,128)S(1)}, u32[]{:S(2)}, u32[]{:S(2)}) collective-permute-start(f32[4,8,128]{2,1,0:T(8,128)S(1)} %collective-permute-done.21.got), channel_id=1, source_target_pairs={{0,1},{1,0},{2,3},{3,2},{4,5},{5,4},{6,7},{7,6},{8,9},{9,8},{10,11... | collective-permute-start | bytes 49160 | tf_op jit(solution)/shard_map/ppermute | solution.py:25
  78.2 4.6 %shard_map.67 = (bf16[432,1024]{1,0:T(8,128)(2,1)S(1)}, f32[384,1024]{1,0:T(8,128)S(1)}, f32[48,128]{1,0:T(8,128)S(1)}) custom-call(f32[1,2048]{1,0:T(1,128)S(1)} %get-tuple-element.53.energy, f32[1024,1280]{1,0:T(8,128)S(1)} %get-tuple-element.54.refs_0_, f32[1024,512]{1,0:T(8,128)S(1)} %get-tuple-element.55.refs_1_, ...), custom_call_target="tpu_custom_call" | custom-call | flops 3221225472 | bytes 10485760 | tf_op jit(solution)/shard_map/pallas_call | solution.py:262
  83.2 2.3 %shard_map.66 = (bf16[144,1024]{1,0:T(8,128)(2,1)S(1)}, f32[128,1024]{1,0:T(8,128)S(1)}, f32[16,128]{1,0:T(8,128)S(1)}) custom-call(f32[1,2048]{1,0:T(1,128)S(1)} %get-tuple-element.53.energy, f32[1024,1280]{1,0:T(8,128)S(1)} %get-tuple-element.54.refs_0_, f32[1024,512]{1,0:T(8,128)S(1)} %get-tuple-element.55.refs_1_, ...), custom_call_target="tpu_custom_call" | custom-call | flops 1073741824 | bytes 6291456 | tf_op jit(solution)/shard_map/pallas_call | solution.py:262
  86.0 3.0 %collective-permute-start.25 = (bf16[144,1024]{1,0:T(8,128)(2,1)S(1)}, bf16[144,1024]{1,0:T(8,128)(2,1)S(1)}, u32[]{:S(2)}, u32[]{:S(2)}) collective-permute-start(bf16[144,1024]{1,0:T(8,128)(2,1)S(1)} %get-tuple-element.63), channel_id=1, source_target_pairs={{0,128},{64,192},{128,0},{192,64},{1,129},{65,193},{129,1},{193,65... | collective-permute-start | bytes 884744 | tf_op jit(solution)/shard_map/ppermute | solution.py:21
  89.3 2.3 %collective-permute-start.27 = (bf16[144,1024]{1,0:T(8,128)(2,1)S(1)}, bf16[144,1024]{1,0:T(8,128)(2,1)S(1)}, u32[]{:S(2)}, u32[]{:S(2)}) collective-permute-start(bf16[144,1024]{1,0:T(8,128)(2,1)S(1)} %get-tuple-element.65), channel_id=1, source_target_pairs={{0,192},{64,0},{128,64},{192,128},{1,193},{65,1},{129,65},{193,129... | collective-permute-start | bytes 884744 | tf_op jit(solution)/shard_map/ppermute | solution.py:21
  91.7 4.2 %collective-permute-done.25.one = bf16[144,1024]{1,0:T(8,128)(2,1)S(1)} collective-permute-done((bf16[144,1024]{1,0:T(8,128)(2,1)S(1)}, bf16[144,1024]{1,0:T(8,128)(2,1)S(1)}, u32[]{:S(2)}, u32[]{:S(2)}) %collective-permute-start.25) | collective-permute-done | bytes 294944 | tf_op jit(solution)/shard_map/ppermute | solution.py:21
  95.9 7.0 %collective-permute-done.26.two = bf16[144,1024]{1,0:T(8,128)(2,1)S(1)} collective-permute-done((bf16[144,1024]{1,0:T(8,128)(2,1)S(1)}, bf16[144,1024]{1,0:T(8,128)(2,1)S(1)}, u32[]{:S(2)}, u32[]{:S(2)}) %collective-permute-start.26) | collective-permute-done | bytes 294944 | tf_op jit(solution)/shard_map/ppermute | solution.py:21
  (48 shorter events, 10.9 us)
Async XLA Ops:
  0.6 1.2 %copy-start = (bf16[512,1024]{1,0:T(8,128)(2,1)S(1)}, bf16[512,1024]{1,0:T(8,128)(2,1)}, u32[]{:S(2)}) copy-start(bf16[512,1024]{1,0:T(8,128)(2,1)} %param.3) | copy-start | bytes 3145732
  0.6 40.0 %copy-start.1 = (bf16[128,1024]{1,0:T(8,128)(2,1)S(1)}, bf16[128,1024]{1,0:T(8,128)(2,1)}, u32[]{:S(2)}) copy-start(bf16[128,1024]{1,0:T(8,128)(2,1)} %centroids.1) | copy-start | bytes 786436
  1.9 14.0 %collective-permute-start = (bf16[256,1024]{1,0:T(8,128)(2,1)S(1)}, bf16[256,1024]{1,0:T(8,128)(2,1)S(1)}, u32[]{:S(2)}, u32[]{:S(2)}) collective-permute-start(bf16[256,1024]{1,0:T(8,128)(2,1)S(1)} %constant_dynamic-slice_fusion.2), channel_id=1, source_target_pairs={{0,8},{1,57},{8,16},{9,1},{16,24},{17,9},{24,32},{25,17},{32,40},{... | collective-permute-start | bytes 1572872 | tf_op jit(solution)/shard_map/ppermute | solution.py:33
  8.4 7.2 %collective-permute-start.2 = (bf16[128,1024]{1,0:T(8,128)(2,1)}, bf16[128,1024]{1,0:T(8,128)(2,1)}, u32[]{:S(2)}, u32[]{:S(2)}) collective-permute-start(bf16[128,1024]{1,0:T(8,128)(2,1)} %centroids.1), channel_id=1, source_target_pairs={{0,64},{64,128},{128,192},{192,0},{1,65},{65,129},{129,193},{193,1... | collective-permute-start | bytes 786440 | tf_op jit(solution)/shard_map/ppermute | solution.py:21
  9.6 6.3 %collective-permute-start.1 = (bf16[128,1024]{1,0:T(8,128)(2,1)}, bf16[128,1024]{1,0:T(8,128)(2,1)}, u32[]{:S(2)}, u32[]{:S(2)}) collective-permute-start(bf16[128,1024]{1,0:T(8,128)(2,1)} %centroids.1), channel_id=1, source_target_pairs={{0,192},{64,0},{128,64},{192,128},{1,193},{65,1},{129,65},{193,129... | collective-permute-start | bytes 786440 | tf_op jit(solution)/shard_map/ppermute | solution.py:21
  15.9 10.0 %collective-permute-start.3 = (bf16[256,1024]{1,0:T(8,128)(2,1)S(1)}, bf16[256,1024]{1,0:T(8,128)(2,1)S(1)}, u32[]{:S(2)}, u32[]{:S(2)}) collective-permute-start(bf16[256,1024]{1,0:T(8,128)(2,1)S(1)} %collective-permute-done.refs_9_.refs_4_), channel_id=1, source_target_pairs={{0,8},{1,57},{8,16},{9,1},{16,24},{17,9},{24,32},{25,17},{32,40},{... | collective-permute-start | bytes 1572872 | tf_op jit(solution)/shard_map/ppermute | solution.py:33
  18.5 7.3 %collective-permute-start.4 = (bf16[128,1024]{1,0:T(8,128)(2,1)}, bf16[128,1024]{1,0:T(8,128)(2,1)}, u32[]{:S(2)}, u32[]{:S(2)}) collective-permute-start(bf16[128,1024]{1,0:T(8,128)(2,1)} %collective-permute-done.1.refs_2_), channel_id=1, source_target_pairs={{0,192},{64,0},{128,64},{192,128},{1,193},{65,1},{129,65},{193,129... | collective-permute-start | bytes 786440 | tf_op jit(solution)/shard_map/ppermute | solution.py:21
  20.9 9.3 %collective-permute-start.9 = (bf16[256,1024]{1,0:T(8,128)(2,1)S(1)}, bf16[256,1024]{1,0:T(8,128)(2,1)S(1)}, u32[]{:S(2)}, u32[]{:S(2)}) collective-permute-start(bf16[256,1024]{1,0:T(8,128)(2,1)S(1)} %collective-permute-done.refs_9_.refs_4_), channel_id=1, source_target_pairs={{0,2},{1,7},{2,0},{3,5},{4,6},{5,3},{6,4},{7,1},{8,10},{9,15},{10,... | collective-permute-start | bytes 1572872 | tf_op jit(solution)/shard_map/ppermute | solution.py:45
  25.9 8.4 %collective-permute-start.11 = (bf16[256,1024]{1,0:T(8,128)(2,1)S(1)}, bf16[256,1024]{1,0:T(8,128)(2,1)S(1)}, u32[]{:S(2)}, u32[]{:S(2)}) collective-permute-start(bf16[256,1024]{1,0:T(8,128)(2,1)S(1)} %collective-permute-done.3.refs_11_.refs_6_), channel_id=1, source_target_pairs={{0,8},{1,57},{8,16},{9,1},{16,24},{17,9},{24,32},{25,17},{32,40},{... | collective-permute-start | bytes 1572872 | tf_op jit(solution)/shard_map/ppermute | solution.py:33
  30.2 10.4 %collective-permute-start.10 = (bf16[256,1024]{1,0:T(8,128)(2,1)S(1)}, bf16[256,1024]{1,0:T(8,128)(2,1)}, u32[]{:S(2)}, u32[]{:S(2)}) collective-permute-start(bf16[256,1024]{1,0:T(8,128)(2,1)S(1)} %collective-permute-done.3.refs_11_.refs_6_), channel_id=1, source_target_pairs={{0,2},{1,7},{2,0},{3,5},{4,6},{5,3},{6,4},{7,1},{8,10},{9,15},{10,... | collective-permute-start | bytes 1572872 | tf_op jit(solution)/shard_map/ppermute | solution.py:45
  32.9 4.5 %collective-permute-start.8 = (bf16[128,1024]{1,0:T(8,128)(2,1)}, bf16[128,1024]{1,0:T(8,128)(2,1)}, u32[]{:S(2)}, u32[]{:S(2)}) collective-permute-start(bf16[128,1024]{1,0:T(8,128)(2,1)} %centroids.1), channel_id=1, source_target_pairs={{0,1},{1,0},{2,3},{3,2},{4,5},{5,4},{6,7},{7,6},{8,9},{9,8},{10,11... | collective-permute-start | bytes 786440 | tf_op jit(solution)/shard_map/ppermute | solution.py:25
  32.9 7.8 %collective-permute-start.6 = (bf16[128,1024]{1,0:T(8,128)(2,1)}, bf16[128,1024]{1,0:T(8,128)(2,1)}, u32[]{:S(2)}, u32[]{:S(2)}) collective-permute-start(bf16[128,1024]{1,0:T(8,128)(2,1)} %collective-permute-done.1.refs_2_), channel_id=1, source_target_pairs={{0,1},{1,0},{2,3},{3,2},{4,5},{5,4},{6,7},{7,6},{8,9},{9,8},{10,11... | collective-permute-start | bytes 786440 | tf_op jit(solution)/shard_map/ppermute | solution.py:25
  33.4 4.5 %collective-permute-start.7 = (bf16[128,1024]{1,0:T(8,128)(2,1)}, bf16[128,1024]{1,0:T(8,128)(2,1)}, u32[]{:S(2)}, u32[]{:S(2)}) collective-permute-start(bf16[128,1024]{1,0:T(8,128)(2,1)} %collective-permute-done.2.refs_4_), channel_id=1, source_target_pairs={{0,1},{1,0},{2,3},{3,2},{4,5},{5,4},{6,7},{7,6},{8,9},{9,8},{10,11... | collective-permute-start | bytes 786440 | tf_op jit(solution)/shard_map/ppermute | solution.py:25
  34.3 6.3 %collective-permute-start.5 = (bf16[128,1024]{1,0:T(8,128)(2,1)}, bf16[128,1024]{1,0:T(8,128)(2,1)}, u32[]{:S(2)}, u32[]{:S(2)}) collective-permute-start(bf16[128,1024]{1,0:T(8,128)(2,1)} %collective-permute-done.4.refs_0_), channel_id=1, source_target_pairs={{0,1},{1,0},{2,3},{3,2},{4,5},{5,4},{6,7},{7,6},{8,9},{9,8},{10,11... | collective-permute-start | bytes 786440 | tf_op jit(solution)/shard_map/ppermute | solution.py:25
  37.4 8.8 %collective-permute-start.13 = (bf16[128,1024]{1,0:T(8,128)(2,1)S(1)}, bf16[128,1024]{1,0:T(8,128)(2,1)S(1)}, u32[]{:S(2)}, u32[]{:S(2)}) collective-permute-start(bf16[128,1024]{1,0:T(8,128)(2,1)S(1)} %constant_dynamic-slice_fusion), channel_id=1, source_target_pairs={{0,8},{1,57},{8,16},{9,1},{16,24},{17,9},{24,32},{25,17},{32,40},{... | collective-permute-start | bytes 786440 | tf_op jit(solution)/shard_map/ppermute | solution.py:33
  37.9 10.0 %collective-permute-start.12 = (bf16[256,1024]{1,0:T(8,128)(2,1)S(1)}, bf16[256,1024]{1,0:T(8,128)(2,1)S(1)}, u32[]{:S(2)}, u32[]{:S(2)}) collective-permute-start(bf16[256,1024]{1,0:T(8,128)(2,1)S(1)} %collective-permute-done.11.refs_8_), channel_id=1, source_target_pairs={{0,2},{1,7},{2,0},{3,5},{4,6},{5,3},{6,4},{7,1},{8,10},{9,15},{10,... | collective-permute-start | bytes 1572872 | tf_op jit(solution)/shard_map/ppermute | solution.py:45
  46.2 6.5 %collective-permute-start.14 = (bf16[128,1024]{1,0:T(8,128)(2,1)S(1)}, bf16[128,1024]{1,0:T(8,128)(2,1)S(1)}, u32[]{:S(2)}, u32[]{:S(2)}) collective-permute-start(bf16[128,1024]{1,0:T(8,128)(2,1)S(1)} %collective-permute-done.13.refs_8_.refs_10_), channel_id=1, source_target_pairs={{0,2},{1,7},{2,0},{3,5},{4,6},{5,3},{6,4},{7,1},{8,10},{9,15},{10,... | collective-permute-start | bytes 786440 | tf_op jit(solution)/shard_map/ppermute | solution.py:45
  55.1 2.6 %collective-permute-start.17 = (f32[16,128]{1,0:T(8,128)S(1)}, f32[16,128]{1,0:T(8,128)S(1)}, u32[]{:S(2)}, u32[]{:S(2)}) collective-permute-start(f32[16,128]{1,0:T(8,128)S(1)} %shard_map.61.own), channel_id=1, source_target_pairs={{0,6},{2,0},{4,2},{6,4},{1,7},{3,1},{5,3},{7,5},{8,14},{10,8},{12,... | collective-permute-start | bytes 24584 | tf_op jit(solution)/shard_map/ppermute | solution.py:37
  56.7 4.0 %collective-permute-start.16 = (f32[16,128]{1,0:T(8,128)S(1)}, f32[16,128]{1,0:T(8,128)S(1)}, u32[]{:S(2)}, u32[]{:S(2)}) collective-permute-start(f32[16,128]{1,0:T(8,128)S(1)} %shard_map.61.own), channel_id=1, source_target_pairs={{0,4},{2,6},{4,0},{6,2},{1,5},{3,7},{5,1},{7,3},{8,12},{10,14},{12... | collective-permute-start | bytes 24584 | tf_op jit(solution)/shard_map/ppermute | solution.py:37
  56.7 4.0 %collective-permute-start.15 = (f32[16,128]{1,0:T(8,128)S(1)}, f32[16,128]{1,0:T(8,128)S(1)}, u32[]{:S(2)}, u32[]{:S(2)}) collective-permute-start(f32[16,128]{1,0:T(8,128)S(1)} %shard_map.61.own), channel_id=1, source_target_pairs={{0,2},{2,4},{4,6},{6,0},{1,3},{3,5},{5,7},{7,1},{8,10},{10,12},{12... | collective-permute-start | bytes 24584 | tf_op jit(solution)/shard_map/ppermute | solution.py:37
  60.8 2.5 %collective-permute-start.18 = (f32[16,128]{1,0:T(8,128)S(1)}, f32[16,128]{1,0:T(8,128)S(1)}, u32[]{:S(2)}, u32[]{:S(2)}) collective-permute-start(f32[16,128]{1,0:T(8,128)S(1)} %shard_map.62.mine), channel_id=1, source_target_pairs={{0,1},{1,0},{2,3},{3,2},{4,5},{5,4},{6,7},{7,6},{8,9},{9,8},{10,11... | collective-permute-start | bytes 24584 | tf_op jit(solution)/shard_map/ppermute | solution.py:25
  63.3 2.9 %collective-permute-start.19 = (f32[4,8,128]{2,1,0:T(8,128)S(1)}, f32[4,8,128]{2,1,0:T(8,128)S(1)}, u32[]{:S(2)}, u32[]{:S(2)}) collective-permute-start(f32[4,8,128]{2,1,0:T(8,128)S(1)} %shard_map.63.block), channel_id=1, source_target_pairs={{0,8},{1,57},{8,16},{9,1},{16,24},{17,9},{24,32},{25,17},{32,40},{... | collective-permute-start | bytes 49160 | tf_op jit(solution)/shard_map/ppermute | solution.py:33
  66.2 3.3 %collective-permute-start.20 = (f32[4,8,128]{2,1,0:T(8,128)S(1)}, f32[4,8,128]{2,1,0:T(8,128)S(1)}, u32[]{:S(2)}, u32[]{:S(2)}) collective-permute-start(f32[4,8,128]{2,1,0:T(8,128)S(1)} %collective-permute-done.19.near), channel_id=1, source_target_pairs={{0,1},{1,0},{2,3},{3,2},{4,5},{5,4},{6,7},{7,6},{8,9},{9,8},{10,11... | collective-permute-start | bytes 49160 | tf_op jit(solution)/shard_map/ppermute | solution.py:25
  69.6 4.5 %collective-permute-start.21 = (f32[4,8,128]{2,1,0:T(8,128)S(1)}, f32[4,8,128]{2,1,0:T(8,128)S(1)}, u32[]{:S(2)}, u32[]{:S(2)}) collective-permute-start(f32[4,8,128]{2,1,0:T(8,128)S(1)} %get-tuple-element.52), channel_id=1, source_target_pairs={{0,24},{1,41},{8,32},{9,49},{16,40},{17,57},{24,48},{25,1},{32,56}... | collective-permute-start | bytes 49160 | tf_op jit(solution)/shard_map/ppermute | solution.py:33
  74.0 3.5 %collective-permute-start.22 = (f32[4,8,128]{2,1,0:T(8,128)S(1)}, f32[4,8,128]{2,1,0:T(8,128)S(1)}, u32[]{:S(2)}, u32[]{:S(2)}) collective-permute-start(f32[4,8,128]{2,1,0:T(8,128)S(1)} %collective-permute-done.21.got), channel_id=1, source_target_pairs={{0,1},{1,0},{2,3},{3,2},{4,5},{5,4},{6,7},{7,6},{8,9},{9,8},{10,11... | collective-permute-start | bytes 49160 | tf_op jit(solution)/shard_map/ppermute | solution.py:25
  82.8 3.0 %collective-permute-start.24 = (bf16[432,1024]{1,0:T(8,128)(2,1)S(1)}, bf16[432,1024]{1,0:T(8,128)(2,1)S(1)}, u32[]{:S(2)}, u32[]{:S(2)}) collective-permute-start(bf16[432,1024]{1,0:T(8,128)(2,1)S(1)} %get-tuple-element.60), channel_id=1, source_target_pairs={{0,1},{1,0},{2,3},{3,2},{4,5},{5,4},{6,7},{7,6},{8,9},{9,8},{10,11... | collective-permute-start | bytes 2654216 | tf_op jit(solution)/shard_map/ppermute | solution.py:25
  85.6 17.3 %copy-start.2 = (f32[128]{0:T(128)S(1)}, f32[128]{0:T(128)}, u32[]{:S(2)}) copy-start(f32[128]{0:T(128)} %param.5) | copy-start | bytes 1540
  85.6 6.1 %collective-permute-start.23 = (bf16[144,1024]{1,0:T(8,128)(2,1)S(1)}, bf16[144,1024]{1,0:T(8,128)(2,1)S(1)}, u32[]{:S(2)}, u32[]{:S(2)}) collective-permute-start(bf16[144,1024]{1,0:T(8,128)(2,1)S(1)} %get-tuple-element.59), channel_id=1, source_target_pairs={{0,1},{1,0},{2,3},{3,2},{4,5},{5,4},{6,7},{7,6},{8,9},{9,8},{10,11... | collective-permute-start | bytes 884744 | tf_op jit(solution)/shard_map/ppermute | solution.py:25
  86.0 9.9 %collective-permute-start.25 = (bf16[144,1024]{1,0:T(8,128)(2,1)S(1)}, bf16[144,1024]{1,0:T(8,128)(2,1)S(1)}, u32[]{:S(2)}, u32[]{:S(2)}) collective-permute-start(bf16[144,1024]{1,0:T(8,128)(2,1)S(1)} %get-tuple-element.63), channel_id=1, source_target_pairs={{0,128},{64,192},{128,0},{192,64},{1,129},{65,193},{129,1},{193,65... | collective-permute-start | bytes 884744 | tf_op jit(solution)/shard_map/ppermute | solution.py:21
  89.0 13.8 %collective-permute-start.26 = (bf16[144,1024]{1,0:T(8,128)(2,1)S(1)}, bf16[144,1024]{1,0:T(8,128)(2,1)S(1)}, u32[]{:S(2)}, u32[]{:S(2)}) collective-permute-start(bf16[144,1024]{1,0:T(8,128)(2,1)S(1)} %get-tuple-element.64), channel_id=1, source_target_pairs={{0,64},{64,128},{128,192},{192,0},{1,65},{65,129},{129,193},{193,1... | collective-permute-start | bytes 884744 | tf_op jit(solution)/shard_map/ppermute | solution.py:21
  89.3 13.5 %collective-permute-start.27 = (bf16[144,1024]{1,0:T(8,128)(2,1)S(1)}, bf16[144,1024]{1,0:T(8,128)(2,1)S(1)}, u32[]{:S(2)}, u32[]{:S(2)}) collective-permute-start(bf16[144,1024]{1,0:T(8,128)(2,1)S(1)} %get-tuple-element.65), channel_id=1, source_target_pairs={{0,192},{64,0},{128,64},{192,128},{1,193},{65,1},{129,65},{193,129... | collective-permute-start | bytes 884744 | tf_op jit(solution)/shard_map/ppermute | solution.py:21

commit v10 on v9

--- a/solution.py
+++ b/solution.py
@@ -10,7 +10,7 @@
 NX, NZ, NY, NC = 4, 8, 4, 2
 BF16, F32 = jnp.bfloat16, jnp.float32
 TAIL = 16
-ORDER = (2, 1, 3, 0)
+ORDER = (1, 3, 2, 0)
 BATCH = 512
 VMEM_LIMIT = 20 * 1024 * 1024
 SMALL_LIMIT = 4 * 1024 * 1024
@@ -164,18 +164,23 @@
     return total, tail[:, :n] + tail[:, n : 2 * n]
 
 
-def score_kernel(parts, sizes, given, *refs):
-    table, refs = refs[:parts], refs[parts:]
-    pieces, refs = refs[: len(sizes)], refs[len(sizes) :]
-    squares, logits, energy = refs
-    n = table[0].shape[0]
-    span = n * NC
-    blocks = [jnp.concatenate([table[p + i][...] for i in range(NC)]) for p in range(0, parts, NC)]
-    if not given:
-        for p, block in enumerate(blocks):
-            wide = block.astype(F32)
+def score_kernel(parts, sizes, *refs):
+    if parts:
+        table, pieces, (block, squares, logits, energy) = refs[:parts], refs[parts:-4], refs[-4:]
+    else:
+        block, squares, *pieces = refs[:-2]
+        logits, energy = refs[-2:]
+    height = block.shape[0]
+    span = height // NX
+    if parts:
+        n = table[0].shape[0]
+        for p in range(parts):
+            lot = slice(p * n, (p + 1) * n)
+            part = table[p][...]
+            block[lot, :] = part
+            wide = part.astype(F32)
             total = jnp.sum(wide * wide, axis=1, keepdims=True)
-            squares[p * span : (p + 1) * span, :] = jnp.broadcast_to(total, (span, squares.shape[1]))
+            squares[lot, :] = jnp.broadcast_to(total, (n, squares.shape[1]))
     batches, at = [[]], 0
     for piece, size in zip(pieces, sizes):
         if sum(k for _, k in batches[-1]) >= BATCH:
@@ -186,31 +191,34 @@
         lot = slice(at, at + rows.shape[0])
         at += rows.shape[0]
         high = None
-        for p, block in enumerate(blocks):
-            product = lax.dot_general(block, rows, (((1,), (1,)), ((), ())), preferred_element_type=F32)
-            scores = 2.0 * product - squares[p * span : (p + 1) * span, :1]
-            logits[p * span : (p + 1) * span, lot] = scores
+        for k in range(0, height, span):
+            product = lax.dot_general(
+                block[k : k + span, :], rows, (((1,), (1,)), ((), ())), preferred_element_type=F32
+            )
+            scores = 2.0 * product - squares[k : k + span, :1]
+            logits[k : k + span, lot] = scores
             top = jnp.max(scores, axis=0, keepdims=True)
             high = top if high is None else jnp.maximum(high, top)
         total = None
-        for p in range(len(blocks)):
-            part = jnp.sum(jnp.exp(logits[p * span : (p + 1) * span, lot] - high), axis=0, keepdims=True)
+        for k in range(0, height, span):
+            part = jnp.sum(jnp.exp(logits[k : k + span, lot] - high), axis=0, keepdims=True)
             total = part if total is None else total + part
         energy[:, lot] = high + jnp.log(total)
 
 
-def score(table, pieces, squares=None):
-    count, width = sum(t.shape[0] for t in table), table[0].shape[1]
-    sizes = tuple(p.shape[0] for p in pieces)
-    rows, given = sum(sizes), squares is not None
+def score(table, pieces):
+    whole = len(table) == 2
+    count = table[0].shape[0] if whole else sum(t.shape[0] for t in table)
+    width, sizes = table[0].shape[1], tuple(p.shape[0] for p in pieces)
+    rows = sum(sizes)
     out = [
         pltpu.VMEM((count, rows), F32) if PIN else jax.ShapeDtypeStruct((count, rows), F32),
         jax.ShapeDtypeStruct((1, rows), F32),
     ]
-    if not given:
-        out.insert(0, jax.ShapeDtypeStruct((count, 128), F32))
-    got = pl.pallas_call(
-        functools.partial(score_kernel, len(table), sizes, given),
+    if not whole:
+        out = [jax.ShapeDtypeStruct((count, width), BF16), jax.ShapeDtypeStruct((count, 128), F32)] + out
+    return pl.pallas_call(
+        functools.partial(score_kernel, 0 if whole else len(table), sizes),
         out_shape=out,
         compiler_params=pltpu.CompilerParams(vmem_limit_bytes=VMEM_LIMIT),
         cost_estimate=pl.CostEstimate(
@@ -218,8 +226,7 @@
             bytes_accessed=4 * count * rows + 2 * (count + rows) * width,
             transcendentals=count * rows,
         ),
-    )(*table, *pieces, *([squares] if given else []))
-    return (squares, *got) if given else got
+    )(*table, *pieces)
 
 
 def weigh_kernel(first, groups, sizes, energy, *refs):
@@ -342,17 +349,17 @@
 
     four = along_z(lax.dynamic_slice_in_dim(three, c * sub, sub, 0), 1)
     lots = [[fixed(v) for v in (own, one, first, two, swap_halves(two))]]
-    squares, scores, energy = score(table, lots[0])
-    squares, logits, local = fixed(squares), [scores], [energy]
+    *table, scores, energy = score(table, lots[0])
+    table, logits, local = [fixed(v) for v in table], [scores], [energy]
     last, _ = lax.optimization_barrier((four, energy))
     last = swap_halves(last)
     lots.append([fixed(v) for v in (three, swap_halves(three))])
-    _, scores, energy = score(table, lots[1], squares)
+    scores, energy = score(table, lots[1])
     last, _ = lax.optimization_barrier((last, energy))
     logits.append(scores)
     local.append(energy)
     lots.append([fixed(four), fixed(last)])
-    _, scores, energy = score(table, lots[2], squares)
+    scores, energy = score(table, lots[2])
     logits.append(scores)
     local.append(energy)
     energy, row_energy = energies(local, place, sub)

time: 104 us -> 103 us (level)
  waiting for transfers between devices: 32.4 us -> 35.4 us
  Pallas kernels: 19.8 us -> 17.1 us
  starting transfers between devices: 49.6 us -> 48.2 us
    pallas_call x3, Pallas kernels: 10.9 us -> 8.2 us  [score(): pl.pallas_call(functools.partial(score_kernel, 0 if whole else len(table)...]
    ppermute x6, waiting for transfers between devices: 18.2 us -> 19.9 us  [shift_x(): return lax.ppermute(value, 'x', [(i, (i + by) % NX) for i in range(NX)])]
    ppermute x4, waiting for transfers between devices: 4.22 us -> 5.65 us  [swap_halves(): return lax.ppermute(value, ('y', 'c'), pairs)]
    ppermute x6, starting transfers between devices: 10.7 us -> 9.33 us  [shift_x(): return lax.ppermute(value, 'x', [(i, (i + by) % NX) for i in range(NX)])]
  transfers between devices with their start and end apart: 28 -> 28, of which waited for: 15 -> 15; matrix products, arithmetic and copies ran while one was open for 0% -> 0% of each run, Pallas kernels for 11% -> 9%
where the time goes in v10:
time: 103 us
  starting transfers between devices  48.2 us (47%)
  waiting for transfers between devices  35.4 us (34%)
  Pallas kernels  17.1 us (17%)
  local copies, waits for them, and re-layouts  1.29 us (1%)
    ppermute x6, waiting for transfers between devices, shift_x(): return lax.ppermute(value, 'x', [(i, (i + by) % NX) for i in range(NX)])  19.9 us
    ppermute x6, starting transfers between devices, along_z(): return lax.ppermute(value, ('z', 'c'), pairs)  16 us
    ppermute x9, starting transfers between devices, swap_cores(): return lax.ppermute(value, 'c', [(0, 1), (1, 0)])  10.8 us
    ppermute x4, starting transfers between devices, swap_halves(): return lax.ppermute(value, ('y', 'c'), pairs)  9.79 us
    ppermute x6, starting transfers between devices, shift_x(): return lax.ppermute(value, 'x', [(i, (i + by) % NX) for i in range(NX)])  9.33 us
    pallas_call x3, Pallas kernels, score(): pl.pallas_call(functools.partial(score_kernel, 0 if whole else len(table)...  8.2 us
    pallas_call x2, Pallas kernels, weigh(): pl.pallas_call(functools.partial(weigh_kernel, first, groups, sizes), out...  6.92 us
    ppermute x4, waiting for transfers between devices, swap_halves(): return lax.ppermute(value, ('y', 'c'), pairs)  5.65 us
  transfers between devices with their start and end apart: 28, of which 15 were waited for; matrix products, arithmetic and copies ran while one was open for 0% of the time, Pallas kernels for 9%

profile of v10, /device:TPU:1, one launch (start us, length us, event | category | flops | bytes accessed | tf_op | source)
XLA Modules:
  0.0 102.8 jit_solution(7548772669399914050)
XLA Ops:
  1.9 6.5 %collective-permute-start = (bf16[256,1024]{1,0:T(8,128)(2,1)S(1)}, bf16[256,1024]{1,0:T(8,128)(2,1)S(1)}, u32[]{:S(2)}, u32[]{:S(2)}) collective-permute-start(bf16[256,1024]{1,0:T(8,128)(2,1)S(1)} %constant_dynamic-slice_fusion.2), channel_id=1, source_target_pairs={{0,8},{1,57},{8,16},{9,1},{16,24},{17,9},{24,32},{25,17},{32,40},{... | collective-permute-start | bytes 1572872 | tf_op jit(solution)/shard_map/ppermute | solution.py:33
  8.4 1.2 %collective-permute-start.2 = (bf16[128,1024]{1,0:T(8,128)(2,1)}, bf16[128,1024]{1,0:T(8,128)(2,1)}, u32[]{:S(2)}, u32[]{:S(2)}) collective-permute-start(bf16[128,1024]{1,0:T(8,128)(2,1)} %centroids.1), channel_id=1, source_target_pairs={{0,64},{64,128},{128,192},{192,0},{1,65},{65,129},{129,193},{193,1... | collective-permute-start | bytes 786440 | tf_op jit(solution)/shard_map/ppermute | solution.py:21
  9.6 1.5 %collective-permute-start.1 = (bf16[128,1024]{1,0:T(8,128)(2,1)}, bf16[128,1024]{1,0:T(8,128)(2,1)}, u32[]{:S(2)}, u32[]{:S(2)}) collective-permute-start(bf16[128,1024]{1,0:T(8,128)(2,1)} %centroids.1), channel_id=1, source_target_pairs={{0,192},{64,0},{128,64},{192,128},{1,193},{65,1},{129,65},{193,129... | collective-permute-start | bytes 786440 | tf_op jit(solution)/shard_map/ppermute | solution.py:21
  11.1 4.5 %collective-permute-done.2.refs_2_ = bf16[128,1024]{1,0:T(8,128)(2,1)} collective-permute-done((bf16[128,1024]{1,0:T(8,128)(2,1)}, bf16[128,1024]{1,0:T(8,128)(2,1)}, u32[]{:S(2)}, u32[]{:S(2)}) %collective-permute-start.2) | collective-permute-done | bytes 262176 | tf_op jit(solution)/shard_map/ppermute | solution.py:21
  15.9 2.7 %collective-permute-start.5 = (bf16[256,1024]{1,0:T(8,128)(2,1)S(1)}, bf16[256,1024]{1,0:T(8,128)(2,1)S(1)}, u32[]{:S(2)}, u32[]{:S(2)}) collective-permute-start(bf16[256,1024]{1,0:T(8,128)(2,1)S(1)} %collective-permute-done.refs_9_.refs_4_), channel_id=1, source_target_pairs={{0,8},{1,57},{8,16},{9,1},{16,24},{17,9},{24,32},{25,17},{32,40},{... | collective-permute-start | bytes 1572872 | tf_op jit(solution)/shard_map/ppermute | solution.py:33
  18.5 2.4 %collective-permute-start.6 = (bf16[128,1024]{1,0:T(8,128)(2,1)}, bf16[128,1024]{1,0:T(8,128)(2,1)}, u32[]{:S(2)}, u32[]{:S(2)}) collective-permute-start(bf16[128,1024]{1,0:T(8,128)(2,1)} %collective-permute-done.1.refs_0_), channel_id=1, source_target_pairs={{0,192},{64,0},{128,64},{192,128},{1,193},{65,1},{129,65},{193,129... | collective-permute-start | bytes 786440 | tf_op jit(solution)/shard_map/ppermute | solution.py:21
  20.9 2.7 %collective-permute-start.9 = (bf16[256,1024]{1,0:T(8,128)(2,1)S(1)}, bf16[256,1024]{1,0:T(8,128)(2,1)S(1)}, u32[]{:S(2)}, u32[]{:S(2)}) collective-permute-start(bf16[256,1024]{1,0:T(8,128)(2,1)S(1)} %collective-permute-done.refs_9_.refs_4_), channel_id=1, source_target_pairs={{0,2},{1,7},{2,0},{3,5},{4,6},{5,3},{6,4},{7,1},{8,10},{9,15},{10,... | collective-permute-start | bytes 1572872 | tf_op jit(solution)/shard_map/ppermute | solution.py:45
  23.6 2.2 %collective-permute-done.6.refs_4_ = bf16[128,1024]{1,0:T(8,128)(2,1)} collective-permute-done((bf16[128,1024]{1,0:T(8,128)(2,1)}, bf16[128,1024]{1,0:T(8,128)(2,1)}, u32[]{:S(2)}, u32[]{:S(2)}) %collective-permute-start.6) | collective-permute-done | bytes 262176 | tf_op jit(solution)/shard_map/ppermute | solution.py:21
  25.9 1.9 %collective-permute-start.11 = (bf16[256,1024]{1,0:T(8,128)(2,1)S(1)}, bf16[256,1024]{1,0:T(8,128)(2,1)S(1)}, u32[]{:S(2)}, u32[]{:S(2)}) collective-permute-start(bf16[256,1024]{1,0:T(8,128)(2,1)S(1)} %collective-permute-done.5.refs_11_.refs_6_), channel_id=1, source_target_pairs={{0,8},{1,57},{8,16},{9,1},{16,24},{17,9},{24,32},{25,17},{32,40},{... | collective-permute-start | bytes 1572872 | tf_op jit(solution)/shard_map/ppermute | solution.py:33
  27.8 2.4 %collective-permute-done.9.refs_10_.refs_5_ = bf16[256,1024]{1,0:T(8,128)(2,1)S(1)} collective-permute-done((bf16[256,1024]{1,0:T(8,128)(2,1)S(1)}, bf16[256,1024]{1,0:T(8,128)(2,1)S(1)}, u32[]{:S(2)}, u32[]{:S(2)}) %collective-permute-start.9) | collective-permute-done | bytes 524320 | tf_op jit(solution)/shard_map/ppermute | solution.py:45
  30.2 2.7 %collective-permute-start.10 = (bf16[256,1024]{1,0:T(8,128)(2,1)S(1)}, bf16[256,1024]{1,0:T(8,128)(2,1)}, u32[]{:S(2)}, u32[]{:S(2)}) collective-permute-start(bf16[256,1024]{1,0:T(8,128)(2,1)S(1)} %collective-permute-done.5.refs_11_.refs_6_), channel_id=1, source_target_pairs={{0,2},{1,7},{2,0},{3,5},{4,6},{5,3},{6,4},{7,1},{8,10},{9,15},{10,... | collective-permute-start | bytes 1572872 | tf_op jit(solution)/shard_map/ppermute | solution.py:45
  34.3 3.0 %collective-permute-start.7 = (bf16[128,1024]{1,0:T(8,128)(2,1)}, bf16[128,1024]{1,0:T(8,128)(2,1)}, u32[]{:S(2)}, u32[]{:S(2)}) collective-permute-start(bf16[128,1024]{1,0:T(8,128)(2,1)} %collective-permute-done.6.refs_4_), channel_id=1, source_target_pairs={{0,1},{1,0},{2,3},{3,2},{4,5},{5,4},{6,7},{7,6},{8,9},{9,8},{10,11... | collective-permute-start | bytes 786440 | tf_op jit(solution)/shard_map/ppermute | solution.py:25
  37.9 2.7 %collective-permute-start.12 = (bf16[256,1024]{1,0:T(8,128)(2,1)S(1)}, bf16[256,1024]{1,0:T(8,128)(2,1)S(1)}, u32[]{:S(2)}, u32[]{:S(2)}) collective-permute-start(bf16[256,1024]{1,0:T(8,128)(2,1)S(1)} %collective-permute-done.11.refs_2_.refs_8_), channel_id=1, source_target_pairs={{0,2},{1,7},{2,0},{3,5},{4,6},{5,3},{6,4},{7,1},{8,10},{9,15},{10,... | collective-permute-start | bytes 1572872 | tf_op jit(solution)/shard_map/ppermute | solution.py:45
  40.7 5.7 %shard_map.58 = (bf16[1024,1024]{1,0:T(8,128)(2,1)S(1)}, f32[1024,128]{1,0:T(8,128)S(1)}, f32[1024,1280]{1,0:T(8,128)S(1)}, f32[1,1280]{1,0:T(1,128)S(1)}) custom-call(bf16[128,1024]{1,0:T(8,128)(2,1)} %collective-permute-done.1.refs_0_, bf16[128,1024]{1,0:T(8,128)(2,1)} %collective-permute-done.3.refs_1_, bf16[128,1024]{1,0:T(8,128)(2,1)} %collective-permute-done.2.refs_2_, ...), custom_call_target="tpu_custom_call" | custom-call | flops 5368709120 | bytes 9961472 | tf_op jit(solution)/shard_map/pallas_call | solution.py:220
  46.3 1.7 %collective-permute-start.14 = (bf16[128,1024]{1,0:T(8,128)(2,1)S(1)}, bf16[128,1024]{1,0:T(8,128)(2,1)S(1)}, u32[]{:S(2)}, u32[]{:S(2)}) collective-permute-start(bf16[128,1024]{1,0:T(8,128)(2,1)S(1)} %collective-permute-done.13.refs_2_.refs_10_), channel_id=1, source_target_pairs={{0,2},{1,7},{2,0},{3,5},{4,6},{5,3},{6,4},{7,1},{8,10},{9,15},{10,... | collective-permute-start | bytes 786440 | tf_op jit(solution)/shard_map/ppermute | solution.py:45
  48.0 1.6 %shard_map.59 = (f32[1024,512]{1,0:T(8,128)S(1)}, f32[1,512]{1,0:T(1,128)S(1)}) custom-call(bf16[1024,1024]{1,0:T(8,128)(2,1)S(1)} %get-tuple-element.47.refs_0_, f32[1024,128]{1,0:T(8,128)S(1)} %get-tuple-element.48.refs_1_, bf16[256,1024]{1,0:T(8,128)(2,1)S(1)} %collective-permute-done.11.refs_2_.refs_8_, ...), custom_call_target="tpu_custom_call" | custom-call | flops 2147483648 | bytes 5242880 | tf_op jit(solution)/shard_map/pallas_call | solution.py:220
  49.6 3.2 %collective-permute-done.14.refs_3_.refs_11_ = bf16[128,1024]{1,0:T(8,128)(2,1)S(1)} collective-permute-done((bf16[128,1024]{1,0:T(8,128)(2,1)S(1)}, bf16[128,1024]{1,0:T(8,128)(2,1)S(1)}, u32[]{:S(2)}, u32[]{:S(2)}) %collective-permute-start.14) | collective-permute-done | bytes 262176 | tf_op jit(solution)/shard_map/ppermute | solution.py:45
  53.8 1.6 %collective-permute-start.17 = (f32[16,128]{1,0:T(8,128)S(1)}, f32[16,128]{1,0:T(8,128)S(1)}, u32[]{:S(2)}, u32[]{:S(2)}) collective-permute-start(f32[16,128]{1,0:T(8,128)S(1)} %shard_map.61.own), channel_id=1, source_target_pairs={{0,6},{2,0},{4,2},{6,4},{1,7},{3,1},{5,3},{7,5},{8,14},{10,8},{12,... | collective-permute-start | bytes 24584 | tf_op jit(solution)/shard_map/ppermute | solution.py:37
  56.4 3.1 %collective-permute-done.16.refs_1_ = f32[16,128]{1,0:T(8,128)S(1)} collective-permute-done((f32[16,128]{1,0:T(8,128)S(1)}, f32[16,128]{1,0:T(8,128)S(1)}, u32[]{:S(2)}, u32[]{:S(2)}) %collective-permute-start.16) | collective-permute-done | bytes 8224 | tf_op jit(solution)/shard_map/ppermute | solution.py:37
  59.5 1.6 %collective-permute-start.18 = (f32[16,128]{1,0:T(8,128)S(1)}, f32[16,128]{1,0:T(8,128)S(1)}, u32[]{:S(2)}, u32[]{:S(2)}) collective-permute-start(f32[16,128]{1,0:T(8,128)S(1)} %shard_map.62.mine), channel_id=1, source_target_pairs={{0,1},{1,0},{2,3},{3,2},{4,5},{5,4},{6,7},{7,6},{8,9},{9,8},{10,11... | collective-permute-start | bytes 24584 | tf_op jit(solution)/shard_map/ppermute | solution.py:25
  61.9 2.2 %collective-permute-start.19 = (f32[4,8,128]{2,1,0:T(8,128)S(1)}, f32[4,8,128]{2,1,0:T(8,128)S(1)}, u32[]{:S(2)}, u32[]{:S(2)}) collective-permute-start(f32[4,8,128]{2,1,0:T(8,128)S(1)} %shard_map.63.block), channel_id=1, source_target_pairs={{0,8},{1,57},{8,16},{9,1},{16,24},{17,9},{24,32},{25,17},{32,40},{... | collective-permute-start | bytes 49160 | tf_op jit(solution)/shard_map/ppermute | solution.py:33
  64.9 2.3 %collective-permute-start.20 = (f32[4,8,128]{2,1,0:T(8,128)S(1)}, f32[4,8,128]{2,1,0:T(8,128)S(1)}, u32[]{:S(2)}, u32[]{:S(2)}) collective-permute-start(f32[4,8,128]{2,1,0:T(8,128)S(1)} %collective-permute-done.19.near), channel_id=1, source_target_pairs={{0,1},{1,0},{2,3},{3,2},{4,5},{5,4},{6,7},{7,6},{8,9},{9,8},{10,11... | collective-permute-start | bytes 49160 | tf_op jit(solution)/shard_map/ppermute | solution.py:25
  68.1 2.3 %collective-permute-start.21 = (f32[4,8,128]{2,1,0:T(8,128)S(1)}, f32[4,8,128]{2,1,0:T(8,128)S(1)}, u32[]{:S(2)}, u32[]{:S(2)}) collective-permute-start(f32[4,8,128]{2,1,0:T(8,128)S(1)} %get-tuple-element.54), channel_id=1, source_target_pairs={{0,24},{1,41},{8,32},{9,49},{16,40},{17,57},{24,48},{25,1},{32,56}... | collective-permute-start | bytes 49160 | tf_op jit(solution)/shard_map/ppermute | solution.py:33
  70.4 2.2 %collective-permute-done.21.got = f32[4,8,128]{2,1,0:T(8,128)S(1)} collective-permute-done((f32[4,8,128]{2,1,0:T(8,128)S(1)}, f32[4,8,128]{2,1,0:T(8,128)S(1)}, u32[]{:S(2)}, u32[]{:S(2)}) %collective-permute-start.21) | collective-permute-done | bytes 16416 | tf_op jit(solution)/shard_map/ppermute | solution.py:33
  72.6 2.7 %collective-permute-start.22 = (f32[4,8,128]{2,1,0:T(8,128)S(1)}, f32[4,8,128]{2,1,0:T(8,128)S(1)}, u32[]{:S(2)}, u32[]{:S(2)}) collective-permute-start(f32[4,8,128]{2,1,0:T(8,128)S(1)} %collective-permute-done.21.got), channel_id=1, source_target_pairs={{0,1},{1,0},{2,3},{3,2},{4,5},{5,4},{6,7},{7,6},{8,9},{9,8},{10,11... | collective-permute-start | bytes 49160 | tf_op jit(solution)/shard_map/ppermute | solution.py:25
  76.8 4.6 %shard_map.67 = (bf16[432,1024]{1,0:T(8,128)(2,1)S(1)}, f32[384,1024]{1,0:T(8,128)S(1)}, f32[48,128]{1,0:T(8,128)S(1)}) custom-call(f32[1,2048]{1,0:T(1,128)S(1)} %get-tuple-element.55.energy, f32[1024,1280]{1,0:T(8,128)S(1)} %get-tuple-element.56.refs_0_, f32[1024,512]{1,0:T(8,128)S(1)} %get-tuple-element.57.refs_1_, ...), custom_call_target="tpu_custom_call" | custom-call | flops 3221225472 | bytes 10485760 | tf_op jit(solution)/shard_map/pallas_call | solution.py:269
  81.8 2.3 %shard_map.66 = (bf16[144,1024]{1,0:T(8,128)(2,1)S(1)}, f32[128,1024]{1,0:T(8,128)S(1)}, f32[16,128]{1,0:T(8,128)S(1)}) custom-call(f32[1,2048]{1,0:T(1,128)S(1)} %get-tuple-element.55.energy, f32[1024,1280]{1,0:T(8,128)S(1)} %get-tuple-element.56.refs_0_, f32[1024,512]{1,0:T(8,128)S(1)} %get-tuple-element.57.refs_1_, ...), custom_call_target="tpu_custom_call" | custom-call | flops 1073741824 | bytes 6291456 | tf_op jit(solution)/shard_map/pallas_call | solution.py:269
  84.5 1.3 %collective-permute-start.25 = (bf16[144,1024]{1,0:T(8,128)(2,1)S(1)}, bf16[144,1024]{1,0:T(8,128)(2,1)S(1)}, u32[]{:S(2)}, u32[]{:S(2)}) collective-permute-start(bf16[144,1024]{1,0:T(8,128)(2,1)S(1)} %get-tuple-element.65), channel_id=1, source_target_pairs={{0,64},{64,128},{128,192},{192,0},{1,65},{65,129},{129,193},{193,1... | collective-permute-start | bytes 884744 | tf_op jit(solution)/shard_map/ppermute | solution.py:21
  85.8 1.6 %collective-permute-start.26 = (bf16[144,1024]{1,0:T(8,128)(2,1)S(1)}, bf16[144,1024]{1,0:T(8,128)(2,1)S(1)}, u32[]{:S(2)}, u32[]{:S(2)}) collective-permute-start(bf16[144,1024]{1,0:T(8,128)(2,1)S(1)} %get-tuple-element.66), channel_id=1, source_target_pairs={{0,192},{64,0},{128,64},{192,128},{1,193},{65,1},{129,65},{193,129... | collective-permute-start | bytes 884744 | tf_op jit(solution)/shard_map/ppermute | solution.py:21
  87.5 1.4 %collective-permute-start.27 = (bf16[144,1024]{1,0:T(8,128)(2,1)S(1)}, bf16[144,1024]{1,0:T(8,128)(2,1)S(1)}, u32[]{:S(2)}, u32[]{:S(2)}) collective-permute-start(bf16[144,1024]{1,0:T(8,128)(2,1)S(1)} %get-tuple-element.67), channel_id=1, source_target_pairs={{0,128},{64,192},{128,0},{192,64},{1,129},{65,193},{129,1},{193,65... | collective-permute-start | bytes 884744 | tf_op jit(solution)/shard_map/ppermute | solution.py:21
  88.8 5.4 %collective-permute-done.25.one = bf16[144,1024]{1,0:T(8,128)(2,1)S(1)} collective-permute-done((bf16[144,1024]{1,0:T(8,128)(2,1)S(1)}, bf16[144,1024]{1,0:T(8,128)(2,1)S(1)}, u32[]{:S(2)}, u32[]{:S(2)}) %collective-permute-start.25) | collective-permute-done | bytes 294944 | tf_op jit(solution)/shard_map/ppermute | solution.py:21
  94.3 7.4 %collective-permute-done.27.three = bf16[144,1024]{1,0:T(8,128)(2,1)S(1)} collective-permute-done((bf16[144,1024]{1,0:T(8,128)(2,1)S(1)}, bf16[144,1024]{1,0:T(8,128)(2,1)S(1)}, u32[]{:S(2)}, u32[]{:S(2)}) %collective-permute-start.27) | collective-permute-done | bytes 294944 | tf_op jit(solution)/shard_map/ppermute | solution.py:21
  (48 shorter events, 11.4 us)
Async XLA Ops:
  0.6 1.2 %copy-start = (bf16[512,1024]{1,0:T(8,128)(2,1)S(1)}, bf16[512,1024]{1,0:T(8,128)(2,1)}, u32[]{:S(2)}) copy-start(bf16[512,1024]{1,0:T(8,128)(2,1)} %param.3) | copy-start | bytes 3145732
  0.6 40.0 %copy-start.1 = (bf16[128,1024]{1,0:T(8,128)(2,1)S(1)}, bf16[128,1024]{1,0:T(8,128)(2,1)}, u32[]{:S(2)}) copy-start(bf16[128,1024]{1,0:T(8,128)(2,1)} %centroids.1) | copy-start | bytes 786436
  1.9 14.0 %collective-permute-start = (bf16[256,1024]{1,0:T(8,128)(2,1)S(1)}, bf16[256,1024]{1,0:T(8,128)(2,1)S(1)}, u32[]{:S(2)}, u32[]{:S(2)}) collective-permute-start(bf16[256,1024]{1,0:T(8,128)(2,1)S(1)} %constant_dynamic-slice_fusion.2), channel_id=1, source_target_pairs={{0,8},{1,57},{8,16},{9,1},{16,24},{17,9},{24,32},{25,17},{32,40},{... | collective-permute-start | bytes 1572872 | tf_op jit(solution)/shard_map/ppermute | solution.py:33
  8.4 7.2 %collective-permute-start.2 = (bf16[128,1024]{1,0:T(8,128)(2,1)}, bf16[128,1024]{1,0:T(8,128)(2,1)}, u32[]{:S(2)}, u32[]{:S(2)}) collective-permute-start(bf16[128,1024]{1,0:T(8,128)(2,1)} %centroids.1), channel_id=1, source_target_pairs={{0,64},{64,128},{128,192},{192,0},{1,65},{65,129},{129,193},{193,1... | collective-permute-start | bytes 786440 | tf_op jit(solution)/shard_map/ppermute | solution.py:21
  9.6 6.3 %collective-permute-start.1 = (bf16[128,1024]{1,0:T(8,128)(2,1)}, bf16[128,1024]{1,0:T(8,128)(2,1)}, u32[]{:S(2)}, u32[]{:S(2)}) collective-permute-start(bf16[128,1024]{1,0:T(8,128)(2,1)} %centroids.1), channel_id=1, source_target_pairs={{0,192},{64,0},{128,64},{192,128},{1,193},{65,1},{129,65},{193,129... | collective-permute-start | bytes 786440 | tf_op jit(solution)/shard_map/ppermute | solution.py:21
  15.9 10.0 %collective-permute-start.5 = (bf16[256,1024]{1,0:T(8,128)(2,1)S(1)}, bf16[256,1024]{1,0:T(8,128)(2,1)S(1)}, u32[]{:S(2)}, u32[]{:S(2)}) collective-permute-start(bf16[256,1024]{1,0:T(8,128)(2,1)S(1)} %collective-permute-done.refs_9_.refs_4_), channel_id=1, source_target_pairs={{0,8},{1,57},{8,16},{9,1},{16,24},{17,9},{24,32},{25,17},{32,40},{... | collective-permute-start | bytes 1572872 | tf_op jit(solution)/shard_map/ppermute | solution.py:33
  18.5 7.3 %collective-permute-start.6 = (bf16[128,1024]{1,0:T(8,128)(2,1)}, bf16[128,1024]{1,0:T(8,128)(2,1)}, u32[]{:S(2)}, u32[]{:S(2)}) collective-permute-start(bf16[128,1024]{1,0:T(8,128)(2,1)} %collective-permute-done.1.refs_0_), channel_id=1, source_target_pairs={{0,192},{64,0},{128,64},{192,128},{1,193},{65,1},{129,65},{193,129... | collective-permute-start | bytes 786440 | tf_op jit(solution)/shard_map/ppermute | solution.py:21
  20.9 9.3 %collective-permute-start.9 = (bf16[256,1024]{1,0:T(8,128)(2,1)S(1)}, bf16[256,1024]{1,0:T(8,128)(2,1)S(1)}, u32[]{:S(2)}, u32[]{:S(2)}) collective-permute-start(bf16[256,1024]{1,0:T(8,128)(2,1)S(1)} %collective-permute-done.refs_9_.refs_4_), channel_id=1, source_target_pairs={{0,2},{1,7},{2,0},{3,5},{4,6},{5,3},{6,4},{7,1},{8,10},{9,15},{10,... | collective-permute-start | bytes 1572872 | tf_op jit(solution)/shard_map/ppermute | solution.py:45
  25.9 8.4 %collective-permute-start.11 = (bf16[256,1024]{1,0:T(8,128)(2,1)S(1)}, bf16[256,1024]{1,0:T(8,128)(2,1)S(1)}, u32[]{:S(2)}, u32[]{:S(2)}) collective-permute-start(bf16[256,1024]{1,0:T(8,128)(2,1)S(1)} %collective-permute-done.5.refs_11_.refs_6_), channel_id=1, source_target_pairs={{0,8},{1,57},{8,16},{9,1},{16,24},{17,9},{24,32},{25,17},{32,40},{... | collective-permute-start | bytes 1572872 | tf_op jit(solution)/shard_map/ppermute | solution.py:33
  30.2 10.4 %collective-permute-start.10 = (bf16[256,1024]{1,0:T(8,128)(2,1)S(1)}, bf16[256,1024]{1,0:T(8,128)(2,1)}, u32[]{:S(2)}, u32[]{:S(2)}) collective-permute-start(bf16[256,1024]{1,0:T(8,128)(2,1)S(1)} %collective-permute-done.5.refs_11_.refs_6_), channel_id=1, source_target_pairs={{0,2},{1,7},{2,0},{3,5},{4,6},{5,3},{6,4},{7,1},{8,10},{9,15},{10,... | collective-permute-start | bytes 1572872 | tf_op jit(solution)/shard_map/ppermute | solution.py:45
  32.9 4.5 %collective-permute-start.8 = (bf16[128,1024]{1,0:T(8,128)(2,1)}, bf16[128,1024]{1,0:T(8,128)(2,1)}, u32[]{:S(2)}, u32[]{:S(2)}) collective-permute-start(bf16[128,1024]{1,0:T(8,128)(2,1)} %centroids.1), channel_id=1, source_target_pairs={{0,1},{1,0},{2,3},{3,2},{4,5},{5,4},{6,7},{7,6},{8,9},{9,8},{10,11... | collective-permute-start | bytes 786440 | tf_op jit(solution)/shard_map/ppermute | solution.py:25
  32.9 7.8 %collective-permute-start.3 = (bf16[128,1024]{1,0:T(8,128)(2,1)}, bf16[128,1024]{1,0:T(8,128)(2,1)}, u32[]{:S(2)}, u32[]{:S(2)}) collective-permute-start(bf16[128,1024]{1,0:T(8,128)(2,1)} %collective-permute-done.1.refs_0_), channel_id=1, source_target_pairs={{0,1},{1,0},{2,3},{3,2},{4,5},{5,4},{6,7},{7,6},{8,9},{9,8},{10,11... | collective-permute-start | bytes 786440 | tf_op jit(solution)/shard_map/ppermute | solution.py:25
  33.4 4.5 %collective-permute-start.4 = (bf16[128,1024]{1,0:T(8,128)(2,1)}, bf16[128,1024]{1,0:T(8,128)(2,1)}, u32[]{:S(2)}, u32[]{:S(2)}) collective-permute-start(bf16[128,1024]{1,0:T(8,128)(2,1)} %collective-permute-done.2.refs_2_), channel_id=1, source_target_pairs={{0,1},{1,0},{2,3},{3,2},{4,5},{5,4},{6,7},{7,6},{8,9},{9,8},{10,11... | collective-permute-start | bytes 786440 | tf_op jit(solution)/shard_map/ppermute | solution.py:25
  34.3 6.3 %collective-permute-start.7 = (bf16[128,1024]{1,0:T(8,128)(2,1)}, bf16[128,1024]{1,0:T(8,128)(2,1)}, u32[]{:S(2)}, u32[]{:S(2)}) collective-permute-start(bf16[128,1024]{1,0:T(8,128)(2,1)} %collective-permute-done.6.refs_4_), channel_id=1, source_target_pairs={{0,1},{1,0},{2,3},{3,2},{4,5},{5,4},{6,7},{7,6},{8,9},{9,8},{10,11... | collective-permute-start | bytes 786440 | tf_op jit(solution)/shard_map/ppermute | solution.py:25
  37.4 9.0 %collective-permute-start.13 = (bf16[128,1024]{1,0:T(8,128)(2,1)S(1)}, bf16[128,1024]{1,0:T(8,128)(2,1)S(1)}, u32[]{:S(2)}, u32[]{:S(2)}) collective-permute-start(bf16[128,1024]{1,0:T(8,128)(2,1)S(1)} %constant_dynamic-slice_fusion), channel_id=1, source_target_pairs={{0,8},{1,57},{8,16},{9,1},{16,24},{17,9},{24,32},{25,17},{32,40},{... | collective-permute-start | bytes 786440 | tf_op jit(solution)/shard_map/ppermute | solution.py:33
  37.9 10.1 %collective-permute-start.12 = (bf16[256,1024]{1,0:T(8,128)(2,1)S(1)}, bf16[256,1024]{1,0:T(8,128)(2,1)S(1)}, u32[]{:S(2)}, u32[]{:S(2)}) collective-permute-start(bf16[256,1024]{1,0:T(8,128)(2,1)S(1)} %collective-permute-done.11.refs_2_.refs_8_), channel_id=1, source_target_pairs={{0,2},{1,7},{2,0},{3,5},{4,6},{5,3},{6,4},{7,1},{8,10},{9,15},{10,... | collective-permute-start | bytes 1572872 | tf_op jit(solution)/shard_map/ppermute | solution.py:45
  46.3 6.5 %collective-permute-start.14 = (bf16[128,1024]{1,0:T(8,128)(2,1)S(1)}, bf16[128,1024]{1,0:T(8,128)(2,1)S(1)}, u32[]{:S(2)}, u32[]{:S(2)}) collective-permute-start(bf16[128,1024]{1,0:T(8,128)(2,1)S(1)} %collective-permute-done.13.refs_2_.refs_10_), channel_id=1, source_target_pairs={{0,2},{1,7},{2,0},{3,5},{4,6},{5,3},{6,4},{7,1},{8,10},{9,15},{10,... | collective-permute-start | bytes 786440 | tf_op jit(solution)/shard_map/ppermute | solution.py:45
  53.8 2.6 %collective-permute-start.17 = (f32[16,128]{1,0:T(8,128)S(1)}, f32[16,128]{1,0:T(8,128)S(1)}, u32[]{:S(2)}, u32[]{:S(2)}) collective-permute-start(f32[16,128]{1,0:T(8,128)S(1)} %shard_map.61.own), channel_id=1, source_target_pairs={{0,6},{2,0},{4,2},{6,4},{1,7},{3,1},{5,3},{7,5},{8,14},{10,8},{12,... | collective-permute-start | bytes 24584 | tf_op jit(solution)/shard_map/ppermute | solution.py:37
  55.4 4.0 %collective-permute-start.16 = (f32[16,128]{1,0:T(8,128)S(1)}, f32[16,128]{1,0:T(8,128)S(1)}, u32[]{:S(2)}, u32[]{:S(2)}) collective-permute-start(f32[16,128]{1,0:T(8,128)S(1)} %shard_map.61.own), channel_id=1, source_target_pairs={{0,4},{2,6},{4,0},{6,2},{1,5},{3,7},{5,1},{7,3},{8,12},{10,14},{12... | collective-permute-start | bytes 24584 | tf_op jit(solution)/shard_map/ppermute | solution.py:37
  55.4 4.0 %collective-permute-start.15 = (f32[16,128]{1,0:T(8,128)S(1)}, f32[16,128]{1,0:T(8,128)S(1)}, u32[]{:S(2)}, u32[]{:S(2)}) collective-permute-start(f32[16,128]{1,0:T(8,128)S(1)} %shard_map.61.own), channel_id=1, source_target_pairs={{0,2},{2,4},{4,6},{6,0},{1,3},{3,5},{5,7},{7,1},{8,10},{10,12},{12... | collective-permute-start | bytes 24584 | tf_op jit(solution)/shard_map/ppermute | solution.py:37
  59.5 2.4 %collective-permute-start.18 = (f32[16,128]{1,0:T(8,128)S(1)}, f32[16,128]{1,0:T(8,128)S(1)}, u32[]{:S(2)}, u32[]{:S(2)}) collective-permute-start(f32[16,128]{1,0:T(8,128)S(1)} %shard_map.62.mine), channel_id=1, source_target_pairs={{0,1},{1,0},{2,3},{3,2},{4,5},{5,4},{6,7},{7,6},{8,9},{9,8},{10,11... | collective-permute-start | bytes 24584 | tf_op jit(solution)/shard_map/ppermute | solution.py:25
  61.9 3.0 %collective-permute-start.19 = (f32[4,8,128]{2,1,0:T(8,128)S(1)}, f32[4,8,128]{2,1,0:T(8,128)S(1)}, u32[]{:S(2)}, u32[]{:S(2)}) collective-permute-start(f32[4,8,128]{2,1,0:T(8,128)S(1)} %shard_map.63.block), channel_id=1, source_target_pairs={{0,8},{1,57},{8,16},{9,1},{16,24},{17,9},{24,32},{25,17},{32,40},{... | collective-permute-start | bytes 49160 | tf_op jit(solution)/shard_map/ppermute | solution.py:33
  64.9 3.2 %collective-permute-start.20 = (f32[4,8,128]{2,1,0:T(8,128)S(1)}, f32[4,8,128]{2,1,0:T(8,128)S(1)}, u32[]{:S(2)}, u32[]{:S(2)}) collective-permute-start(f32[4,8,128]{2,1,0:T(8,128)S(1)} %collective-permute-done.19.near), channel_id=1, source_target_pairs={{0,1},{1,0},{2,3},{3,2},{4,5},{5,4},{6,7},{7,6},{8,9},{9,8},{10,11... | collective-permute-start | bytes 49160 | tf_op jit(solution)/shard_map/ppermute | solution.py:25
  68.1 4.5 %collective-permute-start.21 = (f32[4,8,128]{2,1,0:T(8,128)S(1)}, f32[4,8,128]{2,1,0:T(8,128)S(1)}, u32[]{:S(2)}, u32[]{:S(2)}) collective-permute-start(f32[4,8,128]{2,1,0:T(8,128)S(1)} %get-tuple-element.54), channel_id=1, source_target_pairs={{0,24},{1,41},{8,32},{9,49},{16,40},{17,57},{24,48},{25,1},{32,56}... | collective-permute-start | bytes 49160 | tf_op jit(solution)/shard_map/ppermute | solution.py:33
  72.6 3.5 %collective-permute-start.22 = (f32[4,8,128]{2,1,0:T(8,128)S(1)}, f32[4,8,128]{2,1,0:T(8,128)S(1)}, u32[]{:S(2)}, u32[]{:S(2)}) collective-permute-start(f32[4,8,128]{2,1,0:T(8,128)S(1)} %collective-permute-done.21.got), channel_id=1, source_target_pairs={{0,1},{1,0},{2,3},{3,2},{4,5},{5,4},{6,7},{7,6},{8,9},{9,8},{10,11... | collective-permute-start | bytes 49160 | tf_op jit(solution)/shard_map/ppermute | solution.py:25
  81.4 3.0 %collective-permute-start.24 = (bf16[432,1024]{1,0:T(8,128)(2,1)S(1)}, bf16[432,1024]{1,0:T(8,128)(2,1)S(1)}, u32[]{:S(2)}, u32[]{:S(2)}) collective-permute-start(bf16[432,1024]{1,0:T(8,128)(2,1)S(1)} %get-tuple-element.62), channel_id=1, source_target_pairs={{0,1},{1,0},{2,3},{3,2},{4,5},{5,4},{6,7},{7,6},{8,9},{9,8},{10,11... | collective-permute-start | bytes 2654216 | tf_op jit(solution)/shard_map/ppermute | solution.py:25
  84.1 17.5 %copy-start.2 = (f32[128]{0:T(128)S(1)}, f32[128]{0:T(128)}, u32[]{:S(2)}) copy-start(f32[128]{0:T(128)} %param.5) | copy-start | bytes 1540
  84.1 4.7 %collective-permute-start.23 = (bf16[144,1024]{1,0:T(8,128)(2,1)S(1)}, bf16[144,1024]{1,0:T(8,128)(2,1)S(1)}, u32[]{:S(2)}, u32[]{:S(2)}) collective-permute-start(bf16[144,1024]{1,0:T(8,128)(2,1)S(1)} %get-tuple-element.61), channel_id=1, source_target_pairs={{0,1},{1,0},{2,3},{3,2},{4,5},{5,4},{6,7},{7,6},{8,9},{9,8},{10,11... | collective-permute-start | bytes 884744 | tf_op jit(solution)/shard_map/ppermute | solution.py:25
  84.5 9.7 %collective-permute-start.25 = (bf16[144,1024]{1,0:T(8,128)(2,1)S(1)}, bf16[144,1024]{1,0:T(8,128)(2,1)S(1)}, u32[]{:S(2)}, u32[]{:S(2)}) collective-permute-start(bf16[144,1024]{1,0:T(8,128)(2,1)S(1)} %get-tuple-element.65), channel_id=1, source_target_pairs={{0,64},{64,128},{128,192},{192,0},{1,65},{65,129},{129,193},{193,1... | collective-permute-start | bytes 884744 | tf_op jit(solution)/shard_map/ppermute | solution.py:21
  85.8 8.4 %collective-permute-start.26 = (bf16[144,1024]{1,0:T(8,128)(2,1)S(1)}, bf16[144,1024]{1,0:T(8,128)(2,1)S(1)}, u32[]{:S(2)}, u32[]{:S(2)}) collective-permute-start(bf16[144,1024]{1,0:T(8,128)(2,1)S(1)} %get-tuple-element.66), channel_id=1, source_target_pairs={{0,192},{64,0},{128,64},{192,128},{1,193},{65,1},{129,65},{193,129... | collective-permute-start | bytes 884744 | tf_op jit(solution)/shard_map/ppermute | solution.py:21
  87.5 14.2 %collective-permute-start.27 = (bf16[144,1024]{1,0:T(8,128)(2,1)S(1)}, bf16[144,1024]{1,0:T(8,128)(2,1)S(1)}, u32[]{:S(2)}, u32[]{:S(2)}) collective-permute-start(bf16[144,1024]{1,0:T(8,128)(2,1)S(1)} %get-tuple-element.67), channel_id=1, source_target_pairs={{0,128},{64,192},{128,0},{192,64},{1,129},{65,193},{129,1},{193,65... | collective-permute-start | bytes 884744 | tf_op jit(solution)/shard_map/ppermute | solution.py:21

commit v11 on v10

--- a/solution.py
+++ b/solution.py
@@ -229,50 +229,71 @@
     )(*table, *pieces)
 
 
-def weigh_kernel(first, groups, sizes, energy, *refs):
+def weigh_kernel(lots, groups, sizes, keeps, sends, energy, *refs):
     logits, refs = refs[: len(groups)], refs[len(groups) :]
-    slab, (message, keep, keep_count) = refs[: len(sizes)], refs[len(sizes) :]
-    n, width = keep_count.shape[1], keep.shape[1]
-    span, step = n * NC, min(sizes)
-    tile = min(256, width)
-    for i in range(keep.shape[0] // n):
-        lot = slice((first + i) * span, (first + i + 1) * span)
-        counts, sets, at = None, [], 0
-        for p, size in enumerate(groups):
-            for cut in range(0, size, step):
-                w = jnp.exp(logits[p][lot, cut : cut + step] - energy[:, at + cut : at + cut + step])
-                counts = w if counts is None else counts + w
-                sets.append(w.astype(BF16))
-            at += size
-        column = jnp.sum(counts, axis=1, keepdims=True)
-        pairs = [jnp.concatenate(sets[p : p + 2], axis=1) for p in range(0, len(sets), 2)]
-        totals = []
-        for at in range(0, width, tile):
-            acc = None
-            for p, pair in enumerate(pairs):
-                rows = slab[p][:, at : at + tile]
-                if rows.shape[0] < pair.shape[1]:
-                    rows = jnp.concatenate([rows, slab[p + 1][:, at : at + tile]])
-                term = jnp.dot(pair, rows, preferred_element_type=F32)
-                acc = term if acc is None else acc + term
-            keep[i * n : (i + 1) * n, at : at + tile] = acc[:n]
-            totals.append(acc[n:])
-        keep_count[i * TAIL : (i + 1) * TAIL, :] = turned(column[:n])[:TAIL]
-        write_message(message, i * (n + TAIL), jnp.concatenate(totals, axis=1), turned(column[n:])[:TAIL])
-
-
-def weigh(first, count, logits, energy, slab):
-    span, width = logits[0].shape[0] // NX, slab[0].shape[1]
-    n = span // NC
+    slab, out = refs[: len(sizes)], list(refs[len(sizes) :])
+    n, width = logits[0].shape[0] // (NX * NC), slab[0].shape[1]
+    step, tile = min(sizes), min(256, width)
+    places, at, g, edge = [], 0, 0, 0
+    for size in sizes:
+        if at - edge == groups[g]:
+            g, edge = g + 1, at
+        places.append((logits[g], at - edge, at, size))
+        at += size
+    units = [[p] for p, size in enumerate(sizes) if size > step]
+    units.append([p for p, size in enumerate(sizes) if size == step])
+    counts, sets = [None] * len(lots), []
+    for unit in units:
+        parts = []
+        for i, lot in enumerate(lots):
+            row = []
+            for ref, col, at, size in (places[p] for p in unit):
+                for cut in range(0, size, step):
+                    w = jnp.exp(ref[lot : lot + n, col + cut : col + cut + step] - energy[:, at + cut : at + cut + step])
+                    counts[i] = w if counts[i] is None else counts[i] + w
+                    row.append(w.astype(BF16))
+            parts.append(jnp.concatenate(row, axis=1))
+        sets.append(jnp.concatenate(parts))
+    rows = [turned(jnp.sum(v, axis=1, keepdims=True))[:TAIL] for v in counts]
+    message = out.pop(0) if sends else None
+    if keeps:
+        keep, keep_count = out
+        for i in range(keeps):
+            keep_count[i * TAIL : (i + 1) * TAIL, :] = rows[i]
+    for i, row in enumerate(rows[keeps:]):
+        at = i * (n + TAIL) + n
+        high = row.astype(BF16)
+        message[at : at + TAIL, :n] = high
+        message[at : at + TAIL, n : 2 * n] = (row - high.astype(F32)).astype(BF16)
+        if width > 2 * n:
+            message[at : at + TAIL, 2 * n :] = jnp.zeros((TAIL, width - 2 * n), BF16)
+    for at in range(0, width, tile):
+        acc = None
+        for unit, w in zip(units, sets):
+            block = jnp.concatenate([slab[p][:, at : at + tile] for p in unit])
+            term = jnp.dot(w, block, preferred_element_type=F32)
+            acc = term if acc is None else acc + term
+        if keeps:
+            keep[:, at : at + tile] = acc[: keeps * n]
+        for i in range(sends):
+            part = acc[(keeps + i) * n : (keeps + i + 1) * n]
+            message[i * (n + TAIL) : i * (n + TAIL) + n, at : at + tile] = part.astype(BF16)
+
+
+def weigh(keeps, sends, logits, energy, slab):
+    n, width = logits[0].shape[0] // (NX * NC), slab[0].shape[1]
     sizes, groups = tuple(p.shape[0] for p in slab), tuple(v.shape[1] for v in logits)
-    total, height = sum(sizes), count * span
+    lots = [k * NC * n for k in keeps] + [k * NC * n + n for k in sends]
+    out = []
+    if sends:
+        out.append(jax.ShapeDtypeStruct((len(sends) * (n + TAIL), width), BF16))
+    if keeps:
+        out.append(jax.ShapeDtypeStruct((len(keeps) * n, width), F32))
+        out.append(jax.ShapeDtypeStruct((len(keeps) * TAIL, n), F32))
+    total, height = sum(sizes), len(lots) * n
     return pl.pallas_call(
-        functools.partial(weigh_kernel, first, groups, sizes),
-        out_shape=(
-            jax.ShapeDtypeStruct((count * (n + TAIL), width), BF16),
-            jax.ShapeDtypeStruct((count * n, width), F32),
-            jax.ShapeDtypeStruct((count * TAIL, n), F32),
-        ),
+        functools.partial(weigh_kernel, lots, groups, sizes, len(keeps), len(sends)),
+        out_shape=out,
         compiler_params=pltpu.CompilerParams(vmem_limit_bytes=VMEM_LIMIT),
         cost_estimate=pl.CostEstimate(
             flops=2 * height * total * width,
@@ -365,10 +386,13 @@
     energy, row_energy = energies(local, place, sub)
     logits, pieces = [fixed(v) for v in logits], [v for lot in lots for v in lot]
 
-    message, keep, keep_count = weigh(0, NX - 1, logits, energy, pieces)
-    sent = add(swap_cores(message), keep, keep_count)
-    message, keep, keep_count = weigh(NX - 1, 1, logits, energy, pieces)
-    others = [shift_x(m, d) for m, d in zip(sent, ORDER)]
+    sent = list(range(NX - 1))
+    (message,) = weigh([], sent, logits, energy, pieces)
+    got = swap_cores(message)
+    keep, keep_count = weigh(sent, [], logits, energy, pieces)
+    others = [shift_x(m, d) for m, d in zip(add(got, keep, keep_count), ORDER)]
+    energy, others[0] = lax.optimization_barrier((energy, others[0]))
+    message, keep, keep_count = weigh([NX - 1], [NX - 1], logits, energy, pieces)
     new_centroids, new_masses = update(keep, keep_count, swap_cores(message), others, masses, centroids)
     return new_centroids, new_masses.reshape(-1), row_energy
 

time: 103 us -> 102 us (level)
  waiting for transfers between devices: 35.4 us -> 32.3 us
  Pallas kernels: 17.1 us -> 18.2 us
    ppermute x6, waiting for transfers between devices: 19.9 us -> 16.8 us  [shift_x(): return lax.ppermute(value, 'x', [(i, (i + by) % NX) for i in range(NX)])]
    pallas_call x2 -> x3, Pallas kernels: 6.92 us -> 8.06 us  [weigh(): pl.pallas_call(functools.partial(weigh_kernel, lots, groups, sizes, len(k...]
  transfers between devices with their start and end apart: 28 -> 28, of which waited for: 15 -> 15; matrix products, arithmetic and copies ran while one was open for 0% -> 0% of each run, Pallas kernels for 9% -> 12%
where the time goes in v11:
time: 102 us
  starting transfers between devices  48.9 us (48%)
  waiting for transfers between devices  32.3 us (32%)
  Pallas kernels  18.2 us (18%)
  local copies, waits for them, and re-layouts  1.29 us (1%)
    ppermute x6, waiting for transfers between devices, shift_x(): return lax.ppermute(value, 'x', [(i, (i + by) % NX) for i in range(NX)])  16.8 us
    ppermute x6, starting transfers between devices, along_z(): return lax.ppermute(value, ('z', 'c'), pairs)  16 us
    ppermute x9, starting transfers between devices, swap_cores(): return lax.ppermute(value, 'c', [(0, 1), (1, 0)])  11.5 us
    ppermute x4, starting transfers between devices, swap_halves(): return lax.ppermute(value, ('y', 'c'), pairs)  9.79 us
    ppermute x6, starting transfers between devices, shift_x(): return lax.ppermute(value, 'x', [(i, (i + by) % NX) for i in range(NX)])  9.32 us
    pallas_call x3, Pallas kernels, score(): pl.pallas_call(functools.partial(score_kernel, 0 if whole else len(table)...  8.2 us
    pallas_call x3, Pallas kernels, weigh(): pl.pallas_call(functools.partial(weigh_kernel, lots, groups, sizes, len(k...  8.06 us
    ppermute x4, waiting for transfers between devices, swap_halves(): return lax.ppermute(value, ('y', 'c'), pairs)  5.66 us
  transfers between devices with their start and end apart: 28, of which 15 were waited for; matrix products, arithmetic and copies ran while one was open for 0% of the time, Pallas kernels for 12%

profile of v11, /device:TPU:1, one launch (start us, length us, event | category | flops | bytes accessed | tf_op | source)
XLA Modules:
  0.0 101.5 jit_solution(3324624727742018161)
XLA Ops:
  1.9 6.5 %collective-permute-start = (bf16[256,1024]{1,0:T(8,128)(2,1)S(1)}, bf16[256,1024]{1,0:T(8,128)(2,1)S(1)}, u32[]{:S(2)}, u32[]{:S(2)}) collective-permute-start(bf16[256,1024]{1,0:T(8,128)(2,1)S(1)} %constant_dynamic-slice_fusion.2), channel_id=1, source_target_pairs={{0,8},{1,57},{8,16},{9,1},{16,24},{17,9},{24,32},{25,17},{32,40},{... | collective-permute-start | bytes 1572872 | tf_op jit(solution)/shard_map/ppermute | solution.py:33
  9.6 1.5 %collective-permute-start.1 = (bf16[128,1024]{1,0:T(8,128)(2,1)}, bf16[128,1024]{1,0:T(8,128)(2,1)}, u32[]{:S(2)}, u32[]{:S(2)}) collective-permute-start(bf16[128,1024]{1,0:T(8,128)(2,1)} %centroids.1), channel_id=1, source_target_pairs={{0,192},{64,0},{128,64},{192,128},{1,193},{65,1},{129,65},{193,129... | collective-permute-start | bytes 786440 | tf_op jit(solution)/shard_map/ppermute | solution.py:21
  11.1 4.5 %collective-permute-done.2.refs_2_ = bf16[128,1024]{1,0:T(8,128)(2,1)} collective-permute-done((bf16[128,1024]{1,0:T(8,128)(2,1)}, bf16[128,1024]{1,0:T(8,128)(2,1)}, u32[]{:S(2)}, u32[]{:S(2)}) %collective-permute-start.2) | collective-permute-done | bytes 262176 | tf_op jit(solution)/shard_map/ppermute | solution.py:21
  15.9 2.7 %collective-permute-start.5 = (bf16[256,1024]{1,0:T(8,128)(2,1)S(1)}, bf16[256,1024]{1,0:T(8,128)(2,1)S(1)}, u32[]{:S(2)}, u32[]{:S(2)}) collective-permute-start(bf16[256,1024]{1,0:T(8,128)(2,1)S(1)} %collective-permute-done.refs_9_.refs_4_), channel_id=1, source_target_pairs={{0,8},{1,57},{8,16},{9,1},{16,24},{17,9},{24,32},{25,17},{32,40},{... | collective-permute-start | bytes 1572872 | tf_op jit(solution)/shard_map/ppermute | solution.py:33
  18.5 2.4 %collective-permute-start.6 = (bf16[128,1024]{1,0:T(8,128)(2,1)}, bf16[128,1024]{1,0:T(8,128)(2,1)}, u32[]{:S(2)}, u32[]{:S(2)}) collective-permute-start(bf16[128,1024]{1,0:T(8,128)(2,1)} %collective-permute-done.1.refs_0_), channel_id=1, source_target_pairs={{0,192},{64,0},{128,64},{192,128},{1,193},{65,1},{129,65},{193,129... | collective-permute-start | bytes 786440 | tf_op jit(solution)/shard_map/ppermute | solution.py:21
  20.9 2.7 %collective-permute-start.9 = (bf16[256,1024]{1,0:T(8,128)(2,1)S(1)}, bf16[256,1024]{1,0:T(8,128)(2,1)S(1)}, u32[]{:S(2)}, u32[]{:S(2)}) collective-permute-start(bf16[256,1024]{1,0:T(8,128)(2,1)S(1)} %collective-permute-done.refs_9_.refs_4_), channel_id=1, source_target_pairs={{0,2},{1,7},{2,0},{3,5},{4,6},{5,3},{6,4},{7,1},{8,10},{9,15},{10,... | collective-permute-start | bytes 1572872 | tf_op jit(solution)/shard_map/ppermute | solution.py:45
  23.6 2.2 %collective-permute-done.6.refs_4_ = bf16[128,1024]{1,0:T(8,128)(2,1)} collective-permute-done((bf16[128,1024]{1,0:T(8,128)(2,1)}, bf16[128,1024]{1,0:T(8,128)(2,1)}, u32[]{:S(2)}, u32[]{:S(2)}) %collective-permute-start.6) | collective-permute-done | bytes 262176 | tf_op jit(solution)/shard_map/ppermute | solution.py:21
  25.9 1.9 %collective-permute-start.11 = (bf16[256,1024]{1,0:T(8,128)(2,1)S(1)}, bf16[256,1024]{1,0:T(8,128)(2,1)S(1)}, u32[]{:S(2)}, u32[]{:S(2)}) collective-permute-start(bf16[256,1024]{1,0:T(8,128)(2,1)S(1)} %collective-permute-done.5.refs_11_.refs_6_), channel_id=1, source_target_pairs={{0,8},{1,57},{8,16},{9,1},{16,24},{17,9},{24,32},{25,17},{32,40},{... | collective-permute-start | bytes 1572872 | tf_op jit(solution)/shard_map/ppermute | solution.py:33
  27.8 2.4 %collective-permute-done.9.refs_10_.refs_5_ = bf16[256,1024]{1,0:T(8,128)(2,1)S(1)} collective-permute-done((bf16[256,1024]{1,0:T(8,128)(2,1)S(1)}, bf16[256,1024]{1,0:T(8,128)(2,1)S(1)}, u32[]{:S(2)}, u32[]{:S(2)}) %collective-permute-start.9) | collective-permute-done | bytes 524320 | tf_op jit(solution)/shard_map/ppermute | solution.py:45
  30.2 2.7 %collective-permute-start.10 = (bf16[256,1024]{1,0:T(8,128)(2,1)S(1)}, bf16[256,1024]{1,0:T(8,128)(2,1)}, u32[]{:S(2)}, u32[]{:S(2)}) collective-permute-start(bf16[256,1024]{1,0:T(8,128)(2,1)S(1)} %collective-permute-done.5.refs_11_.refs_6_), channel_id=1, source_target_pairs={{0,2},{1,7},{2,0},{3,5},{4,6},{5,3},{6,4},{7,1},{8,10},{9,15},{10,... | collective-permute-start | bytes 1572872 | tf_op jit(solution)/shard_map/ppermute | solution.py:45
  34.3 3.0 %collective-permute-start.7 = (bf16[128,1024]{1,0:T(8,128)(2,1)}, bf16[128,1024]{1,0:T(8,128)(2,1)}, u32[]{:S(2)}, u32[]{:S(2)}) collective-permute-start(bf16[128,1024]{1,0:T(8,128)(2,1)} %collective-permute-done.6.refs_4_), channel_id=1, source_target_pairs={{0,1},{1,0},{2,3},{3,2},{4,5},{5,4},{6,7},{7,6},{8,9},{9,8},{10,11... | collective-permute-start | bytes 786440 | tf_op jit(solution)/shard_map/ppermute | solution.py:25
  37.9 2.7 %collective-permute-start.12 = (bf16[256,1024]{1,0:T(8,128)(2,1)S(1)}, bf16[256,1024]{1,0:T(8,128)(2,1)S(1)}, u32[]{:S(2)}, u32[]{:S(2)}) collective-permute-start(bf16[256,1024]{1,0:T(8,128)(2,1)S(1)} %collective-permute-done.11.refs_2_.refs_8_), channel_id=1, source_target_pairs={{0,2},{1,7},{2,0},{3,5},{4,6},{5,3},{6,4},{7,1},{8,10},{9,15},{10,... | collective-permute-start | bytes 1572872 | tf_op jit(solution)/shard_map/ppermute | solution.py:45
  40.7 5.7 %shard_map.58 = (bf16[1024,1024]{1,0:T(8,128)(2,1)S(1)}, f32[1024,128]{1,0:T(8,128)S(1)}, f32[1024,1280]{1,0:T(8,128)S(1)}, f32[1,1280]{1,0:T(1,128)S(1)}) custom-call(bf16[128,1024]{1,0:T(8,128)(2,1)} %collective-permute-done.1.refs_0_, bf16[128,1024]{1,0:T(8,128)(2,1)} %collective-permute-done.3.refs_1_, bf16[128,1024]{1,0:T(8,128)(2,1)} %collective-permute-done.2.refs_2_, ...), custom_call_target="tpu_custom_call" | custom-call | flops 5368709120 | bytes 9961472 | tf_op jit(solution)/shard_map/pallas_call | solution.py:220
  46.3 1.7 %collective-permute-start.14 = (bf16[128,1024]{1,0:T(8,128)(2,1)S(1)}, bf16[128,1024]{1,0:T(8,128)(2,1)S(1)}, u32[]{:S(2)}, u32[]{:S(2)}) collective-permute-start(bf16[128,1024]{1,0:T(8,128)(2,1)S(1)} %collective-permute-done.13.refs_2_.refs_10_), channel_id=1, source_target_pairs={{0,2},{1,7},{2,0},{3,5},{4,6},{5,3},{6,4},{7,1},{8,10},{9,15},{10,... | collective-permute-start | bytes 786440 | tf_op jit(solution)/shard_map/ppermute | solution.py:45
  48.0 1.6 %shard_map.59 = (f32[1024,512]{1,0:T(8,128)S(1)}, f32[1,512]{1,0:T(1,128)S(1)}) custom-call(bf16[1024,1024]{1,0:T(8,128)(2,1)S(1)} %get-tuple-element.48.refs_0_, f32[1024,128]{1,0:T(8,128)S(1)} %get-tuple-element.49.refs_1_, bf16[256,1024]{1,0:T(8,128)(2,1)S(1)} %collective-permute-done.11.refs_2_.refs_8_, ...), custom_call_target="tpu_custom_call" | custom-call | flops 2147483648 | bytes 5242880 | tf_op jit(solution)/shard_map/pallas_call | solution.py:220
  49.6 3.2 %collective-permute-done.14.refs_3_.refs_11_ = bf16[128,1024]{1,0:T(8,128)(2,1)S(1)} collective-permute-done((bf16[128,1024]{1,0:T(8,128)(2,1)S(1)}, bf16[128,1024]{1,0:T(8,128)(2,1)S(1)}, u32[]{:S(2)}, u32[]{:S(2)}) %collective-permute-start.14) | collective-permute-done | bytes 262176 | tf_op jit(solution)/shard_map/ppermute | solution.py:45
  53.8 1.6 %collective-permute-start.17 = (f32[16,128]{1,0:T(8,128)S(1)}, f32[16,128]{1,0:T(8,128)S(1)}, u32[]{:S(2)}, u32[]{:S(2)}) collective-permute-start(f32[16,128]{1,0:T(8,128)S(1)} %shard_map.61.own), channel_id=1, source_target_pairs={{0,6},{2,0},{4,2},{6,4},{1,7},{3,1},{5,3},{7,5},{8,14},{10,8},{12,... | collective-permute-start | bytes 24584 | tf_op jit(solution)/shard_map/ppermute | solution.py:37
  56.4 3.1 %collective-permute-done.16.refs_1_ = f32[16,128]{1,0:T(8,128)S(1)} collective-permute-done((f32[16,128]{1,0:T(8,128)S(1)}, f32[16,128]{1,0:T(8,128)S(1)}, u32[]{:S(2)}, u32[]{:S(2)}) %collective-permute-start.16) | collective-permute-done | bytes 8224 | tf_op jit(solution)/shard_map/ppermute | solution.py:37
  59.5 1.6 %collective-permute-start.18 = (f32[16,128]{1,0:T(8,128)S(1)}, f32[16,128]{1,0:T(8,128)S(1)}, u32[]{:S(2)}, u32[]{:S(2)}) collective-permute-start(f32[16,128]{1,0:T(8,128)S(1)} %shard_map.62.mine), channel_id=1, source_target_pairs={{0,1},{1,0},{2,3},{3,2},{4,5},{5,4},{6,7},{7,6},{8,9},{9,8},{10,11... | collective-permute-start | bytes 24584 | tf_op jit(solution)/shard_map/ppermute | solution.py:25
  61.9 2.2 %collective-permute-start.19 = (f32[4,8,128]{2,1,0:T(8,128)S(1)}, f32[4,8,128]{2,1,0:T(8,128)S(1)}, u32[]{:S(2)}, u32[]{:S(2)}) collective-permute-start(f32[4,8,128]{2,1,0:T(8,128)S(1)} %shard_map.63.block), channel_id=1, source_target_pairs={{0,8},{1,57},{8,16},{9,1},{16,24},{17,9},{24,32},{25,17},{32,40},{... | collective-permute-start | bytes 49160 | tf_op jit(solution)/shard_map/ppermute | solution.py:33
  64.9 2.3 %collective-permute-start.20 = (f32[4,8,128]{2,1,0:T(8,128)S(1)}, f32[4,8,128]{2,1,0:T(8,128)S(1)}, u32[]{:S(2)}, u32[]{:S(2)}) collective-permute-start(f32[4,8,128]{2,1,0:T(8,128)S(1)} %collective-permute-done.19.near), channel_id=1, source_target_pairs={{0,1},{1,0},{2,3},{3,2},{4,5},{5,4},{6,7},{7,6},{8,9},{9,8},{10,11... | collective-permute-start | bytes 49160 | tf_op jit(solution)/shard_map/ppermute | solution.py:25
  68.1 2.3 %collective-permute-start.21 = (f32[4,8,128]{2,1,0:T(8,128)S(1)}, f32[4,8,128]{2,1,0:T(8,128)S(1)}, u32[]{:S(2)}, u32[]{:S(2)}) collective-permute-start(f32[4,8,128]{2,1,0:T(8,128)S(1)} %get-tuple-element.55), channel_id=1, source_target_pairs={{0,24},{1,41},{8,32},{9,49},{16,40},{17,57},{24,48},{25,1},{32,56}... | collective-permute-start | bytes 49160 | tf_op jit(solution)/shard_map/ppermute | solution.py:33
  70.4 2.2 %collective-permute-done.21.got = f32[4,8,128]{2,1,0:T(8,128)S(1)} collective-permute-done((f32[4,8,128]{2,1,0:T(8,128)S(1)}, f32[4,8,128]{2,1,0:T(8,128)S(1)}, u32[]{:S(2)}, u32[]{:S(2)}) %collective-permute-start.21) | collective-permute-done | bytes 16416 | tf_op jit(solution)/shard_map/ppermute | solution.py:33
  72.6 2.7 %collective-permute-start.22 = (f32[4,8,128]{2,1,0:T(8,128)S(1)}, f32[4,8,128]{2,1,0:T(8,128)S(1)}, u32[]{:S(2)}, u32[]{:S(2)}) collective-permute-start(f32[4,8,128]{2,1,0:T(8,128)S(1)} %collective-permute-done.21.got), channel_id=1, source_target_pairs={{0,1},{1,0},{2,3},{3,2},{4,5},{5,4},{6,7},{7,6},{8,9},{9,8},{10,11... | collective-permute-start | bytes 49160 | tf_op jit(solution)/shard_map/ppermute | solution.py:25
  76.8 2.9 %shard_map.66 = bf16[432,1024]{1,0:T(8,128)(2,1)S(1)} custom-call(f32[1,2048]{1,0:T(1,128)S(1)} %get-tuple-element.63.energy, f32[1024,1280]{1,0:T(8,128)S(1)} %get-tuple-element.57.refs_0_, f32[1024,512]{1,0:T(8,128)S(1)} %get-tuple-element.58.refs_1_, f32[1024,256]{1,0:T(8,128)S(1)} %get-tuple-element.59.refs_2_, bf16[256,1024]{1,0:T(8,128)(2,1)S(1)} %bitcast.9, ...), custom_call_target="tpu_custom_call" | custom-call | flops 1610612736 | bytes 7340032 | tf_op jit(solution)/shard_map/pallas_call | solution.py:294
  80.1 2.9 %shard_map.67 = (f32[384,1024]{1,0:T(8,128)S(1)}, f32[48,128]{1,0:T(8,128)S(1)}) custom-call(f32[1,2048]{1,0:T(1,128)S(1)} %get-tuple-element.63.energy, f32[1024,1280]{1,0:T(8,128)S(1)} %get-tuple-element.57.refs_0_, f32[1024,512]{1,0:T(8,128)S(1)} %get-tuple-element.58.refs_1_, f32[1024,256]{1,0:T(8,128)S(1)} %get-tuple-element.59.refs_2_, ...), custom_call_target="tpu_custom_call" | custom-call | flops 1610612736 | bytes 7340032 | tf_op jit(solution)/shard_map/pallas_call | solution.py:294
  83.1 1.3 %collective-permute-start.24 = (bf16[144,1024]{1,0:T(8,128)(2,1)S(1)}, bf16[144,1024]{1,0:T(8,128)(2,1)S(1)}, u32[]{:S(2)}, u32[]{:S(2)}) collective-permute-start(bf16[144,1024]{1,0:T(8,128)(2,1)S(1)} %get-tuple-element.62), channel_id=1, source_target_pairs={{0,64},{64,128},{128,192},{192,0},{1,65},{65,129},{129,193},{193,1... | collective-permute-start | bytes 884744 | tf_op jit(solution)/shard_map/ppermute | solution.py:21
  84.4 1.6 %collective-permute-start.26 = (bf16[144,1024]{1,0:T(8,128)(2,1)S(1)}, bf16[144,1024]{1,0:T(8,128)(2,1)S(1)}, u32[]{:S(2)}, u32[]{:S(2)}) collective-permute-start(bf16[144,1024]{1,0:T(8,128)(2,1)S(1)} %get-tuple-element.68), channel_id=1, source_target_pairs={{0,192},{64,0},{128,64},{192,128},{1,193},{65,1},{129,65},{193,129... | collective-permute-start | bytes 884744 | tf_op jit(solution)/shard_map/ppermute | solution.py:21
  86.0 1.4 %collective-permute-start.27 = (bf16[144,1024]{1,0:T(8,128)(2,1)S(1)}, bf16[144,1024]{1,0:T(8,128)(2,1)S(1)}, u32[]{:S(2)}, u32[]{:S(2)}) collective-permute-start(bf16[144,1024]{1,0:T(8,128)(2,1)S(1)} %get-tuple-element.69), channel_id=1, source_target_pairs={{0,128},{64,192},{128,0},{192,64},{1,129},{65,193},{129,1},{193,65... | collective-permute-start | bytes 884744 | tf_op jit(solution)/shard_map/ppermute | solution.py:21
  87.4 5.6 %collective-permute-done.24.one = bf16[144,1024]{1,0:T(8,128)(2,1)S(1)} collective-permute-done((bf16[144,1024]{1,0:T(8,128)(2,1)S(1)}, bf16[144,1024]{1,0:T(8,128)(2,1)S(1)}, u32[]{:S(2)}, u32[]{:S(2)}) %collective-permute-start.24) | collective-permute-done | bytes 294944 | tf_op jit(solution)/shard_map/ppermute | solution.py:21
  93.0 2.3 %shard_map.69 = (bf16[144,1024]{1,0:T(8,128)(2,1)S(1)}, f32[128,1024]{1,0:T(8,128)S(1)}, f32[16,128]{1,0:T(8,128)S(1)}) custom-call(f32[1,2048]{1,0:T(1,128)S(1)} %get-tuple-element.63.energy, f32[1024,1280]{1,0:T(8,128)S(1)} %get-tuple-element.57.refs_0_, f32[1024,512]{1,0:T(8,128)S(1)} %get-tuple-element.58.refs_1_, ...), custom_call_target="tpu_custom_call" | custom-call | flops 1073741824 | bytes 6291456 | tf_op jit(solution)/shard_map/pallas_call | solution.py:294
  96.3 4.1 %collective-permute-done.27.three = bf16[144,1024]{1,0:T(8,128)(2,1)S(1)} collective-permute-done((bf16[144,1024]{1,0:T(8,128)(2,1)S(1)}, bf16[144,1024]{1,0:T(8,128)(2,1)S(1)}, u32[]{:S(2)}, u32[]{:S(2)}) %collective-permute-start.27) | collective-permute-done | bytes 294944 | tf_op jit(solution)/shard_map/ppermute | solution.py:21
  (49 shorter events, 13.3 us)
Async XLA Ops:
  0.6 1.2 %copy-start = (bf16[512,1024]{1,0:T(8,128)(2,1)S(1)}, bf16[512,1024]{1,0:T(8,128)(2,1)}, u32[]{:S(2)}) copy-start(bf16[512,1024]{1,0:T(8,128)(2,1)} %param.3) | copy-start | bytes 3145732
  0.6 40.0 %copy-start.1 = (bf16[128,1024]{1,0:T(8,128)(2,1)S(1)}, bf16[128,1024]{1,0:T(8,128)(2,1)}, u32[]{:S(2)}) copy-start(bf16[128,1024]{1,0:T(8,128)(2,1)} %centroids.1) | copy-start | bytes 786436
  1.9 14.0 %collective-permute-start = (bf16[256,1024]{1,0:T(8,128)(2,1)S(1)}, bf16[256,1024]{1,0:T(8,128)(2,1)S(1)}, u32[]{:S(2)}, u32[]{:S(2)}) collective-permute-start(bf16[256,1024]{1,0:T(8,128)(2,1)S(1)} %constant_dynamic-slice_fusion.2), channel_id=1, source_target_pairs={{0,8},{1,57},{8,16},{9,1},{16,24},{17,9},{24,32},{25,17},{32,40},{... | collective-permute-start | bytes 1572872 | tf_op jit(solution)/shard_map/ppermute | solution.py:33
  8.4 7.2 %collective-permute-start.2 = (bf16[128,1024]{1,0:T(8,128)(2,1)}, bf16[128,1024]{1,0:T(8,128)(2,1)}, u32[]{:S(2)}, u32[]{:S(2)}) collective-permute-start(bf16[128,1024]{1,0:T(8,128)(2,1)} %centroids.1), channel_id=1, source_target_pairs={{0,64},{64,128},{128,192},{192,0},{1,65},{65,129},{129,193},{193,1... | collective-permute-start | bytes 786440 | tf_op jit(solution)/shard_map/ppermute | solution.py:21
  9.6 6.3 %collective-permute-start.1 = (bf16[128,1024]{1,0:T(8,128)(2,1)}, bf16[128,1024]{1,0:T(8,128)(2,1)}, u32[]{:S(2)}, u32[]{:S(2)}) collective-permute-start(bf16[128,1024]{1,0:T(8,128)(2,1)} %centroids.1), channel_id=1, source_target_pairs={{0,192},{64,0},{128,64},{192,128},{1,193},{65,1},{129,65},{193,129... | collective-permute-start | bytes 786440 | tf_op jit(solution)/shard_map/ppermute | solution.py:21
  15.9 10.0 %collective-permute-start.5 = (bf16[256,1024]{1,0:T(8,128)(2,1)S(1)}, bf16[256,1024]{1,0:T(8,128)(2,1)S(1)}, u32[]{:S(2)}, u32[]{:S(2)}) collective-permute-start(bf16[256,1024]{1,0:T(8,128)(2,1)S(1)} %collective-permute-done.refs_9_.refs_4_), channel_id=1, source_target_pairs={{0,8},{1,57},{8,16},{9,1},{16,24},{17,9},{24,32},{25,17},{32,40},{... | collective-permute-start | bytes 1572872 | tf_op jit(solution)/shard_map/ppermute | solution.py:33
  18.5 7.3 %collective-permute-start.6 = (bf16[128,1024]{1,0:T(8,128)(2,1)}, bf16[128,1024]{1,0:T(8,128)(2,1)}, u32[]{:S(2)}, u32[]{:S(2)}) collective-permute-start(bf16[128,1024]{1,0:T(8,128)(2,1)} %collective-permute-done.1.refs_0_), channel_id=1, source_target_pairs={{0,192},{64,0},{128,64},{192,128},{1,193},{65,1},{129,65},{193,129... | collective-permute-start | bytes 786440 | tf_op jit(solution)/shard_map/ppermute | solution.py:21
  20.9 9.3 %collective-permute-start.9 = (bf16[256,1024]{1,0:T(8,128)(2,1)S(1)}, bf16[256,1024]{1,0:T(8,128)(2,1)S(1)}, u32[]{:S(2)}, u32[]{:S(2)}) collective-permute-start(bf16[256,1024]{1,0:T(8,128)(2,1)S(1)} %collective-permute-done.refs_9_.refs_4_), channel_id=1, source_target_pairs={{0,2},{1,7},{2,0},{3,5},{4,6},{5,3},{6,4},{7,1},{8,10},{9,15},{10,... | collective-permute-start | bytes 1572872 | tf_op jit(solution)/shard_map/ppermute | solution.py:45
  25.9 8.4 %collective-permute-start.11 = (bf16[256,1024]{1,0:T(8,128)(2,1)S(1)}, bf16[256,1024]{1,0:T(8,128)(2,1)S(1)}, u32[]{:S(2)}, u32[]{:S(2)}) collective-permute-start(bf16[256,1024]{1,0:T(8,128)(2,1)S(1)} %collective-permute-done.5.refs_11_.refs_6_), channel_id=1, source_target_pairs={{0,8},{1,57},{8,16},{9,1},{16,24},{17,9},{24,32},{25,17},{32,40},{... | collective-permute-start | bytes 1572872 | tf_op jit(solution)/shard_map/ppermute | solution.py:33
  30.2 10.4 %collective-permute-start.10 = (bf16[256,1024]{1,0:T(8,128)(2,1)S(1)}, bf16[256,1024]{1,0:T(8,128)(2,1)}, u32[]{:S(2)}, u32[]{:S(2)}) collective-permute-start(bf16[256,1024]{1,0:T(8,128)(2,1)S(1)} %collective-permute-done.5.refs_11_.refs_6_), channel_id=1, source_target_pairs={{0,2},{1,7},{2,0},{3,5},{4,6},{5,3},{6,4},{7,1},{8,10},{9,15},{10,... | collective-permute-start | bytes 1572872 | tf_op jit(solution)/shard_map/ppermute | solution.py:45
  32.9 4.5 %collective-permute-start.8 = (bf16[128,1024]{1,0:T(8,128)(2,1)}, bf16[128,1024]{1,0:T(8,128)(2,1)}, u32[]{:S(2)}, u32[]{:S(2)}) collective-permute-start(bf16[128,1024]{1,0:T(8,128)(2,1)} %centroids.1), channel_id=1, source_target_pairs={{0,1},{1,0},{2,3},{3,2},{4,5},{5,4},{6,7},{7,6},{8,9},{9,8},{10,11... | collective-permute-start | bytes 786440 | tf_op jit(solution)/shard_map/ppermute | solution.py:25
  32.9 7.8 %collective-permute-start.3 = (bf16[128,1024]{1,0:T(8,128)(2,1)}, bf16[128,1024]{1,0:T(8,128)(2,1)}, u32[]{:S(2)}, u32[]{:S(2)}) collective-permute-start(bf16[128,1024]{1,0:T(8,128)(2,1)} %collective-permute-done.1.refs_0_), channel_id=1, source_target_pairs={{0,1},{1,0},{2,3},{3,2},{4,5},{5,4},{6,7},{7,6},{8,9},{9,8},{10,11... | collective-permute-start | bytes 786440 | tf_op jit(solution)/shard_map/ppermute | solution.py:25
  33.4 4.5 %collective-permute-start.4 = (bf16[128,1024]{1,0:T(8,128)(2,1)}, bf16[128,1024]{1,0:T(8,128)(2,1)}, u32[]{:S(2)}, u32[]{:S(2)}) collective-permute-start(bf16[128,1024]{1,0:T(8,128)(2,1)} %collective-permute-done.2.refs_2_), channel_id=1, source_target_pairs={{0,1},{1,0},{2,3},{3,2},{4,5},{5,4},{6,7},{7,6},{8,9},{9,8},{10,11... | collective-permute-start | bytes 786440 | tf_op jit(solution)/shard_map/ppermute | solution.py:25
  34.3 6.3 %collective-permute-start.7 = (bf16[128,1024]{1,0:T(8,128)(2,1)}, bf16[128,1024]{1,0:T(8,128)(2,1)}, u32[]{:S(2)}, u32[]{:S(2)}) collective-permute-start(bf16[128,1024]{1,0:T(8,128)(2,1)} %collective-permute-done.6.refs_4_), channel_id=1, source_target_pairs={{0,1},{1,0},{2,3},{3,2},{4,5},{5,4},{6,7},{7,6},{8,9},{9,8},{10,11... | collective-permute-start | bytes 786440 | tf_op jit(solution)/shard_map/ppermute | solution.py:25
  37.4 9.0 %collective-permute-start.13 = (bf16[128,1024]{1,0:T(8,128)(2,1)S(1)}, bf16[128,1024]{1,0:T(8,128)(2,1)S(1)}, u32[]{:S(2)}, u32[]{:S(2)}) collective-permute-start(bf16[128,1024]{1,0:T(8,128)(2,1)S(1)} %constant_dynamic-slice_fusion), channel_id=1, source_target_pairs={{0,8},{1,57},{8,16},{9,1},{16,24},{17,9},{24,32},{25,17},{32,40},{... | collective-permute-start | bytes 786440 | tf_op jit(solution)/shard_map/ppermute | solution.py:33
  37.9 10.1 %collective-permute-start.12 = (bf16[256,1024]{1,0:T(8,128)(2,1)S(1)}, bf16[256,1024]{1,0:T(8,128)(2,1)S(1)}, u32[]{:S(2)}, u32[]{:S(2)}) collective-permute-start(bf16[256,1024]{1,0:T(8,128)(2,1)S(1)} %collective-permute-done.11.refs_2_.refs_8_), channel_id=1, source_target_pairs={{0,2},{1,7},{2,0},{3,5},{4,6},{5,3},{6,4},{7,1},{8,10},{9,15},{10,... | collective-permute-start | bytes 1572872 | tf_op jit(solution)/shard_map/ppermute | solution.py:45
  46.3 6.5 %collective-permute-start.14 = (bf16[128,1024]{1,0:T(8,128)(2,1)S(1)}, bf16[128,1024]{1,0:T(8,128)(2,1)S(1)}, u32[]{:S(2)}, u32[]{:S(2)}) collective-permute-start(bf16[128,1024]{1,0:T(8,128)(2,1)S(1)} %collective-permute-done.13.refs_2_.refs_10_), channel_id=1, source_target_pairs={{0,2},{1,7},{2,0},{3,5},{4,6},{5,3},{6,4},{7,1},{8,10},{9,15},{10,... | collective-permute-start | bytes 786440 | tf_op jit(solution)/shard_map/ppermute | solution.py:45
  53.8 2.6 %collective-permute-start.17 = (f32[16,128]{1,0:T(8,128)S(1)}, f32[16,128]{1,0:T(8,128)S(1)}, u32[]{:S(2)}, u32[]{:S(2)}) collective-permute-start(f32[16,128]{1,0:T(8,128)S(1)} %shard_map.61.own), channel_id=1, source_target_pairs={{0,6},{2,0},{4,2},{6,4},{1,7},{3,1},{5,3},{7,5},{8,14},{10,8},{12,... | collective-permute-start | bytes 24584 | tf_op jit(solution)/shard_map/ppermute | solution.py:37
  55.4 4.0 %collective-permute-start.16 = (f32[16,128]{1,0:T(8,128)S(1)}, f32[16,128]{1,0:T(8,128)S(1)}, u32[]{:S(2)}, u32[]{:S(2)}) collective-permute-start(f32[16,128]{1,0:T(8,128)S(1)} %shard_map.61.own), channel_id=1, source_target_pairs={{0,4},{2,6},{4,0},{6,2},{1,5},{3,7},{5,1},{7,3},{8,12},{10,14},{12... | collective-permute-start | bytes 24584 | tf_op jit(solution)/shard_map/ppermute | solution.py:37
  55.4 4.0 %collective-permute-start.15 = (f32[16,128]{1,0:T(8,128)S(1)}, f32[16,128]{1,0:T(8,128)S(1)}, u32[]{:S(2)}, u32[]{:S(2)}) collective-permute-start(f32[16,128]{1,0:T(8,128)S(1)} %shard_map.61.own), channel_id=1, source_target_pairs={{0,2},{2,4},{4,6},{6,0},{1,3},{3,5},{5,7},{7,1},{8,10},{10,12},{12... | collective-permute-start | bytes 24584 | tf_op jit(solution)/shard_map/ppermute | solution.py:37
  59.5 2.4 %collective-permute-start.18 = (f32[16,128]{1,0:T(8,128)S(1)}, f32[16,128]{1,0:T(8,128)S(1)}, u32[]{:S(2)}, u32[]{:S(2)}) collective-permute-start(f32[16,128]{1,0:T(8,128)S(1)} %shard_map.62.mine), channel_id=1, source_target_pairs={{0,1},{1,0},{2,3},{3,2},{4,5},{5,4},{6,7},{7,6},{8,9},{9,8},{10,11... | collective-permute-start | bytes 24584 | tf_op jit(solution)/shard_map/ppermute | solution.py:25
  61.9 3.0 %collective-permute-start.19 = (f32[4,8,128]{2,1,0:T(8,128)S(1)}, f32[4,8,128]{2,1,0:T(8,128)S(1)}, u32[]{:S(2)}, u32[]{:S(2)}) collective-permute-start(f32[4,8,128]{2,1,0:T(8,128)S(1)} %shard_map.63.block), channel_id=1, source_target_pairs={{0,8},{1,57},{8,16},{9,1},{16,24},{17,9},{24,32},{25,17},{32,40},{... | collective-permute-start | bytes 49160 | tf_op jit(solution)/shard_map/ppermute | solution.py:33
  64.9 3.2 %collective-permute-start.20 = (f32[4,8,128]{2,1,0:T(8,128)S(1)}, f32[4,8,128]{2,1,0:T(8,128)S(1)}, u32[]{:S(2)}, u32[]{:S(2)}) collective-permute-start(f32[4,8,128]{2,1,0:T(8,128)S(1)} %collective-permute-done.19.near), channel_id=1, source_target_pairs={{0,1},{1,0},{2,3},{3,2},{4,5},{5,4},{6,7},{7,6},{8,9},{9,8},{10,11... | collective-permute-start | bytes 49160 | tf_op jit(solution)/shard_map/ppermute | solution.py:25
  68.1 4.5 %collective-permute-start.21 = (f32[4,8,128]{2,1,0:T(8,128)S(1)}, f32[4,8,128]{2,1,0:T(8,128)S(1)}, u32[]{:S(2)}, u32[]{:S(2)}) collective-permute-start(f32[4,8,128]{2,1,0:T(8,128)S(1)} %get-tuple-element.55), channel_id=1, source_target_pairs={{0,24},{1,41},{8,32},{9,49},{16,40},{17,57},{24,48},{25,1},{32,56}... | collective-permute-start | bytes 49160 | tf_op jit(solution)/shard_map/ppermute | solution.py:33
  72.6 3.5 %collective-permute-start.22 = (f32[4,8,128]{2,1,0:T(8,128)S(1)}, f32[4,8,128]{2,1,0:T(8,128)S(1)}, u32[]{:S(2)}, u32[]{:S(2)}) collective-permute-start(f32[4,8,128]{2,1,0:T(8,128)S(1)} %collective-permute-done.21.got), channel_id=1, source_target_pairs={{0,1},{1,0},{2,3},{3,2},{4,5},{5,4},{6,7},{7,6},{8,9},{9,8},{10,11... | collective-permute-start | bytes 49160 | tf_op jit(solution)/shard_map/ppermute | solution.py:25
  79.6 3.3 %collective-permute-start.23 = (bf16[432,1024]{1,0:T(8,128)(2,1)S(1)}, bf16[432,1024]{1,0:T(8,128)(2,1)S(1)}, u32[]{:S(2)}, u32[]{:S(2)}) collective-permute-start(bf16[432,1024]{1,0:T(8,128)(2,1)S(1)} %shard_map.66), channel_id=1, source_target_pairs={{0,1},{1,0},{2,3},{3,2},{4,5},{5,4},{6,7},{7,6},{8,9},{9,8},{10,11... | collective-permute-start | bytes 2654216 | tf_op jit(solution)/shard_map/ppermute | solution.py:25
  83.1 9.9 %collective-permute-start.24 = (bf16[144,1024]{1,0:T(8,128)(2,1)S(1)}, bf16[144,1024]{1,0:T(8,128)(2,1)S(1)}, u32[]{:S(2)}, u32[]{:S(2)}) collective-permute-start(bf16[144,1024]{1,0:T(8,128)(2,1)S(1)} %get-tuple-element.62), channel_id=1, source_target_pairs={{0,64},{64,128},{128,192},{192,0},{1,65},{65,129},{129,193},{193,1... | collective-permute-start | bytes 884744 | tf_op jit(solution)/shard_map/ppermute | solution.py:21
  84.4 11.9 %collective-permute-start.26 = (bf16[144,1024]{1,0:T(8,128)(2,1)S(1)}, bf16[144,1024]{1,0:T(8,128)(2,1)S(1)}, u32[]{:S(2)}, u32[]{:S(2)}) collective-permute-start(bf16[144,1024]{1,0:T(8,128)(2,1)S(1)} %get-tuple-element.68), channel_id=1, source_target_pairs={{0,192},{64,0},{128,64},{192,128},{1,193},{65,1},{129,65},{193,129... | collective-permute-start | bytes 884744 | tf_op jit(solution)/shard_map/ppermute | solution.py:21
  86.0 14.4 %copy-start.2 = (f32[128]{0:T(128)S(1)}, f32[128]{0:T(128)}, u32[]{:S(2)}) copy-start(f32[128]{0:T(128)} %param.5) | copy-start | bytes 1540
  86.0 14.4 %collective-permute-start.27 = (bf16[144,1024]{1,0:T(8,128)(2,1)S(1)}, bf16[144,1024]{1,0:T(8,128)(2,1)S(1)}, u32[]{:S(2)}, u32[]{:S(2)}) collective-permute-start(bf16[144,1024]{1,0:T(8,128)(2,1)S(1)} %get-tuple-element.69), channel_id=1, source_target_pairs={{0,128},{64,192},{128,0},{192,64},{1,129},{65,193},{129,1},{193,65... | collective-permute-start | bytes 884744 | tf_op jit(solution)/shard_map/ppermute | solution.py:21
  95.3 5.1 %collective-permute-start.25 = (bf16[144,1024]{1,0:T(8,128)(2,1)S(1)}, bf16[144,1024]{1,0:T(8,128)(2,1)S(1)}, u32[]{:S(2)}, u32[]{:S(2)}) collective-permute-start(bf16[144,1024]{1,0:T(8,128)(2,1)S(1)} %get-tuple-element.66), channel_id=1, source_target_pairs={{0,1},{1,0},{2,3},{3,2},{4,5},{5,4},{6,7},{7,6},{8,9},{9,8},{10,11... | collective-permute-start | bytes 884744 | tf_op jit(solution)/shard_map/ppermute | solution.py:25

commit v12 on v11

--- a/solution.py
+++ b/solution.py
@@ -10,7 +10,7 @@
 NX, NZ, NY, NC = 4, 8, 4, 2
 BF16, F32 = jnp.bfloat16, jnp.float32
 TAIL = 16
-ORDER = (1, 3, 2, 0)
+ORDER = (2, 1, 3, 0)
 BATCH = 512
 VMEM_LIMIT = 20 * 1024 * 1024
 SMALL_LIMIT = 4 * 1024 * 1024
@@ -242,8 +242,14 @@
         at += size
     units = [[p] for p, size in enumerate(sizes) if size > step]
     units.append([p for p, size in enumerate(sizes) if size == step])
-    counts, sets = [None] * len(lots), []
-    for unit in units:
+    units = [units[k] + units[k + 1] for k in range(0, len(units), 2)]
+    message = out.pop(0) if sends else None
+    if keeps:
+        keep, keep_count, total = out
+    else:
+        (total,) = out
+    counts = [None] * len(lots)
+    for k, unit in enumerate(units):
         parts = []
         for i, lot in enumerate(lots):
             row = []
@@ -253,13 +259,23 @@
                     counts[i] = w if counts[i] is None else counts[i] + w
                     row.append(w.astype(BF16))
             parts.append(jnp.concatenate(row, axis=1))
-        sets.append(jnp.concatenate(parts))
+        w = jnp.concatenate(parts)
+        for at in range(0, width, tile):
+            block = jnp.concatenate([slab[p][:, at : at + tile] for p in unit])
+            term = jnp.dot(w, block, preferred_element_type=F32)
+            if k:
+                term = total[:, at : at + tile] + term
+            if k < len(units) - 1:
+                total[:, at : at + tile] = term
+                continue
+            if keeps:
+                keep[:, at : at + tile] = term[: keeps * n]
+            for i in range(sends):
+                part = term[(keeps + i) * n : (keeps + i + 1) * n]
+                message[i * (n + TAIL) : i * (n + TAIL) + n, at : at + tile] = part.astype(BF16)
     rows = [turned(jnp.sum(v, axis=1, keepdims=True))[:TAIL] for v in counts]
-    message = out.pop(0) if sends else None
-    if keeps:
-        keep, keep_count = out
-        for i in range(keeps):
-            keep_count[i * TAIL : (i + 1) * TAIL, :] = rows[i]
+    for i, row in enumerate(rows[:keeps]):
+        keep_count[i * TAIL : (i + 1) * TAIL, :] = row
     for i, row in enumerate(rows[keeps:]):
         at = i * (n + TAIL) + n
         high = row.astype(BF16)
@@ -267,17 +283,6 @@
         message[at : at + TAIL, n : 2 * n] = (row - high.astype(F32)).astype(BF16)
         if width > 2 * n:
             message[at : at + TAIL, 2 * n :] = jnp.zeros((TAIL, width - 2 * n), BF16)
-    for at in range(0, width, tile):
-        acc = None
-        for unit, w in zip(units, sets):
-            block = jnp.concatenate([slab[p][:, at : at + tile] for p in unit])
-            term = jnp.dot(w, block, preferred_element_type=F32)
-            acc = term if acc is None else acc + term
-        if keeps:
-            keep[:, at : at + tile] = acc[: keeps * n]
-        for i in range(sends):
-            part = acc[(keeps + i) * n : (keeps + i + 1) * n]
-            message[i * (n + TAIL) : i * (n + TAIL) + n, at : at + tile] = part.astype(BF16)
 
 
 def weigh(keeps, sends, logits, energy, slab):
@@ -294,6 +299,7 @@
     return pl.pallas_call(
         functools.partial(weigh_kernel, lots, groups, sizes, len(keeps), len(sends)),
         out_shape=out,
+        scratch_shapes=[pltpu.VMEM((height, width), F32)],
         compiler_params=pltpu.CompilerParams(vmem_limit_bytes=VMEM_LIMIT),
         cost_estimate=pl.CostEstimate(
             flops=2 * height * total * width,

time: 102 us -> 101 us (level)
  waiting for transfers between devices: 32.3 us -> 30 us
  starting transfers between devices: 48.9 us -> 50.8 us
    ppermute x6, waiting for transfers between devices: 16.8 us -> 14.5 us  [shift_x(): return lax.ppermute(value, 'x', [(i, (i + by) % NX) for i in range(NX)])]
    ppermute x6, starting transfers between devices: 9.32 us -> 10.5 us  [shift_x(): return lax.ppermute(value, 'x', [(i, (i + by) % NX) for i in range(NX)])]
where the time goes in v12:
time: 101 us
  starting transfers between devices  50.8 us (50%)
  waiting for transfers between devices  30 us (30%)
  Pallas kernels  18.2 us (18%)
  local copies, waits for them, and re-layouts  1.29 us (1%)
    ppermute x6, starting transfers between devices, along_z(): return lax.ppermute(value, ('z', 'c'), pairs)  16 us
    ppermute x6, waiting for transfers between devices, shift_x(): return lax.ppermute(value, 'x', [(i, (i + by) % NX) for i in range(NX)])  14.5 us
    ppermute x9, starting transfers between devices, swap_cores(): return lax.ppermute(value, 'c', [(0, 1), (1, 0)])  12.1 us
    ppermute x6, starting transfers between devices, shift_x(): return lax.ppermute(value, 'x', [(i, (i + by) % NX) for i in range(NX)])  10.5 us
    ppermute x4, starting transfers between devices, swap_halves(): return lax.ppermute(value, ('y', 'c'), pairs)  9.79 us
    pallas_call x3, Pallas kernels, score(): pl.pallas_call(functools.partial(score_kernel, 0 if whole else len(table)...  8.2 us
    pallas_call x3, Pallas kernels, weigh(): pl.pallas_call(functools.partial(weigh_kernel, lots, groups, sizes, len(k...  8.07 us
    ppermute x4, waiting for transfers between devices, swap_halves(): return lax.ppermute(value, ('y', 'c'), pairs)  5.66 us
  transfers between devices with their start and end apart: 28, of which 15 were waited for; matrix products, arithmetic and copies ran while one was open for 0% of the time, Pallas kernels for 12%

profile of v12, /device:TPU:1, one launch (start us, length us, event | category | flops | bytes accessed | tf_op | source)
XLA Modules:
  0.0 101.1 jit_solution(6445250917178367586)
XLA Ops:
  1.9 6.5 %collective-permute-start = (bf16[256,1024]{1,0:T(8,128)(2,1)S(1)}, bf16[256,1024]{1,0:T(8,128)(2,1)S(1)}, u32[]{:S(2)}, u32[]{:S(2)}) collective-permute-start(bf16[256,1024]{1,0:T(8,128)(2,1)S(1)} %constant_dynamic-slice_fusion.2), channel_id=1, source_target_pairs={{0,8},{1,57},{8,16},{9,1},{16,24},{17,9},{24,32},{25,17},{32,40},{... | collective-permute-start | bytes 1572872 | tf_op jit(solution)/shard_map/ppermute | solution.py:33
  9.6 1.5 %collective-permute-start.1 = (bf16[128,1024]{1,0:T(8,128)(2,1)}, bf16[128,1024]{1,0:T(8,128)(2,1)}, u32[]{:S(2)}, u32[]{:S(2)}) collective-permute-start(bf16[128,1024]{1,0:T(8,128)(2,1)} %centroids.1), channel_id=1, source_target_pairs={{0,192},{64,0},{128,64},{192,128},{1,193},{65,1},{129,65},{193,129... | collective-permute-start | bytes 786440 | tf_op jit(solution)/shard_map/ppermute | solution.py:21
  11.1 4.5 %collective-permute-done.2.refs_4_ = bf16[128,1024]{1,0:T(8,128)(2,1)} collective-permute-done((bf16[128,1024]{1,0:T(8,128)(2,1)}, bf16[128,1024]{1,0:T(8,128)(2,1)}, u32[]{:S(2)}, u32[]{:S(2)}) %collective-permute-start.2) | collective-permute-done | bytes 262176 | tf_op jit(solution)/shard_map/ppermute | solution.py:21
  15.9 2.7 %collective-permute-start.3 = (bf16[256,1024]{1,0:T(8,128)(2,1)S(1)}, bf16[256,1024]{1,0:T(8,128)(2,1)S(1)}, u32[]{:S(2)}, u32[]{:S(2)}) collective-permute-start(bf16[256,1024]{1,0:T(8,128)(2,1)S(1)} %collective-permute-done.refs_9_.refs_4_), channel_id=1, source_target_pairs={{0,8},{1,57},{8,16},{9,1},{16,24},{17,9},{24,32},{25,17},{32,40},{... | collective-permute-start | bytes 1572872 | tf_op jit(solution)/shard_map/ppermute | solution.py:33
  18.5 2.4 %collective-permute-start.4 = (bf16[128,1024]{1,0:T(8,128)(2,1)}, bf16[128,1024]{1,0:T(8,128)(2,1)}, u32[]{:S(2)}, u32[]{:S(2)}) collective-permute-start(bf16[128,1024]{1,0:T(8,128)(2,1)} %collective-permute-done.1.refs_2_), channel_id=1, source_target_pairs={{0,192},{64,0},{128,64},{192,128},{1,193},{65,1},{129,65},{193,129... | collective-permute-start | bytes 786440 | tf_op jit(solution)/shard_map/ppermute | solution.py:21
  20.9 2.7 %collective-permute-start.9 = (bf16[256,1024]{1,0:T(8,128)(2,1)S(1)}, bf16[256,1024]{1,0:T(8,128)(2,1)S(1)}, u32[]{:S(2)}, u32[]{:S(2)}) collective-permute-start(bf16[256,1024]{1,0:T(8,128)(2,1)S(1)} %collective-permute-done.refs_9_.refs_4_), channel_id=1, source_target_pairs={{0,2},{1,7},{2,0},{3,5},{4,6},{5,3},{6,4},{7,1},{8,10},{9,15},{10,... | collective-permute-start | bytes 1572872 | tf_op jit(solution)/shard_map/ppermute | solution.py:45
  23.6 2.2 %collective-permute-done.4.refs_0_ = bf16[128,1024]{1,0:T(8,128)(2,1)} collective-permute-done((bf16[128,1024]{1,0:T(8,128)(2,1)}, bf16[128,1024]{1,0:T(8,128)(2,1)}, u32[]{:S(2)}, u32[]{:S(2)}) %collective-permute-start.4) | collective-permute-done | bytes 262176 | tf_op jit(solution)/shard_map/ppermute | solution.py:21
  25.9 1.9 %collective-permute-start.11 = (bf16[256,1024]{1,0:T(8,128)(2,1)S(1)}, bf16[256,1024]{1,0:T(8,128)(2,1)S(1)}, u32[]{:S(2)}, u32[]{:S(2)}) collective-permute-start(bf16[256,1024]{1,0:T(8,128)(2,1)S(1)} %collective-permute-done.3.refs_11_.refs_6_), channel_id=1, source_target_pairs={{0,8},{1,57},{8,16},{9,1},{16,24},{17,9},{24,32},{25,17},{32,40},{... | collective-permute-start | bytes 1572872 | tf_op jit(solution)/shard_map/ppermute | solution.py:33
  27.8 2.4 %collective-permute-done.9.refs_10_.refs_5_ = bf16[256,1024]{1,0:T(8,128)(2,1)S(1)} collective-permute-done((bf16[256,1024]{1,0:T(8,128)(2,1)S(1)}, bf16[256,1024]{1,0:T(8,128)(2,1)S(1)}, u32[]{:S(2)}, u32[]{:S(2)}) %collective-permute-start.9) | collective-permute-done | bytes 524320 | tf_op jit(solution)/shard_map/ppermute | solution.py:45
  30.2 2.7 %collective-permute-start.10 = (bf16[256,1024]{1,0:T(8,128)(2,1)S(1)}, bf16[256,1024]{1,0:T(8,128)(2,1)}, u32[]{:S(2)}, u32[]{:S(2)}) collective-permute-start(bf16[256,1024]{1,0:T(8,128)(2,1)S(1)} %collective-permute-done.3.refs_11_.refs_6_), channel_id=1, source_target_pairs={{0,2},{1,7},{2,0},{3,5},{4,6},{5,3},{6,4},{7,1},{8,10},{9,15},{10,... | collective-permute-start | bytes 1572872 | tf_op jit(solution)/shard_map/ppermute | solution.py:45
  34.3 3.0 %collective-permute-start.5 = (bf16[128,1024]{1,0:T(8,128)(2,1)}, bf16[128,1024]{1,0:T(8,128)(2,1)}, u32[]{:S(2)}, u32[]{:S(2)}) collective-permute-start(bf16[128,1024]{1,0:T(8,128)(2,1)} %collective-permute-done.4.refs_0_), channel_id=1, source_target_pairs={{0,1},{1,0},{2,3},{3,2},{4,5},{5,4},{6,7},{7,6},{8,9},{9,8},{10,11... | collective-permute-start | bytes 786440 | tf_op jit(solution)/shard_map/ppermute | solution.py:25
  37.9 2.7 %collective-permute-start.12 = (bf16[256,1024]{1,0:T(8,128)(2,1)S(1)}, bf16[256,1024]{1,0:T(8,128)(2,1)S(1)}, u32[]{:S(2)}, u32[]{:S(2)}) collective-permute-start(bf16[256,1024]{1,0:T(8,128)(2,1)S(1)} %collective-permute-done.11.refs_2_.refs_8_), channel_id=1, source_target_pairs={{0,2},{1,7},{2,0},{3,5},{4,6},{5,3},{6,4},{7,1},{8,10},{9,15},{10,... | collective-permute-start | bytes 1572872 | tf_op jit(solution)/shard_map/ppermute | solution.py:45
  40.7 5.7 %shard_map.58 = (bf16[1024,1024]{1,0:T(8,128)(2,1)S(1)}, f32[1024,128]{1,0:T(8,128)S(1)}, f32[1024,1280]{1,0:T(8,128)S(1)}, f32[1,1280]{1,0:T(1,128)S(1)}) custom-call(bf16[128,1024]{1,0:T(8,128)(2,1)} %collective-permute-done.4.refs_0_, bf16[128,1024]{1,0:T(8,128)(2,1)} %collective-permute-done.5.refs_1_, bf16[128,1024]{1,0:T(8,128)(2,1)} %collective-permute-done.1.refs_2_, ...), custom_call_target="tpu_custom_call" | custom-call | flops 5368709120 | bytes 9961472 | tf_op jit(solution)/shard_map/pallas_call | solution.py:220
  46.3 1.7 %collective-permute-start.14 = (bf16[128,1024]{1,0:T(8,128)(2,1)S(1)}, bf16[128,1024]{1,0:T(8,128)(2,1)S(1)}, u32[]{:S(2)}, u32[]{:S(2)}) collective-permute-start(bf16[128,1024]{1,0:T(8,128)(2,1)S(1)} %collective-permute-done.13.refs_2_.refs_10_), channel_id=1, source_target_pairs={{0,2},{1,7},{2,0},{3,5},{4,6},{5,3},{6,4},{7,1},{8,10},{9,15},{10,... | collective-permute-start | bytes 786440 | tf_op jit(solution)/shard_map/ppermute | solution.py:45
  48.0 1.6 %shard_map.59 = (f32[1024,512]{1,0:T(8,128)S(1)}, f32[1,512]{1,0:T(1,128)S(1)}) custom-call(bf16[1024,1024]{1,0:T(8,128)(2,1)S(1)} %get-tuple-element.48.refs_0_, f32[1024,128]{1,0:T(8,128)S(1)} %get-tuple-element.49.refs_1_, bf16[256,1024]{1,0:T(8,128)(2,1)S(1)} %collective-permute-done.11.refs_2_.refs_8_, ...), custom_call_target="tpu_custom_call" | custom-call | flops 2147483648 | bytes 5242880 | tf_op jit(solution)/shard_map/pallas_call | solution.py:220
  49.6 3.2 %collective-permute-done.14.refs_3_.refs_11_ = bf16[128,1024]{1,0:T(8,128)(2,1)S(1)} collective-permute-done((bf16[128,1024]{1,0:T(8,128)(2,1)S(1)}, bf16[128,1024]{1,0:T(8,128)(2,1)S(1)}, u32[]{:S(2)}, u32[]{:S(2)}) %collective-permute-start.14) | collective-permute-done | bytes 262176 | tf_op jit(solution)/shard_map/ppermute | solution.py:45
  53.8 1.6 %collective-permute-start.17 = (f32[16,128]{1,0:T(8,128)S(1)}, f32[16,128]{1,0:T(8,128)S(1)}, u32[]{:S(2)}, u32[]{:S(2)}) collective-permute-start(f32[16,128]{1,0:T(8,128)S(1)} %shard_map.61.own), channel_id=1, source_target_pairs={{0,6},{2,0},{4,2},{6,4},{1,7},{3,1},{5,3},{7,5},{8,14},{10,8},{12,... | collective-permute-start | bytes 24584 | tf_op jit(solution)/shard_map/ppermute | solution.py:37
  56.4 3.1 %collective-permute-done.16.refs_1_ = f32[16,128]{1,0:T(8,128)S(1)} collective-permute-done((f32[16,128]{1,0:T(8,128)S(1)}, f32[16,128]{1,0:T(8,128)S(1)}, u32[]{:S(2)}, u32[]{:S(2)}) %collective-permute-start.16) | collective-permute-done | bytes 8224 | tf_op jit(solution)/shard_map/ppermute | solution.py:37
  59.5 1.6 %collective-permute-start.18 = (f32[16,128]{1,0:T(8,128)S(1)}, f32[16,128]{1,0:T(8,128)S(1)}, u32[]{:S(2)}, u32[]{:S(2)}) collective-permute-start(f32[16,128]{1,0:T(8,128)S(1)} %shard_map.62.mine), channel_id=1, source_target_pairs={{0,1},{1,0},{2,3},{3,2},{4,5},{5,4},{6,7},{7,6},{8,9},{9,8},{10,11... | collective-permute-start | bytes 24584 | tf_op jit(solution)/shard_map/ppermute | solution.py:25
  61.9 2.2 %collective-permute-start.19 = (f32[4,8,128]{2,1,0:T(8,128)S(1)}, f32[4,8,128]{2,1,0:T(8,128)S(1)}, u32[]{:S(2)}, u32[]{:S(2)}) collective-permute-start(f32[4,8,128]{2,1,0:T(8,128)S(1)} %shard_map.63.block), channel_id=1, source_target_pairs={{0,8},{1,57},{8,16},{9,1},{16,24},{17,9},{24,32},{25,17},{32,40},{... | collective-permute-start | bytes 49160 | tf_op jit(solution)/shard_map/ppermute | solution.py:33
  64.9 2.3 %collective-permute-start.20 = (f32[4,8,128]{2,1,0:T(8,128)S(1)}, f32[4,8,128]{2,1,0:T(8,128)S(1)}, u32[]{:S(2)}, u32[]{:S(2)}) collective-permute-start(f32[4,8,128]{2,1,0:T(8,128)S(1)} %collective-permute-done.19.near), channel_id=1, source_target_pairs={{0,1},{1,0},{2,3},{3,2},{4,5},{5,4},{6,7},{7,6},{8,9},{9,8},{10,11... | collective-permute-start | bytes 49160 | tf_op jit(solution)/shard_map/ppermute | solution.py:25
  68.1 2.3 %collective-permute-start.21 = (f32[4,8,128]{2,1,0:T(8,128)S(1)}, f32[4,8,128]{2,1,0:T(8,128)S(1)}, u32[]{:S(2)}, u32[]{:S(2)}) collective-permute-start(f32[4,8,128]{2,1,0:T(8,128)S(1)} %get-tuple-element.55), channel_id=1, source_target_pairs={{0,24},{1,41},{8,32},{9,49},{16,40},{17,57},{24,48},{25,1},{32,56}... | collective-permute-start | bytes 49160 | tf_op jit(solution)/shard_map/ppermute | solution.py:33
  70.4 2.2 %collective-permute-done.21.got = f32[4,8,128]{2,1,0:T(8,128)S(1)} collective-permute-done((f32[4,8,128]{2,1,0:T(8,128)S(1)}, f32[4,8,128]{2,1,0:T(8,128)S(1)}, u32[]{:S(2)}, u32[]{:S(2)}) %collective-permute-start.21) | collective-permute-done | bytes 16416 | tf_op jit(solution)/shard_map/ppermute | solution.py:33
  72.6 2.7 %collective-permute-start.22 = (f32[4,8,128]{2,1,0:T(8,128)S(1)}, f32[4,8,128]{2,1,0:T(8,128)S(1)}, u32[]{:S(2)}, u32[]{:S(2)}) collective-permute-start(f32[4,8,128]{2,1,0:T(8,128)S(1)} %collective-permute-done.21.got), channel_id=1, source_target_pairs={{0,1},{1,0},{2,3},{3,2},{4,5},{5,4},{6,7},{7,6},{8,9},{9,8},{10,11... | collective-permute-start | bytes 49160 | tf_op jit(solution)/shard_map/ppermute | solution.py:25
  76.8 2.9 %shard_map.66 = bf16[432,1024]{1,0:T(8,128)(2,1)S(1)} custom-call(f32[1,2048]{1,0:T(1,128)S(1)} %get-tuple-element.63.energy, f32[1024,1280]{1,0:T(8,128)S(1)} %get-tuple-element.57.refs_0_, f32[1024,512]{1,0:T(8,128)S(1)} %get-tuple-element.58.refs_1_, f32[1024,256]{1,0:T(8,128)S(1)} %get-tuple-element.59.refs_2_, bf16[256,1024]{1,0:T(8,128)(2,1)S(1)} %bitcast.9, ...), custom_call_target="tpu_custom_call" | custom-call | flops 1610612736 | bytes 7340032 | tf_op jit(solution)/shard_map/pallas_call | solution.py:299
  80.1 2.9 %shard_map.67 = (f32[384,1024]{1,0:T(8,128)S(1)}, f32[48,128]{1,0:T(8,128)S(1)}) custom-call(f32[1,2048]{1,0:T(1,128)S(1)} %get-tuple-element.63.energy, f32[1024,1280]{1,0:T(8,128)S(1)} %get-tuple-element.57.refs_0_, f32[1024,512]{1,0:T(8,128)S(1)} %get-tuple-element.58.refs_1_, f32[1024,256]{1,0:T(8,128)S(1)} %get-tuple-element.59.refs_2_, ...), custom_call_target="tpu_custom_call" | custom-call | flops 1610612736 | bytes 7340032 | tf_op jit(solution)/shard_map/pallas_call | solution.py:299
  83.1 2.8 %collective-permute-start.24 = (bf16[144,1024]{1,0:T(8,128)(2,1)S(1)}, bf16[144,1024]{1,0:T(8,128)(2,1)S(1)}, u32[]{:S(2)}, u32[]{:S(2)}) collective-permute-start(bf16[144,1024]{1,0:T(8,128)(2,1)S(1)} %get-tuple-element.62), channel_id=1, source_target_pairs={{0,128},{64,192},{128,0},{192,64},{1,129},{65,193},{129,1},{193,65... | collective-permute-start | bytes 884744 | tf_op jit(solution)/shard_map/ppermute | solution.py:21
  86.5 2.1 %collective-permute-start.27 = (bf16[144,1024]{1,0:T(8,128)(2,1)S(1)}, bf16[144,1024]{1,0:T(8,128)(2,1)S(1)}, u32[]{:S(2)}, u32[]{:S(2)}) collective-permute-start(bf16[144,1024]{1,0:T(8,128)(2,1)S(1)} %get-tuple-element.69), channel_id=1, source_target_pairs={{0,192},{64,0},{128,64},{192,128},{1,193},{65,1},{129,65},{193,129... | collective-permute-start | bytes 884744 | tf_op jit(solution)/shard_map/ppermute | solution.py:21
  88.6 4.6 %collective-permute-done.24.one = bf16[144,1024]{1,0:T(8,128)(2,1)S(1)} collective-permute-done((bf16[144,1024]{1,0:T(8,128)(2,1)S(1)}, bf16[144,1024]{1,0:T(8,128)(2,1)S(1)}, u32[]{:S(2)}, u32[]{:S(2)}) %collective-permute-start.24) | collective-permute-done | bytes 294944 | tf_op jit(solution)/shard_map/ppermute | solution.py:21
  93.2 2.3 %shard_map.69 = (bf16[144,1024]{1,0:T(8,128)(2,1)S(1)}, f32[128,1024]{1,0:T(8,128)S(1)}, f32[16,128]{1,0:T(8,128)S(1)}) custom-call(f32[1,2048]{1,0:T(1,128)S(1)} %get-tuple-element.63.energy, f32[1024,1280]{1,0:T(8,128)S(1)} %get-tuple-element.57.refs_0_, f32[1024,512]{1,0:T(8,128)S(1)} %get-tuple-element.58.refs_1_, ...), custom_call_target="tpu_custom_call" | custom-call | flops 1073741824 | bytes 6291456 | tf_op jit(solution)/shard_map/pallas_call | solution.py:299
  95.5 1.6 %collective-permute-start.25 = (bf16[144,1024]{1,0:T(8,128)(2,1)S(1)}, bf16[144,1024]{1,0:T(8,128)(2,1)S(1)}, u32[]{:S(2)}, u32[]{:S(2)}) collective-permute-start(bf16[144,1024]{1,0:T(8,128)(2,1)S(1)} %get-tuple-element.66), channel_id=1, source_target_pairs={{0,1},{1,0},{2,3},{3,2},{4,5},{5,4},{6,7},{7,6},{8,9},{9,8},{10,11... | collective-permute-start | bytes 884744 | tf_op jit(solution)/shard_map/ppermute | solution.py:25
  97.2 2.8 %collective-permute-done.26.two = bf16[144,1024]{1,0:T(8,128)(2,1)S(1)} collective-permute-done((bf16[144,1024]{1,0:T(8,128)(2,1)S(1)}, bf16[144,1024]{1,0:T(8,128)(2,1)S(1)}, u32[]{:S(2)}, u32[]{:S(2)}) %collective-permute-start.26) | collective-permute-done | bytes 294944 | tf_op jit(solution)/shard_map/ppermute | solution.py:21
  (49 shorter events, 13.0 us)
Async XLA Ops:
  0.6 1.2 %copy-start = (bf16[512,1024]{1,0:T(8,128)(2,1)S(1)}, bf16[512,1024]{1,0:T(8,128)(2,1)}, u32[]{:S(2)}) copy-start(bf16[512,1024]{1,0:T(8,128)(2,1)} %param.3) | copy-start | bytes 3145732
  0.6 40.0 %copy-start.1 = (bf16[128,1024]{1,0:T(8,128)(2,1)S(1)}, bf16[128,1024]{1,0:T(8,128)(2,1)}, u32[]{:S(2)}) copy-start(bf16[128,1024]{1,0:T(8,128)(2,1)} %centroids.1) | copy-start | bytes 786436
  1.9 14.0 %collective-permute-start = (bf16[256,1024]{1,0:T(8,128)(2,1)S(1)}, bf16[256,1024]{1,0:T(8,128)(2,1)S(1)}, u32[]{:S(2)}, u32[]{:S(2)}) collective-permute-start(bf16[256,1024]{1,0:T(8,128)(2,1)S(1)} %constant_dynamic-slice_fusion.2), channel_id=1, source_target_pairs={{0,8},{1,57},{8,16},{9,1},{16,24},{17,9},{24,32},{25,17},{32,40},{... | collective-permute-start | bytes 1572872 | tf_op jit(solution)/shard_map/ppermute | solution.py:33
  8.4 7.2 %collective-permute-start.2 = (bf16[128,1024]{1,0:T(8,128)(2,1)}, bf16[128,1024]{1,0:T(8,128)(2,1)}, u32[]{:S(2)}, u32[]{:S(2)}) collective-permute-start(bf16[128,1024]{1,0:T(8,128)(2,1)} %centroids.1), channel_id=1, source_target_pairs={{0,64},{64,128},{128,192},{192,0},{1,65},{65,129},{129,193},{193,1... | collective-permute-start | bytes 786440 | tf_op jit(solution)/shard_map/ppermute | solution.py:21
  9.6 6.3 %collective-permute-start.1 = (bf16[128,1024]{1,0:T(8,128)(2,1)}, bf16[128,1024]{1,0:T(8,128)(2,1)}, u32[]{:S(2)}, u32[]{:S(2)}) collective-permute-start(bf16[128,1024]{1,0:T(8,128)(2,1)} %centroids.1), channel_id=1, source_target_pairs={{0,192},{64,0},{128,64},{192,128},{1,193},{65,1},{129,65},{193,129... | collective-permute-start | bytes 786440 | tf_op jit(solution)/shard_map/ppermute | solution.py:21
  15.9 10.0 %collective-permute-start.3 = (bf16[256,1024]{1,0:T(8,128)(2,1)S(1)}, bf16[256,1024]{1,0:T(8,128)(2,1)S(1)}, u32[]{:S(2)}, u32[]{:S(2)}) collective-permute-start(bf16[256,1024]{1,0:T(8,128)(2,1)S(1)} %collective-permute-done.refs_9_.refs_4_), channel_id=1, source_target_pairs={{0,8},{1,57},{8,16},{9,1},{16,24},{17,9},{24,32},{25,17},{32,40},{... | collective-permute-start | bytes 1572872 | tf_op jit(solution)/shard_map/ppermute | solution.py:33
  18.5 7.3 %collective-permute-start.4 = (bf16[128,1024]{1,0:T(8,128)(2,1)}, bf16[128,1024]{1,0:T(8,128)(2,1)}, u32[]{:S(2)}, u32[]{:S(2)}) collective-permute-start(bf16[128,1024]{1,0:T(8,128)(2,1)} %collective-permute-done.1.refs_2_), channel_id=1, source_target_pairs={{0,192},{64,0},{128,64},{192,128},{1,193},{65,1},{129,65},{193,129... | collective-permute-start | bytes 786440 | tf_op jit(solution)/shard_map/ppermute | solution.py:21
  20.9 9.3 %collective-permute-start.9 = (bf16[256,1024]{1,0:T(8,128)(2,1)S(1)}, bf16[256,1024]{1,0:T(8,128)(2,1)S(1)}, u32[]{:S(2)}, u32[]{:S(2)}) collective-permute-start(bf16[256,1024]{1,0:T(8,128)(2,1)S(1)} %collective-permute-done.refs_9_.refs_4_), channel_id=1, source_target_pairs={{0,2},{1,7},{2,0},{3,5},{4,6},{5,3},{6,4},{7,1},{8,10},{9,15},{10,... | collective-permute-start | bytes 1572872 | tf_op jit(solution)/shard_map/ppermute | solution.py:45
  25.9 8.4 %collective-permute-start.11 = (bf16[256,1024]{1,0:T(8,128)(2,1)S(1)}, bf16[256,1024]{1,0:T(8,128)(2,1)S(1)}, u32[]{:S(2)}, u32[]{:S(2)}) collective-permute-start(bf16[256,1024]{1,0:T(8,128)(2,1)S(1)} %collective-permute-done.3.refs_11_.refs_6_), channel_id=1, source_target_pairs={{0,8},{1,57},{8,16},{9,1},{16,24},{17,9},{24,32},{25,17},{32,40},{... | collective-permute-start | bytes 1572872 | tf_op jit(solution)/shard_map/ppermute | solution.py:33
  30.2 10.4 %collective-permute-start.10 = (bf16[256,1024]{1,0:T(8,128)(2,1)S(1)}, bf16[256,1024]{1,0:T(8,128)(2,1)}, u32[]{:S(2)}, u32[]{:S(2)}) collective-permute-start(bf16[256,1024]{1,0:T(8,128)(2,1)S(1)} %collective-permute-done.3.refs_11_.refs_6_), channel_id=1, source_target_pairs={{0,2},{1,7},{2,0},{3,5},{4,6},{5,3},{6,4},{7,1},{8,10},{9,15},{10,... | collective-permute-start | bytes 1572872 | tf_op jit(solution)/shard_map/ppermute | solution.py:45
  32.9 4.5 %collective-permute-start.8 = (bf16[128,1024]{1,0:T(8,128)(2,1)}, bf16[128,1024]{1,0:T(8,128)(2,1)}, u32[]{:S(2)}, u32[]{:S(2)}) collective-permute-start(bf16[128,1024]{1,0:T(8,128)(2,1)} %centroids.1), channel_id=1, source_target_pairs={{0,1},{1,0},{2,3},{3,2},{4,5},{5,4},{6,7},{7,6},{8,9},{9,8},{10,11... | collective-permute-start | bytes 786440 | tf_op jit(solution)/shard_map/ppermute | solution.py:25
  32.9 7.8 %collective-permute-start.6 = (bf16[128,1024]{1,0:T(8,128)(2,1)}, bf16[128,1024]{1,0:T(8,128)(2,1)}, u32[]{:S(2)}, u32[]{:S(2)}) collective-permute-start(bf16[128,1024]{1,0:T(8,128)(2,1)} %collective-permute-done.1.refs_2_), channel_id=1, source_target_pairs={{0,1},{1,0},{2,3},{3,2},{4,5},{5,4},{6,7},{7,6},{8,9},{9,8},{10,11... | collective-permute-start | bytes 786440 | tf_op jit(solution)/shard_map/ppermute | solution.py:25
  33.4 4.5 %collective-permute-start.7 = (bf16[128,1024]{1,0:T(8,128)(2,1)}, bf16[128,1024]{1,0:T(8,128)(2,1)}, u32[]{:S(2)}, u32[]{:S(2)}) collective-permute-start(bf16[128,1024]{1,0:T(8,128)(2,1)} %collective-permute-done.2.refs_4_), channel_id=1, source_target_pairs={{0,1},{1,0},{2,3},{3,2},{4,5},{5,4},{6,7},{7,6},{8,9},{9,8},{10,11... | collective-permute-start | bytes 786440 | tf_op jit(solution)/shard_map/ppermute | solution.py:25
  34.3 6.3 %collective-permute-start.5 = (bf16[128,1024]{1,0:T(8,128)(2,1)}, bf16[128,1024]{1,0:T(8,128)(2,1)}, u32[]{:S(2)}, u32[]{:S(2)}) collective-permute-start(bf16[128,1024]{1,0:T(8,128)(2,1)} %collective-permute-done.4.refs_0_), channel_id=1, source_target_pairs={{0,1},{1,0},{2,3},{3,2},{4,5},{5,4},{6,7},{7,6},{8,9},{9,8},{10,11... | collective-permute-start | bytes 786440 | tf_op jit(solution)/shard_map/ppermute | solution.py:25
  37.4 9.0 %collective-permute-start.13 = (bf16[128,1024]{1,0:T(8,128)(2,1)S(1)}, bf16[128,1024]{1,0:T(8,128)(2,1)S(1)}, u32[]{:S(2)}, u32[]{:S(2)}) collective-permute-start(bf16[128,1024]{1,0:T(8,128)(2,1)S(1)} %constant_dynamic-slice_fusion), channel_id=1, source_target_pairs={{0,8},{1,57},{8,16},{9,1},{16,24},{17,9},{24,32},{25,17},{32,40},{... | collective-permute-start | bytes 786440 | tf_op jit(solution)/shard_map/ppermute | solution.py:33
  37.9 10.1 %collective-permute-start.12 = (bf16[256,1024]{1,0:T(8,128)(2,1)S(1)}, bf16[256,1024]{1,0:T(8,128)(2,1)S(1)}, u32[]{:S(2)}, u32[]{:S(2)}) collective-permute-start(bf16[256,1024]{1,0:T(8,128)(2,1)S(1)} %collective-permute-done.11.refs_2_.refs_8_), channel_id=1, source_target_pairs={{0,2},{1,7},{2,0},{3,5},{4,6},{5,3},{6,4},{7,1},{8,10},{9,15},{10,... | collective-permute-start | bytes 1572872 | tf_op jit(solution)/shard_map/ppermute | solution.py:45
  46.3 6.5 %collective-permute-start.14 = (bf16[128,1024]{1,0:T(8,128)(2,1)S(1)}, bf16[128,1024]{1,0:T(8,128)(2,1)S(1)}, u32[]{:S(2)}, u32[]{:S(2)}) collective-permute-start(bf16[128,1024]{1,0:T(8,128)(2,1)S(1)} %collective-permute-done.13.refs_2_.refs_10_), channel_id=1, source_target_pairs={{0,2},{1,7},{2,0},{3,5},{4,6},{5,3},{6,4},{7,1},{8,10},{9,15},{10,... | collective-permute-start | bytes 786440 | tf_op jit(solution)/shard_map/ppermute | solution.py:45
  53.8 2.6 %collective-permute-start.17 = (f32[16,128]{1,0:T(8,128)S(1)}, f32[16,128]{1,0:T(8,128)S(1)}, u32[]{:S(2)}, u32[]{:S(2)}) collective-permute-start(f32[16,128]{1,0:T(8,128)S(1)} %shard_map.61.own), channel_id=1, source_target_pairs={{0,6},{2,0},{4,2},{6,4},{1,7},{3,1},{5,3},{7,5},{8,14},{10,8},{12,... | collective-permute-start | bytes 24584 | tf_op jit(solution)/shard_map/ppermute | solution.py:37
  55.4 4.0 %collective-permute-start.16 = (f32[16,128]{1,0:T(8,128)S(1)}, f32[16,128]{1,0:T(8,128)S(1)}, u32[]{:S(2)}, u32[]{:S(2)}) collective-permute-start(f32[16,128]{1,0:T(8,128)S(1)} %shard_map.61.own), channel_id=1, source_target_pairs={{0,4},{2,6},{4,0},{6,2},{1,5},{3,7},{5,1},{7,3},{8,12},{10,14},{12... | collective-permute-start | bytes 24584 | tf_op jit(solution)/shard_map/ppermute | solution.py:37
  55.4 4.0 %collective-permute-start.15 = (f32[16,128]{1,0:T(8,128)S(1)}, f32[16,128]{1,0:T(8,128)S(1)}, u32[]{:S(2)}, u32[]{:S(2)}) collective-permute-start(f32[16,128]{1,0:T(8,128)S(1)} %shard_map.61.own), channel_id=1, source_target_pairs={{0,2},{2,4},{4,6},{6,0},{1,3},{3,5},{5,7},{7,1},{8,10},{10,12},{12... | collective-permute-start | bytes 24584 | tf_op jit(solution)/shard_map/ppermute | solution.py:37
  59.5 2.4 %collective-permute-start.18 = (f32[16,128]{1,0:T(8,128)S(1)}, f32[16,128]{1,0:T(8,128)S(1)}, u32[]{:S(2)}, u32[]{:S(2)}) collective-permute-start(f32[16,128]{1,0:T(8,128)S(1)} %shard_map.62.mine), channel_id=1, source_target_pairs={{0,1},{1,0},{2,3},{3,2},{4,5},{5,4},{6,7},{7,6},{8,9},{9,8},{10,11... | collective-permute-start | bytes 24584 | tf_op jit(solution)/shard_map/ppermute | solution.py:25
  61.9 3.0 %collective-permute-start.19 = (f32[4,8,128]{2,1,0:T(8,128)S(1)}, f32[4,8,128]{2,1,0:T(8,128)S(1)}, u32[]{:S(2)}, u32[]{:S(2)}) collective-permute-start(f32[4,8,128]{2,1,0:T(8,128)S(1)} %shard_map.63.block), channel_id=1, source_target_pairs={{0,8},{1,57},{8,16},{9,1},{16,24},{17,9},{24,32},{25,17},{32,40},{... | collective-permute-start | bytes 49160 | tf_op jit(solution)/shard_map/ppermute | solution.py:33
  64.9 3.2 %collective-permute-start.20 = (f32[4,8,128]{2,1,0:T(8,128)S(1)}, f32[4,8,128]{2,1,0:T(8,128)S(1)}, u32[]{:S(2)}, u32[]{:S(2)}) collective-permute-start(f32[4,8,128]{2,1,0:T(8,128)S(1)} %collective-permute-done.19.near), channel_id=1, source_target_pairs={{0,1},{1,0},{2,3},{3,2},{4,5},{5,4},{6,7},{7,6},{8,9},{9,8},{10,11... | collective-permute-start | bytes 49160 | tf_op jit(solution)/shard_map/ppermute | solution.py:25
  68.1 4.5 %collective-permute-start.21 = (f32[4,8,128]{2,1,0:T(8,128)S(1)}, f32[4,8,128]{2,1,0:T(8,128)S(1)}, u32[]{:S(2)}, u32[]{:S(2)}) collective-permute-start(f32[4,8,128]{2,1,0:T(8,128)S(1)} %get-tuple-element.55), channel_id=1, source_target_pairs={{0,24},{1,41},{8,32},{9,49},{16,40},{17,57},{24,48},{25,1},{32,56}... | collective-permute-start | bytes 49160 | tf_op jit(solution)/shard_map/ppermute | solution.py:33
  72.6 3.5 %collective-permute-start.22 = (f32[4,8,128]{2,1,0:T(8,128)S(1)}, f32[4,8,128]{2,1,0:T(8,128)S(1)}, u32[]{:S(2)}, u32[]{:S(2)}) collective-permute-start(f32[4,8,128]{2,1,0:T(8,128)S(1)} %collective-permute-done.21.got), channel_id=1, source_target_pairs={{0,1},{1,0},{2,3},{3,2},{4,5},{5,4},{6,7},{7,6},{8,9},{9,8},{10,11... | collective-permute-start | bytes 49160 | tf_op jit(solution)/shard_map/ppermute | solution.py:25
  79.6 3.3 %collective-permute-start.23 = (bf16[432,1024]{1,0:T(8,128)(2,1)S(1)}, bf16[432,1024]{1,0:T(8,128)(2,1)S(1)}, u32[]{:S(2)}, u32[]{:S(2)}) collective-permute-start(bf16[432,1024]{1,0:T(8,128)(2,1)S(1)} %shard_map.66), channel_id=1, source_target_pairs={{0,1},{1,0},{2,3},{3,2},{4,5},{5,4},{6,7},{7,6},{8,9},{9,8},{10,11... | collective-permute-start | bytes 2654216 | tf_op jit(solution)/shard_map/ppermute | solution.py:25
  83.1 10.1 %collective-permute-start.24 = (bf16[144,1024]{1,0:T(8,128)(2,1)S(1)}, bf16[144,1024]{1,0:T(8,128)(2,1)S(1)}, u32[]{:S(2)}, u32[]{:S(2)}) collective-permute-start(bf16[144,1024]{1,0:T(8,128)(2,1)S(1)} %get-tuple-element.62), channel_id=1, source_target_pairs={{0,128},{64,192},{128,0},{192,64},{1,129},{65,193},{129,1},{193,65... | collective-permute-start | bytes 884744 | tf_op jit(solution)/shard_map/ppermute | solution.py:21
  85.9 14.0 %collective-permute-start.26 = (bf16[144,1024]{1,0:T(8,128)(2,1)S(1)}, bf16[144,1024]{1,0:T(8,128)(2,1)S(1)}, u32[]{:S(2)}, u32[]{:S(2)}) collective-permute-start(bf16[144,1024]{1,0:T(8,128)(2,1)S(1)} %get-tuple-element.68), channel_id=1, source_target_pairs={{0,64},{64,128},{128,192},{192,0},{1,65},{65,129},{129,193},{193,1... | collective-permute-start | bytes 884744 | tf_op jit(solution)/shard_map/ppermute | solution.py:21
  86.5 13.4 %copy-start.2 = (f32[128]{0:T(128)S(1)}, f32[128]{0:T(128)}, u32[]{:S(2)}) copy-start(f32[128]{0:T(128)} %param.5) | copy-start | bytes 1540
  86.5 13.4 %collective-permute-start.27 = (bf16[144,1024]{1,0:T(8,128)(2,1)S(1)}, bf16[144,1024]{1,0:T(8,128)(2,1)S(1)}, u32[]{:S(2)}, u32[]{:S(2)}) collective-permute-start(bf16[144,1024]{1,0:T(8,128)(2,1)S(1)} %get-tuple-element.69), channel_id=1, source_target_pairs={{0,192},{64,0},{128,64},{192,128},{1,193},{65,1},{129,65},{193,129... | collective-permute-start | bytes 884744 | tf_op jit(solution)/shard_map/ppermute | solution.py:21
  95.5 4.4 %collective-permute-start.25 = (bf16[144,1024]{1,0:T(8,128)(2,1)S(1)}, bf16[144,1024]{1,0:T(8,128)(2,1)S(1)}, u32[]{:S(2)}, u32[]{:S(2)}) collective-permute-start(bf16[144,1024]{1,0:T(8,128)(2,1)S(1)} %get-tuple-element.66), channel_id=1, source_target_pairs={{0,1},{1,0},{2,3},{3,2},{4,5},{5,4},{6,7},{7,6},{8,9},{9,8},{10,11... | collective-permute-start | bytes 884744 | tf_op jit(solution)/shard_map/ppermute | solution.py:25

commit v13 on v12

--- a/solution.py
+++ b/solution.py
@@ -356,13 +356,14 @@
     half, sub = rows // 2, rows // 4
     h = lax.rem(y, 2)
     place = jnp.concatenate([jnp.full((4, sub), c, F32), jnp.full((4, sub), h, F32)])
-    place, embeddings = lax.optimization_barrier((place, embeddings))
+    core, start_c, start_h = (v.astype(jnp.uint32) for v in (c, c * sub, h * half))
+    place, embeddings, core, start_c, start_h = lax.optimization_barrier((place, embeddings, core, start_c, start_h))
 
     near = {0: centroids, 1: shift_x(centroids, -1), 3: shift_x(centroids, 1)}
 
-    mine = lax.dynamic_slice_in_dim(embeddings, h * half, half, 0)
+    mine = lax.dynamic_slice_in_dim(embeddings, start_h, half, 0)
     one = along_z(mine, 1)
-    own = lax.dynamic_slice_in_dim(embeddings.reshape(2, 2, sub, width), c, 1, 1).reshape(half, width)
+    own = lax.dynamic_slice_in_dim(embeddings.reshape(2, 2, sub, width), core, 1, 1).reshape(half, width)
     one, near[1], near[3] = lax.optimization_barrier((one, near[1], near[3]))
     near[2] = shift_x(near[1], -1)
     first = swap_halves(one)
@@ -374,7 +375,7 @@
     fixed = lambda v: pltpu.with_memory_space_constraint(v, pltpu.VMEM) if PIN else v
     table = [fixed(v) for d in ORDER for v in (near[d], swap_cores(near[d]))]
 
-    four = along_z(lax.dynamic_slice_in_dim(three, c * sub, sub, 0), 1)
+    four = along_z(lax.dynamic_slice_in_dim(three, start_c, sub, 0), 1)
     lots = [[fixed(v) for v in (own, one, first, two, swap_halves(two))]]
     *table, scores, energy = score(table, lots[0])
     table, logits, local = [fixed(v) for v in table], [scores], [energy]

time: 101 us -> 99.5 us (0.985)
  Pallas kernels: 18.2 us -> 13.4 us
  waiting for transfers between devices: 30 us -> 31.7 us
  starting transfers between devices: 50.8 us -> 52 us
    pallas_call x3, Pallas kernels: 8.07 us -> 4.94 us  [weigh(): pl.pallas_call(functools.partial(weigh_kernel, lots, groups, sizes, len(k...]
    ppermute x9, starting transfers between devices: 12.1 us -> 15.2 us  [swap_cores(): return lax.ppermute(value, 'c', [(0, 1), (1, 0)])]
    ppermute x6, starting transfers between devices: 16 us -> 14.3 us  [along_z(): return lax.ppermute(value, ('z', 'c'), pairs)]
    pallas_call x3, Pallas kernels: 8.2 us -> 6.52 us  [score(): pl.pallas_call(functools.partial(score_kernel, 0 if whole else len(table)...]
  transfers between devices with their start and end apart: 28 -> 28, of which waited for: 15 -> 17; matrix products, arithmetic and copies ran while one was open for 0% -> 0% of each run, Pallas kernels for 12% -> 9%
where the time goes in v13:
time: 99.5 us; the launch traced here: 99.4 us
  starting transfers between devices  52 us (52%)
  waiting for transfers between devices  31.7 us (32%)
  Pallas kernels  13.4 us (13%)
  local copies, waits for them, and re-layouts  1.43 us (1%)
    ppermute x9, starting transfers between devices, swap_cores(): return lax.ppermute(value, 'c', [(0, 1), (1, 0)])  15.2 us
    ppermute x6, waiting for transfers between devices, shift_x(): return lax.ppermute(value, 'x', [(i, (i + by) % NX) for i in range(NX)])  14.9 us
    ppermute x6, starting transfers between devices, along_z(): return lax.ppermute(value, ('z', 'c'), pairs)  14.3 us
    ppermute x6, starting transfers between devices, shift_x(): return lax.ppermute(value, 'x', [(i, (i + by) % NX) for i in range(NX)])  10.5 us
    ppermute x4, starting transfers between devices, swap_halves(): return lax.ppermute(value, ('y', 'c'), pairs)  9.66 us
    pallas_call x3, Pallas kernels, score(): pl.pallas_call(functools.partial(score_kernel, 0 if whole else len(table)...  6.52 us
    ppermute x4, waiting for transfers between devices, swap_halves(): return lax.ppermute(value, ('y', 'c'), pairs)  5.78 us
    ppermute x6, waiting for transfers between devices, along_z(): return lax.ppermute(value, ('z', 'c'), pairs)  4.99 us
  transfers between devices with their start and end apart: 28, of which 17 were waited for; matrix products, arithmetic and copies ran while one was open for 0% of the time, Pallas kernels for 9%

profile of v13, /device:TPU:1, one launch (start us, length us, event | category | flops | bytes accessed | tf_op | source)
XLA Modules:
  0.0 99.4 jit_solution(15188352895738227832)
XLA Ops:
  2.0 6.5 %collective-permute-start = (bf16[256,1024]{1,0:T(8,128)(2,1)S(1)}, bf16[256,1024]{1,0:T(8,128)(2,1)S(1)}, u32[]{:S(2)}, u32[]{:S(2)}) collective-permute-start(bf16[256,1024]{1,0:T(8,128)(2,1)S(1)} %constant_dynamic-slice_fusion.2), channel_id=1, source_target_pairs={{0,8},{1,57},{8,16},{9,1},{16,24},{17,9},{24,32},{25,17},{32,40},{... | collective-permute-start | bytes 1572872 | tf_op jit(solution)/shard_map/ppermute | solution.py:33
  9.7 1.5 %collective-permute-start.1 = (bf16[128,1024]{1,0:T(8,128)(2,1)}, bf16[128,1024]{1,0:T(8,128)(2,1)S(1)}, u32[]{:S(2)}, u32[]{:S(2)}) collective-permute-start(bf16[128,1024]{1,0:T(8,128)(2,1)} %centroids.1), channel_id=1, source_target_pairs={{0,192},{64,0},{128,64},{192,128},{1,193},{65,1},{129,65},{193,129... | collective-permute-start | bytes 786440 | tf_op jit(solution)/shard_map/ppermute | solution.py:21
  11.2 4.5 %collective-permute-done.2.refs_4_ = bf16[128,1024]{1,0:T(8,128)(2,1)S(1)} collective-permute-done((bf16[128,1024]{1,0:T(8,128)(2,1)}, bf16[128,1024]{1,0:T(8,128)(2,1)S(1)}, u32[]{:S(2)}, u32[]{:S(2)}) %collective-permute-start.2) | collective-permute-done | bytes 262176 | tf_op jit(solution)/shard_map/ppermute | solution.py:21
  16.0 2.5 %collective-permute-start.3 = (bf16[256,1024]{1,0:T(8,128)(2,1)S(1)}, bf16[256,1024]{1,0:T(8,128)(2,1)S(1)}, u32[]{:S(2)}, u32[]{:S(2)}) collective-permute-start(bf16[256,1024]{1,0:T(8,128)(2,1)S(1)} %collective-permute-done.refs_9_.refs_4_), channel_id=1, source_target_pairs={{0,8},{1,57},{8,16},{9,1},{16,24},{17,9},{24,32},{25,17},{32,40},{... | collective-permute-start | bytes 1572872 | tf_op jit(solution)/shard_map/ppermute | solution.py:33
  18.5 2.4 %collective-permute-start.4 = (bf16[128,1024]{1,0:T(8,128)(2,1)S(1)}, bf16[128,1024]{1,0:T(8,128)(2,1)S(1)}, u32[]{:S(2)}, u32[]{:S(2)}) collective-permute-start(bf16[128,1024]{1,0:T(8,128)(2,1)S(1)} %collective-permute-done.1.refs_2_), channel_id=1, source_target_pairs={{0,192},{64,0},{128,64},{192,128},{1,193},{65,1},{129,65},{193,129... | collective-permute-start | bytes 786440 | tf_op jit(solution)/shard_map/ppermute | solution.py:21
  20.9 2.7 %collective-permute-start.9 = (bf16[256,1024]{1,0:T(8,128)(2,1)S(1)}, bf16[256,1024]{1,0:T(8,128)(2,1)S(1)}, u32[]{:S(2)}, u32[]{:S(2)}) collective-permute-start(bf16[256,1024]{1,0:T(8,128)(2,1)S(1)} %collective-permute-done.refs_9_.refs_4_), channel_id=1, source_target_pairs={{0,2},{1,7},{2,0},{3,5},{4,6},{5,3},{6,4},{7,1},{8,10},{9,15},{10,... | collective-permute-start | bytes 1572872 | tf_op jit(solution)/shard_map/ppermute | solution.py:45
  23.6 2.0 %collective-permute-done.4.refs_0_ = bf16[128,1024]{1,0:T(8,128)(2,1)S(1)} collective-permute-done((bf16[128,1024]{1,0:T(8,128)(2,1)S(1)}, bf16[128,1024]{1,0:T(8,128)(2,1)S(1)}, u32[]{:S(2)}, u32[]{:S(2)}) %collective-permute-start.4) | collective-permute-done | bytes 262176 | tf_op jit(solution)/shard_map/ppermute | solution.py:21
  25.7 2.1 %collective-permute-start.11 = (bf16[256,1024]{1,0:T(8,128)(2,1)S(1)}, bf16[256,1024]{1,0:T(8,128)(2,1)S(1)}, u32[]{:S(2)}, u32[]{:S(2)}) collective-permute-start(bf16[256,1024]{1,0:T(8,128)(2,1)S(1)} %collective-permute-done.3.refs_11_.refs_6_), channel_id=1, source_target_pairs={{0,8},{1,57},{8,16},{9,1},{16,24},{17,9},{24,32},{25,17},{32,40},{... | collective-permute-start | bytes 1572872 | tf_op jit(solution)/shard_map/ppermute | solution.py:33
  27.8 2.4 %collective-permute-done.9.refs_10_.refs_5_ = bf16[256,1024]{1,0:T(8,128)(2,1)S(1)} collective-permute-done((bf16[256,1024]{1,0:T(8,128)(2,1)S(1)}, bf16[256,1024]{1,0:T(8,128)(2,1)S(1)}, u32[]{:S(2)}, u32[]{:S(2)}) %collective-permute-start.9) | collective-permute-done | bytes 524320 | tf_op jit(solution)/shard_map/ppermute | solution.py:45
  30.2 2.7 %collective-permute-start.10 = (bf16[256,1024]{1,0:T(8,128)(2,1)S(1)}, bf16[256,1024]{1,0:T(8,128)(2,1)S(1)}, u32[]{:S(2)}, u32[]{:S(2)}) collective-permute-start(bf16[256,1024]{1,0:T(8,128)(2,1)S(1)} %collective-permute-done.3.refs_11_.refs_6_), channel_id=1, source_target_pairs={{0,2},{1,7},{2,0},{3,5},{4,6},{5,3},{6,4},{7,1},{8,10},{9,15},{10,... | collective-permute-start | bytes 1572872 | tf_op jit(solution)/shard_map/ppermute | solution.py:45
  34.0 3.4 %collective-permute-start.5 = (bf16[128,1024]{1,0:T(8,128)(2,1)S(1)}, bf16[128,1024]{1,0:T(8,128)(2,1)S(1)}, u32[]{:S(2)}, u32[]{:S(2)}) collective-permute-start(bf16[128,1024]{1,0:T(8,128)(2,1)S(1)} %collective-permute-done.4.refs_0_), channel_id=1, source_target_pairs={{0,1},{1,0},{2,3},{3,2},{4,5},{5,4},{6,7},{7,6},{8,9},{9,8},{10,11... | collective-permute-start | bytes 786440 | tf_op jit(solution)/shard_map/ppermute | solution.py:25
  37.9 2.7 %collective-permute-start.12 = (bf16[256,1024]{1,0:T(8,128)(2,1)S(1)}, bf16[256,1024]{1,0:T(8,128)(2,1)S(1)}, u32[]{:S(2)}, u32[]{:S(2)}) collective-permute-start(bf16[256,1024]{1,0:T(8,128)(2,1)S(1)} %collective-permute-done.11.refs_2_.refs_8_), channel_id=1, source_target_pairs={{0,2},{1,7},{2,0},{3,5},{4,6},{5,3},{6,4},{7,1},{8,10},{9,15},{10,... | collective-permute-start | bytes 1572872 | tf_op jit(solution)/shard_map/ppermute | solution.py:45
  40.7 4.0 %shard_map.58 = (bf16[1024,1024]{1,0:T(8,128)(2,1)S(1)}, f32[1024,128]{1,0:T(8,128)S(1)}, f32[1024,1280]{1,0:T(8,128)S(1)}, f32[1,1280]{1,0:T(1,128)S(1)}) custom-call(bf16[128,1024]{1,0:T(8,128)(2,1)S(1)} %collective-permute-done.4.refs_0_, bf16[128,1024]{1,0:T(8,128)(2,1)S(1)} %collective-permute-done.5.refs_1_, ...), custom_call_target="tpu_custom_call" | custom-call | flops 5368709120 | bytes 9961472 | tf_op jit(solution)/shard_map/pallas_call | solution.py:220
  44.7 1.5 %collective-permute-start.14 = (bf16[128,1024]{1,0:T(8,128)(2,1)S(1)}, bf16[128,1024]{1,0:T(8,128)(2,1)S(1)}, u32[]{:S(2)}, u32[]{:S(2)}) collective-permute-start(bf16[128,1024]{1,0:T(8,128)(2,1)S(1)} %collective-permute-done.13.refs_2_.refs_10_), channel_id=1, source_target_pairs={{0,2},{1,7},{2,0},{3,5},{4,6},{5,3},{6,4},{7,1},{8,10},{9,15},{10,... | collective-permute-start | bytes 786440 | tf_op jit(solution)/shard_map/ppermute | solution.py:45
  47.2 1.6 %shard_map.59 = (f32[1024,512]{1,0:T(8,128)S(1)}, f32[1,512]{1,0:T(1,128)S(1)}) custom-call(bf16[1024,1024]{1,0:T(8,128)(2,1)S(1)} %get-tuple-element.53.refs_0_, f32[1024,128]{1,0:T(8,128)S(1)} %get-tuple-element.54.refs_1_, bf16[256,1024]{1,0:T(8,128)(2,1)S(1)} %collective-permute-done.11.refs_2_.refs_8_, ...), custom_call_target="tpu_custom_call" | custom-call | flops 2147483648 | bytes 5242880 | tf_op jit(solution)/shard_map/pallas_call | solution.py:220
  48.9 2.3 %collective-permute-done.14.refs_3_.refs_11_ = bf16[128,1024]{1,0:T(8,128)(2,1)S(1)} collective-permute-done((bf16[128,1024]{1,0:T(8,128)(2,1)S(1)}, bf16[128,1024]{1,0:T(8,128)(2,1)S(1)}, u32[]{:S(2)}, u32[]{:S(2)}) %collective-permute-start.14) | collective-permute-done | bytes 262176 | tf_op jit(solution)/shard_map/ppermute | solution.py:45
  52.1 1.6 %collective-permute-start.17 = (f32[16,128]{1,0:T(8,128)S(1)}, f32[16,128]{1,0:T(8,128)S(1)}, u32[]{:S(2)}, u32[]{:S(2)}) collective-permute-start(f32[16,128]{1,0:T(8,128)S(1)} %shard_map.61.own), channel_id=1, source_target_pairs={{0,6},{2,0},{4,2},{6,4},{1,7},{3,1},{5,3},{7,5},{8,14},{10,8},{12,... | collective-permute-start | bytes 24584 | tf_op jit(solution)/shard_map/ppermute | solution.py:37
  54.7 3.0 %collective-permute-done.16.refs_1_ = f32[16,128]{1,0:T(8,128)S(1)} collective-permute-done((f32[16,128]{1,0:T(8,128)S(1)}, f32[16,128]{1,0:T(8,128)S(1)}, u32[]{:S(2)}, u32[]{:S(2)}) %collective-permute-start.16) | collective-permute-done | bytes 8224 | tf_op jit(solution)/shard_map/ppermute | solution.py:37
  57.8 3.4 %collective-permute-start.18 = (f32[16,128]{1,0:T(8,128)S(1)}, f32[16,128]{1,0:T(8,128)S(1)}, u32[]{:S(2)}, u32[]{:S(2)}) collective-permute-start(f32[16,128]{1,0:T(8,128)S(1)} %shard_map.62.mine), channel_id=1, source_target_pairs={{0,1},{1,0},{2,3},{3,2},{4,5},{5,4},{6,7},{7,6},{8,9},{9,8},{10,11... | collective-permute-start | bytes 24584 | tf_op jit(solution)/shard_map/ppermute | solution.py:25
  63.1 1.6 %collective-permute-done.19.near = f32[4,8,128]{2,1,0:T(8,128)S(1)} collective-permute-done((f32[4,8,128]{2,1,0:T(8,128)S(1)}, f32[4,8,128]{2,1,0:T(8,128)S(1)}, u32[]{:S(2)}, u32[]{:S(2)}) %collective-permute-start.19) | collective-permute-done | bytes 16416 | tf_op jit(solution)/shard_map/ppermute | solution.py:33
  64.7 2.7 %collective-permute-start.20 = (f32[4,8,128]{2,1,0:T(8,128)S(1)}, f32[4,8,128]{2,1,0:T(8,128)S(1)}, u32[]{:S(2)}, u32[]{:S(2)}) collective-permute-start(f32[4,8,128]{2,1,0:T(8,128)S(1)} %collective-permute-done.19.near), channel_id=1, source_target_pairs={{0,1},{1,0},{2,3},{3,2},{4,5},{5,4},{6,7},{7,6},{8,9},{9,8},{10,11... | collective-permute-start | bytes 49160 | tf_op jit(solution)/shard_map/ppermute | solution.py:25
  68.3 1.7 %collective-permute-start.21 = (f32[4,8,128]{2,1,0:T(8,128)S(1)}, f32[4,8,128]{2,1,0:T(8,128)S(1)}, u32[]{:S(2)}, u32[]{:S(2)}) collective-permute-start(f32[4,8,128]{2,1,0:T(8,128)S(1)} %get-tuple-element.61), channel_id=1, source_target_pairs={{0,24},{1,41},{8,32},{9,49},{16,40},{17,57},{24,48},{25,1},{32,56}... | collective-permute-start | bytes 49160 | tf_op jit(solution)/shard_map/ppermute | solution.py:33
  70.0 2.8 %collective-permute-done.21.got = f32[4,8,128]{2,1,0:T(8,128)S(1)} collective-permute-done((f32[4,8,128]{2,1,0:T(8,128)S(1)}, f32[4,8,128]{2,1,0:T(8,128)S(1)}, u32[]{:S(2)}, u32[]{:S(2)}) %collective-permute-start.21) | collective-permute-done | bytes 16416 | tf_op jit(solution)/shard_map/ppermute | solution.py:33
  72.7 2.7 %collective-permute-start.22 = (f32[4,8,128]{2,1,0:T(8,128)S(1)}, f32[4,8,128]{2,1,0:T(8,128)S(1)}, u32[]{:S(2)}, u32[]{:S(2)}) collective-permute-start(f32[4,8,128]{2,1,0:T(8,128)S(1)} %collective-permute-done.21.got), channel_id=1, source_target_pairs={{0,1},{1,0},{2,3},{3,2},{4,5},{5,4},{6,7},{7,6},{8,9},{9,8},{10,11... | collective-permute-start | bytes 49160 | tf_op jit(solution)/shard_map/ppermute | solution.py:25
  76.9 1.8 %shard_map.66 = bf16[432,1024]{1,0:T(8,128)(2,1)S(1)} custom-call(f32[1,2048]{1,0:T(1,128)S(1)} %get-tuple-element.69.energy, f32[1024,1280]{1,0:T(8,128)S(1)} %get-tuple-element.63.refs_0_, f32[1024,512]{1,0:T(8,128)S(1)} %get-tuple-element.64.refs_1_, f32[1024,256]{1,0:T(8,128)S(1)} %get-tuple-element.65.refs_2_, bf16[256,1024]{1,0:T(8,128)(2,1)S(1)} %bitcast.9, ...), custom_call_target="tpu_custom_call" | custom-call | flops 1610612736 | bytes 7340032 | tf_op jit(solution)/shard_map/pallas_call | solution.py:299
  79.2 1.8 %shard_map.67 = (f32[384,1024]{1,0:T(8,128)S(1)}, f32[48,128]{1,0:T(8,128)S(1)}) custom-call(f32[1,2048]{1,0:T(1,128)S(1)} %get-tuple-element.69.energy, f32[1024,1280]{1,0:T(8,128)S(1)} %get-tuple-element.63.refs_0_, f32[1024,512]{1,0:T(8,128)S(1)} %get-tuple-element.64.refs_1_, f32[1024,256]{1,0:T(8,128)S(1)} %get-tuple-element.65.refs_2_, ...), custom_call_target="tpu_custom_call" | custom-call | flops 1610612736 | bytes 7340032 | tf_op jit(solution)/shard_map/pallas_call | solution.py:299
  81.4 2.8 %collective-permute-start.24 = (bf16[144,1024]{1,0:T(8,128)(2,1)S(1)}, bf16[144,1024]{1,0:T(8,128)(2,1)S(1)}, u32[]{:S(2)}, u32[]{:S(2)}) collective-permute-start(bf16[144,1024]{1,0:T(8,128)(2,1)S(1)} %get-tuple-element.68), channel_id=1, source_target_pairs={{0,128},{64,192},{128,0},{192,64},{1,129},{65,193},{129,1},{193,65... | collective-permute-start | bytes 884744 | tf_op jit(solution)/shard_map/ppermute | solution.py:21
  84.5 2.4 %collective-permute-start.27 = (bf16[144,1024]{1,0:T(8,128)(2,1)S(1)}, bf16[144,1024]{1,0:T(8,128)(2,1)S(1)}, u32[]{:S(2)}, u32[]{:S(2)}) collective-permute-start(bf16[144,1024]{1,0:T(8,128)(2,1)S(1)} %get-tuple-element.75), channel_id=1, source_target_pairs={{0,192},{64,0},{128,64},{192,128},{1,193},{65,1},{129,65},{193,129... | collective-permute-start | bytes 884744 | tf_op jit(solution)/shard_map/ppermute | solution.py:21
  86.9 4.4 %collective-permute-done.24.one = bf16[144,1024]{1,0:T(8,128)(2,1)S(1)} collective-permute-done((bf16[144,1024]{1,0:T(8,128)(2,1)S(1)}, bf16[144,1024]{1,0:T(8,128)(2,1)S(1)}, u32[]{:S(2)}, u32[]{:S(2)}) %collective-permute-start.24) | collective-permute-done | bytes 294944 | tf_op jit(solution)/shard_map/ppermute | solution.py:21
  91.3 1.3 %shard_map.69 = (bf16[144,1024]{1,0:T(8,128)(2,1)S(1)}, f32[128,1024]{1,0:T(8,128)S(1)}, f32[16,128]{1,0:T(8,128)S(1)}) custom-call(f32[1,2048]{1,0:T(1,128)S(1)} %get-tuple-element.69.energy, f32[1024,1280]{1,0:T(8,128)S(1)} %get-tuple-element.63.refs_0_, f32[1024,512]{1,0:T(8,128)S(1)} %get-tuple-element.64.refs_1_, ...), custom_call_target="tpu_custom_call" | custom-call | flops 1073741824 | bytes 6291456 | tf_op jit(solution)/shard_map/pallas_call | solution.py:299
  92.6 2.0 %collective-permute-start.25 = (bf16[144,1024]{1,0:T(8,128)(2,1)S(1)}, bf16[144,1024]{1,0:T(8,128)(2,1)S(1)}, u32[]{:S(2)}, u32[]{:S(2)}) collective-permute-start(bf16[144,1024]{1,0:T(8,128)(2,1)S(1)} %get-tuple-element.72), channel_id=1, source_target_pairs={{0,1},{1,0},{2,3},{3,2},{4,5},{5,4},{6,7},{7,6},{8,9},{9,8},{10,11... | collective-permute-start | bytes 884744 | tf_op jit(solution)/shard_map/ppermute | solution.py:25
  94.6 3.6 %collective-permute-done.26.two = bf16[144,1024]{1,0:T(8,128)(2,1)S(1)} collective-permute-done((bf16[144,1024]{1,0:T(8,128)(2,1)S(1)}, bf16[144,1024]{1,0:T(8,128)(2,1)S(1)}, u32[]{:S(2)}, u32[]{:S(2)}) %collective-permute-start.26) | collective-permute-done | bytes 294944 | tf_op jit(solution)/shard_map/ppermute | solution.py:21
  (49 shorter events, 13.9 us)
Async XLA Ops:
  0.6 1.2 %copy-start = (bf16[512,1024]{1,0:T(8,128)(2,1)S(1)}, bf16[512,1024]{1,0:T(8,128)(2,1)}, u32[]{:S(2)}) copy-start(bf16[512,1024]{1,0:T(8,128)(2,1)} %param.3) | copy-start | bytes 3145732
  0.6 40.0 %copy-start.1 = (bf16[128,1024]{1,0:T(8,128)(2,1)S(1)}, bf16[128,1024]{1,0:T(8,128)(2,1)}, u32[]{:S(2)}) copy-start(bf16[128,1024]{1,0:T(8,128)(2,1)} %centroids.1) | copy-start | bytes 786436
  2.0 14.0 %collective-permute-start = (bf16[256,1024]{1,0:T(8,128)(2,1)S(1)}, bf16[256,1024]{1,0:T(8,128)(2,1)S(1)}, u32[]{:S(2)}, u32[]{:S(2)}) collective-permute-start(bf16[256,1024]{1,0:T(8,128)(2,1)S(1)} %constant_dynamic-slice_fusion.2), channel_id=1, source_target_pairs={{0,8},{1,57},{8,16},{9,1},{16,24},{17,9},{24,32},{25,17},{32,40},{... | collective-permute-start | bytes 1572872 | tf_op jit(solution)/shard_map/ppermute | solution.py:33
  8.5 7.2 %collective-permute-start.2 = (bf16[128,1024]{1,0:T(8,128)(2,1)}, bf16[128,1024]{1,0:T(8,128)(2,1)S(1)}, u32[]{:S(2)}, u32[]{:S(2)}) collective-permute-start(bf16[128,1024]{1,0:T(8,128)(2,1)} %centroids.1), channel_id=1, source_target_pairs={{0,64},{64,128},{128,192},{192,0},{1,65},{65,129},{129,193},{193,1... | collective-permute-start | bytes 786440 | tf_op jit(solution)/shard_map/ppermute | solution.py:21
  9.7 6.3 %collective-permute-start.1 = (bf16[128,1024]{1,0:T(8,128)(2,1)}, bf16[128,1024]{1,0:T(8,128)(2,1)S(1)}, u32[]{:S(2)}, u32[]{:S(2)}) collective-permute-start(bf16[128,1024]{1,0:T(8,128)(2,1)} %centroids.1), channel_id=1, source_target_pairs={{0,192},{64,0},{128,64},{192,128},{1,193},{65,1},{129,65},{193,129... | collective-permute-start | bytes 786440 | tf_op jit(solution)/shard_map/ppermute | solution.py:21
  16.0 9.7 %collective-permute-start.3 = (bf16[256,1024]{1,0:T(8,128)(2,1)S(1)}, bf16[256,1024]{1,0:T(8,128)(2,1)S(1)}, u32[]{:S(2)}, u32[]{:S(2)}) collective-permute-start(bf16[256,1024]{1,0:T(8,128)(2,1)S(1)} %collective-permute-done.refs_9_.refs_4_), channel_id=1, source_target_pairs={{0,8},{1,57},{8,16},{9,1},{16,24},{17,9},{24,32},{25,17},{32,40},{... | collective-permute-start | bytes 1572872 | tf_op jit(solution)/shard_map/ppermute | solution.py:33
  18.5 7.1 %collective-permute-start.4 = (bf16[128,1024]{1,0:T(8,128)(2,1)S(1)}, bf16[128,1024]{1,0:T(8,128)(2,1)S(1)}, u32[]{:S(2)}, u32[]{:S(2)}) collective-permute-start(bf16[128,1024]{1,0:T(8,128)(2,1)S(1)} %collective-permute-done.1.refs_2_), channel_id=1, source_target_pairs={{0,192},{64,0},{128,64},{192,128},{1,193},{65,1},{129,65},{193,129... | collective-permute-start | bytes 786440 | tf_op jit(solution)/shard_map/ppermute | solution.py:21
  20.9 9.3 %collective-permute-start.9 = (bf16[256,1024]{1,0:T(8,128)(2,1)S(1)}, bf16[256,1024]{1,0:T(8,128)(2,1)S(1)}, u32[]{:S(2)}, u32[]{:S(2)}) collective-permute-start(bf16[256,1024]{1,0:T(8,128)(2,1)S(1)} %collective-permute-done.refs_9_.refs_4_), channel_id=1, source_target_pairs={{0,2},{1,7},{2,0},{3,5},{4,6},{5,3},{6,4},{7,1},{8,10},{9,15},{10,... | collective-permute-start | bytes 1572872 | tf_op jit(solution)/shard_map/ppermute | solution.py:45
  25.7 8.3 %collective-permute-start.11 = (bf16[256,1024]{1,0:T(8,128)(2,1)S(1)}, bf16[256,1024]{1,0:T(8,128)(2,1)S(1)}, u32[]{:S(2)}, u32[]{:S(2)}) collective-permute-start(bf16[256,1024]{1,0:T(8,128)(2,1)S(1)} %collective-permute-done.3.refs_11_.refs_6_), channel_id=1, source_target_pairs={{0,8},{1,57},{8,16},{9,1},{16,24},{17,9},{24,32},{25,17},{32,40},{... | collective-permute-start | bytes 1572872 | tf_op jit(solution)/shard_map/ppermute | solution.py:33
  30.2 10.5 %collective-permute-start.10 = (bf16[256,1024]{1,0:T(8,128)(2,1)S(1)}, bf16[256,1024]{1,0:T(8,128)(2,1)S(1)}, u32[]{:S(2)}, u32[]{:S(2)}) collective-permute-start(bf16[256,1024]{1,0:T(8,128)(2,1)S(1)} %collective-permute-done.3.refs_11_.refs_6_), channel_id=1, source_target_pairs={{0,2},{1,7},{2,0},{3,5},{4,6},{5,3},{6,4},{7,1},{8,10},{9,15},{10,... | collective-permute-start | bytes 1572872 | tf_op jit(solution)/shard_map/ppermute | solution.py:45
  32.9 4.6 %collective-permute-start.8 = (bf16[128,1024]{1,0:T(8,128)(2,1)}, bf16[128,1024]{1,0:T(8,128)(2,1)S(1)}, u32[]{:S(2)}, u32[]{:S(2)}) collective-permute-start(bf16[128,1024]{1,0:T(8,128)(2,1)} %centroids.1), channel_id=1, source_target_pairs={{0,1},{1,0},{2,3},{3,2},{4,5},{5,4},{6,7},{7,6},{8,9},{9,8},{10,11... | collective-permute-start | bytes 786440 | tf_op jit(solution)/shard_map/ppermute | solution.py:25
  32.9 7.8 %collective-permute-start.6 = (bf16[128,1024]{1,0:T(8,128)(2,1)S(1)}, bf16[128,1024]{1,0:T(8,128)(2,1)S(1)}, u32[]{:S(2)}, u32[]{:S(2)}) collective-permute-start(bf16[128,1024]{1,0:T(8,128)(2,1)S(1)} %collective-permute-done.1.refs_2_), channel_id=1, source_target_pairs={{0,1},{1,0},{2,3},{3,2},{4,5},{5,4},{6,7},{7,6},{8,9},{9,8},{10,11... | collective-permute-start | bytes 786440 | tf_op jit(solution)/shard_map/ppermute | solution.py:25
  33.4 4.6 %collective-permute-start.7 = (bf16[128,1024]{1,0:T(8,128)(2,1)S(1)}, bf16[128,1024]{1,0:T(8,128)(2,1)S(1)}, u32[]{:S(2)}, u32[]{:S(2)}) collective-permute-start(bf16[128,1024]{1,0:T(8,128)(2,1)S(1)} %collective-permute-done.2.refs_4_), channel_id=1, source_target_pairs={{0,1},{1,0},{2,3},{3,2},{4,5},{5,4},{6,7},{7,6},{8,9},{9,8},{10,11... | collective-permute-start | bytes 786440 | tf_op jit(solution)/shard_map/ppermute | solution.py:25
  34.0 6.7 %collective-permute-start.5 = (bf16[128,1024]{1,0:T(8,128)(2,1)S(1)}, bf16[128,1024]{1,0:T(8,128)(2,1)S(1)}, u32[]{:S(2)}, u32[]{:S(2)}) collective-permute-start(bf16[128,1024]{1,0:T(8,128)(2,1)S(1)} %collective-permute-done.4.refs_0_), channel_id=1, source_target_pairs={{0,1},{1,0},{2,3},{3,2},{4,5},{5,4},{6,7},{7,6},{8,9},{9,8},{10,11... | collective-permute-start | bytes 786440 | tf_op jit(solution)/shard_map/ppermute | solution.py:25
  37.5 7.2 %collective-permute-start.13 = (bf16[128,1024]{1,0:T(8,128)(2,1)S(1)}, bf16[128,1024]{1,0:T(8,128)(2,1)S(1)}, u32[]{:S(2)}, u32[]{:S(2)}) collective-permute-start(bf16[128,1024]{1,0:T(8,128)(2,1)S(1)} %constant_dynamic-slice_fusion), channel_id=1, source_target_pairs={{0,8},{1,57},{8,16},{9,1},{16,24},{17,9},{24,32},{25,17},{32,40},{... | collective-permute-start | bytes 786440 | tf_op jit(solution)/shard_map/ppermute | solution.py:33
  37.9 9.3 %collective-permute-start.12 = (bf16[256,1024]{1,0:T(8,128)(2,1)S(1)}, bf16[256,1024]{1,0:T(8,128)(2,1)S(1)}, u32[]{:S(2)}, u32[]{:S(2)}) collective-permute-start(bf16[256,1024]{1,0:T(8,128)(2,1)S(1)} %collective-permute-done.11.refs_2_.refs_8_), channel_id=1, source_target_pairs={{0,2},{1,7},{2,0},{3,5},{4,6},{5,3},{6,4},{7,1},{8,10},{9,15},{10,... | collective-permute-start | bytes 1572872 | tf_op jit(solution)/shard_map/ppermute | solution.py:45
  44.7 6.5 %collective-permute-start.14 = (bf16[128,1024]{1,0:T(8,128)(2,1)S(1)}, bf16[128,1024]{1,0:T(8,128)(2,1)S(1)}, u32[]{:S(2)}, u32[]{:S(2)}) collective-permute-start(bf16[128,1024]{1,0:T(8,128)(2,1)S(1)} %collective-permute-done.13.refs_2_.refs_10_), channel_id=1, source_target_pairs={{0,2},{1,7},{2,0},{3,5},{4,6},{5,3},{6,4},{7,1},{8,10},{9,15},{10,... | collective-permute-start | bytes 786440 | tf_op jit(solution)/shard_map/ppermute | solution.py:45
  52.1 2.6 %collective-permute-start.17 = (f32[16,128]{1,0:T(8,128)S(1)}, f32[16,128]{1,0:T(8,128)S(1)}, u32[]{:S(2)}, u32[]{:S(2)}) collective-permute-start(f32[16,128]{1,0:T(8,128)S(1)} %shard_map.61.own), channel_id=1, source_target_pairs={{0,6},{2,0},{4,2},{6,4},{1,7},{3,1},{5,3},{7,5},{8,14},{10,8},{12,... | collective-permute-start | bytes 24584 | tf_op jit(solution)/shard_map/ppermute | solution.py:37
  53.7 4.0 %collective-permute-start.16 = (f32[16,128]{1,0:T(8,128)S(1)}, f32[16,128]{1,0:T(8,128)S(1)}, u32[]{:S(2)}, u32[]{:S(2)}) collective-permute-start(f32[16,128]{1,0:T(8,128)S(1)} %shard_map.61.own), channel_id=1, source_target_pairs={{0,4},{2,6},{4,0},{6,2},{1,5},{3,7},{5,1},{7,3},{8,12},{10,14},{12... | collective-permute-start | bytes 24584 | tf_op jit(solution)/shard_map/ppermute | solution.py:37
  53.7 4.0 %collective-permute-start.15 = (f32[16,128]{1,0:T(8,128)S(1)}, f32[16,128]{1,0:T(8,128)S(1)}, u32[]{:S(2)}, u32[]{:S(2)}) collective-permute-start(f32[16,128]{1,0:T(8,128)S(1)} %shard_map.61.own), channel_id=1, source_target_pairs={{0,2},{2,4},{4,6},{6,0},{1,3},{3,5},{5,7},{7,1},{8,10},{10,12},{12... | collective-permute-start | bytes 24584 | tf_op jit(solution)/shard_map/ppermute | solution.py:37
  57.8 4.2 %collective-permute-start.18 = (f32[16,128]{1,0:T(8,128)S(1)}, f32[16,128]{1,0:T(8,128)S(1)}, u32[]{:S(2)}, u32[]{:S(2)}) collective-permute-start(f32[16,128]{1,0:T(8,128)S(1)} %shard_map.62.mine), channel_id=1, source_target_pairs={{0,1},{1,0},{2,3},{3,2},{4,5},{5,4},{6,7},{7,6},{8,9},{9,8},{10,11... | collective-permute-start | bytes 24584 | tf_op jit(solution)/shard_map/ppermute | solution.py:25
  62.0 2.7 %collective-permute-start.19 = (f32[4,8,128]{2,1,0:T(8,128)S(1)}, f32[4,8,128]{2,1,0:T(8,128)S(1)}, u32[]{:S(2)}, u32[]{:S(2)}) collective-permute-start(f32[4,8,128]{2,1,0:T(8,128)S(1)} %shard_map.63.block), channel_id=1, source_target_pairs={{0,8},{1,57},{8,16},{9,1},{16,24},{17,9},{24,32},{25,17},{32,40},{... | collective-permute-start | bytes 49160 | tf_op jit(solution)/shard_map/ppermute | solution.py:33
  64.7 3.5 %collective-permute-start.20 = (f32[4,8,128]{2,1,0:T(8,128)S(1)}, f32[4,8,128]{2,1,0:T(8,128)S(1)}, u32[]{:S(2)}, u32[]{:S(2)}) collective-permute-start(f32[4,8,128]{2,1,0:T(8,128)S(1)} %collective-permute-done.19.near), channel_id=1, source_target_pairs={{0,1},{1,0},{2,3},{3,2},{4,5},{5,4},{6,7},{7,6},{8,9},{9,8},{10,11... | collective-permute-start | bytes 49160 | tf_op jit(solution)/shard_map/ppermute | solution.py:25
  68.3 4.5 %collective-permute-start.21 = (f32[4,8,128]{2,1,0:T(8,128)S(1)}, f32[4,8,128]{2,1,0:T(8,128)S(1)}, u32[]{:S(2)}, u32[]{:S(2)}) collective-permute-start(f32[4,8,128]{2,1,0:T(8,128)S(1)} %get-tuple-element.61), channel_id=1, source_target_pairs={{0,24},{1,41},{8,32},{9,49},{16,40},{17,57},{24,48},{25,1},{32,56}... | collective-permute-start | bytes 49160 | tf_op jit(solution)/shard_map/ppermute | solution.py:33
  72.7 3.5 %collective-permute-start.22 = (f32[4,8,128]{2,1,0:T(8,128)S(1)}, f32[4,8,128]{2,1,0:T(8,128)S(1)}, u32[]{:S(2)}, u32[]{:S(2)}) collective-permute-start(f32[4,8,128]{2,1,0:T(8,128)S(1)} %collective-permute-done.21.got), channel_id=1, source_target_pairs={{0,1},{1,0},{2,3},{3,2},{4,5},{5,4},{6,7},{7,6},{8,9},{9,8},{10,11... | collective-permute-start | bytes 49160 | tf_op jit(solution)/shard_map/ppermute | solution.py:25
  78.7 2.5 %collective-permute-start.23 = (bf16[432,1024]{1,0:T(8,128)(2,1)S(1)}, bf16[432,1024]{1,0:T(8,128)(2,1)S(1)}, u32[]{:S(2)}, u32[]{:S(2)}) collective-permute-start(bf16[432,1024]{1,0:T(8,128)(2,1)S(1)} %shard_map.66), channel_id=1, source_target_pairs={{0,1},{1,0},{2,3},{3,2},{4,5},{5,4},{6,7},{7,6},{8,9},{9,8},{10,11... | collective-permute-start | bytes 2654216 | tf_op jit(solution)/shard_map/ppermute | solution.py:25
  81.4 9.9 %collective-permute-start.24 = (bf16[144,1024]{1,0:T(8,128)(2,1)S(1)}, bf16[144,1024]{1,0:T(8,128)(2,1)S(1)}, u32[]{:S(2)}, u32[]{:S(2)}) collective-permute-start(bf16[144,1024]{1,0:T(8,128)(2,1)S(1)} %get-tuple-element.68), channel_id=1, source_target_pairs={{0,128},{64,192},{128,0},{192,64},{1,129},{65,193},{129,1},{193,65... | collective-permute-start | bytes 884744 | tf_op jit(solution)/shard_map/ppermute | solution.py:21
  84.2 14.0 %collective-permute-start.26 = (bf16[144,1024]{1,0:T(8,128)(2,1)S(1)}, bf16[144,1024]{1,0:T(8,128)(2,1)S(1)}, u32[]{:S(2)}, u32[]{:S(2)}) collective-permute-start(bf16[144,1024]{1,0:T(8,128)(2,1)S(1)} %get-tuple-element.74), channel_id=1, source_target_pairs={{0,64},{64,128},{128,192},{192,0},{1,65},{65,129},{129,193},{193,1... | collective-permute-start | bytes 884744 | tf_op jit(solution)/shard_map/ppermute | solution.py:21
  84.5 13.7 %copy-start.2 = (f32[128]{0:T(128)S(1)}, f32[128]{0:T(128)}, u32[]{:S(2)}) copy-start(f32[128]{0:T(128)} %param.5) | copy-start | bytes 1540
  84.5 13.7 %collective-permute-start.27 = (bf16[144,1024]{1,0:T(8,128)(2,1)S(1)}, bf16[144,1024]{1,0:T(8,128)(2,1)S(1)}, u32[]{:S(2)}, u32[]{:S(2)}) collective-permute-start(bf16[144,1024]{1,0:T(8,128)(2,1)S(1)} %get-tuple-element.75), channel_id=1, source_target_pairs={{0,192},{64,0},{128,64},{192,128},{1,193},{65,1},{129,65},{193,129... | collective-permute-start | bytes 884744 | tf_op jit(solution)/shard_map/ppermute | solution.py:21
  92.6 5.7 %collective-permute-start.25 = (bf16[144,1024]{1,0:T(8,128)(2,1)S(1)}, bf16[144,1024]{1,0:T(8,128)(2,1)S(1)}, u32[]{:S(2)}, u32[]{:S(2)}) collective-permute-start(bf16[144,1024]{1,0:T(8,128)(2,1)S(1)} %get-tuple-element.72), channel_id=1, source_target_pairs={{0,1},{1,0},{2,3},{3,2},{4,5},{5,4},{6,7},{7,6},{8,9},{9,8},{10,11... | collective-permute-start | bytes 884744 | tf_op jit(solution)/shard_map/ppermute | solution.py:25

commit v14 on v13

--- a/solution.py
+++ b/solution.py
@@ -48,6 +48,15 @@
 def combine(parts):
     high = functools.reduce(jnp.maximum, parts)
     return high + jnp.log(sum(jnp.exp(p - high) for p in parts))
+
+
+def from_partner(value):
+    pairs = []
+    for z in range(NZ):
+        for y in range(NY):
+            for c, to, side in ((0, z + 1, y ^ 1), (1, z - 1, (y + 1 if y % 2 else y - 1) % NY)):
+                pairs.append(((z * NY + y) * NC + c, (to % NZ * NY + side) * NC + c))
+    return lax.ppermute(value, ("z", "y", "c"), pairs)
 
 
 def pick(place, first, second):
@@ -375,13 +384,14 @@
     fixed = lambda v: pltpu.with_memory_space_constraint(v, pltpu.VMEM) if PIN else v
     table = [fixed(v) for d in ORDER for v in (near[d], swap_cores(near[d]))]
 
-    four = along_z(lax.dynamic_slice_in_dim(three, start_c, sub, 0), 1)
-    lots = [[fixed(v) for v in (own, one, first, two, swap_halves(two))]]
+    sides = [swap_halves(two), swap_halves(three)]
+    part = lax.dynamic_slice_in_dim(three, start_c, sub, 0)
+    four, last = along_z(part, 1), from_partner(part)
+    lots = [[fixed(v) for v in (own, one, first, two, sides[0])]]
     *table, scores, energy = score(table, lots[0])
     table, logits, local = [fixed(v) for v in table], [scores], [energy]
-    last, _ = lax.optimization_barrier((four, energy))
-    last = swap_halves(last)
-    lots.append([fixed(v) for v in (three, swap_halves(three))])
+    sides[1], _ = lax.optimization_barrier((sides[1], energy))
+    lots.append([fixed(v) for v in (three, sides[1])])
     scores, energy = score(table, lots[1])
     last, _ = lax.optimization_barrier((last, energy))
     logits.append(scores)

time: 99.5 us -> 99.1 us (level)
  starting transfers between devices: 52 us -> 48.7 us
  waiting for transfers between devices: 31.7 us -> 34.6 us
    ppermute x6, waiting for transfers between devices: 4.99 us -> 9.06 us  [along_z(): return lax.ppermute(value, ('z', 'c'), pairs)]
    ppermute x4 -> x3, starting transfers between devices: 9.66 us -> 5.66 us  [swap_halves(): return lax.ppermute(value, ('y', 'c'), pairs)]
    ppermute x0 -> x1, starting transfers between devices: none -> 3.7 us  [from_partner(): return lax.ppermute(value, ('z', 'y', 'c'), pairs)]
    ppermute x4 -> x3, waiting for transfers between devices: 5.78 us -> 2.65 us  [swap_halves(): return lax.ppermute(value, ('y', 'c'), pairs)]
    ppermute x9, starting transfers between devices: 15.2 us -> 12.7 us  [swap_cores(): return lax.ppermute(value, 'c', [(0, 1), (1, 0)])]
    ppermute x6, waiting for transfers between devices: 14.9 us -> 16.6 us  [shift_x(): return lax.ppermute(value, 'x', [(i, (i + by) % NX) for i in range(NX)])]
where the time goes in v14:
time: 99.1 us; the launch traced here: 99 us
  starting transfers between devices  48.7 us (49%)
  waiting for transfers between devices  34.6 us (35%)
  Pallas kernels  13.4 us (14%)
  local copies, waits for them, and re-layouts  1.43 us (1%)
    ppermute x6, waiting for transfers between devices, shift_x(): return lax.ppermute(value, 'x', [(i, (i + by) % NX) for i in range(NX)])  16.6 us
    ppermute x6, starting transfers between devices, along_z(): return lax.ppermute(value, ('z', 'c'), pairs)  13.5 us
    ppermute x9, starting transfers between devices, swap_cores(): return lax.ppermute(value, 'c', [(0, 1), (1, 0)])  12.7 us
    ppermute x6, starting transfers between devices, shift_x(): return lax.ppermute(value, 'x', [(i, (i + by) % NX) for i in range(NX)])  10.5 us
    ppermute x6, waiting for transfers between devices, along_z(): return lax.ppermute(value, ('z', 'c'), pairs)  9.06 us
    pallas_call x3, Pallas kernels, score(): pl.pallas_call(functools.partial(score_kernel, 0 if whole else len(table)...  6.55 us
    ppermute x3, starting transfers between devices, swap_halves(): return lax.ppermute(value, ('y', 'c'), pairs)  5.66 us
    pallas_call x3, Pallas kernels, weigh(): pl.pallas_call(functools.partial(weigh_kernel, lots, groups, sizes, len(k...  4.95 us
  transfers between devices with their start and end apart: 28, of which 17 were waited for; matrix products, arithmetic and copies ran while one was open for 0% of the time, Pallas kernels for 9%

profile of v14, /device:TPU:1, one launch (start us, length us, event | category | flops | bytes accessed | tf_op | source)
XLA Modules:
  0.0 99.0 jit_solution(15779392752557818210)
XLA Ops:
  2.0 6.5 %collective-permute-start = (bf16[256,1024]{1,0:T(8,128)(2,1)S(1)}, bf16[256,1024]{1,0:T(8,128)(2,1)S(1)}, u32[]{:S(2)}, u32[]{:S(2)}) collective-permute-start(bf16[256,1024]{1,0:T(8,128)(2,1)S(1)} %constant_dynamic-slice_fusion.2), channel_id=1, source_target_pairs={{0,8},{1,57},{8,16},{9,1},{16,24},{17,9},{24,32},{25,17},{32,40},{... | collective-permute-start | bytes 1572872 | tf_op jit(solution)/shard_map/ppermute | solution.py:33
  8.5 1.2 %collective-permute-start.2 = (bf16[128,1024]{1,0:T(8,128)(2,1)}, bf16[128,1024]{1,0:T(8,128)(2,1)S(1)}, u32[]{:S(2)}, u32[]{:S(2)}) collective-permute-start(bf16[128,1024]{1,0:T(8,128)(2,1)} %centroids.1), channel_id=1, source_target_pairs={{0,64},{64,128},{128,192},{192,0},{1,65},{65,129},{129,193},{193,1... | collective-permute-start | bytes 786440 | tf_op jit(solution)/shard_map/ppermute | solution.py:21
  9.7 1.5 %collective-permute-start.1 = (bf16[128,1024]{1,0:T(8,128)(2,1)}, bf16[128,1024]{1,0:T(8,128)(2,1)S(1)}, u32[]{:S(2)}, u32[]{:S(2)}) collective-permute-start(bf16[128,1024]{1,0:T(8,128)(2,1)} %centroids.1), channel_id=1, source_target_pairs={{0,192},{64,0},{128,64},{192,128},{1,193},{65,1},{129,65},{193,129... | collective-permute-start | bytes 786440 | tf_op jit(solution)/shard_map/ppermute | solution.py:21
  11.2 4.5 %collective-permute-done.2.refs_4_ = bf16[128,1024]{1,0:T(8,128)(2,1)S(1)} collective-permute-done((bf16[128,1024]{1,0:T(8,128)(2,1)}, bf16[128,1024]{1,0:T(8,128)(2,1)S(1)}, u32[]{:S(2)}, u32[]{:S(2)}) %collective-permute-start.2) | collective-permute-done | bytes 262176 | tf_op jit(solution)/shard_map/ppermute | solution.py:21
  16.0 2.5 %collective-permute-start.3 = (bf16[256,1024]{1,0:T(8,128)(2,1)S(1)}, bf16[256,1024]{1,0:T(8,128)(2,1)S(1)}, u32[]{:S(2)}, u32[]{:S(2)}) collective-permute-start(bf16[256,1024]{1,0:T(8,128)(2,1)S(1)} %collective-permute-done.refs_9_.refs_4_), channel_id=1, source_target_pairs={{0,8},{1,57},{8,16},{9,1},{16,24},{17,9},{24,32},{25,17},{32,40},{... | collective-permute-start | bytes 1572872 | tf_op jit(solution)/shard_map/ppermute | solution.py:33
  18.5 2.7 %collective-permute-start.9 = (bf16[256,1024]{1,0:T(8,128)(2,1)S(1)}, bf16[256,1024]{1,0:T(8,128)(2,1)S(1)}, u32[]{:S(2)}, u32[]{:S(2)}) collective-permute-start(bf16[256,1024]{1,0:T(8,128)(2,1)S(1)} %collective-permute-done.refs_9_.refs_4_), channel_id=1, source_target_pairs={{0,2},{1,7},{2,0},{3,5},{4,6},{5,3},{6,4},{7,1},{8,10},{9,15},{10,... | collective-permute-start | bytes 1572872 | tf_op jit(solution)/shard_map/ppermute | solution.py:45
  21.3 2.4 %collective-permute-start.4 = (bf16[128,1024]{1,0:T(8,128)(2,1)S(1)}, bf16[128,1024]{1,0:T(8,128)(2,1)S(1)}, u32[]{:S(2)}, u32[]{:S(2)}) collective-permute-start(bf16[128,1024]{1,0:T(8,128)(2,1)S(1)} %collective-permute-done.1.refs_2_), channel_id=1, source_target_pairs={{0,192},{64,0},{128,64},{192,128},{1,193},{65,1},{129,65},{193,129... | collective-permute-start | bytes 786440 | tf_op jit(solution)/shard_map/ppermute | solution.py:21
  23.6 3.6 %collective-permute-done.4.refs_0_ = bf16[128,1024]{1,0:T(8,128)(2,1)S(1)} collective-permute-done((bf16[128,1024]{1,0:T(8,128)(2,1)S(1)}, bf16[128,1024]{1,0:T(8,128)(2,1)S(1)}, u32[]{:S(2)}, u32[]{:S(2)}) %collective-permute-start.4) | collective-permute-done | bytes 262176 | tf_op jit(solution)/shard_map/ppermute | solution.py:21
  27.2 2.2 %collective-permute-start.11 = (bf16[256,1024]{1,0:T(8,128)(2,1)S(1)}, bf16[256,1024]{1,0:T(8,128)(2,1)S(1)}, u32[]{:S(2)}, u32[]{:S(2)}) collective-permute-start(bf16[256,1024]{1,0:T(8,128)(2,1)S(1)} %collective-permute-done.3.refs_11_.refs_6_), channel_id=1, source_target_pairs={{0,8},{1,57},{8,16},{9,1},{16,24},{17,9},{24,32},{25,17},{32,40},{... | collective-permute-start | bytes 1572872 | tf_op jit(solution)/shard_map/ppermute | solution.py:33
  31.4 4.2 %collective-permute-done.11.refs_2_.refs_8_ = bf16[256,1024]{1,0:T(8,128)(2,1)S(1)} collective-permute-done((bf16[256,1024]{1,0:T(8,128)(2,1)S(1)}, bf16[256,1024]{1,0:T(8,128)(2,1)S(1)}, u32[]{:S(2)}, u32[]{:S(2)}) %collective-permute-start.11) | collective-permute-done | bytes 524320 | tf_op jit(solution)/shard_map/ppermute | solution.py:33
  35.6 1.9 %collective-permute-start.12 = (bf16[256,1024]{1,0:T(8,128)(2,1)S(1)}, bf16[256,1024]{1,0:T(8,128)(2,1)S(1)}, u32[]{:S(2)}, u32[]{:S(2)}) collective-permute-start(bf16[256,1024]{1,0:T(8,128)(2,1)S(1)} %collective-permute-done.11.refs_2_.refs_8_), channel_id=1, source_target_pairs={{0,2},{1,7},{2,0},{3,5},{4,6},{5,3},{6,4},{7,1},{8,10},{9,15},{10,... | collective-permute-start | bytes 1572872 | tf_op jit(solution)/shard_map/ppermute | solution.py:45
  37.6 3.7 %collective-permute-start.14 = (bf16[128,1024]{1,0:T(8,128)(2,1)S(1)}, bf16[128,1024]{1,0:T(8,128)(2,1)S(1)}, u32[]{:S(2)}, u32[]{:S(2)}) collective-permute-start(bf16[128,1024]{1,0:T(8,128)(2,1)S(1)} %constant_dynamic-slice_fusion), channel_id=1, source_target_pairs={{0,10},{1,63},{2,8},{3,61},{4,14},{5,59},{6,12},{7,57},{8,18},{9,7... | collective-permute-start | bytes 786440 | tf_op jit(solution)/shard_map/ppermute | solution.py:59
  41.3 4.0 %shard_map.58 = (bf16[1024,1024]{1,0:T(8,128)(2,1)S(1)}, f32[1024,128]{1,0:T(8,128)S(1)}, f32[1024,1280]{1,0:T(8,128)S(1)}, f32[1,1280]{1,0:T(1,128)S(1)}) custom-call(bf16[128,1024]{1,0:T(8,128)(2,1)S(1)} %collective-permute-done.4.refs_0_, bf16[128,1024]{1,0:T(8,128)(2,1)S(1)} %collective-permute-done.5.refs_1_, ...), custom_call_target="tpu_custom_call" | custom-call | flops 5368709120 | bytes 9961472 | tf_op jit(solution)/shard_map/pallas_call | solution.py:229
  45.3 2.6 %collective-permute-done.12.refs_3_.refs_9_ = bf16[256,1024]{1,0:T(8,128)(2,1)S(1)} collective-permute-done((bf16[256,1024]{1,0:T(8,128)(2,1)S(1)}, bf16[256,1024]{1,0:T(8,128)(2,1)S(1)}, u32[]{:S(2)}, u32[]{:S(2)}) %collective-permute-start.12) | collective-permute-done | bytes 524320 | tf_op jit(solution)/shard_map/ppermute | solution.py:45
  47.9 1.6 %shard_map.59 = (f32[1024,512]{1,0:T(8,128)S(1)}, f32[1,512]{1,0:T(1,128)S(1)}) custom-call(bf16[1024,1024]{1,0:T(8,128)(2,1)S(1)} %get-tuple-element.53.refs_0_, f32[1024,128]{1,0:T(8,128)S(1)} %get-tuple-element.54.refs_1_, bf16[256,1024]{1,0:T(8,128)(2,1)S(1)} %collective-permute-done.11.refs_2_.refs_8_, ...), custom_call_target="tpu_custom_call" | custom-call | flops 2147483648 | bytes 5242880 | tf_op jit(solution)/shard_map/pallas_call | solution.py:229
  50.5 2.0 %collective-permute-start.17 = (f32[16,128]{1,0:T(8,128)S(1)}, f32[16,128]{1,0:T(8,128)S(1)}, u32[]{:S(2)}, u32[]{:S(2)}) collective-permute-start(f32[16,128]{1,0:T(8,128)S(1)} %shard_map.61.own), channel_id=1, source_target_pairs={{0,6},{2,0},{4,2},{6,4},{1,7},{3,1},{5,3},{7,5},{8,14},{10,8},{12,... | collective-permute-start | bytes 24584 | tf_op jit(solution)/shard_map/ppermute | solution.py:37
  53.3 3.2 %collective-permute-done.16.refs_1_ = f32[16,128]{1,0:T(8,128)S(1)} collective-permute-done((f32[16,128]{1,0:T(8,128)S(1)}, f32[16,128]{1,0:T(8,128)S(1)}, u32[]{:S(2)}, u32[]{:S(2)}) %collective-permute-start.16) | collective-permute-done | bytes 8224 | tf_op jit(solution)/shard_map/ppermute | solution.py:37
  56.5 4.1 %collective-permute-start.18 = (f32[16,128]{1,0:T(8,128)S(1)}, f32[16,128]{1,0:T(8,128)S(1)}, u32[]{:S(2)}, u32[]{:S(2)}) collective-permute-start(f32[16,128]{1,0:T(8,128)S(1)} %shard_map.62.mine), channel_id=1, source_target_pairs={{0,1},{1,0},{2,3},{3,2},{4,5},{5,4},{6,7},{7,6},{8,9},{9,8},{10,11... | collective-permute-start | bytes 24584 | tf_op jit(solution)/shard_map/ppermute | solution.py:25
  62.1 2.1 %collective-permute-done.19.near = f32[4,8,128]{2,1,0:T(8,128)S(1)} collective-permute-done((f32[4,8,128]{2,1,0:T(8,128)S(1)}, f32[4,8,128]{2,1,0:T(8,128)S(1)}, u32[]{:S(2)}, u32[]{:S(2)}) %collective-permute-start.19) | collective-permute-done | bytes 16416 | tf_op jit(solution)/shard_map/ppermute | solution.py:33
  64.2 2.7 %collective-permute-start.20 = (f32[4,8,128]{2,1,0:T(8,128)S(1)}, f32[4,8,128]{2,1,0:T(8,128)S(1)}, u32[]{:S(2)}, u32[]{:S(2)}) collective-permute-start(f32[4,8,128]{2,1,0:T(8,128)S(1)} %collective-permute-done.19.near), channel_id=1, source_target_pairs={{0,1},{1,0},{2,3},{3,2},{4,5},{5,4},{6,7},{7,6},{8,9},{9,8},{10,11... | collective-permute-start | bytes 49160 | tf_op jit(solution)/shard_map/ppermute | solution.py:25
  67.8 1.7 %collective-permute-start.21 = (f32[4,8,128]{2,1,0:T(8,128)S(1)}, f32[4,8,128]{2,1,0:T(8,128)S(1)}, u32[]{:S(2)}, u32[]{:S(2)}) collective-permute-start(f32[4,8,128]{2,1,0:T(8,128)S(1)} %get-tuple-element.61), channel_id=1, source_target_pairs={{0,24},{1,41},{8,32},{9,49},{16,40},{17,57},{24,48},{25,1},{32,56}... | collective-permute-start | bytes 49160 | tf_op jit(solution)/shard_map/ppermute | solution.py:33
  69.5 2.8 %collective-permute-done.21.got = f32[4,8,128]{2,1,0:T(8,128)S(1)} collective-permute-done((f32[4,8,128]{2,1,0:T(8,128)S(1)}, f32[4,8,128]{2,1,0:T(8,128)S(1)}, u32[]{:S(2)}, u32[]{:S(2)}) %collective-permute-start.21) | collective-permute-done | bytes 16416 | tf_op jit(solution)/shard_map/ppermute | solution.py:33
  72.2 2.7 %collective-permute-start.22 = (f32[4,8,128]{2,1,0:T(8,128)S(1)}, f32[4,8,128]{2,1,0:T(8,128)S(1)}, u32[]{:S(2)}, u32[]{:S(2)}) collective-permute-start(f32[4,8,128]{2,1,0:T(8,128)S(1)} %collective-permute-done.21.got), channel_id=1, source_target_pairs={{0,1},{1,0},{2,3},{3,2},{4,5},{5,4},{6,7},{7,6},{8,9},{9,8},{10,11... | collective-permute-start | bytes 49160 | tf_op jit(solution)/shard_map/ppermute | solution.py:25
  76.4 1.8 %shard_map.66 = bf16[432,1024]{1,0:T(8,128)(2,1)S(1)} custom-call(f32[1,2048]{1,0:T(1,128)S(1)} %get-tuple-element.69.energy, f32[1024,1280]{1,0:T(8,128)S(1)} %get-tuple-element.63.refs_0_, f32[1024,512]{1,0:T(8,128)S(1)} %get-tuple-element.64.refs_1_, f32[1024,256]{1,0:T(8,128)S(1)} %get-tuple-element.65.refs_2_, bf16[256,1024]{1,0:T(8,128)(2,1)S(1)} %bitcast.9, ...), custom_call_target="tpu_custom_call" | custom-call | flops 1610612736 | bytes 7340032 | tf_op jit(solution)/shard_map/pallas_call | solution.py:308
  78.6 1.8 %shard_map.67 = (f32[384,1024]{1,0:T(8,128)S(1)}, f32[48,128]{1,0:T(8,128)S(1)}) custom-call(f32[1,2048]{1,0:T(1,128)S(1)} %get-tuple-element.69.energy, f32[1024,1280]{1,0:T(8,128)S(1)} %get-tuple-element.63.refs_0_, f32[1024,512]{1,0:T(8,128)S(1)} %get-tuple-element.64.refs_1_, f32[1024,256]{1,0:T(8,128)S(1)} %get-tuple-element.65.refs_2_, ...), custom_call_target="tpu_custom_call" | custom-call | flops 1610612736 | bytes 7340032 | tf_op jit(solution)/shard_map/pallas_call | solution.py:308
  80.9 2.8 %collective-permute-start.24 = (bf16[144,1024]{1,0:T(8,128)(2,1)S(1)}, bf16[144,1024]{1,0:T(8,128)(2,1)S(1)}, u32[]{:S(2)}, u32[]{:S(2)}) collective-permute-start(bf16[144,1024]{1,0:T(8,128)(2,1)S(1)} %get-tuple-element.68), channel_id=1, source_target_pairs={{0,128},{64,192},{128,0},{192,64},{1,129},{65,193},{129,1},{193,65... | collective-permute-start | bytes 884744 | tf_op jit(solution)/shard_map/ppermute | solution.py:21
  84.7 1.7 %collective-permute-start.27 = (bf16[144,1024]{1,0:T(8,128)(2,1)S(1)}, bf16[144,1024]{1,0:T(8,128)(2,1)S(1)}, u32[]{:S(2)}, u32[]{:S(2)}) collective-permute-start(bf16[144,1024]{1,0:T(8,128)(2,1)S(1)} %get-tuple-element.75), channel_id=1, source_target_pairs={{0,192},{64,0},{128,64},{192,128},{1,193},{65,1},{129,65},{193,129... | collective-permute-start | bytes 884744 | tf_op jit(solution)/shard_map/ppermute | solution.py:21
  86.4 4.4 %collective-permute-done.24.one = bf16[144,1024]{1,0:T(8,128)(2,1)S(1)} collective-permute-done((bf16[144,1024]{1,0:T(8,128)(2,1)S(1)}, bf16[144,1024]{1,0:T(8,128)(2,1)S(1)}, u32[]{:S(2)}, u32[]{:S(2)}) %collective-permute-start.24) | collective-permute-done | bytes 294944 | tf_op jit(solution)/shard_map/ppermute | solution.py:21
  90.8 1.3 %shard_map.69 = (bf16[144,1024]{1,0:T(8,128)(2,1)S(1)}, f32[128,1024]{1,0:T(8,128)S(1)}, f32[16,128]{1,0:T(8,128)S(1)}) custom-call(f32[1,2048]{1,0:T(1,128)S(1)} %get-tuple-element.69.energy, f32[1024,1280]{1,0:T(8,128)S(1)} %get-tuple-element.63.refs_0_, f32[1024,512]{1,0:T(8,128)S(1)} %get-tuple-element.64.refs_1_, ...), custom_call_target="tpu_custom_call" | custom-call | flops 1073741824 | bytes 6291456 | tf_op jit(solution)/shard_map/pallas_call | solution.py:308
  92.1 2.0 %collective-permute-start.25 = (bf16[144,1024]{1,0:T(8,128)(2,1)S(1)}, bf16[144,1024]{1,0:T(8,128)(2,1)S(1)}, u32[]{:S(2)}, u32[]{:S(2)}) collective-permute-start(bf16[144,1024]{1,0:T(8,128)(2,1)S(1)} %get-tuple-element.72), channel_id=1, source_target_pairs={{0,1},{1,0},{2,3},{3,2},{4,5},{5,4},{6,7},{7,6},{8,9},{9,8},{10,11... | collective-permute-start | bytes 884744 | tf_op jit(solution)/shard_map/ppermute | solution.py:25
  94.1 3.6 %collective-permute-done.26.two = bf16[144,1024]{1,0:T(8,128)(2,1)S(1)} collective-permute-done((bf16[144,1024]{1,0:T(8,128)(2,1)S(1)}, bf16[144,1024]{1,0:T(8,128)(2,1)S(1)}, u32[]{:S(2)}, u32[]{:S(2)}) %collective-permute-start.26) | collective-permute-done | bytes 294944 | tf_op jit(solution)/shard_map/ppermute | solution.py:21
  97.9 1.1 %shard_map.70 = (f32[128,1024]{1,0:T(8,128)}, f32[1,128]{1,0:T(1,128)}) custom-call(f32[128,1024]{1,0:T(8,128)S(1)} %get-tuple-element.70.keep, f32[16,128]{1,0:T(8,128)S(1)} %get-tuple-element.71.keep_count, bf16[144,1024]{1,0:T(8,128)(2,1)S(1)} %collective-permute-done.25.got, bf16[144,1024]{1,0:T(8,128)(2,1)S(1)} %collective-permute-done.24.one, ...), custom_call_target="tpu_custom_call" | custom-call | tf_op jit(solution)/shard_map/pallas_call | solution.py:322
  (49 shorter events, 11.1 us)
Async XLA Ops:
  0.6 1.2 %copy-start = (bf16[512,1024]{1,0:T(8,128)(2,1)S(1)}, bf16[512,1024]{1,0:T(8,128)(2,1)}, u32[]{:S(2)}) copy-start(bf16[512,1024]{1,0:T(8,128)(2,1)} %param.3) | copy-start | bytes 3145732
  0.6 40.6 %copy-start.1 = (bf16[128,1024]{1,0:T(8,128)(2,1)S(1)}, bf16[128,1024]{1,0:T(8,128)(2,1)}, u32[]{:S(2)}) copy-start(bf16[128,1024]{1,0:T(8,128)(2,1)} %centroids.1) | copy-start | bytes 786436
  2.0 14.0 %collective-permute-start = (bf16[256,1024]{1,0:T(8,128)(2,1)S(1)}, bf16[256,1024]{1,0:T(8,128)(2,1)S(1)}, u32[]{:S(2)}, u32[]{:S(2)}) collective-permute-start(bf16[256,1024]{1,0:T(8,128)(2,1)S(1)} %constant_dynamic-slice_fusion.2), channel_id=1, source_target_pairs={{0,8},{1,57},{8,16},{9,1},{16,24},{17,9},{24,32},{25,17},{32,40},{... | collective-permute-start | bytes 1572872 | tf_op jit(solution)/shard_map/ppermute | solution.py:33
  8.5 7.2 %collective-permute-start.2 = (bf16[128,1024]{1,0:T(8,128)(2,1)}, bf16[128,1024]{1,0:T(8,128)(2,1)S(1)}, u32[]{:S(2)}, u32[]{:S(2)}) collective-permute-start(bf16[128,1024]{1,0:T(8,128)(2,1)} %centroids.1), channel_id=1, source_target_pairs={{0,64},{64,128},{128,192},{192,0},{1,65},{65,129},{129,193},{193,1... | collective-permute-start | bytes 786440 | tf_op jit(solution)/shard_map/ppermute | solution.py:21
  9.7 6.3 %collective-permute-start.1 = (bf16[128,1024]{1,0:T(8,128)(2,1)}, bf16[128,1024]{1,0:T(8,128)(2,1)S(1)}, u32[]{:S(2)}, u32[]{:S(2)}) collective-permute-start(bf16[128,1024]{1,0:T(8,128)(2,1)} %centroids.1), channel_id=1, source_target_pairs={{0,192},{64,0},{128,64},{192,128},{1,193},{65,1},{129,65},{193,129... | collective-permute-start | bytes 786440 | tf_op jit(solution)/shard_map/ppermute | solution.py:21
  16.0 11.3 %collective-permute-start.3 = (bf16[256,1024]{1,0:T(8,128)(2,1)S(1)}, bf16[256,1024]{1,0:T(8,128)(2,1)S(1)}, u32[]{:S(2)}, u32[]{:S(2)}) collective-permute-start(bf16[256,1024]{1,0:T(8,128)(2,1)S(1)} %collective-permute-done.refs_9_.refs_4_), channel_id=1, source_target_pairs={{0,8},{1,57},{8,16},{9,1},{16,24},{17,9},{24,32},{25,17},{32,40},{... | collective-permute-start | bytes 1572872 | tf_op jit(solution)/shard_map/ppermute | solution.py:33
  18.5 10.9 %collective-permute-start.9 = (bf16[256,1024]{1,0:T(8,128)(2,1)S(1)}, bf16[256,1024]{1,0:T(8,128)(2,1)S(1)}, u32[]{:S(2)}, u32[]{:S(2)}) collective-permute-start(bf16[256,1024]{1,0:T(8,128)(2,1)S(1)} %collective-permute-done.refs_9_.refs_4_), channel_id=1, source_target_pairs={{0,2},{1,7},{2,0},{3,5},{4,6},{5,3},{6,4},{7,1},{8,10},{9,15},{10,... | collective-permute-start | bytes 1572872 | tf_op jit(solution)/shard_map/ppermute | solution.py:45
  21.3 6.0 %collective-permute-start.4 = (bf16[128,1024]{1,0:T(8,128)(2,1)S(1)}, bf16[128,1024]{1,0:T(8,128)(2,1)S(1)}, u32[]{:S(2)}, u32[]{:S(2)}) collective-permute-start(bf16[128,1024]{1,0:T(8,128)(2,1)S(1)} %collective-permute-done.1.refs_2_), channel_id=1, source_target_pairs={{0,192},{64,0},{128,64},{192,128},{1,193},{65,1},{129,65},{193,129... | collective-permute-start | bytes 786440 | tf_op jit(solution)/shard_map/ppermute | solution.py:21
  27.2 8.3 %collective-permute-start.11 = (bf16[256,1024]{1,0:T(8,128)(2,1)S(1)}, bf16[256,1024]{1,0:T(8,128)(2,1)S(1)}, u32[]{:S(2)}, u32[]{:S(2)}) collective-permute-start(bf16[256,1024]{1,0:T(8,128)(2,1)S(1)} %collective-permute-done.3.refs_11_.refs_6_), channel_id=1, source_target_pairs={{0,8},{1,57},{8,16},{9,1},{16,24},{17,9},{24,32},{25,17},{32,40},{... | collective-permute-start | bytes 1572872 | tf_op jit(solution)/shard_map/ppermute | solution.py:33
  29.5 1.7 %collective-permute-start.8 = (bf16[128,1024]{1,0:T(8,128)(2,1)}, bf16[128,1024]{1,0:T(8,128)(2,1)S(1)}, u32[]{:S(2)}, u32[]{:S(2)}) collective-permute-start(bf16[128,1024]{1,0:T(8,128)(2,1)} %centroids.1), channel_id=1, source_target_pairs={{0,1},{1,0},{2,3},{3,2},{4,5},{5,4},{6,7},{7,6},{8,9},{9,8},{10,11... | collective-permute-start | bytes 786440 | tf_op jit(solution)/shard_map/ppermute | solution.py:25
  29.5 11.8 %collective-permute-start.10 = (bf16[256,1024]{1,0:T(8,128)(2,1)S(1)}, bf16[256,1024]{1,0:T(8,128)(2,1)S(1)}, u32[]{:S(2)}, u32[]{:S(2)}) collective-permute-start(bf16[256,1024]{1,0:T(8,128)(2,1)S(1)} %collective-permute-done.3.refs_11_.refs_6_), channel_id=1, source_target_pairs={{0,2},{1,7},{2,0},{3,5},{4,6},{5,3},{6,4},{7,1},{8,10},{9,15},{10,... | collective-permute-start | bytes 1572872 | tf_op jit(solution)/shard_map/ppermute | solution.py:45
  30.5 7.0 %collective-permute-start.7 = (bf16[128,1024]{1,0:T(8,128)(2,1)S(1)}, bf16[128,1024]{1,0:T(8,128)(2,1)S(1)}, u32[]{:S(2)}, u32[]{:S(2)}) collective-permute-start(bf16[128,1024]{1,0:T(8,128)(2,1)S(1)} %collective-permute-done.2.refs_4_), channel_id=1, source_target_pairs={{0,1},{1,0},{2,3},{3,2},{4,5},{5,4},{6,7},{7,6},{8,9},{9,8},{10,11... | collective-permute-start | bytes 786440 | tf_op jit(solution)/shard_map/ppermute | solution.py:25
  30.5 10.7 %collective-permute-start.6 = (bf16[128,1024]{1,0:T(8,128)(2,1)S(1)}, bf16[128,1024]{1,0:T(8,128)(2,1)S(1)}, u32[]{:S(2)}, u32[]{:S(2)}) collective-permute-start(bf16[128,1024]{1,0:T(8,128)(2,1)S(1)} %collective-permute-done.1.refs_2_), channel_id=1, source_target_pairs={{0,1},{1,0},{2,3},{3,2},{4,5},{5,4},{6,7},{7,6},{8,9},{9,8},{10,11... | collective-permute-start | bytes 786440 | tf_op jit(solution)/shard_map/ppermute | solution.py:25
  31.2 10.1 %collective-permute-start.5 = (bf16[128,1024]{1,0:T(8,128)(2,1)S(1)}, bf16[128,1024]{1,0:T(8,128)(2,1)S(1)}, u32[]{:S(2)}, u32[]{:S(2)}) collective-permute-start(bf16[128,1024]{1,0:T(8,128)(2,1)S(1)} %collective-permute-done.4.refs_0_), channel_id=1, source_target_pairs={{0,1},{1,0},{2,3},{3,2},{4,5},{5,4},{6,7},{7,6},{8,9},{9,8},{10,11... | collective-permute-start | bytes 786440 | tf_op jit(solution)/shard_map/ppermute | solution.py:25
  35.6 12.3 %collective-permute-start.12 = (bf16[256,1024]{1,0:T(8,128)(2,1)S(1)}, bf16[256,1024]{1,0:T(8,128)(2,1)S(1)}, u32[]{:S(2)}, u32[]{:S(2)}) collective-permute-start(bf16[256,1024]{1,0:T(8,128)(2,1)S(1)} %collective-permute-done.11.refs_2_.refs_8_), channel_id=1, source_target_pairs={{0,2},{1,7},{2,0},{3,5},{4,6},{5,3},{6,4},{7,1},{8,10},{9,15},{10,... | collective-permute-start | bytes 1572872 | tf_op jit(solution)/shard_map/ppermute | solution.py:45
  37.6 12.0 %collective-permute-start.14 = (bf16[128,1024]{1,0:T(8,128)(2,1)S(1)}, bf16[128,1024]{1,0:T(8,128)(2,1)S(1)}, u32[]{:S(2)}, u32[]{:S(2)}) collective-permute-start(bf16[128,1024]{1,0:T(8,128)(2,1)S(1)} %constant_dynamic-slice_fusion), channel_id=1, source_target_pairs={{0,10},{1,63},{2,8},{3,61},{4,14},{5,59},{6,12},{7,57},{8,18},{9,7... | collective-permute-start | bytes 786440 | tf_op jit(solution)/shard_map/ppermute | solution.py:59
  41.3 8.3 %collective-permute-start.13 = (bf16[128,1024]{1,0:T(8,128)(2,1)S(1)}, bf16[128,1024]{1,0:T(8,128)(2,1)S(1)}, u32[]{:S(2)}, u32[]{:S(2)}) collective-permute-start(bf16[128,1024]{1,0:T(8,128)(2,1)S(1)} %constant_dynamic-slice_fusion), channel_id=1, source_target_pairs={{0,8},{1,57},{8,16},{9,1},{16,24},{17,9},{24,32},{25,17},{32,40},{... | collective-permute-start | bytes 786440 | tf_op jit(solution)/shard_map/ppermute | solution.py:33
  50.5 2.7 %collective-permute-start.17 = (f32[16,128]{1,0:T(8,128)S(1)}, f32[16,128]{1,0:T(8,128)S(1)}, u32[]{:S(2)}, u32[]{:S(2)}) collective-permute-start(f32[16,128]{1,0:T(8,128)S(1)} %shard_map.61.own), channel_id=1, source_target_pairs={{0,6},{2,0},{4,2},{6,4},{1,7},{3,1},{5,3},{7,5},{8,14},{10,8},{12,... | collective-permute-start | bytes 24584 | tf_op jit(solution)/shard_map/ppermute | solution.py:37
  52.5 4.0 %collective-permute-start.16 = (f32[16,128]{1,0:T(8,128)S(1)}, f32[16,128]{1,0:T(8,128)S(1)}, u32[]{:S(2)}, u32[]{:S(2)}) collective-permute-start(f32[16,128]{1,0:T(8,128)S(1)} %shard_map.61.own), channel_id=1, source_target_pairs={{0,4},{2,6},{4,0},{6,2},{1,5},{3,7},{5,1},{7,3},{8,12},{10,14},{12... | collective-permute-start | bytes 24584 | tf_op jit(solution)/shard_map/ppermute | solution.py:37
  52.5 4.0 %collective-permute-start.15 = (f32[16,128]{1,0:T(8,128)S(1)}, f32[16,128]{1,0:T(8,128)S(1)}, u32[]{:S(2)}, u32[]{:S(2)}) collective-permute-start(f32[16,128]{1,0:T(8,128)S(1)} %shard_map.61.own), channel_id=1, source_target_pairs={{0,2},{2,4},{4,6},{6,0},{1,3},{3,5},{5,7},{7,1},{8,10},{10,12},{12... | collective-permute-start | bytes 24584 | tf_op jit(solution)/shard_map/ppermute | solution.py:37
  56.5 5.0 %collective-permute-start.18 = (f32[16,128]{1,0:T(8,128)S(1)}, f32[16,128]{1,0:T(8,128)S(1)}, u32[]{:S(2)}, u32[]{:S(2)}) collective-permute-start(f32[16,128]{1,0:T(8,128)S(1)} %shard_map.62.mine), channel_id=1, source_target_pairs={{0,1},{1,0},{2,3},{3,2},{4,5},{5,4},{6,7},{7,6},{8,9},{9,8},{10,11... | collective-permute-start | bytes 24584 | tf_op jit(solution)/shard_map/ppermute | solution.py:25
  61.5 2.7 %collective-permute-start.19 = (f32[4,8,128]{2,1,0:T(8,128)S(1)}, f32[4,8,128]{2,1,0:T(8,128)S(1)}, u32[]{:S(2)}, u32[]{:S(2)}) collective-permute-start(f32[4,8,128]{2,1,0:T(8,128)S(1)} %shard_map.63.block), channel_id=1, source_target_pairs={{0,8},{1,57},{8,16},{9,1},{16,24},{17,9},{24,32},{25,17},{32,40},{... | collective-permute-start | bytes 49160 | tf_op jit(solution)/shard_map/ppermute | solution.py:33
  64.2 3.5 %collective-permute-start.20 = (f32[4,8,128]{2,1,0:T(8,128)S(1)}, f32[4,8,128]{2,1,0:T(8,128)S(1)}, u32[]{:S(2)}, u32[]{:S(2)}) collective-permute-start(f32[4,8,128]{2,1,0:T(8,128)S(1)} %collective-permute-done.19.near), channel_id=1, source_target_pairs={{0,1},{1,0},{2,3},{3,2},{4,5},{5,4},{6,7},{7,6},{8,9},{9,8},{10,11... | collective-permute-start | bytes 49160 | tf_op jit(solution)/shard_map/ppermute | solution.py:25
  67.8 4.5 %collective-permute-start.21 = (f32[4,8,128]{2,1,0:T(8,128)S(1)}, f32[4,8,128]{2,1,0:T(8,128)S(1)}, u32[]{:S(2)}, u32[]{:S(2)}) collective-permute-start(f32[4,8,128]{2,1,0:T(8,128)S(1)} %get-tuple-element.61), channel_id=1, source_target_pairs={{0,24},{1,41},{8,32},{9,49},{16,40},{17,57},{24,48},{25,1},{32,56}... | collective-permute-start | bytes 49160 | tf_op jit(solution)/shard_map/ppermute | solution.py:33
  72.2 3.5 %collective-permute-start.22 = (f32[4,8,128]{2,1,0:T(8,128)S(1)}, f32[4,8,128]{2,1,0:T(8,128)S(1)}, u32[]{:S(2)}, u32[]{:S(2)}) collective-permute-start(f32[4,8,128]{2,1,0:T(8,128)S(1)} %collective-permute-done.21.got), channel_id=1, source_target_pairs={{0,1},{1,0},{2,3},{3,2},{4,5},{5,4},{6,7},{7,6},{8,9},{9,8},{10,11... | collective-permute-start | bytes 49160 | tf_op jit(solution)/shard_map/ppermute | solution.py:25
  78.2 2.5 %collective-permute-start.23 = (bf16[432,1024]{1,0:T(8,128)(2,1)S(1)}, bf16[432,1024]{1,0:T(8,128)(2,1)S(1)}, u32[]{:S(2)}, u32[]{:S(2)}) collective-permute-start(bf16[432,1024]{1,0:T(8,128)(2,1)S(1)} %shard_map.66), channel_id=1, source_target_pairs={{0,1},{1,0},{2,3},{3,2},{4,5},{5,4},{6,7},{7,6},{8,9},{9,8},{10,11... | collective-permute-start | bytes 2654216 | tf_op jit(solution)/shard_map/ppermute | solution.py:25
  80.9 9.9 %collective-permute-start.24 = (bf16[144,1024]{1,0:T(8,128)(2,1)S(1)}, bf16[144,1024]{1,0:T(8,128)(2,1)S(1)}, u32[]{:S(2)}, u32[]{:S(2)}) collective-permute-start(bf16[144,1024]{1,0:T(8,128)(2,1)S(1)} %get-tuple-element.68), channel_id=1, source_target_pairs={{0,128},{64,192},{128,0},{192,64},{1,129},{65,193},{129,1},{193,65... | collective-permute-start | bytes 884744 | tf_op jit(solution)/shard_map/ppermute | solution.py:21
  83.7 14.0 %collective-permute-start.26 = (bf16[144,1024]{1,0:T(8,128)(2,1)S(1)}, bf16[144,1024]{1,0:T(8,128)(2,1)S(1)}, u32[]{:S(2)}, u32[]{:S(2)}) collective-permute-start(bf16[144,1024]{1,0:T(8,128)(2,1)S(1)} %get-tuple-element.74), channel_id=1, source_target_pairs={{0,64},{64,128},{128,192},{192,0},{1,65},{65,129},{129,193},{193,1... | collective-permute-start | bytes 884744 | tf_op jit(solution)/shard_map/ppermute | solution.py:21
  84.7 13.2 %copy-start.2 = (f32[128]{0:T(128)S(1)}, f32[128]{0:T(128)}, u32[]{:S(2)}) copy-start(f32[128]{0:T(128)} %param.5) | copy-start | bytes 1540
  84.7 13.1 %collective-permute-start.27 = (bf16[144,1024]{1,0:T(8,128)(2,1)S(1)}, bf16[144,1024]{1,0:T(8,128)(2,1)S(1)}, u32[]{:S(2)}, u32[]{:S(2)}) collective-permute-start(bf16[144,1024]{1,0:T(8,128)(2,1)S(1)} %get-tuple-element.75), channel_id=1, source_target_pairs={{0,192},{64,0},{128,64},{192,128},{1,193},{65,1},{129,65},{193,129... | collective-permute-start | bytes 884744 | tf_op jit(solution)/shard_map/ppermute | solution.py:21
  92.1 5.8 %collective-permute-start.25 = (bf16[144,1024]{1,0:T(8,128)(2,1)S(1)}, bf16[144,1024]{1,0:T(8,128)(2,1)S(1)}, u32[]{:S(2)}, u32[]{:S(2)}) collective-permute-start(bf16[144,1024]{1,0:T(8,128)(2,1)S(1)} %get-tuple-element.72), channel_id=1, source_target_pairs={{0,1},{1,0},{2,3},{3,2},{4,5},{5,4},{6,7},{7,6},{8,9},{9,8},{10,11... | collective-permute-start | bytes 884744 | tf_op jit(solution)/shard_map/ppermute | solution.py:25

commit v15 on v14

--- a/solution.py
+++ b/solution.py
@@ -385,18 +385,19 @@
     table = [fixed(v) for d in ORDER for v in (near[d], swap_cores(near[d]))]
 
     sides = [swap_halves(two), swap_halves(three)]
-    part = lax.dynamic_slice_in_dim(three, start_c, sub, 0)
+    part, *table = lax.optimization_barrier([three, *table])
+    part = lax.dynamic_slice_in_dim(part, start_c, sub, 0)
     four, last = along_z(part, 1), from_partner(part)
     lots = [[fixed(v) for v in (own, one, first, two, sides[0])]]
     *table, scores, energy = score(table, lots[0])
     table, logits, local = [fixed(v) for v in table], [scores], [energy]
-    sides[1], _ = lax.optimization_barrier((sides[1], energy))
-    lots.append([fixed(v) for v in (three, sides[1])])
+    middle, _ = lax.optimization_barrier((three, energy))
+    lots.append([fixed(middle)])
     scores, energy = score(table, lots[1])
     last, _ = lax.optimization_barrier((last, energy))
     logits.append(scores)
     local.append(energy)
-    lots.append([fixed(four), fixed(last)])
+    lots.append([fixed(sides[1]), fixed(four), fixed(last)])
     scores, energy = score(table, lots[2])
     logits.append(scores)
     local.append(energy)

time: 99.1 us -> 99.2 us (level)
    ppermute x6, waiting for transfers between devices: 9.06 us -> 7.43 us  [along_z(): return lax.ppermute(value, ('z', 'c'), pairs)]
    ppermute x9, waiting for transfers between devices: 2.94 us -> 4.48 us  [swap_cores(): return lax.ppermute(value, 'c', [(0, 1), (1, 0)])]
  transfers between devices with their start and end apart: 28 -> 28, of which waited for: 17 -> 18; matrix products, arithmetic and copies ran while one was open for 0% -> 0% of each run, Pallas kernels for 9% -> 8%
where the time goes in v15:
time: 99.2 us; the launch traced here: 99.1 us
  starting transfers between devices  48.4 us (49%)
  waiting for transfers between devices  34.8 us (35%)
  Pallas kernels  13.7 us (14%)
  local copies, waits for them, and re-layouts  1.43 us (1%)
    ppermute x6, waiting for transfers between devices, shift_x(): return lax.ppermute(value, 'x', [(i, (i + by) % NX) for i in range(NX)])  17.1 us
    ppermute x6, starting transfers between devices, along_z(): return lax.ppermute(value, ('z', 'c'), pairs)  13.8 us
    ppermute x9, starting transfers between devices, swap_cores(): return lax.ppermute(value, 'c', [(0, 1), (1, 0)])  12.6 us
    ppermute x6, starting transfers between devices, shift_x(): return lax.ppermute(value, 'x', [(i, (i + by) % NX) for i in range(NX)])  10.3 us
    ppermute x6, waiting for transfers between devices, along_z(): return lax.ppermute(value, ('z', 'c'), pairs)  7.43 us
    pallas_call x3, Pallas kernels, score(): pl.pallas_call(functools.partial(score_kernel, 0 if whole else len(table)...  6.78 us
    ppermute x3, starting transfers between devices, swap_halves(): return lax.ppermute(value, ('y', 'c'), pairs)  5.41 us
    pallas_call x3, Pallas kernels, weigh(): pl.pallas_call(functools.partial(weigh_kernel, lots, groups, sizes, len(k...  4.95 us
  transfers between devices with their start and end apart: 28, of which 18 were waited for; matrix products, arithmetic and copies ran while one was open for 0% of the time, Pallas kernels for 8%

profile of v15, /device:TPU:1, one launch (start us, length us, event | category | flops | bytes accessed | tf_op | source)
XLA Modules:
  0.0 99.1 jit_solution(7055361180619922574)
XLA Ops:
  2.0 6.5 %collective-permute-start = (bf16[256,1024]{1,0:T(8,128)(2,1)S(1)}, bf16[256,1024]{1,0:T(8,128)(2,1)S(1)}, u32[]{:S(2)}, u32[]{:S(2)}) collective-permute-start(bf16[256,1024]{1,0:T(8,128)(2,1)S(1)} %constant_dynamic-slice_fusion.2), channel_id=1, source_target_pairs={{0,8},{1,57},{8,16},{9,1},{16,24},{17,9},{24,32},{25,17},{32,40},{... | collective-permute-start | bytes 1572872 | tf_op jit(solution)/shard_map/ppermute | solution.py:33
  8.5 1.2 %collective-permute-start.2 = (bf16[128,1024]{1,0:T(8,128)(2,1)}, bf16[128,1024]{1,0:T(8,128)(2,1)S(1)}, u32[]{:S(2)}, u32[]{:S(2)}) collective-permute-start(bf16[128,1024]{1,0:T(8,128)(2,1)} %centroids.1), channel_id=1, source_target_pairs={{0,64},{64,128},{128,192},{192,0},{1,65},{65,129},{129,193},{193,1... | collective-permute-start | bytes 786440 | tf_op jit(solution)/shard_map/ppermute | solution.py:21
  9.7 1.5 %collective-permute-start.1 = (bf16[128,1024]{1,0:T(8,128)(2,1)}, bf16[128,1024]{1,0:T(8,128)(2,1)S(1)}, u32[]{:S(2)}, u32[]{:S(2)}) collective-permute-start(bf16[128,1024]{1,0:T(8,128)(2,1)} %centroids.1), channel_id=1, source_target_pairs={{0,192},{64,0},{128,64},{192,128},{1,193},{65,1},{129,65},{193,129... | collective-permute-start | bytes 786440 | tf_op jit(solution)/shard_map/ppermute | solution.py:21
  11.2 4.5 %collective-permute-done.2.refs_4_ = bf16[128,1024]{1,0:T(8,128)(2,1)S(1)} collective-permute-done((bf16[128,1024]{1,0:T(8,128)(2,1)}, bf16[128,1024]{1,0:T(8,128)(2,1)S(1)}, u32[]{:S(2)}, u32[]{:S(2)}) %collective-permute-start.2) | collective-permute-done | bytes 262176 | tf_op jit(solution)/shard_map/ppermute | solution.py:21
  16.0 2.5 %collective-permute-start.3 = (bf16[256,1024]{1,0:T(8,128)(2,1)S(1)}, bf16[256,1024]{1,0:T(8,128)(2,1)S(1)}, u32[]{:S(2)}, u32[]{:S(2)}) collective-permute-start(bf16[256,1024]{1,0:T(8,128)(2,1)S(1)} %collective-permute-done.refs_9_.refs_4_), channel_id=1, source_target_pairs={{0,8},{1,57},{8,16},{9,1},{16,24},{17,9},{24,32},{25,17},{32,40},{... | collective-permute-start | bytes 1572872 | tf_op jit(solution)/shard_map/ppermute | solution.py:33
  18.5 2.7 %collective-permute-start.10 = (bf16[256,1024]{1,0:T(8,128)(2,1)S(1)}, bf16[256,1024]{1,0:T(8,128)(2,1)S(1)}, u32[]{:S(2)}, u32[]{:S(2)}) collective-permute-start(bf16[256,1024]{1,0:T(8,128)(2,1)S(1)} %collective-permute-done.refs_9_.refs_4_), channel_id=1, source_target_pairs={{0,2},{1,7},{2,0},{3,5},{4,6},{5,3},{6,4},{7,1},{8,10},{9,15},{10,... | collective-permute-start | bytes 1572872 | tf_op jit(solution)/shard_map/ppermute | solution.py:45
  21.3 2.4 %collective-permute-start.4 = (bf16[128,1024]{1,0:T(8,128)(2,1)S(1)}, bf16[128,1024]{1,0:T(8,128)(2,1)S(1)}, u32[]{:S(2)}, u32[]{:S(2)}) collective-permute-start(bf16[128,1024]{1,0:T(8,128)(2,1)S(1)} %collective-permute-done.1.refs_2_), channel_id=1, source_target_pairs={{0,192},{64,0},{128,64},{192,128},{1,193},{65,1},{129,65},{193,129... | collective-permute-start | bytes 786440 | tf_op jit(solution)/shard_map/ppermute | solution.py:21
  23.6 3.6 %collective-permute-done.4.refs_0_ = bf16[128,1024]{1,0:T(8,128)(2,1)S(1)} collective-permute-done((bf16[128,1024]{1,0:T(8,128)(2,1)S(1)}, bf16[128,1024]{1,0:T(8,128)(2,1)S(1)}, u32[]{:S(2)}, u32[]{:S(2)}) %collective-permute-start.4) | collective-permute-done | bytes 262176 | tf_op jit(solution)/shard_map/ppermute | solution.py:21
  27.2 2.2 %collective-permute-start.5 = (bf16[256,1024]{1,0:T(8,128)(2,1)S(1)}, bf16[256,1024]{1,0:T(8,128)(2,1)S(1)}, u32[]{:S(2)}, u32[]{:S(2)}) collective-permute-start(bf16[256,1024]{1,0:T(8,128)(2,1)S(1)} %collective-permute-done.3.refs_11_.refs_6_), channel_id=1, source_target_pairs={{0,8},{1,57},{8,16},{9,1},{16,24},{17,9},{24,32},{25,17},{32,40},{... | collective-permute-start | bytes 1572872 | tf_op jit(solution)/shard_map/ppermute | solution.py:33
  31.1 1.4 %collective-permute-done.8.refs_5_ = bf16[128,1024]{1,0:T(8,128)(2,1)S(1)} collective-permute-done((bf16[128,1024]{1,0:T(8,128)(2,1)S(1)}, bf16[128,1024]{1,0:T(8,128)(2,1)S(1)}, u32[]{:S(2)}, u32[]{:S(2)}) %collective-permute-start.8) | collective-permute-done | bytes 262176 | tf_op jit(solution)/shard_map/ppermute | solution.py:25
  32.8 2.8 %collective-permute-done.5.refs_2_.refs_8_ = bf16[256,1024]{1,0:T(8,128)(2,1)S(1)} collective-permute-done((bf16[256,1024]{1,0:T(8,128)(2,1)S(1)}, bf16[256,1024]{1,0:T(8,128)(2,1)S(1)}, u32[]{:S(2)}, u32[]{:S(2)}) %collective-permute-start.5) | collective-permute-done | bytes 524320 | tf_op jit(solution)/shard_map/ppermute | solution.py:33
  35.7 4.0 %collective-permute-start.14 = (bf16[128,1024]{1,0:T(8,128)(2,1)S(1)}, bf16[128,1024]{1,0:T(8,128)(2,1)S(1)}, u32[]{:S(2)}, u32[]{:S(2)}) collective-permute-start(bf16[128,1024]{1,0:T(8,128)(2,1)S(1)} %constant_dynamic-slice_fusion), channel_id=1, source_target_pairs={{0,10},{1,63},{2,8},{3,61},{4,14},{5,59},{6,12},{7,57},{8,18},{9,7... | collective-permute-start | bytes 786440 | tf_op jit(solution)/shard_map/ppermute | solution.py:59
  39.6 1.6 %collective-permute-start.12 = (bf16[256,1024]{1,0:T(8,128)(2,1)S(1)}, bf16[256,1024]{1,0:T(8,128)(2,1)S(1)}, u32[]{:S(2)}, u32[]{:S(2)}) collective-permute-start(bf16[256,1024]{1,0:T(8,128)(2,1)S(1)} %collective-permute-done.5.refs_2_.refs_8_), channel_id=1, source_target_pairs={{0,2},{1,7},{2,0},{3,5},{4,6},{5,3},{6,4},{7,1},{8,10},{9,15},{10,... | collective-permute-start | bytes 1572872 | tf_op jit(solution)/shard_map/ppermute | solution.py:45
  41.3 4.2 %shard_map.58 = (bf16[1024,1024]{1,0:T(8,128)(2,1)S(1)}, f32[1024,128]{1,0:T(8,128)S(1)}, f32[1024,1280]{1,0:T(8,128)S(1)}, f32[1,1280]{1,0:T(1,128)S(1)}) custom-call(bf16[128,1024]{1,0:T(8,128)(2,1)S(1)} %collective-permute-done.4.refs_0_, bf16[128,1024]{1,0:T(8,128)(2,1)S(1)} %collective-permute-done.6.refs_1_, ...), custom_call_target="tpu_custom_call" | custom-call | flops 5368709120 | bytes 9961472 | tf_op jit(solution)/shard_map/pallas_call | solution.py:229
  46.4 2.5 %collective-permute-done.12.refs_2_.refs_9_ = bf16[256,1024]{1,0:T(8,128)(2,1)S(1)} collective-permute-done((bf16[256,1024]{1,0:T(8,128)(2,1)S(1)}, bf16[256,1024]{1,0:T(8,128)(2,1)S(1)}, u32[]{:S(2)}, u32[]{:S(2)}) %collective-permute-start.12) | collective-permute-done | bytes 524320 | tf_op jit(solution)/shard_map/ppermute | solution.py:45
  48.9 1.7 %shard_map.60 = (f32[1024,512]{1,0:T(8,128)S(1)}, f32[1,512]{1,0:T(1,128)S(1)}) custom-call(bf16[1024,1024]{1,0:T(8,128)(2,1)S(1)} %get-tuple-element.70.refs_0_, f32[1024,128]{1,0:T(8,128)S(1)} %get-tuple-element.71.refs_1_, bf16[256,1024]{1,0:T(8,128)(2,1)S(1)} %collective-permute-done.12.refs_2_.refs_9_, ...), custom_call_target="tpu_custom_call" | custom-call | flops 2147483648 | bytes 5242880 | tf_op jit(solution)/shard_map/pallas_call | solution.py:229
  50.6 1.8 %collective-permute-start.17 = (f32[16,128]{1,0:T(8,128)S(1)}, f32[16,128]{1,0:T(8,128)S(1)}, u32[]{:S(2)}, u32[]{:S(2)}) collective-permute-start(f32[16,128]{1,0:T(8,128)S(1)} %shard_map.61.own), channel_id=1, source_target_pairs={{0,6},{2,0},{4,2},{6,4},{1,7},{3,1},{5,3},{7,5},{8,14},{10,8},{12,... | collective-permute-start | bytes 24584 | tf_op jit(solution)/shard_map/ppermute | solution.py:37
  53.2 3.2 %collective-permute-done.16.refs_1_ = f32[16,128]{1,0:T(8,128)S(1)} collective-permute-done((f32[16,128]{1,0:T(8,128)S(1)}, f32[16,128]{1,0:T(8,128)S(1)}, u32[]{:S(2)}, u32[]{:S(2)}) %collective-permute-start.16) | collective-permute-done | bytes 8224 | tf_op jit(solution)/shard_map/ppermute | solution.py:37
  56.4 4.2 %collective-permute-start.18 = (f32[16,128]{1,0:T(8,128)S(1)}, f32[16,128]{1,0:T(8,128)S(1)}, u32[]{:S(2)}, u32[]{:S(2)}) collective-permute-start(f32[16,128]{1,0:T(8,128)S(1)} %shard_map.62.mine), channel_id=1, source_target_pairs={{0,1},{1,0},{2,3},{3,2},{4,5},{5,4},{6,7},{7,6},{8,9},{9,8},{10,11... | collective-permute-start | bytes 24584 | tf_op jit(solution)/shard_map/ppermute | solution.py:25
  62.2 1.8 %collective-permute-done.19.near = f32[4,8,128]{2,1,0:T(8,128)S(1)} collective-permute-done((f32[4,8,128]{2,1,0:T(8,128)S(1)}, f32[4,8,128]{2,1,0:T(8,128)S(1)}, u32[]{:S(2)}, u32[]{:S(2)}) %collective-permute-start.19) | collective-permute-done | bytes 16416 | tf_op jit(solution)/shard_map/ppermute | solution.py:33
  64.1 2.7 %collective-permute-start.20 = (f32[4,8,128]{2,1,0:T(8,128)S(1)}, f32[4,8,128]{2,1,0:T(8,128)S(1)}, u32[]{:S(2)}, u32[]{:S(2)}) collective-permute-start(f32[4,8,128]{2,1,0:T(8,128)S(1)} %collective-permute-done.19.near), channel_id=1, source_target_pairs={{0,1},{1,0},{2,3},{3,2},{4,5},{5,4},{6,7},{7,6},{8,9},{9,8},{10,11... | collective-permute-start | bytes 49160 | tf_op jit(solution)/shard_map/ppermute | solution.py:25
  67.7 1.7 %collective-permute-start.21 = (f32[4,8,128]{2,1,0:T(8,128)S(1)}, f32[4,8,128]{2,1,0:T(8,128)S(1)}, u32[]{:S(2)}, u32[]{:S(2)}) collective-permute-start(f32[4,8,128]{2,1,0:T(8,128)S(1)} %get-tuple-element.79), channel_id=1, source_target_pairs={{0,24},{1,41},{8,32},{9,49},{16,40},{17,57},{24,48},{25,1},{32,56}... | collective-permute-start | bytes 49160 | tf_op jit(solution)/shard_map/ppermute | solution.py:33
  69.3 2.8 %collective-permute-done.21.got = f32[4,8,128]{2,1,0:T(8,128)S(1)} collective-permute-done((f32[4,8,128]{2,1,0:T(8,128)S(1)}, f32[4,8,128]{2,1,0:T(8,128)S(1)}, u32[]{:S(2)}, u32[]{:S(2)}) %collective-permute-start.21) | collective-permute-done | bytes 16416 | tf_op jit(solution)/shard_map/ppermute | solution.py:33
  72.1 2.7 %collective-permute-start.22 = (f32[4,8,128]{2,1,0:T(8,128)S(1)}, f32[4,8,128]{2,1,0:T(8,128)S(1)}, u32[]{:S(2)}, u32[]{:S(2)}) collective-permute-start(f32[4,8,128]{2,1,0:T(8,128)S(1)} %collective-permute-done.21.got), channel_id=1, source_target_pairs={{0,1},{1,0},{2,3},{3,2},{4,5},{5,4},{6,7},{7,6},{8,9},{9,8},{10,11... | collective-permute-start | bytes 49160 | tf_op jit(solution)/shard_map/ppermute | solution.py:25
  76.3 1.8 %shard_map.66 = bf16[432,1024]{1,0:T(8,128)(2,1)S(1)} custom-call(f32[1,2048]{1,0:T(1,128)S(1)} %get-tuple-element.87.energy, f32[1024,1280]{1,0:T(8,128)S(1)} %get-tuple-element.81.refs_0_, f32[1024,256]{1,0:T(8,128)S(1)} %get-tuple-element.82.refs_1_, f32[1024,512]{1,0:T(8,128)S(1)} %get-tuple-element.83.refs_2_, bf16[256,1024]{1,0:T(8,128)(2,1)S(1)} %bitcast.9, ...), custom_call_target="tpu_custom_call" | custom-call | flops 1610612736 | bytes 7340032 | tf_op jit(solution)/shard_map/pallas_call | solution.py:308
  78.5 1.8 %shard_map.67 = (f32[384,1024]{1,0:T(8,128)S(1)}, f32[48,128]{1,0:T(8,128)S(1)}) custom-call(f32[1,2048]{1,0:T(1,128)S(1)} %get-tuple-element.87.energy, f32[1024,1280]{1,0:T(8,128)S(1)} %get-tuple-element.81.refs_0_, f32[1024,256]{1,0:T(8,128)S(1)} %get-tuple-element.82.refs_1_, f32[1024,512]{1,0:T(8,128)S(1)} %get-tuple-element.83.refs_2_, ...), custom_call_target="tpu_custom_call" | custom-call | flops 1610612736 | bytes 7340032 | tf_op jit(solution)/shard_map/pallas_call | solution.py:308
  80.8 2.6 %collective-permute-start.24 = (bf16[144,1024]{1,0:T(8,128)(2,1)S(1)}, bf16[144,1024]{1,0:T(8,128)(2,1)S(1)}, u32[]{:S(2)}, u32[]{:S(2)}) collective-permute-start(bf16[144,1024]{1,0:T(8,128)(2,1)S(1)} %get-tuple-element.86), channel_id=1, source_target_pairs={{0,128},{64,192},{128,0},{192,64},{1,129},{65,193},{129,1},{193,65... | collective-permute-start | bytes 884744 | tf_op jit(solution)/shard_map/ppermute | solution.py:21
  83.3 1.5 %collective-permute-start.26 = (bf16[144,1024]{1,0:T(8,128)(2,1)S(1)}, bf16[144,1024]{1,0:T(8,128)(2,1)S(1)}, u32[]{:S(2)}, u32[]{:S(2)}) collective-permute-start(bf16[144,1024]{1,0:T(8,128)(2,1)S(1)} %get-tuple-element.92), channel_id=1, source_target_pairs={{0,64},{64,128},{128,192},{192,0},{1,65},{65,129},{129,193},{193,1... | collective-permute-start | bytes 884744 | tf_op jit(solution)/shard_map/ppermute | solution.py:21
  86.0 4.7 %collective-permute-done.24.one = bf16[144,1024]{1,0:T(8,128)(2,1)S(1)} collective-permute-done((bf16[144,1024]{1,0:T(8,128)(2,1)S(1)}, bf16[144,1024]{1,0:T(8,128)(2,1)S(1)}, u32[]{:S(2)}, u32[]{:S(2)}) %collective-permute-start.24) | collective-permute-done | bytes 294944 | tf_op jit(solution)/shard_map/ppermute | solution.py:21
  90.7 1.3 %shard_map.69 = (bf16[144,1024]{1,0:T(8,128)(2,1)S(1)}, f32[128,1024]{1,0:T(8,128)S(1)}, f32[16,128]{1,0:T(8,128)S(1)}) custom-call(f32[1,2048]{1,0:T(1,128)S(1)} %get-tuple-element.87.energy, f32[1024,1280]{1,0:T(8,128)S(1)} %get-tuple-element.81.refs_0_, f32[1024,256]{1,0:T(8,128)S(1)} %get-tuple-element.82.refs_1_, ...), custom_call_target="tpu_custom_call" | custom-call | flops 1073741824 | bytes 6291456 | tf_op jit(solution)/shard_map/pallas_call | solution.py:308
  92.0 2.0 %collective-permute-start.25 = (bf16[144,1024]{1,0:T(8,128)(2,1)S(1)}, bf16[144,1024]{1,0:T(8,128)(2,1)S(1)}, u32[]{:S(2)}, u32[]{:S(2)}) collective-permute-start(bf16[144,1024]{1,0:T(8,128)(2,1)S(1)} %get-tuple-element.90), channel_id=1, source_target_pairs={{0,1},{1,0},{2,3},{3,2},{4,5},{5,4},{6,7},{7,6},{8,9},{9,8},{10,11... | collective-permute-start | bytes 884744 | tf_op jit(solution)/shard_map/ppermute | solution.py:25
  94.0 3.6 %collective-permute-done.26.two = bf16[144,1024]{1,0:T(8,128)(2,1)S(1)} collective-permute-done((bf16[144,1024]{1,0:T(8,128)(2,1)S(1)}, bf16[144,1024]{1,0:T(8,128)(2,1)S(1)}, u32[]{:S(2)}, u32[]{:S(2)}) %collective-permute-start.26) | collective-permute-done | bytes 294944 | tf_op jit(solution)/shard_map/ppermute | solution.py:21
  (49 shorter events, 12.9 us)
Async XLA Ops:
  0.6 1.2 %copy-start = (bf16[512,1024]{1,0:T(8,128)(2,1)S(1)}, bf16[512,1024]{1,0:T(8,128)(2,1)}, u32[]{:S(2)}) copy-start(bf16[512,1024]{1,0:T(8,128)(2,1)} %param.3) | copy-start | bytes 3145732
  0.6 40.6 %copy-start.1 = (bf16[128,1024]{1,0:T(8,128)(2,1)S(1)}, bf16[128,1024]{1,0:T(8,128)(2,1)}, u32[]{:S(2)}) copy-start(bf16[128,1024]{1,0:T(8,128)(2,1)} %centroids.1) | copy-start | bytes 786436
  2.0 14.0 %collective-permute-start = (bf16[256,1024]{1,0:T(8,128)(2,1)S(1)}, bf16[256,1024]{1,0:T(8,128)(2,1)S(1)}, u32[]{:S(2)}, u32[]{:S(2)}) collective-permute-start(bf16[256,1024]{1,0:T(8,128)(2,1)S(1)} %constant_dynamic-slice_fusion.2), channel_id=1, source_target_pairs={{0,8},{1,57},{8,16},{9,1},{16,24},{17,9},{24,32},{25,17},{32,40},{... | collective-permute-start | bytes 1572872 | tf_op jit(solution)/shard_map/ppermute | solution.py:33
  8.5 7.2 %collective-permute-start.2 = (bf16[128,1024]{1,0:T(8,128)(2,1)}, bf16[128,1024]{1,0:T(8,128)(2,1)S(1)}, u32[]{:S(2)}, u32[]{:S(2)}) collective-permute-start(bf16[128,1024]{1,0:T(8,128)(2,1)} %centroids.1), channel_id=1, source_target_pairs={{0,64},{64,128},{128,192},{192,0},{1,65},{65,129},{129,193},{193,1... | collective-permute-start | bytes 786440 | tf_op jit(solution)/shard_map/ppermute | solution.py:21
  9.7 6.3 %collective-permute-start.1 = (bf16[128,1024]{1,0:T(8,128)(2,1)}, bf16[128,1024]{1,0:T(8,128)(2,1)S(1)}, u32[]{:S(2)}, u32[]{:S(2)}) collective-permute-start(bf16[128,1024]{1,0:T(8,128)(2,1)} %centroids.1), channel_id=1, source_target_pairs={{0,192},{64,0},{128,64},{192,128},{1,193},{65,1},{129,65},{193,129... | collective-permute-start | bytes 786440 | tf_op jit(solution)/shard_map/ppermute | solution.py:21
  16.0 11.3 %collective-permute-start.3 = (bf16[256,1024]{1,0:T(8,128)(2,1)S(1)}, bf16[256,1024]{1,0:T(8,128)(2,1)S(1)}, u32[]{:S(2)}, u32[]{:S(2)}) collective-permute-start(bf16[256,1024]{1,0:T(8,128)(2,1)S(1)} %collective-permute-done.refs_9_.refs_4_), channel_id=1, source_target_pairs={{0,8},{1,57},{8,16},{9,1},{16,24},{17,9},{24,32},{25,17},{32,40},{... | collective-permute-start | bytes 1572872 | tf_op jit(solution)/shard_map/ppermute | solution.py:33
  18.5 10.9 %collective-permute-start.10 = (bf16[256,1024]{1,0:T(8,128)(2,1)S(1)}, bf16[256,1024]{1,0:T(8,128)(2,1)S(1)}, u32[]{:S(2)}, u32[]{:S(2)}) collective-permute-start(bf16[256,1024]{1,0:T(8,128)(2,1)S(1)} %collective-permute-done.refs_9_.refs_4_), channel_id=1, source_target_pairs={{0,2},{1,7},{2,0},{3,5},{4,6},{5,3},{6,4},{7,1},{8,10},{9,15},{10,... | collective-permute-start | bytes 1572872 | tf_op jit(solution)/shard_map/ppermute | solution.py:45
  21.3 6.0 %collective-permute-start.4 = (bf16[128,1024]{1,0:T(8,128)(2,1)S(1)}, bf16[128,1024]{1,0:T(8,128)(2,1)S(1)}, u32[]{:S(2)}, u32[]{:S(2)}) collective-permute-start(bf16[128,1024]{1,0:T(8,128)(2,1)S(1)} %collective-permute-done.1.refs_2_), channel_id=1, source_target_pairs={{0,192},{64,0},{128,64},{192,128},{1,193},{65,1},{129,65},{193,129... | collective-permute-start | bytes 786440 | tf_op jit(solution)/shard_map/ppermute | solution.py:21
  23.6 7.4 %collective-permute-start.9 = (bf16[128,1024]{1,0:T(8,128)(2,1)}, bf16[128,1024]{1,0:T(8,128)(2,1)S(1)}, u32[]{:S(2)}, u32[]{:S(2)}) collective-permute-start(bf16[128,1024]{1,0:T(8,128)(2,1)} %centroids.1), channel_id=1, source_target_pairs={{0,1},{1,0},{2,3},{3,2},{4,5},{5,4},{6,7},{7,6},{8,9},{9,8},{10,11... | collective-permute-start | bytes 786440 | tf_op jit(solution)/shard_map/ppermute | solution.py:25
  27.2 8.3 %collective-permute-start.5 = (bf16[256,1024]{1,0:T(8,128)(2,1)S(1)}, bf16[256,1024]{1,0:T(8,128)(2,1)S(1)}, u32[]{:S(2)}, u32[]{:S(2)}) collective-permute-start(bf16[256,1024]{1,0:T(8,128)(2,1)S(1)} %collective-permute-done.3.refs_11_.refs_6_), channel_id=1, source_target_pairs={{0,8},{1,57},{8,16},{9,1},{16,24},{17,9},{24,32},{25,17},{32,40},{... | collective-permute-start | bytes 1572872 | tf_op jit(solution)/shard_map/ppermute | solution.py:33
  29.5 11.8 %collective-permute-start.11 = (bf16[256,1024]{1,0:T(8,128)(2,1)S(1)}, bf16[256,1024]{1,0:T(8,128)(2,1)S(1)}, u32[]{:S(2)}, u32[]{:S(2)}) collective-permute-start(bf16[256,1024]{1,0:T(8,128)(2,1)S(1)} %collective-permute-done.3.refs_11_.refs_6_), channel_id=1, source_target_pairs={{0,2},{1,7},{2,0},{3,5},{4,6},{5,3},{6,4},{7,1},{8,10},{9,15},{10,... | collective-permute-start | bytes 1572872 | tf_op jit(solution)/shard_map/ppermute | solution.py:45
  30.5 1.9 %collective-permute-start.7 = (bf16[128,1024]{1,0:T(8,128)(2,1)S(1)}, bf16[128,1024]{1,0:T(8,128)(2,1)S(1)}, u32[]{:S(2)}, u32[]{:S(2)}) collective-permute-start(bf16[128,1024]{1,0:T(8,128)(2,1)S(1)} %collective-permute-done.1.refs_2_), channel_id=1, source_target_pairs={{0,1},{1,0},{2,3},{3,2},{4,5},{5,4},{6,7},{7,6},{8,9},{9,8},{10,11... | collective-permute-start | bytes 786440 | tf_op jit(solution)/shard_map/ppermute | solution.py:25
  30.5 1.9 %collective-permute-start.8 = (bf16[128,1024]{1,0:T(8,128)(2,1)S(1)}, bf16[128,1024]{1,0:T(8,128)(2,1)S(1)}, u32[]{:S(2)}, u32[]{:S(2)}) collective-permute-start(bf16[128,1024]{1,0:T(8,128)(2,1)S(1)} %collective-permute-done.2.refs_4_), channel_id=1, source_target_pairs={{0,1},{1,0},{2,3},{3,2},{4,5},{5,4},{6,7},{7,6},{8,9},{9,8},{10,11... | collective-permute-start | bytes 786440 | tf_op jit(solution)/shard_map/ppermute | solution.py:25
  31.0 1.8 %collective-permute-start.6 = (bf16[128,1024]{1,0:T(8,128)(2,1)S(1)}, bf16[128,1024]{1,0:T(8,128)(2,1)S(1)}, u32[]{:S(2)}, u32[]{:S(2)}) collective-permute-start(bf16[128,1024]{1,0:T(8,128)(2,1)S(1)} %collective-permute-done.4.refs_0_), channel_id=1, source_target_pairs={{0,1},{1,0},{2,3},{3,2},{4,5},{5,4},{6,7},{7,6},{8,9},{9,8},{10,11... | collective-permute-start | bytes 786440 | tf_op jit(solution)/shard_map/ppermute | solution.py:25
  35.7 10.7 %collective-permute-start.14 = (bf16[128,1024]{1,0:T(8,128)(2,1)S(1)}, bf16[128,1024]{1,0:T(8,128)(2,1)S(1)}, u32[]{:S(2)}, u32[]{:S(2)}) collective-permute-start(bf16[128,1024]{1,0:T(8,128)(2,1)S(1)} %constant_dynamic-slice_fusion), channel_id=1, source_target_pairs={{0,10},{1,63},{2,8},{3,61},{4,14},{5,59},{6,12},{7,57},{8,18},{9,7... | collective-permute-start | bytes 786440 | tf_op jit(solution)/shard_map/ppermute | solution.py:59
  39.6 6.8 %collective-permute-start.13 = (bf16[128,1024]{1,0:T(8,128)(2,1)S(1)}, bf16[128,1024]{1,0:T(8,128)(2,1)S(1)}, u32[]{:S(2)}, u32[]{:S(2)}) collective-permute-start(bf16[128,1024]{1,0:T(8,128)(2,1)S(1)} %constant_dynamic-slice_fusion), channel_id=1, source_target_pairs={{0,8},{1,57},{8,16},{9,1},{16,24},{17,9},{24,32},{25,17},{32,40},{... | collective-permute-start | bytes 786440 | tf_op jit(solution)/shard_map/ppermute | solution.py:33
  39.6 9.2 %collective-permute-start.12 = (bf16[256,1024]{1,0:T(8,128)(2,1)S(1)}, bf16[256,1024]{1,0:T(8,128)(2,1)S(1)}, u32[]{:S(2)}, u32[]{:S(2)}) collective-permute-start(bf16[256,1024]{1,0:T(8,128)(2,1)S(1)} %collective-permute-done.5.refs_2_.refs_8_), channel_id=1, source_target_pairs={{0,2},{1,7},{2,0},{3,5},{4,6},{5,3},{6,4},{7,1},{8,10},{9,15},{10,... | collective-permute-start | bytes 1572872 | tf_op jit(solution)/shard_map/ppermute | solution.py:45
  50.6 2.6 %collective-permute-start.17 = (f32[16,128]{1,0:T(8,128)S(1)}, f32[16,128]{1,0:T(8,128)S(1)}, u32[]{:S(2)}, u32[]{:S(2)}) collective-permute-start(f32[16,128]{1,0:T(8,128)S(1)} %shard_map.61.own), channel_id=1, source_target_pairs={{0,6},{2,0},{4,2},{6,4},{1,7},{3,1},{5,3},{7,5},{8,14},{10,8},{12,... | collective-permute-start | bytes 24584 | tf_op jit(solution)/shard_map/ppermute | solution.py:37
  52.4 4.0 %collective-permute-start.16 = (f32[16,128]{1,0:T(8,128)S(1)}, f32[16,128]{1,0:T(8,128)S(1)}, u32[]{:S(2)}, u32[]{:S(2)}) collective-permute-start(f32[16,128]{1,0:T(8,128)S(1)} %shard_map.61.own), channel_id=1, source_target_pairs={{0,4},{2,6},{4,0},{6,2},{1,5},{3,7},{5,1},{7,3},{8,12},{10,14},{12... | collective-permute-start | bytes 24584 | tf_op jit(solution)/shard_map/ppermute | solution.py:37
  52.4 4.0 %collective-permute-start.15 = (f32[16,128]{1,0:T(8,128)S(1)}, f32[16,128]{1,0:T(8,128)S(1)}, u32[]{:S(2)}, u32[]{:S(2)}) collective-permute-start(f32[16,128]{1,0:T(8,128)S(1)} %shard_map.61.own), channel_id=1, source_target_pairs={{0,2},{2,4},{4,6},{6,0},{1,3},{3,5},{5,7},{7,1},{8,10},{10,12},{12... | collective-permute-start | bytes 24584 | tf_op jit(solution)/shard_map/ppermute | solution.py:37
  56.4 5.0 %collective-permute-start.18 = (f32[16,128]{1,0:T(8,128)S(1)}, f32[16,128]{1,0:T(8,128)S(1)}, u32[]{:S(2)}, u32[]{:S(2)}) collective-permute-start(f32[16,128]{1,0:T(8,128)S(1)} %shard_map.62.mine), channel_id=1, source_target_pairs={{0,1},{1,0},{2,3},{3,2},{4,5},{5,4},{6,7},{7,6},{8,9},{9,8},{10,11... | collective-permute-start | bytes 24584 | tf_op jit(solution)/shard_map/ppermute | solution.py:25
  61.4 2.7 %collective-permute-start.19 = (f32[4,8,128]{2,1,0:T(8,128)S(1)}, f32[4,8,128]{2,1,0:T(8,128)S(1)}, u32[]{:S(2)}, u32[]{:S(2)}) collective-permute-start(f32[4,8,128]{2,1,0:T(8,128)S(1)} %shard_map.63.block), channel_id=1, source_target_pairs={{0,8},{1,57},{8,16},{9,1},{16,24},{17,9},{24,32},{25,17},{32,40},{... | collective-permute-start | bytes 49160 | tf_op jit(solution)/shard_map/ppermute | solution.py:33
  64.1 3.5 %collective-permute-start.20 = (f32[4,8,128]{2,1,0:T(8,128)S(1)}, f32[4,8,128]{2,1,0:T(8,128)S(1)}, u32[]{:S(2)}, u32[]{:S(2)}) collective-permute-start(f32[4,8,128]{2,1,0:T(8,128)S(1)} %collective-permute-done.19.near), channel_id=1, source_target_pairs={{0,1},{1,0},{2,3},{3,2},{4,5},{5,4},{6,7},{7,6},{8,9},{9,8},{10,11... | collective-permute-start | bytes 49160 | tf_op jit(solution)/shard_map/ppermute | solution.py:25
  67.7 4.5 %collective-permute-start.21 = (f32[4,8,128]{2,1,0:T(8,128)S(1)}, f32[4,8,128]{2,1,0:T(8,128)S(1)}, u32[]{:S(2)}, u32[]{:S(2)}) collective-permute-start(f32[4,8,128]{2,1,0:T(8,128)S(1)} %get-tuple-element.79), channel_id=1, source_target_pairs={{0,24},{1,41},{8,32},{9,49},{16,40},{17,57},{24,48},{25,1},{32,56}... | collective-permute-start | bytes 49160 | tf_op jit(solution)/shard_map/ppermute | solution.py:33
  72.1 3.6 %collective-permute-start.22 = (f32[4,8,128]{2,1,0:T(8,128)S(1)}, f32[4,8,128]{2,1,0:T(8,128)S(1)}, u32[]{:S(2)}, u32[]{:S(2)}) collective-permute-start(f32[4,8,128]{2,1,0:T(8,128)S(1)} %collective-permute-done.21.got), channel_id=1, source_target_pairs={{0,1},{1,0},{2,3},{3,2},{4,5},{5,4},{6,7},{7,6},{8,9},{9,8},{10,11... | collective-permute-start | bytes 49160 | tf_op jit(solution)/shard_map/ppermute | solution.py:25
  78.1 2.5 %collective-permute-start.23 = (bf16[432,1024]{1,0:T(8,128)(2,1)S(1)}, bf16[432,1024]{1,0:T(8,128)(2,1)S(1)}, u32[]{:S(2)}, u32[]{:S(2)}) collective-permute-start(bf16[432,1024]{1,0:T(8,128)(2,1)S(1)} %shard_map.66), channel_id=1, source_target_pairs={{0,1},{1,0},{2,3},{3,2},{4,5},{5,4},{6,7},{7,6},{8,9},{9,8},{10,11... | collective-permute-start | bytes 2654216 | tf_op jit(solution)/shard_map/ppermute | solution.py:25
  80.8 9.9 %collective-permute-start.24 = (bf16[144,1024]{1,0:T(8,128)(2,1)S(1)}, bf16[144,1024]{1,0:T(8,128)(2,1)S(1)}, u32[]{:S(2)}, u32[]{:S(2)}) collective-permute-start(bf16[144,1024]{1,0:T(8,128)(2,1)S(1)} %get-tuple-element.86), channel_id=1, source_target_pairs={{0,128},{64,192},{128,0},{192,64},{1,129},{65,193},{129,1},{193,65... | collective-permute-start | bytes 884744 | tf_op jit(solution)/shard_map/ppermute | solution.py:21
  83.3 14.3 %collective-permute-start.26 = (bf16[144,1024]{1,0:T(8,128)(2,1)S(1)}, bf16[144,1024]{1,0:T(8,128)(2,1)S(1)}, u32[]{:S(2)}, u32[]{:S(2)}) collective-permute-start(bf16[144,1024]{1,0:T(8,128)(2,1)S(1)} %get-tuple-element.92), channel_id=1, source_target_pairs={{0,64},{64,128},{128,192},{192,0},{1,65},{65,129},{129,193},{193,1... | collective-permute-start | bytes 884744 | tf_op jit(solution)/shard_map/ppermute | solution.py:21
  84.8 13.2 %copy-start.2 = (f32[128]{0:T(128)S(1)}, f32[128]{0:T(128)}, u32[]{:S(2)}) copy-start(f32[128]{0:T(128)} %param.5) | copy-start | bytes 1540
  84.8 13.1 %collective-permute-start.27 = (bf16[144,1024]{1,0:T(8,128)(2,1)S(1)}, bf16[144,1024]{1,0:T(8,128)(2,1)S(1)}, u32[]{:S(2)}, u32[]{:S(2)}) collective-permute-start(bf16[144,1024]{1,0:T(8,128)(2,1)S(1)} %get-tuple-element.93), channel_id=1, source_target_pairs={{0,192},{64,0},{128,64},{192,128},{1,193},{65,1},{129,65},{193,129... | collective-permute-start | bytes 884744 | tf_op jit(solution)/shard_map/ppermute | solution.py:21
  92.0 6.0 %collective-permute-start.25 = (bf16[144,1024]{1,0:T(8,128)(2,1)S(1)}, bf16[144,1024]{1,0:T(8,128)(2,1)S(1)}, u32[]{:S(2)}, u32[]{:S(2)}) collective-permute-start(bf16[144,1024]{1,0:T(8,128)(2,1)S(1)} %get-tuple-element.90), channel_id=1, source_target_pairs={{0,1},{1,0},{2,3},{3,2},{4,5},{5,4},{6,7},{7,6},{8,9},{9,8},{10,11... | collective-permute-start | bytes 884744 | tf_op jit(solution)/shard_map/ppermute | solution.py:25

commit v16 on v15

--- a/solution.py
+++ b/solution.py
@@ -142,7 +142,7 @@
 
 def energies(local, place, sub):
     (mine,) = small(pack_kernel, place, [(16, sub)], *local)
-    (mine,) = small(sum_kernel, place, [(16, sub)], mine, *[shift_y(mine, d) for d in (1, 2, 3)])
+    (mine,) = small(sum_kernel, place, [(16, sub)], mine, *[shift_y(mine, d) for d in (1, 3, 2)])
     shape = (4, NZ, sub)
     (block,) = small(block_kernel, place, [shape], mine, swap_cores(mine))
     near = along_z(block, 1)

time: 99.2 us -> 99.8 us (level)
  starting transfers between devices: 48.4 us -> 49.6 us
where the time goes in v16:
time: 99.8 us; the launch traced here: 99.7 us
  starting transfers between devices  49.6 us (50%)
  waiting for transfers between devices  34.3 us (34%)
  Pallas kernels  13.7 us (14%)
  local copies, waits for them, and re-layouts  1.43 us (1%)
    ppermute x6, waiting for transfers between devices, shift_x(): return lax.ppermute(value, 'x', [(i, (i + by) % NX) for i in range(NX)])  17.1 us
    ppermute x6, starting transfers between devices, along_z(): return lax.ppermute(value, ('z', 'c'), pairs)  13.8 us
    ppermute x9, starting transfers between devices, swap_cores(): return lax.ppermute(value, 'c', [(0, 1), (1, 0)])  13.1 us
    ppermute x6, starting transfers between devices, shift_x(): return lax.ppermute(value, 'x', [(i, (i + by) % NX) for i in range(NX)])  10.3 us
    ppermute x6, waiting for transfers between devices, along_z(): return lax.ppermute(value, ('z', 'c'), pairs)  7.34 us
    pallas_call x3, Pallas kernels, score(): pl.pallas_call(functools.partial(score_kernel, 0 if whole else len(table)...  6.78 us
    ppermute x3, starting transfers between devices, swap_halves(): return lax.ppermute(value, ('y', 'c'), pairs)  5.41 us
    pallas_call x3, Pallas kernels, weigh(): pl.pallas_call(functools.partial(weigh_kernel, lots, groups, sizes, len(k...  4.95 us
  transfers between devices with their start and end apart: 28, of which 18 were waited for; matrix products, arithmetic and copies ran while one was open for 0% of the time, Pallas kernels for 8%

profile of v16, /device:TPU:1, one launch (start us, length us, event | category | flops | bytes accessed | tf_op | source)
XLA Modules:
  0.0 99.7 jit_solution(2151070478283834141)
XLA Ops:
  2.0 6.5 %collective-permute-start = (bf16[256,1024]{1,0:T(8,128)(2,1)S(1)}, bf16[256,1024]{1,0:T(8,128)(2,1)S(1)}, u32[]{:S(2)}, u32[]{:S(2)}) collective-permute-start(bf16[256,1024]{1,0:T(8,128)(2,1)S(1)} %constant_dynamic-slice_fusion.2), channel_id=1, source_target_pairs={{0,8},{1,57},{8,16},{9,1},{16,24},{17,9},{24,32},{25,17},{32,40},{... | collective-permute-start | bytes 1572872 | tf_op jit(solution)/shard_map/ppermute | solution.py:33
  8.5 1.2 %collective-permute-start.2 = (bf16[128,1024]{1,0:T(8,128)(2,1)}, bf16[128,1024]{1,0:T(8,128)(2,1)S(1)}, u32[]{:S(2)}, u32[]{:S(2)}) collective-permute-start(bf16[128,1024]{1,0:T(8,128)(2,1)} %centroids.1), channel_id=1, source_target_pairs={{0,64},{64,128},{128,192},{192,0},{1,65},{65,129},{129,193},{193,1... | collective-permute-start | bytes 786440 | tf_op jit(solution)/shard_map/ppermute | solution.py:21
  9.7 1.5 %collective-permute-start.1 = (bf16[128,1024]{1,0:T(8,128)(2,1)}, bf16[128,1024]{1,0:T(8,128)(2,1)S(1)}, u32[]{:S(2)}, u32[]{:S(2)}) collective-permute-start(bf16[128,1024]{1,0:T(8,128)(2,1)} %centroids.1), channel_id=1, source_target_pairs={{0,192},{64,0},{128,64},{192,128},{1,193},{65,1},{129,65},{193,129... | collective-permute-start | bytes 786440 | tf_op jit(solution)/shard_map/ppermute | solution.py:21
  11.2 4.5 %collective-permute-done.2.refs_4_ = bf16[128,1024]{1,0:T(8,128)(2,1)S(1)} collective-permute-done((bf16[128,1024]{1,0:T(8,128)(2,1)}, bf16[128,1024]{1,0:T(8,128)(2,1)S(1)}, u32[]{:S(2)}, u32[]{:S(2)}) %collective-permute-start.2) | collective-permute-done | bytes 262176 | tf_op jit(solution)/shard_map/ppermute | solution.py:21
  16.0 2.5 %collective-permute-start.3 = (bf16[256,1024]{1,0:T(8,128)(2,1)S(1)}, bf16[256,1024]{1,0:T(8,128)(2,1)S(1)}, u32[]{:S(2)}, u32[]{:S(2)}) collective-permute-start(bf16[256,1024]{1,0:T(8,128)(2,1)S(1)} %collective-permute-done.refs_9_.refs_4_), channel_id=1, source_target_pairs={{0,8},{1,57},{8,16},{9,1},{16,24},{17,9},{24,32},{25,17},{32,40},{... | collective-permute-start | bytes 1572872 | tf_op jit(solution)/shard_map/ppermute | solution.py:33
  18.5 2.7 %collective-permute-start.10 = (bf16[256,1024]{1,0:T(8,128)(2,1)S(1)}, bf16[256,1024]{1,0:T(8,128)(2,1)S(1)}, u32[]{:S(2)}, u32[]{:S(2)}) collective-permute-start(bf16[256,1024]{1,0:T(8,128)(2,1)S(1)} %collective-permute-done.refs_9_.refs_4_), channel_id=1, source_target_pairs={{0,2},{1,7},{2,0},{3,5},{4,6},{5,3},{6,4},{7,1},{8,10},{9,15},{10,... | collective-permute-start | bytes 1572872 | tf_op jit(solution)/shard_map/ppermute | solution.py:45
  21.3 2.4 %collective-permute-start.4 = (bf16[128,1024]{1,0:T(8,128)(2,1)S(1)}, bf16[128,1024]{1,0:T(8,128)(2,1)S(1)}, u32[]{:S(2)}, u32[]{:S(2)}) collective-permute-start(bf16[128,1024]{1,0:T(8,128)(2,1)S(1)} %collective-permute-done.1.refs_2_), channel_id=1, source_target_pairs={{0,192},{64,0},{128,64},{192,128},{1,193},{65,1},{129,65},{193,129... | collective-permute-start | bytes 786440 | tf_op jit(solution)/shard_map/ppermute | solution.py:21
  23.6 3.6 %collective-permute-done.4.refs_0_ = bf16[128,1024]{1,0:T(8,128)(2,1)S(1)} collective-permute-done((bf16[128,1024]{1,0:T(8,128)(2,1)S(1)}, bf16[128,1024]{1,0:T(8,128)(2,1)S(1)}, u32[]{:S(2)}, u32[]{:S(2)}) %collective-permute-start.4) | collective-permute-done | bytes 262176 | tf_op jit(solution)/shard_map/ppermute | solution.py:21
  27.2 2.2 %collective-permute-start.5 = (bf16[256,1024]{1,0:T(8,128)(2,1)S(1)}, bf16[256,1024]{1,0:T(8,128)(2,1)S(1)}, u32[]{:S(2)}, u32[]{:S(2)}) collective-permute-start(bf16[256,1024]{1,0:T(8,128)(2,1)S(1)} %collective-permute-done.3.refs_11_.refs_6_), channel_id=1, source_target_pairs={{0,8},{1,57},{8,16},{9,1},{16,24},{17,9},{24,32},{25,17},{32,40},{... | collective-permute-start | bytes 1572872 | tf_op jit(solution)/shard_map/ppermute | solution.py:33
  31.1 1.4 %collective-permute-done.8.refs_5_ = bf16[128,1024]{1,0:T(8,128)(2,1)S(1)} collective-permute-done((bf16[128,1024]{1,0:T(8,128)(2,1)S(1)}, bf16[128,1024]{1,0:T(8,128)(2,1)S(1)}, u32[]{:S(2)}, u32[]{:S(2)}) %collective-permute-start.8) | collective-permute-done | bytes 262176 | tf_op jit(solution)/shard_map/ppermute | solution.py:25
  32.8 2.8 %collective-permute-done.5.refs_2_.refs_8_ = bf16[256,1024]{1,0:T(8,128)(2,1)S(1)} collective-permute-done((bf16[256,1024]{1,0:T(8,128)(2,1)S(1)}, bf16[256,1024]{1,0:T(8,128)(2,1)S(1)}, u32[]{:S(2)}, u32[]{:S(2)}) %collective-permute-start.5) | collective-permute-done | bytes 524320 | tf_op jit(solution)/shard_map/ppermute | solution.py:33
  35.7 4.0 %collective-permute-start.14 = (bf16[128,1024]{1,0:T(8,128)(2,1)S(1)}, bf16[128,1024]{1,0:T(8,128)(2,1)S(1)}, u32[]{:S(2)}, u32[]{:S(2)}) collective-permute-start(bf16[128,1024]{1,0:T(8,128)(2,1)S(1)} %constant_dynamic-slice_fusion), channel_id=1, source_target_pairs={{0,10},{1,63},{2,8},{3,61},{4,14},{5,59},{6,12},{7,57},{8,18},{9,7... | collective-permute-start | bytes 786440 | tf_op jit(solution)/shard_map/ppermute | solution.py:59
  39.6 1.6 %collective-permute-start.12 = (bf16[256,1024]{1,0:T(8,128)(2,1)S(1)}, bf16[256,1024]{1,0:T(8,128)(2,1)S(1)}, u32[]{:S(2)}, u32[]{:S(2)}) collective-permute-start(bf16[256,1024]{1,0:T(8,128)(2,1)S(1)} %collective-permute-done.5.refs_2_.refs_8_), channel_id=1, source_target_pairs={{0,2},{1,7},{2,0},{3,5},{4,6},{5,3},{6,4},{7,1},{8,10},{9,15},{10,... | collective-permute-start | bytes 1572872 | tf_op jit(solution)/shard_map/ppermute | solution.py:45
  41.3 4.2 %shard_map.58 = (bf16[1024,1024]{1,0:T(8,128)(2,1)S(1)}, f32[1024,128]{1,0:T(8,128)S(1)}, f32[1024,1280]{1,0:T(8,128)S(1)}, f32[1,1280]{1,0:T(1,128)S(1)}) custom-call(bf16[128,1024]{1,0:T(8,128)(2,1)S(1)} %collective-permute-done.4.refs_0_, bf16[128,1024]{1,0:T(8,128)(2,1)S(1)} %collective-permute-done.6.refs_1_, ...), custom_call_target="tpu_custom_call" | custom-call | flops 5368709120 | bytes 9961472 | tf_op jit(solution)/shard_map/pallas_call | solution.py:229
  46.4 2.5 %collective-permute-done.12.refs_2_.refs_9_ = bf16[256,1024]{1,0:T(8,128)(2,1)S(1)} collective-permute-done((bf16[256,1024]{1,0:T(8,128)(2,1)S(1)}, bf16[256,1024]{1,0:T(8,128)(2,1)S(1)}, u32[]{:S(2)}, u32[]{:S(2)}) %collective-permute-start.12) | collective-permute-done | bytes 524320 | tf_op jit(solution)/shard_map/ppermute | solution.py:45
  48.9 1.7 %shard_map.60 = (f32[1024,512]{1,0:T(8,128)S(1)}, f32[1,512]{1,0:T(1,128)S(1)}) custom-call(bf16[1024,1024]{1,0:T(8,128)(2,1)S(1)} %get-tuple-element.70.refs_0_, f32[1024,128]{1,0:T(8,128)S(1)} %get-tuple-element.71.refs_1_, bf16[256,1024]{1,0:T(8,128)(2,1)S(1)} %collective-permute-done.12.refs_2_.refs_9_, ...), custom_call_target="tpu_custom_call" | custom-call | flops 2147483648 | bytes 5242880 | tf_op jit(solution)/shard_map/pallas_call | solution.py:229
  50.6 1.6 %collective-permute-start.17 = (f32[16,128]{1,0:T(8,128)S(1)}, f32[16,128]{1,0:T(8,128)S(1)}, u32[]{:S(2)}, u32[]{:S(2)}) collective-permute-start(f32[16,128]{1,0:T(8,128)S(1)} %shard_map.61.own), channel_id=1, source_target_pairs={{0,4},{2,6},{4,0},{6,2},{1,5},{3,7},{5,1},{7,3},{8,12},{10,14},{12... | collective-permute-start | bytes 24584 | tf_op jit(solution)/shard_map/ppermute | solution.py:37
  54.7 1.8 %collective-permute-done.15.refs_0_ = f32[16,128]{1,0:T(8,128)S(1)} collective-permute-done((f32[16,128]{1,0:T(8,128)S(1)}, f32[16,128]{1,0:T(8,128)S(1)}, u32[]{:S(2)}, u32[]{:S(2)}) %collective-permute-start.15) | collective-permute-done | bytes 8224 | tf_op jit(solution)/shard_map/ppermute | solution.py:37
  56.5 4.7 %collective-permute-start.18 = (f32[16,128]{1,0:T(8,128)S(1)}, f32[16,128]{1,0:T(8,128)S(1)}, u32[]{:S(2)}, u32[]{:S(2)}) collective-permute-start(f32[16,128]{1,0:T(8,128)S(1)} %shard_map.62.mine), channel_id=1, source_target_pairs={{0,1},{1,0},{2,3},{3,2},{4,5},{5,4},{6,7},{7,6},{8,9},{9,8},{10,11... | collective-permute-start | bytes 24584 | tf_op jit(solution)/shard_map/ppermute | solution.py:25
  62.9 1.8 %collective-permute-done.19.near = f32[4,8,128]{2,1,0:T(8,128)S(1)} collective-permute-done((f32[4,8,128]{2,1,0:T(8,128)S(1)}, f32[4,8,128]{2,1,0:T(8,128)S(1)}, u32[]{:S(2)}, u32[]{:S(2)}) %collective-permute-start.19) | collective-permute-done | bytes 16416 | tf_op jit(solution)/shard_map/ppermute | solution.py:33
  64.7 2.7 %collective-permute-start.20 = (f32[4,8,128]{2,1,0:T(8,128)S(1)}, f32[4,8,128]{2,1,0:T(8,128)S(1)}, u32[]{:S(2)}, u32[]{:S(2)}) collective-permute-start(f32[4,8,128]{2,1,0:T(8,128)S(1)} %collective-permute-done.19.near), channel_id=1, source_target_pairs={{0,1},{1,0},{2,3},{3,2},{4,5},{5,4},{6,7},{7,6},{8,9},{9,8},{10,11... | collective-permute-start | bytes 49160 | tf_op jit(solution)/shard_map/ppermute | solution.py:25
  68.3 1.8 %collective-permute-start.21 = (f32[4,8,128]{2,1,0:T(8,128)S(1)}, f32[4,8,128]{2,1,0:T(8,128)S(1)}, u32[]{:S(2)}, u32[]{:S(2)}) collective-permute-start(f32[4,8,128]{2,1,0:T(8,128)S(1)} %get-tuple-element.79), channel_id=1, source_target_pairs={{0,24},{1,41},{8,32},{9,49},{16,40},{17,57},{24,48},{25,1},{32,56}... | collective-permute-start | bytes 49160 | tf_op jit(solution)/shard_map/ppermute | solution.py:33
  70.0 2.7 %collective-permute-done.21.got = f32[4,8,128]{2,1,0:T(8,128)S(1)} collective-permute-done((f32[4,8,128]{2,1,0:T(8,128)S(1)}, f32[4,8,128]{2,1,0:T(8,128)S(1)}, u32[]{:S(2)}, u32[]{:S(2)}) %collective-permute-start.21) | collective-permute-done | bytes 16416 | tf_op jit(solution)/shard_map/ppermute | solution.py:33
  72.7 2.7 %collective-permute-start.22 = (f32[4,8,128]{2,1,0:T(8,128)S(1)}, f32[4,8,128]{2,1,0:T(8,128)S(1)}, u32[]{:S(2)}, u32[]{:S(2)}) collective-permute-start(f32[4,8,128]{2,1,0:T(8,128)S(1)} %collective-permute-done.21.got), channel_id=1, source_target_pairs={{0,1},{1,0},{2,3},{3,2},{4,5},{5,4},{6,7},{7,6},{8,9},{9,8},{10,11... | collective-permute-start | bytes 49160 | tf_op jit(solution)/shard_map/ppermute | solution.py:25
  76.9 1.8 %shard_map.66 = bf16[432,1024]{1,0:T(8,128)(2,1)S(1)} custom-call(f32[1,2048]{1,0:T(1,128)S(1)} %get-tuple-element.87.energy, f32[1024,1280]{1,0:T(8,128)S(1)} %get-tuple-element.81.refs_0_, f32[1024,256]{1,0:T(8,128)S(1)} %get-tuple-element.82.refs_1_, f32[1024,512]{1,0:T(8,128)S(1)} %get-tuple-element.83.refs_2_, bf16[256,1024]{1,0:T(8,128)(2,1)S(1)} %bitcast.9, ...), custom_call_target="tpu_custom_call" | custom-call | flops 1610612736 | bytes 7340032 | tf_op jit(solution)/shard_map/pallas_call | solution.py:308
  79.2 1.8 %shard_map.67 = (f32[384,1024]{1,0:T(8,128)S(1)}, f32[48,128]{1,0:T(8,128)S(1)}) custom-call(f32[1,2048]{1,0:T(1,128)S(1)} %get-tuple-element.87.energy, f32[1024,1280]{1,0:T(8,128)S(1)} %get-tuple-element.81.refs_0_, f32[1024,256]{1,0:T(8,128)S(1)} %get-tuple-element.82.refs_1_, f32[1024,512]{1,0:T(8,128)S(1)} %get-tuple-element.83.refs_2_, ...), custom_call_target="tpu_custom_call" | custom-call | flops 1610612736 | bytes 7340032 | tf_op jit(solution)/shard_map/pallas_call | solution.py:308
  81.4 2.5 %collective-permute-start.24 = (bf16[144,1024]{1,0:T(8,128)(2,1)S(1)}, bf16[144,1024]{1,0:T(8,128)(2,1)S(1)}, u32[]{:S(2)}, u32[]{:S(2)}) collective-permute-start(bf16[144,1024]{1,0:T(8,128)(2,1)S(1)} %get-tuple-element.86), channel_id=1, source_target_pairs={{0,128},{64,192},{128,0},{192,64},{1,129},{65,193},{129,1},{193,65... | collective-permute-start | bytes 884744 | tf_op jit(solution)/shard_map/ppermute | solution.py:21
  83.9 1.5 %collective-permute-start.26 = (bf16[144,1024]{1,0:T(8,128)(2,1)S(1)}, bf16[144,1024]{1,0:T(8,128)(2,1)S(1)}, u32[]{:S(2)}, u32[]{:S(2)}) collective-permute-start(bf16[144,1024]{1,0:T(8,128)(2,1)S(1)} %get-tuple-element.92), channel_id=1, source_target_pairs={{0,64},{64,128},{128,192},{192,0},{1,65},{65,129},{129,193},{193,1... | collective-permute-start | bytes 884744 | tf_op jit(solution)/shard_map/ppermute | solution.py:21
  86.6 4.7 %collective-permute-done.24.one = bf16[144,1024]{1,0:T(8,128)(2,1)S(1)} collective-permute-done((bf16[144,1024]{1,0:T(8,128)(2,1)S(1)}, bf16[144,1024]{1,0:T(8,128)(2,1)S(1)}, u32[]{:S(2)}, u32[]{:S(2)}) %collective-permute-start.24) | collective-permute-done | bytes 294944 | tf_op jit(solution)/shard_map/ppermute | solution.py:21
  91.3 1.3 %shard_map.69 = (bf16[144,1024]{1,0:T(8,128)(2,1)S(1)}, f32[128,1024]{1,0:T(8,128)S(1)}, f32[16,128]{1,0:T(8,128)S(1)}) custom-call(f32[1,2048]{1,0:T(1,128)S(1)} %get-tuple-element.87.energy, f32[1024,1280]{1,0:T(8,128)S(1)} %get-tuple-element.81.refs_0_, f32[1024,256]{1,0:T(8,128)S(1)} %get-tuple-element.82.refs_1_, ...), custom_call_target="tpu_custom_call" | custom-call | flops 1073741824 | bytes 6291456 | tf_op jit(solution)/shard_map/pallas_call | solution.py:308
  92.6 2.0 %collective-permute-start.25 = (bf16[144,1024]{1,0:T(8,128)(2,1)S(1)}, bf16[144,1024]{1,0:T(8,128)(2,1)S(1)}, u32[]{:S(2)}, u32[]{:S(2)}) collective-permute-start(bf16[144,1024]{1,0:T(8,128)(2,1)S(1)} %get-tuple-element.90), channel_id=1, source_target_pairs={{0,1},{1,0},{2,3},{3,2},{4,5},{5,4},{6,7},{7,6},{8,9},{9,8},{10,11... | collective-permute-start | bytes 884744 | tf_op jit(solution)/shard_map/ppermute | solution.py:25
  94.6 3.6 %collective-permute-done.26.two = bf16[144,1024]{1,0:T(8,128)(2,1)S(1)} collective-permute-done((bf16[144,1024]{1,0:T(8,128)(2,1)S(1)}, bf16[144,1024]{1,0:T(8,128)(2,1)S(1)}, u32[]{:S(2)}, u32[]{:S(2)}) %collective-permute-start.26) | collective-permute-done | bytes 294944 | tf_op jit(solution)/shard_map/ppermute | solution.py:21
  (49 shorter events, 14.6 us)
Async XLA Ops:
  0.6 1.2 %copy-start = (bf16[512,1024]{1,0:T(8,128)(2,1)S(1)}, bf16[512,1024]{1,0:T(8,128)(2,1)}, u32[]{:S(2)}) copy-start(bf16[512,1024]{1,0:T(8,128)(2,1)} %param.3) | copy-start | bytes 3145732
  0.6 40.6 %copy-start.1 = (bf16[128,1024]{1,0:T(8,128)(2,1)S(1)}, bf16[128,1024]{1,0:T(8,128)(2,1)}, u32[]{:S(2)}) copy-start(bf16[128,1024]{1,0:T(8,128)(2,1)} %centroids.1) | copy-start | bytes 786436
  2.0 14.0 %collective-permute-start = (bf16[256,1024]{1,0:T(8,128)(2,1)S(1)}, bf16[256,1024]{1,0:T(8,128)(2,1)S(1)}, u32[]{:S(2)}, u32[]{:S(2)}) collective-permute-start(bf16[256,1024]{1,0:T(8,128)(2,1)S(1)} %constant_dynamic-slice_fusion.2), channel_id=1, source_target_pairs={{0,8},{1,57},{8,16},{9,1},{16,24},{17,9},{24,32},{25,17},{32,40},{... | collective-permute-start | bytes 1572872 | tf_op jit(solution)/shard_map/ppermute | solution.py:33
  8.5 7.2 %collective-permute-start.2 = (bf16[128,1024]{1,0:T(8,128)(2,1)}, bf16[128,1024]{1,0:T(8,128)(2,1)S(1)}, u32[]{:S(2)}, u32[]{:S(2)}) collective-permute-start(bf16[128,1024]{1,0:T(8,128)(2,1)} %centroids.1), channel_id=1, source_target_pairs={{0,64},{64,128},{128,192},{192,0},{1,65},{65,129},{129,193},{193,1... | collective-permute-start | bytes 786440 | tf_op jit(solution)/shard_map/ppermute | solution.py:21
  9.7 6.3 %collective-permute-start.1 = (bf16[128,1024]{1,0:T(8,128)(2,1)}, bf16[128,1024]{1,0:T(8,128)(2,1)S(1)}, u32[]{:S(2)}, u32[]{:S(2)}) collective-permute-start(bf16[128,1024]{1,0:T(8,128)(2,1)} %centroids.1), channel_id=1, source_target_pairs={{0,192},{64,0},{128,64},{192,128},{1,193},{65,1},{129,65},{193,129... | collective-permute-start | bytes 786440 | tf_op jit(solution)/shard_map/ppermute | solution.py:21
  16.0 11.3 %collective-permute-start.3 = (bf16[256,1024]{1,0:T(8,128)(2,1)S(1)}, bf16[256,1024]{1,0:T(8,128)(2,1)S(1)}, u32[]{:S(2)}, u32[]{:S(2)}) collective-permute-start(bf16[256,1024]{1,0:T(8,128)(2,1)S(1)} %collective-permute-done.refs_9_.refs_4_), channel_id=1, source_target_pairs={{0,8},{1,57},{8,16},{9,1},{16,24},{17,9},{24,32},{25,17},{32,40},{... | collective-permute-start | bytes 1572872 | tf_op jit(solution)/shard_map/ppermute | solution.py:33
  18.5 10.9 %collective-permute-start.10 = (bf16[256,1024]{1,0:T(8,128)(2,1)S(1)}, bf16[256,1024]{1,0:T(8,128)(2,1)S(1)}, u32[]{:S(2)}, u32[]{:S(2)}) collective-permute-start(bf16[256,1024]{1,0:T(8,128)(2,1)S(1)} %collective-permute-done.refs_9_.refs_4_), channel_id=1, source_target_pairs={{0,2},{1,7},{2,0},{3,5},{4,6},{5,3},{6,4},{7,1},{8,10},{9,15},{10,... | collective-permute-start | bytes 1572872 | tf_op jit(solution)/shard_map/ppermute | solution.py:45
  21.3 6.0 %collective-permute-start.4 = (bf16[128,1024]{1,0:T(8,128)(2,1)S(1)}, bf16[128,1024]{1,0:T(8,128)(2,1)S(1)}, u32[]{:S(2)}, u32[]{:S(2)}) collective-permute-start(bf16[128,1024]{1,0:T(8,128)(2,1)S(1)} %collective-permute-done.1.refs_2_), channel_id=1, source_target_pairs={{0,192},{64,0},{128,64},{192,128},{1,193},{65,1},{129,65},{193,129... | collective-permute-start | bytes 786440 | tf_op jit(solution)/shard_map/ppermute | solution.py:21
  23.6 7.4 %collective-permute-start.9 = (bf16[128,1024]{1,0:T(8,128)(2,1)}, bf16[128,1024]{1,0:T(8,128)(2,1)S(1)}, u32[]{:S(2)}, u32[]{:S(2)}) collective-permute-start(bf16[128,1024]{1,0:T(8,128)(2,1)} %centroids.1), channel_id=1, source_target_pairs={{0,1},{1,0},{2,3},{3,2},{4,5},{5,4},{6,7},{7,6},{8,9},{9,8},{10,11... | collective-permute-start | bytes 786440 | tf_op jit(solution)/shard_map/ppermute | solution.py:25
  27.2 8.3 %collective-permute-start.5 = (bf16[256,1024]{1,0:T(8,128)(2,1)S(1)}, bf16[256,1024]{1,0:T(8,128)(2,1)S(1)}, u32[]{:S(2)}, u32[]{:S(2)}) collective-permute-start(bf16[256,1024]{1,0:T(8,128)(2,1)S(1)} %collective-permute-done.3.refs_11_.refs_6_), channel_id=1, source_target_pairs={{0,8},{1,57},{8,16},{9,1},{16,24},{17,9},{24,32},{25,17},{32,40},{... | collective-permute-start | bytes 1572872 | tf_op jit(solution)/shard_map/ppermute | solution.py:33
  29.5 11.8 %collective-permute-start.11 = (bf16[256,1024]{1,0:T(8,128)(2,1)S(1)}, bf16[256,1024]{1,0:T(8,128)(2,1)S(1)}, u32[]{:S(2)}, u32[]{:S(2)}) collective-permute-start(bf16[256,1024]{1,0:T(8,128)(2,1)S(1)} %collective-permute-done.3.refs_11_.refs_6_), channel_id=1, source_target_pairs={{0,2},{1,7},{2,0},{3,5},{4,6},{5,3},{6,4},{7,1},{8,10},{9,15},{10,... | collective-permute-start | bytes 1572872 | tf_op jit(solution)/shard_map/ppermute | solution.py:45
  30.5 1.9 %collective-permute-start.7 = (bf16[128,1024]{1,0:T(8,128)(2,1)S(1)}, bf16[128,1024]{1,0:T(8,128)(2,1)S(1)}, u32[]{:S(2)}, u32[]{:S(2)}) collective-permute-start(bf16[128,1024]{1,0:T(8,128)(2,1)S(1)} %collective-permute-done.1.refs_2_), channel_id=1, source_target_pairs={{0,1},{1,0},{2,3},{3,2},{4,5},{5,4},{6,7},{7,6},{8,9},{9,8},{10,11... | collective-permute-start | bytes 786440 | tf_op jit(solution)/shard_map/ppermute | solution.py:25
  30.5 1.9 %collective-permute-start.8 = (bf16[128,1024]{1,0:T(8,128)(2,1)S(1)}, bf16[128,1024]{1,0:T(8,128)(2,1)S(1)}, u32[]{:S(2)}, u32[]{:S(2)}) collective-permute-start(bf16[128,1024]{1,0:T(8,128)(2,1)S(1)} %collective-permute-done.2.refs_4_), channel_id=1, source_target_pairs={{0,1},{1,0},{2,3},{3,2},{4,5},{5,4},{6,7},{7,6},{8,9},{9,8},{10,11... | collective-permute-start | bytes 786440 | tf_op jit(solution)/shard_map/ppermute | solution.py:25
  31.0 1.8 %collective-permute-start.6 = (bf16[128,1024]{1,0:T(8,128)(2,1)S(1)}, bf16[128,1024]{1,0:T(8,128)(2,1)S(1)}, u32[]{:S(2)}, u32[]{:S(2)}) collective-permute-start(bf16[128,1024]{1,0:T(8,128)(2,1)S(1)} %collective-permute-done.4.refs_0_), channel_id=1, source_target_pairs={{0,1},{1,0},{2,3},{3,2},{4,5},{5,4},{6,7},{7,6},{8,9},{9,8},{10,11... | collective-permute-start | bytes 786440 | tf_op jit(solution)/shard_map/ppermute | solution.py:25
  35.7 10.7 %collective-permute-start.14 = (bf16[128,1024]{1,0:T(8,128)(2,1)S(1)}, bf16[128,1024]{1,0:T(8,128)(2,1)S(1)}, u32[]{:S(2)}, u32[]{:S(2)}) collective-permute-start(bf16[128,1024]{1,0:T(8,128)(2,1)S(1)} %constant_dynamic-slice_fusion), channel_id=1, source_target_pairs={{0,10},{1,63},{2,8},{3,61},{4,14},{5,59},{6,12},{7,57},{8,18},{9,7... | collective-permute-start | bytes 786440 | tf_op jit(solution)/shard_map/ppermute | solution.py:59
  39.6 6.8 %collective-permute-start.13 = (bf16[128,1024]{1,0:T(8,128)(2,1)S(1)}, bf16[128,1024]{1,0:T(8,128)(2,1)S(1)}, u32[]{:S(2)}, u32[]{:S(2)}) collective-permute-start(bf16[128,1024]{1,0:T(8,128)(2,1)S(1)} %constant_dynamic-slice_fusion), channel_id=1, source_target_pairs={{0,8},{1,57},{8,16},{9,1},{16,24},{17,9},{24,32},{25,17},{32,40},{... | collective-permute-start | bytes 786440 | tf_op jit(solution)/shard_map/ppermute | solution.py:33
  39.6 9.2 %collective-permute-start.12 = (bf16[256,1024]{1,0:T(8,128)(2,1)S(1)}, bf16[256,1024]{1,0:T(8,128)(2,1)S(1)}, u32[]{:S(2)}, u32[]{:S(2)}) collective-permute-start(bf16[256,1024]{1,0:T(8,128)(2,1)S(1)} %collective-permute-done.5.refs_2_.refs_8_), channel_id=1, source_target_pairs={{0,2},{1,7},{2,0},{3,5},{4,6},{5,3},{6,4},{7,1},{8,10},{9,15},{10,... | collective-permute-start | bytes 1572872 | tf_op jit(solution)/shard_map/ppermute | solution.py:45
  50.6 4.1 %collective-permute-start.17 = (f32[16,128]{1,0:T(8,128)S(1)}, f32[16,128]{1,0:T(8,128)S(1)}, u32[]{:S(2)}, u32[]{:S(2)}) collective-permute-start(f32[16,128]{1,0:T(8,128)S(1)} %shard_map.61.own), channel_id=1, source_target_pairs={{0,4},{2,6},{4,0},{6,2},{1,5},{3,7},{5,1},{7,3},{8,12},{10,14},{12... | collective-permute-start | bytes 24584 | tf_op jit(solution)/shard_map/ppermute | solution.py:37
  52.1 2.5 %collective-permute-start.16 = (f32[16,128]{1,0:T(8,128)S(1)}, f32[16,128]{1,0:T(8,128)S(1)}, u32[]{:S(2)}, u32[]{:S(2)}) collective-permute-start(f32[16,128]{1,0:T(8,128)S(1)} %shard_map.61.own), channel_id=1, source_target_pairs={{0,6},{2,0},{4,2},{6,4},{1,7},{3,1},{5,3},{7,5},{8,14},{10,8},{12,... | collective-permute-start | bytes 24584 | tf_op jit(solution)/shard_map/ppermute | solution.py:37
  52.5 4.0 %collective-permute-start.15 = (f32[16,128]{1,0:T(8,128)S(1)}, f32[16,128]{1,0:T(8,128)S(1)}, u32[]{:S(2)}, u32[]{:S(2)}) collective-permute-start(f32[16,128]{1,0:T(8,128)S(1)} %shard_map.61.own), channel_id=1, source_target_pairs={{0,2},{2,4},{4,6},{6,0},{1,3},{3,5},{5,7},{7,1},{8,10},{10,12},{12... | collective-permute-start | bytes 24584 | tf_op jit(solution)/shard_map/ppermute | solution.py:37
  56.5 5.5 %collective-permute-start.18 = (f32[16,128]{1,0:T(8,128)S(1)}, f32[16,128]{1,0:T(8,128)S(1)}, u32[]{:S(2)}, u32[]{:S(2)}) collective-permute-start(f32[16,128]{1,0:T(8,128)S(1)} %shard_map.62.mine), channel_id=1, source_target_pairs={{0,1},{1,0},{2,3},{3,2},{4,5},{5,4},{6,7},{7,6},{8,9},{9,8},{10,11... | collective-permute-start | bytes 24584 | tf_op jit(solution)/shard_map/ppermute | solution.py:25
  62.0 2.7 %collective-permute-start.19 = (f32[4,8,128]{2,1,0:T(8,128)S(1)}, f32[4,8,128]{2,1,0:T(8,128)S(1)}, u32[]{:S(2)}, u32[]{:S(2)}) collective-permute-start(f32[4,8,128]{2,1,0:T(8,128)S(1)} %shard_map.63.block), channel_id=1, source_target_pairs={{0,8},{1,57},{8,16},{9,1},{16,24},{17,9},{24,32},{25,17},{32,40},{... | collective-permute-start | bytes 49160 | tf_op jit(solution)/shard_map/ppermute | solution.py:33
  64.7 3.5 %collective-permute-start.20 = (f32[4,8,128]{2,1,0:T(8,128)S(1)}, f32[4,8,128]{2,1,0:T(8,128)S(1)}, u32[]{:S(2)}, u32[]{:S(2)}) collective-permute-start(f32[4,8,128]{2,1,0:T(8,128)S(1)} %collective-permute-done.19.near), channel_id=1, source_target_pairs={{0,1},{1,0},{2,3},{3,2},{4,5},{5,4},{6,7},{7,6},{8,9},{9,8},{10,11... | collective-permute-start | bytes 49160 | tf_op jit(solution)/shard_map/ppermute | solution.py:25
  68.3 4.5 %collective-permute-start.21 = (f32[4,8,128]{2,1,0:T(8,128)S(1)}, f32[4,8,128]{2,1,0:T(8,128)S(1)}, u32[]{:S(2)}, u32[]{:S(2)}) collective-permute-start(f32[4,8,128]{2,1,0:T(8,128)S(1)} %get-tuple-element.79), channel_id=1, source_target_pairs={{0,24},{1,41},{8,32},{9,49},{16,40},{17,57},{24,48},{25,1},{32,56}... | collective-permute-start | bytes 49160 | tf_op jit(solution)/shard_map/ppermute | solution.py:33
  72.7 3.5 %collective-permute-start.22 = (f32[4,8,128]{2,1,0:T(8,128)S(1)}, f32[4,8,128]{2,1,0:T(8,128)S(1)}, u32[]{:S(2)}, u32[]{:S(2)}) collective-permute-start(f32[4,8,128]{2,1,0:T(8,128)S(1)} %collective-permute-done.21.got), channel_id=1, source_target_pairs={{0,1},{1,0},{2,3},{3,2},{4,5},{5,4},{6,7},{7,6},{8,9},{9,8},{10,11... | collective-permute-start | bytes 49160 | tf_op jit(solution)/shard_map/ppermute | solution.py:25
  78.7 2.5 %collective-permute-start.23 = (bf16[432,1024]{1,0:T(8,128)(2,1)S(1)}, bf16[432,1024]{1,0:T(8,128)(2,1)S(1)}, u32[]{:S(2)}, u32[]{:S(2)}) collective-permute-start(bf16[432,1024]{1,0:T(8,128)(2,1)S(1)} %shard_map.66), channel_id=1, source_target_pairs={{0,1},{1,0},{2,3},{3,2},{4,5},{5,4},{6,7},{7,6},{8,9},{9,8},{10,11... | collective-permute-start | bytes 2654216 | tf_op jit(solution)/shard_map/ppermute | solution.py:25
  81.4 9.9 %collective-permute-start.24 = (bf16[144,1024]{1,0:T(8,128)(2,1)S(1)}, bf16[144,1024]{1,0:T(8,128)(2,1)S(1)}, u32[]{:S(2)}, u32[]{:S(2)}) collective-permute-start(bf16[144,1024]{1,0:T(8,128)(2,1)S(1)} %get-tuple-element.86), channel_id=1, source_target_pairs={{0,128},{64,192},{128,0},{192,64},{1,129},{65,193},{129,1},{193,65... | collective-permute-start | bytes 884744 | tf_op jit(solution)/shard_map/ppermute | solution.py:21
  83.9 14.3 %collective-permute-start.26 = (bf16[144,1024]{1,0:T(8,128)(2,1)S(1)}, bf16[144,1024]{1,0:T(8,128)(2,1)S(1)}, u32[]{:S(2)}, u32[]{:S(2)}) collective-permute-start(bf16[144,1024]{1,0:T(8,128)(2,1)S(1)} %get-tuple-element.92), channel_id=1, source_target_pairs={{0,64},{64,128},{128,192},{192,0},{1,65},{65,129},{129,193},{193,1... | collective-permute-start | bytes 884744 | tf_op jit(solution)/shard_map/ppermute | solution.py:21
  85.5 13.2 %copy-start.2 = (f32[128]{0:T(128)S(1)}, f32[128]{0:T(128)}, u32[]{:S(2)}) copy-start(f32[128]{0:T(128)} %param.5) | copy-start | bytes 1540
  85.5 13.1 %collective-permute-start.27 = (bf16[144,1024]{1,0:T(8,128)(2,1)S(1)}, bf16[144,1024]{1,0:T(8,128)(2,1)S(1)}, u32[]{:S(2)}, u32[]{:S(2)}) collective-permute-start(bf16[144,1024]{1,0:T(8,128)(2,1)S(1)} %get-tuple-element.93), channel_id=1, source_target_pairs={{0,192},{64,0},{128,64},{192,128},{1,193},{65,1},{129,65},{193,129... | collective-permute-start | bytes 884744 | tf_op jit(solution)/shard_map/ppermute | solution.py:21
  92.6 6.0 %collective-permute-start.25 = (bf16[144,1024]{1,0:T(8,128)(2,1)S(1)}, bf16[144,1024]{1,0:T(8,128)(2,1)S(1)}, u32[]{:S(2)}, u32[]{:S(2)}) collective-permute-start(bf16[144,1024]{1,0:T(8,128)(2,1)S(1)} %get-tuple-element.90), channel_id=1, source_target_pairs={{0,1},{1,0},{2,3},{3,2},{4,5},{5,4},{6,7},{7,6},{8,9},{9,8},{10,11... | collective-permute-start | bytes 884744 | tf_op jit(solution)/shard_map/ppermute | solution.py:25
